TPU v7x, 32 devices: a whole 2x2x4 slice. The times are simulated.
32 devices in a mesh: lon: 16 (over z, x, core), lat: 2 (over y).
Axes of the slice: x: 2, y: 2, z: 4, core: 2. Of those that a mesh axis runs over, the one named last changes fastest.
Arguments:
- fields: bfloat16 [32, 2880, 640], P('lat', 'lon'), may hold values from -6 to 6
- owner_slot: int32 [32], replicated, may hold values from 0 to 31, as said below
- widths: int32 [32], replicated, may hold values from 90 to 360, as said below
- tap_weights: bfloat16 [32, 2880], replicated, may hold values from -0.21875 to 0.21875
Outputs:
- filtered: bfloat16 [32, 2880, 640], P('lat', 'lon')
Inputs may be any that keep to these rules, and one draw needn't show every extreme that they name: `owner_slot`: a permutation of the 32 rows; the 16 rows of each band of 16 rows are sent to every band of positions in equal numbers. `widths`: some row has the largest and some row the smallest value.
All inputs are finite; a program needn't handle non-finite values.
Results may differ from a plain program's by a relative error of at most 0.001.
Values may be sent and summed in bfloat16 or wider, within the bound.
No kernel may reach another device: no remote copies, remote signals or barrier semaphores. Data moves between devices by JAX's collectives and lax.ppermute only.
A program may use at most 128 MiB of HBM per device.

v0:
```python
import jax
import jax.numpy as jnp
from jax import lax
from jax.sharding import PartitionSpec as P


def from_behind(x, axis, by):
    count = lax.axis_size(axis)
    return lax.ppermute(x, axis, [(i, (i + by) % count) for i in range(count)])


def body(fields, owner_slot, widths, tap_weights):
    lat_dev, lon_dev, channels = fields.shape
    n_lon = lax.axis_size("lon")
    n_lat = lax.axis_size("lat")
    circle = lon_dev * n_lon
    reach_dev = n_lon // 8
    my_band = lax.axis_index("lat")
    home_rows = my_band * lat_dev + jnp.arange(lat_dev, dtype=jnp.int32)
    dest_band = owner_slot // lat_dev
    ordering = jnp.argsort(dest_band[home_rows], stable=True)
    others = jnp.argsort((dest_band != my_band).astype(jnp.int32), stable=True)[:lat_dev]
    slot_of = owner_slot[others] % lat_dev
    placed = jnp.argsort(slot_of)
    owner_rows = others[placed]
    outgoing = fields[ordering].reshape(n_lat, lat_dev // n_lat, lon_dev, channels)
    incoming = lax.all_to_all(outgoing, "lat", split_axis=0, concat_axis=0, tiled=True)
    panel_rows = incoming.reshape(lat_dev, lon_dev, channels)[placed]
    offset = jnp.arange(circle, dtype=jnp.int32)
    distance = jnp.minimum(offset, circle - offset)
    active = jnp.where(
        distance[None, :] <= widths[owner_rows][:, None],
        tap_weights[owner_rows],
        jnp.zeros((), tap_weights.dtype),
    )
    columns = jnp.arange(lon_dev, dtype=jnp.int32)

    def sector_term(sector, sectors_off):
        tap_index = (sectors_off * lon_dev + columns[None, :] - columns[:, None]) % circle
        tap_block = jnp.take(active, tap_index, axis=1)
        return jnp.einsum("sim,smc->sic", tap_block, sector, preferred_element_type=jnp.float32)

    farthest = from_behind(panel_rows, "lon", -reach_dev)

    def advance(t, carry):
        summed, sector = carry
        sector = from_behind(sector, "lon", 1)
        return (summed + sector_term(sector, reach_dev - t), sector)

    summed = sector_term(farthest, reach_dev)
    summed, farthest = lax.fori_loop(1, 2 * reach_dev + 1, advance, (summed, farthest))
    return (panel_rows.astype(jnp.float32) + summed).astype(jnp.bfloat16)


def solution(mesh):
    in_specs = (P("lat", "lon", None), P(), P(), P())
    out_specs = P("lat", "lon", None)
    return jax.shard_map(body, mesh=mesh, in_specs=in_specs, out_specs=out_specs, check_vma=False)
```

profile of v0, /device:TPU:0, one launch (start us, length us, event | category | flops | bytes accessed | tf_op | source)
XLA Modules:
  0.0 536.5 jit_solution(12879871436495577216)
XLA Ops:
  0.0 0.7 compare_convert_fusion
  0.7 0.7 gather_fusion.1
  1.4 1.3 sort.51
  2.7 11.1 %gather_fusion.2 = bf16[16,180,640]{2,0,1:T(8,128)(2,1)} fusion(bf16[16,180,640]{2,0,1:T(8,128)(2,1)} %param.8, s32[1024]{0:T(1024)S(1)} %pad_clamp_fusion.5), kind=kCustom, calls=%fused_computation.3 | custom fusion | bytes 7372864 | tf_op jit(solution)/shard_map/gather | solution.py:26
  13.8 4.2 copy.18
  17.9 5.5 %all-to-all-start = ((bf16[2,8,180,640]{3,1,2,0:T(8,128)(2,1)}), bf16[2,8,180,640]{3,1,2,0:T(8,128)(2,1)}, u32[]{:S(2)}, u32[]{:S(2)}) async-start(bf16[2,8,180,640]{3,1,2,0:T(8,128)(2,1)} %copy.18), calls=%async_computation | async-start | bytes 7372800 | tf_op jit(solution)/shard_map/all_to_all | solution.py:27
  23.5 1.6 sort.52
  25.1 0.7 gather_fusion.3
  25.8 1.3 sort.53
  27.1 39.9 %all-to-all-done = bf16[2,8,180,640]{3,1,2,0:T(8,128)(2,1)} async-done(((bf16[2,8,180,640]{3,1,2,0:T(8,128)(2,1)}), bf16[2,8,180,640]{3,1,2,0:T(8,128)(2,1)}, u32[]{:S(2)}, u32[]{:S(2)}) %all-to-all-start) | async-done | bytes 3686432 | tf_op jit(solution)/shard_map/all_to_all | solution.py:27
  66.9 4.3 copy.19
  71.3 5.0 gather_fusion.4
  76.3 4.4 copy.22
  80.6 4.7 collective-permute-start.1
  85.4 0.7 gather_fusion.5
  86.1 0.6 gather_fusion.7
  86.7 0.7 gather_fusion.6
  87.4 0.1 compare_select_fusion.2
  87.5 0.4 copy.20
  87.9 0.1 compare_select_fusion.1
  88.0 0.2 reshape.146
  88.3 65.3 %gather_fusion.8 = bf16[32400,16]{1,0:T(8,128)(2,1)} fusion(bf16[16,2880]{0,1:T(8,128)(2,1)S(1)} %copy.20, s32[32768]{0:T(1024)S(1)} %pad_clamp_fusion.1), kind=kCustom, calls=%fused_computation.clone | custom fusion | bytes 2203200 | tf_op jit(solution)/shard_map/jit(_take)/gather | solution.py:40
  153.5 7.0 %copy.21 = bf16[32400,16]{0,1:T(8,128)(2,1)S(1)} copy(bf16[32400,16]{1,0:T(8,128)(2,1)} %gather_fusion.8) | data formatting | bytes 2073600 | tf_op jit(solution)/shard_map/jit(_take)/gather | solution.py:40
  160.6 2.5 reshape.149
  163.1 0.2 compare_and_fusion.1
  163.3 0.5 collective-permute-done.1
  163.8 7.1 %fusion.16 = f32[16,180,640]{2,1,0:T(8,128)} fusion(bf16[16,180,640]{2,0,1:T(8,128)(2,1)} %collective-permute-done.1, bf16[180,180,16]{1,0,2:T(8,128)(2,1)S(1)} %reshape.149, pred[180,180]{1,0:T(8,128)(4,1)S(1)} %compare_and_fusion.1), kind=kOutput, calls=%fused_computation.29 | convolution fusion | flops 664070400 | bytes 12128400 | tf_op jit(solution)/shard_map/sim,smc->sic/dot_general | solution.py:41
  170.9 358.3 %while.19 = (s32[]{:T(128)}, f32[16,180,640]{2,1,0:T(8,128)}, bf16[16,180,640]{2,0,1:T(8,128)(2,1)}, bf16[16,2880]{0,1:T(8,128)(2,1)S(1)}, s32[]{:T(128)}, /*index=5*/s32[]{:T(128)}, s32[]{:T(128)}) while((s32[]{:T(128)}, f32[16,180,640]{2,1,0:T(8,128)}, bf16[16,180,640]{2,0,1:T(8,128)(2,1)}, ...), condition=%wide.region_4.6_spmd.clone.clone, body=%wide.region_3.5_spmd.clone.clone.sunk | while | flops 666691776 | bytes 48654176 | solution.py:51
  170.9 0.1 compare_select_fusion.14
  171.0 0.2 reshape.156
  171.3 65.3 %gather_fusion = bf16[32400,16]{1,0:T(8,128)(2,1)} fusion(bf16[16,2880]{0,1:T(8,128)(2,1)S(1)} %get-tuple-element.239, s32[32768]{0:T(1024)S(1)} %pad_clamp_fusion.8), kind=kCustom, calls=%fused_computation.1.clone.clone.1 | custom fusion | bytes 2203200 | tf_op jit(solution)/shard_map/while/body/eval_jaxpr/jit(_take)/gather | solution.py:40
  236.5 7.0 %copy.35 = bf16[32400,16]{0,1:T(8,128)(2,1)S(1)} copy(bf16[32400,16]{1,0:T(8,128)(2,1)} %gather_fusion) | data formatting | bytes 2073600 | tf_op jit(solution)/shard_map/while/body/eval_jaxpr/jit(_take)/gather | solution.py:40
  243.5 2.5 reshape.157
  246.1 0.2 compare_and_fusion.3
  246.3 4.2 copy.44
  250.5 9.6 %fusion.35 = f32[16,180,640]{2,1,0:T(8,128)} fusion(f32[16,180,640]{2,1,0:T(8,128)} %get-tuple-element.230, bf16[16,180,640]{2,0,1:T(8,128)(2,1)} %collective-permute-done, bf16[180,180,16]{1,0,2:T(8,128)(2,1)S(1)} %reshape.157, pred[180,180]{1,0:T(8,128)(4,1)S(1)} %compare_and_fusion.3), kind=kOutput, calls=%fused_computation.12.clone.1 | convolution fusion | flops 665913600 | bytes 19501200 | tf_op jit(solution)/shard_map/while/body/eval_jaxpr/sim,smc->sic/dot_general | solution.py:41
  260.1 0.5 collective-permute-start
  260.6 0.1 compare_select_fusion.14
  260.7 0.2 reshape.156
  261.0 65.3 %gather_fusion = bf16[32400,16]{1,0:T(8,128)(2,1)} fusion(bf16[16,2880]{0,1:T(8,128)(2,1)S(1)} %get-tuple-element.239, s32[32768]{0:T(1024)S(1)} %pad_clamp_fusion.8), kind=kCustom, calls=%fused_computation.1.clone.clone.1 | custom fusion | bytes 2203200 | tf_op jit(solution)/shard_map/while/body/eval_jaxpr/jit(_take)/gather | solution.py:40
  326.2 7.0 %copy.35 = bf16[32400,16]{0,1:T(8,128)(2,1)S(1)} copy(bf16[32400,16]{1,0:T(8,128)(2,1)} %gather_fusion) | data formatting | bytes 2073600 | tf_op jit(solution)/shard_map/while/body/eval_jaxpr/jit(_take)/gather | solution.py:40
  333.3 2.5 reshape.157
  335.8 0.2 compare_and_fusion.3
  336.0 4.2 copy.44
  340.2 9.6 %fusion.35 = f32[16,180,640]{2,1,0:T(8,128)} fusion(f32[16,180,640]{2,1,0:T(8,128)} %get-tuple-element.230, bf16[16,180,640]{2,0,1:T(8,128)(2,1)} %collective-permute-done, bf16[180,180,16]{1,0,2:T(8,128)(2,1)S(1)} %reshape.157, pred[180,180]{1,0:T(8,128)(4,1)S(1)} %compare_and_fusion.3), kind=kOutput, calls=%fused_computation.12.clone.1 | convolution fusion | flops 665913600 | bytes 19501200 | tf_op jit(solution)/shard_map/while/body/eval_jaxpr/sim,smc->sic/dot_general | solution.py:41
  349.9 0.1 compare_select_fusion.14
  350.0 0.2 reshape.156
  350.2 65.3 %gather_fusion = bf16[32400,16]{1,0:T(8,128)(2,1)} fusion(bf16[16,2880]{0,1:T(8,128)(2,1)S(1)} %get-tuple-element.239, s32[32768]{0:T(1024)S(1)} %pad_clamp_fusion.8), kind=kCustom, calls=%fused_computation.1.clone.clone.1 | custom fusion | bytes 2203200 | tf_op jit(solution)/shard_map/while/body/eval_jaxpr/jit(_take)/gather | solution.py:40
  415.5 7.0 %copy.35 = bf16[32400,16]{0,1:T(8,128)(2,1)S(1)} copy(bf16[32400,16]{1,0:T(8,128)(2,1)} %gather_fusion) | data formatting | bytes 2073600 | tf_op jit(solution)/shard_map/while/body/eval_jaxpr/jit(_take)/gather | solution.py:40
  422.5 2.5 reshape.157
  425.1 0.2 compare_and_fusion.3
  425.3 4.2 copy.44
  429.5 9.6 %fusion.35 = f32[16,180,640]{2,1,0:T(8,128)} fusion(f32[16,180,640]{2,1,0:T(8,128)} %get-tuple-element.230, bf16[16,180,640]{2,0,1:T(8,128)(2,1)} %collective-permute-done, bf16[180,180,16]{1,0,2:T(8,128)(2,1)S(1)} %reshape.157, pred[180,180]{1,0:T(8,128)(4,1)S(1)} %compare_and_fusion.3), kind=kOutput, calls=%fused_computation.12.clone.1 | convolution fusion | flops 665913600 | bytes 19501200 | tf_op jit(solution)/shard_map/while/body/eval_jaxpr/sim,smc->sic/dot_general | solution.py:41
  439.1 0.8 collective-permute-start
  439.9 0.1 compare_select_fusion.14
  440.0 0.2 reshape.156
  440.3 65.3 %gather_fusion = bf16[32400,16]{1,0:T(8,128)(2,1)} fusion(bf16[16,2880]{0,1:T(8,128)(2,1)S(1)} %get-tuple-element.239, s32[32768]{0:T(1024)S(1)} %pad_clamp_fusion.8), kind=kCustom, calls=%fused_computation.1.clone.clone.1 | custom fusion | bytes 2203200 | tf_op jit(solution)/shard_map/while/body/eval_jaxpr/jit(_take)/gather | solution.py:40
  505.5 7.0 %copy.35 = bf16[32400,16]{0,1:T(8,128)(2,1)S(1)} copy(bf16[32400,16]{1,0:T(8,128)(2,1)} %gather_fusion) | data formatting | bytes 2073600 | tf_op jit(solution)/shard_map/while/body/eval_jaxpr/jit(_take)/gather | solution.py:40
  512.5 2.5 reshape.157
  515.1 0.2 compare_and_fusion.3
  515.3 4.2 copy.44
  519.5 9.6 %fusion.35 = f32[16,180,640]{2,1,0:T(8,128)} fusion(f32[16,180,640]{2,1,0:T(8,128)} %get-tuple-element.230, bf16[16,180,640]{2,0,1:T(8,128)(2,1)} %collective-permute-done, bf16[180,180,16]{1,0,2:T(8,128)(2,1)S(1)} %reshape.157, pred[180,180]{1,0:T(8,128)(4,1)S(1)} %compare_and_fusion.3), kind=kOutput, calls=%fused_computation.12.clone.1 | convolution fusion | flops 665913600 | bytes 19501200 | tf_op jit(solution)/shard_map/while/body/eval_jaxpr/sim,smc->sic/dot_general | solution.py:41
  529.1 5.0 add_convert_fusion
  534.1 2.3 copy.25
  (39 shorter events, 0.2 us)
Async XLA Ops:
  0.0 86.1 %copy-start = (bf16[32,2880]{1,0:T(8,128)(2,1)S(1)}, bf16[32,2880]{1,0:T(8,128)(2,1)}, u32[]{:S(2)}) copy-start(bf16[32,2880]{1,0:T(8,128)(2,1)} %param.11) | copy-start | bytes 552964
  17.9 7.2 %copy-start.2 = (s32[32]{0:T(128)S(1)}, s32[32]{0:T(128)}, u32[]{:S(2)}) copy-start(s32[32]{0:T(128)} %param.9) | copy-start | bytes 388
  17.9 49.0 %all-to-all-start = ((bf16[2,8,180,640]{3,1,2,0:T(8,128)(2,1)}), bf16[2,8,180,640]{3,1,2,0:T(8,128)(2,1)}, u32[]{:S(2)}, u32[]{:S(2)}) async-start(bf16[2,8,180,640]{3,1,2,0:T(8,128)(2,1)} %copy.18), calls=%async_computation | async-start | bytes 7372800 | tf_op jit(solution)/shard_map/all_to_all | solution.py:27
  76.3 10.4 %copy-start.3 = (s32[32]{0:T(128)S(1)}, s32[32]{0:T(128)}, u32[]{:S(2)}) copy-start(s32[32]{0:T(128)} %param.10) | copy-start | bytes 388
  80.6 83.1 %collective-permute-start.1 = (bf16[16,180,640]{2,0,1:T(8,128)(2,1)}, bf16[16,180,640]{2,0,1:T(8,128)(2,1)}, u32[]{:S(2)}, u32[]{:S(2)}) collective-permute-start(bf16[16,180,640]{2,0,1:T(8,128)(2,1)} %copy.22), channel_id=1, source_target_pairs={{0,28},{2,30},{4,0},{6,2},{8,4},{10,6},{12,8},{14,10},{16,12},{18,... | collective-permute-start | bytes 11059208 | tf_op jit(solution)/shard_map/ppermute | solution.py:9
  170.9 75.4 %collective-permute-start = (bf16[16,180,640]{2,0,1:T(8,128)(2,1)}, bf16[16,180,640]{2,0,1:T(8,128)(2,1)}, u32[]{:S(2)}, u32[]{:S(2)}) collective-permute-start(bf16[16,180,640]{2,0,1:T(8,128)(2,1)} %get-tuple-element.231), channel_id=1, source_target_pairs={{0,2},{2,4},{4,6},{6,8},{8,10},{10,12},{12,14},{14,16},{16,18},{18... | collective-permute-start | bytes 11059208 | tf_op jit(solution)/shard_map/while/body/eval_jaxpr/ppermute | solution.py:9
  260.1 75.9 %collective-permute-start = (bf16[16,180,640]{2,0,1:T(8,128)(2,1)}, bf16[16,180,640]{2,0,1:T(8,128)(2,1)}, u32[]{:S(2)}, u32[]{:S(2)}) collective-permute-start(bf16[16,180,640]{2,0,1:T(8,128)(2,1)} %get-tuple-element.231), channel_id=1, source_target_pairs={{0,2},{2,4},{4,6},{6,8},{8,10},{10,12},{12,14},{14,16},{16,18},{18... | collective-permute-start | bytes 11059208 | tf_op jit(solution)/shard_map/while/body/eval_jaxpr/ppermute | solution.py:9
  349.9 75.4 %collective-permute-start = (bf16[16,180,640]{2,0,1:T(8,128)(2,1)}, bf16[16,180,640]{2,0,1:T(8,128)(2,1)}, u32[]{:S(2)}, u32[]{:S(2)}) collective-permute-start(bf16[16,180,640]{2,0,1:T(8,128)(2,1)} %get-tuple-element.231), channel_id=1, source_target_pairs={{0,2},{2,4},{4,6},{6,8},{8,10},{10,12},{12,14},{14,16},{16,18},{18... | collective-permute-start | bytes 11059208 | tf_op jit(solution)/shard_map/while/body/eval_jaxpr/ppermute | solution.py:9
  439.1 76.2 %collective-permute-start = (bf16[16,180,640]{2,0,1:T(8,128)(2,1)}, bf16[16,180,640]{2,0,1:T(8,128)(2,1)}, u32[]{:S(2)}, u32[]{:S(2)}) collective-permute-start(bf16[16,180,640]{2,0,1:T(8,128)(2,1)} %get-tuple-element.231), channel_id=1, source_target_pairs={{0,2},{2,4},{4,6},{6,8},{8,10},{10,12},{12,14},{14,16},{16,18},{18... | collective-permute-start | bytes 11059208 | tf_op jit(solution)/shard_map/while/body/eval_jaxpr/ppermute | solution.py:9
  529.1 7.3 %copy-start.1 = (bf16[32,2880]{1,0:T(8,128)(2,1)S(1)}, bf16[32,2880]{1,0:T(8,128)(2,1)}, u32[]{:S(2)}) copy-start(bf16[32,2880]{1,0:T(8,128)(2,1)} %param.11) | copy-start | bytes 552964
where the time goes:
time: 539 us; the launch traced here: 536 us
  local copies, waits for them, and re-layouts  427 us (79%)
  matrix products  45.6 us (8%)
  waiting for transfers between devices  40.4 us (7%)
  other arithmetic  11.8 us (2%)
  starting transfers between devices  11.5 us (2%)
    gather x15, local copies, waits for them, and re-layouts, sector_term(): tap_block = jnp.take(active, tap_index, axis=1)  374 us
    dot_general x5, matrix products, sector_term(): jnp.einsum('sim,smc->sic', tap_block, sector, preferred_element_type=jnp....  45.6 us
    all_to_all x1, waiting for transfers between devices, body(): lax.all_to_all(outgoing, 'lat', split_axis=0, concat_axis=0, tiled=True)  39.9 us
    while x4, local copies, waits for them, and re-layouts  16.9 us
    gather x1, local copies, waits for them, and re-layouts, body(): fields[ordering].reshape(n_lat, lat_dev // n_lat, lon_dev, channels)  11.1 us
  transfers between devices with their start and end apart: 6, of which 2 were waited for; matrix products, arithmetic and copies ran while one was open for 71% of the time, Pallas kernels for 0%

commit v1 on v0

v1 whole, which is shorter than its diff:
```python
import functools

import jax
import jax.numpy as jnp
from jax import lax
from jax.experimental import pallas as pl
from jax.experimental.pallas import tpu as pltpu
from jax.sharding import PartitionSpec as P

VMEM_LIMIT = 48 * 1024 * 1024


def up_to(value, multiple):
    return -(-value // multiple) * multiple


def shift_by(x, axis, by):
    count = lax.axis_size(axis)
    return lax.ppermute(x, axis, [(i, (i + by) % count) for i in range(count)])


def split_kernel(chunks, lat_dev, slot_ref, band_ref, fields_ref, rows_ref, slots_ref, *rest):
    outs, (home_ref, sems) = rest[:-2], rest[-2:]
    band = band_ref[0]
    half = lat_dev // 2
    stay, leave, come = jnp.int32(0), jnp.int32(half), jnp.int32(half)
    for j in range(lat_dev):
        here = band * lat_dev + j
        there = (1 - band) * lat_dev + j
        stays = slot_ref[here] // lat_dev == band
        home_ref[jnp.where(stays, stay, leave)] = j
        one = stays.astype(jnp.int32)

        @pl.when(stays)
        def _():
            rows_ref[stay] = here
            slots_ref[stay] = slot_ref[here] % lat_dev

        comes = slot_ref[there] // lat_dev == band

        @pl.when(comes)
        def _():
            rows_ref[come] = there
            slots_ref[come] = slot_ref[there] % lat_dev

        stay, leave, come = stay + one, leave + 1 - one, come + comes.astype(jnp.int32)
    copies = []
    at = 0
    for out, count in zip(outs, chunks):
        for i in range(count):
            copies.append(pltpu.make_async_copy(fields_ref.at[home_ref[at]], out.at[i], sems.at[at]))
            copies[-1].start()
            at += 1
    for copy in copies:
        copy.wait()


def split_rows(fields, owner_slot, band, chunks):
    lat_dev, lon_dev, channels = fields.shape
    smem = pl.BlockSpec(memory_space=pltpu.SMEM)
    anywhere = pl.BlockSpec(memory_space=pl.ANY)
    ints = jax.ShapeDtypeStruct((lat_dev,), jnp.int32)
    outs = [jax.ShapeDtypeStruct((n, lon_dev, channels), fields.dtype) for n in chunks]
    return pl.pallas_call(
        functools.partial(split_kernel, chunks, lat_dev),
        out_shape=[ints, ints] + outs,
        in_specs=[smem, smem, anywhere],
        out_specs=[smem, smem] + [anywhere] * len(outs),
        scratch_shapes=[pltpu.SMEM((lat_dev,), jnp.int32), pltpu.SemaphoreType.DMA((lat_dev,))],
        cost_estimate=pl.CostEstimate(flops=0, bytes_accessed=4 * fields.size, transcendentals=0),
        name="split_rows",
    )(owner_slot, jnp.reshape(band, (1,)).astype(jnp.int32), fields)


def tap_windows(widths, tap_weights, lon_dev, reach):
    circle = tap_weights.shape[1]
    offset = jnp.arange(circle, dtype=jnp.int32)
    distance = jnp.minimum(offset, circle - offset)
    active = jnp.where(
        distance[None, :] <= widths[:, None],
        tap_weights.astype(jnp.float32),
        jnp.zeros((), jnp.float32),
    )
    behind = (reach + 1) * lon_dev
    line = jnp.concatenate([active[:, circle - behind :], active[:, :behind]], axis=1)
    lanes = up_to(2 * lon_dev, 128)
    return jnp.stack(
        [
            jnp.pad(line[:, s * lon_dev : (s + 2) * lon_dev], ((0, 0), (0, lanes - 2 * lon_dev)))
            for s in range(2 * reach + 1)
        ],
        axis=1,
    )


def filter_kernel(groups, rows_ref, slots_ref, sector_ref, *refs):
    out_ref = refs[-1]
    win_ref, own_ref = refs[0], refs[1]
    lon_dev, channels = own_ref.shape[1:]
    lanes = win_ref.shape[2]
    step = min(up_to(lon_dev, 16), 96)
    tall = up_to(lon_dev, step)

    def term(group, ref):
        taps = win_ref[0, pl.ds(sector_ref[group], 1), :]
        bands = []
        for start in range(0, tall, step):
            band = jnp.broadcast_to(taps, (step, lanes))
            band = pltpu.roll(band, (lanes - lon_dev + start) % lanes, 1)
            band = pltpu.roll(band, 0, 1, stride=1, stride_axis=0)
            bands.append(band[:, :lon_dev].astype(jnp.bfloat16))
        taps = jnp.concatenate(bands, axis=0)
        return jnp.dot(taps, ref[0], preferred_element_type=jnp.float32)[:lon_dev]

    total = own_ref[0].astype(jnp.float32)
    at = 1
    for group, size in enumerate(groups):
        if size == 1:
            total += term(group, refs[at])
        else:
            first, second = refs[at], refs[at + 1]
            total += lax.cond(
                sector_ref[len(groups)] == 0,
                lambda: term(group, first),
                lambda: term(group, second),
            )
        at += size
    out_ref[0] = total.astype(out_ref.dtype)


def filter_rows(rows, slots, sectors, windows, groups, before, base, lat_dev):
    own = groups[0][0]
    count, lon_dev, channels = own.shape
    arrays = [a for group in groups for a in group]
    row_spec = pl.BlockSpec((1, lon_dev, channels), lambda i, rows, slots, sectors: (i, 0, 0))
    win_spec = pl.BlockSpec((1,) + windows.shape[1:], lambda i, rows, slots, sectors: (rows[base + i], 0, 0))
    out_spec = pl.BlockSpec((1, lon_dev, channels), lambda i, rows, slots, sectors: (slots[base + i], 0, 0))
    in_specs = [win_spec] + [row_spec] * len(arrays)
    operands = [windows] + arrays
    aliases = {}
    kernel = functools.partial(filter_kernel, tuple(len(g) for g in groups))
    if before is not None:
        in_specs = [pl.BlockSpec(memory_space=pl.ANY)] + in_specs
        operands = [before] + operands
        aliases = {3: 0}
        inner = kernel
        kernel = lambda rows_ref, slots_ref, sector_ref, before_ref, *refs: inner(
            rows_ref, slots_ref, sector_ref, *refs
        )
    return pl.pallas_call(
        kernel,
        out_shape=jax.ShapeDtypeStruct((lat_dev, lon_dev, channels), own.dtype),
        grid_spec=pltpu.PrefetchScalarGridSpec(
            num_scalar_prefetch=3,
            grid=(count,),
            in_specs=in_specs,
            out_specs=out_spec,
        ),
        input_output_aliases=aliases,
        compiler_params=pltpu.CompilerParams(vmem_limit_bytes=VMEM_LIMIT),
        cost_estimate=pl.CostEstimate(
            flops=2 * count * len(groups) * up_to(lon_dev, 256) ** 2 * up_to(channels, 256),
            bytes_accessed=2 * (len(arrays) + 1) * own.size,
            transcendentals=0,
        ),
        name="filter_rows",
    )(rows, slots, sectors, *operands)


def chip_aware(fields, owner_slot, widths, tap_weights):
    lat_dev, lon_dev, channels = fields.shape
    n_lon = lax.axis_size("lon")
    at = lax.axis_index("lon")
    band = lax.axis_index("lat")
    core, x = at % 2, at // 2 % 2
    half = lat_dev // 2
    stay_chunks = (4, 4)
    come_chunks = (4, 4)
    chunks = stay_chunks + come_chunks
    split = split_rows(fields, owner_slot, band, chunks)
    rows, slots, own = split[0], split[1], list(split[2:])
    for i in range(len(stay_chunks), len(chunks)):
        own[i] = lax.ppermute(own[i], "lat", [(0, 1), (1, 0)])
    windows = tap_windows(widths, tap_weights, lon_dev, 2)
    sectors = jnp.stack(
        [
            jnp.int32(2),
            jnp.where(core == 0, 3, 1),
            jnp.where(x == 0, 4, 0),
            jnp.where(x == 0, 0, 4),
            jnp.where(core == 0, 1, 3),
            (x == core).astype(jnp.int32),
        ]
    ).astype(jnp.int32)
    across_core = [(i, i ^ 1) for i in range(n_lon)]
    across_x = [(i, i ^ 2) for i in range(n_lon)]
    across_z = [(i, (i + (4 if i // 2 % 2 == 0 else -4)) % n_lon) for i in range(n_lon)]
    second_x = [(i, i ^ 1) for i in range(n_lon) if i // 2 % 2 == i % 2]
    second_z = [(i, i ^ 1) for i in range(n_lon) if i // 2 % 2 != i % 2]
    out = None
    base = 0
    for part in own:
        beside = lax.ppermute(part, "lon", across_core)
        by_x = lax.ppermute(part, "lon", across_x)
        by_z = lax.ppermute(by_x, "lon", across_z)
        from_x = lax.ppermute(by_x, "lon", second_x)
        from_z = lax.ppermute(by_z, "lon", second_z)
        groups = [(part,), (beside,), (by_x,), (by_z,), (from_x, from_z)]
        out = filter_rows(rows, slots, sectors, windows, groups, out, base, lat_dev)
        base += part.shape[0]
    return out


def any_mesh(fields, owner_slot, widths, tap_weights):
    lat_dev, lon_dev, channels = fields.shape
    n_lon = lax.axis_size("lon")
    n_lat = lax.axis_size("lat")
    reach = n_lon // 8
    band = lax.axis_index("lat")
    dest_band = owner_slot // lat_dev
    home_rows = band * lat_dev + jnp.arange(lat_dev, dtype=jnp.int32)
    ordering = jnp.argsort(dest_band[home_rows], stable=True)
    rows = jnp.argsort((dest_band != band).astype(jnp.int32), stable=True)[:lat_dev].astype(jnp.int32)
    slots = (owner_slot[rows] % lat_dev).astype(jnp.int32)
    outgoing = fields[ordering].reshape(n_lat, lat_dev // n_lat, lon_dev, channels)
    incoming = lax.all_to_all(outgoing, "lat", split_axis=0, concat_axis=0, tiled=True)
    own = incoming.reshape(lat_dev, lon_dev, channels)
    windows = tap_windows(widths, tap_weights, lon_dev, reach)
    groups, order = [(own,)], [reach]
    ahead = behind = own
    for step in range(1, reach + 1):
        ahead = shift_by(ahead, "lon", -1)
        behind = shift_by(behind, "lon", 1)
        groups += [(ahead,), (behind,)]
        order += [reach + step, reach - step]
    sectors = jnp.array(order + [0], jnp.int32)
    return filter_rows(rows, slots, sectors, windows, groups, None, 0, lat_dev)


def solution(mesh):
    in_specs = (P("lat", "lon", None), P(), P(), P())
    out_specs = P("lat", "lon", None)
    body = chip_aware if (mesh.shape["lon"], mesh.shape["lat"]) == (16, 2) else any_mesh
    return jax.shard_map(body, mesh=mesh, in_specs=in_specs, out_specs=out_specs, check_vma=False)
```

time: 539 us -> 300 us (0.56)
  local copies, waits for them, and re-layouts: 427 us -> 40.2 us
  Pallas kernels: 0 us -> 140 us
  matrix products: 45.6 us -> 0 us
  waiting for transfers between devices: 40.4 us -> 85.4 us
  starting transfers between devices: 11.5 us -> 30.9 us
  other arithmetic: 11.8 us -> 0.2 us
    gather x23 -> x0, local copies, waits for them, and re-layouts: 398 us -> none  [the longest x15 374 us: sector_term(): tap_block = jnp.take(active, tap_index, axis=1)]
    pallas_call x0 -> x5, Pallas kernels: none -> 140 us  [the longest x1 117 us: split_rows(): pl.pallas_call(functools.partial(split_kernel, chunks, lat_dev), out_shap...]
    ppermute x5 -> x22, waiting for transfers between devices: 0.5 us -> 85.4 us  [the longest x4 50.4 us: chip_aware(): by_x = lax.ppermute(part, 'lon', across_x)]
    dot_general x5 -> x0, matrix products: 45.6 us -> none  [sector_term(): jnp.einsum('sim,smc->sic', tap_block, sector, preferred_element_type=jnp....]
    all_to_all x1 -> x0, waiting for transfers between devices: 39.9 us -> none  [body(): lax.all_to_all(outgoing, 'lat', split_axis=0, concat_axis=0, tiled=True)]
    ppermute x5 -> x22, starting transfers between devices: 5.96 us -> 30.9 us  [the longest x4 9.01 us: chip_aware(): from_x = lax.ppermute(by_x, 'lon', second_x)]
    ppermute x0 -> x22, local copies, waits for them, and re-layouts: none -> 21.7 us  [the longest x4 6.03 us: chip_aware(): by_z = lax.ppermute(by_x, 'lon', across_z)]
    while x4 -> x0, local copies, waits for them, and re-layouts: 16.9 us -> none
  transfers between devices with their start and end apart: 6 -> 22, of which waited for: 2 -> 8; matrix products, arithmetic and copies ran while one was open for 71% -> 8% of each run, Pallas kernels for 0% -> 6%
where the time goes in v1:
time: 300 us; the launch traced here: 298 us
  Pallas kernels  140 us (47%)
  waiting for transfers between devices  85.4 us (28%)
  local copies, waits for them, and re-layouts  40.2 us (13%)
  starting transfers between devices  30.9 us (10%)
    pallas_call x1, Pallas kernels, split_rows(): pl.pallas_call(functools.partial(split_kernel, chunks, lat_dev), out_shap...  117 us
    ppermute x4, waiting for transfers between devices, chip_aware(): by_x = lax.ppermute(part, 'lon', across_x)  50.4 us
    ppermute x4, waiting for transfers between devices, chip_aware(): by_z = lax.ppermute(by_x, 'lon', across_z)  34.8 us
    pallas_call x4, Pallas kernels, filter_rows(): pl.pallas_call(kernel, out_shape=jax.ShapeDtypeStruct((lat_dev, lon_dev,...  23.4 us
    unnamed x63, local copies, waits for them, and re-layouts  9.1 us
    ppermute x4, starting transfers between devices, chip_aware(): from_x = lax.ppermute(by_x, 'lon', second_x)  9.01 us
    ppermute x4, starting transfers between devices, chip_aware(): by_x = lax.ppermute(part, 'lon', across_x)  6.92 us
    ppermute x4, local copies, waits for them, and re-layouts, chip_aware(): by_z = lax.ppermute(by_x, 'lon', across_z)  6.03 us
  transfers between devices with their start and end apart: 22, of which 8 were waited for; matrix products, arithmetic and copies ran while one was open for 8% of the time, Pallas kernels for 6%

profile of v1, /device:TPU:0, one launch (start us, length us, event | category | flops | bytes accessed | tf_op | source)
XLA Modules:
  0.0 297.5 jit_solution(2072596641278141843)
XLA Ops:
  0.0 4.7 %copy.14.fields_ref = bf16[16,180,640]{2,1,0:T(8,128)(2,1)} copy(bf16[16,180,640]{2,0,1:T(8,128)(2,1)} %param.4) | data formatting | bytes 7372800 | tf_op args[0]
  4.7 117.0 %split_rows.1 = (s32[16]{0:T(128)}, s32[16]{0:T(128)}, bf16[4,180,640]{2,1,0:T(8,128)(2,1)}, bf16[4,180,640]{2,1,0:T(8,128)(2,1)}, bf16[4,180,640]{2,1,0:T(8,128)(2,1)}, /*index=5*/bf16[4,180,640]{2,1,0:T(8,128)(2,1)}) custom-call(s32[32]{0:T(128)} %slot_ref.1, s32[1]{0:T(128)} %bitcast.band_ref, bf16[16,180,640]{2,1,0:T(8,128)(2,1)} %copy.14.fields_ref), custom_call_target="tpu_custom_call" | custom-call | bytes 7372800 | tf_op jit(solution)/shard_map/split_rows/pallas_call | solution.py:64
  121.7 1.7 copy.19
  123.4 3.0 %collective-permute-start.1 = (bf16[4,180,640]{2,0,1:T(4,128)(2,1)S(1)}, bf16[4,180,640]{2,0,1:T(4,128)(2,1)S(1)}, u32[]{:S(2)}, u32[]{:S(2)}) collective-permute-start(bf16[4,180,640]{2,0,1:T(4,128)(2,1)S(1)} %copy.19), channel_id=1, source_target_pairs={{0,4},{2,6},{4,0},{6,2},{8,12},{10,14},{12,8},{14,10},{16,20},{18,... | collective-permute-start | bytes 2764808 | tf_op jit(solution)/shard_map/ppermute | solution.py:204
  126.4 1.6 copy.26
  128.0 0.2 collective-permute-start.6
  128.1 0.5 collective-permute-start.5
  128.6 0.4 copy.33
  129.0 1.8 collective-permute-start.10
  130.7 0.4 copy.40
  131.1 16.6 %collective-permute-done.1 = bf16[4,180,640]{2,0,1:T(4,128)(2,1)S(1)} collective-permute-done((bf16[4,180,640]{2,0,1:T(4,128)(2,1)S(1)}, bf16[4,180,640]{2,0,1:T(4,128)(2,1)S(1)}, u32[]{:S(2)}, u32[]{:S(2)}) %collective-permute-start.1) | collective-permute-done | bytes 921632 | tf_op jit(solution)/shard_map/ppermute | solution.py:204
  147.7 2.1 collective-permute-start.16
  149.8 1.6 collective-permute-start.2
  151.3 15.4 %collective-permute-done.6 = bf16[4,180,640]{2,0,1:T(4,128)(2,1)} collective-permute-done((bf16[4,180,640]{2,0,1:T(4,128)(2,1)S(1)}, bf16[4,180,640]{2,0,1:T(4,128)(2,1)}, u32[]{:S(2)}, u32[]{:S(2)}) %collective-permute-start.6) | collective-permute-done | bytes 921632 | tf_op jit(solution)/shard_map/ppermute | solution.py:204
  166.7 1.3 collective-permute-start.3
  168.0 1.9 collective-permute-start.7
  169.9 1.3 collective-permute-start.8
  171.4 3.4 %collective-permute-start.12 = (bf16[4,180,640]{2,0,1:T(4,128)(2,1)S(1)}, bf16[4,180,640]{2,0,1:T(4,128)(2,1)}, u32[]{:S(2)}, u32[]{:S(2)}) collective-permute-start(bf16[4,180,640]{2,0,1:T(4,128)(2,1)S(1)} %collective-permute-done.10), channel_id=1, source_target_pairs={{0,4},{2,6},{4,0},{6,2},{8,12},{10,14},{12,8},{14,10},{16,20},{18,... | collective-permute-start | bytes 2764808 | tf_op jit(solution)/shard_map/ppermute | solution.py:204
  174.8 0.9 collective-permute-start.11
  175.7 0.4 collective-permute-start.18
  176.0 15.7 %collective-permute-done.7 = bf16[4,180,640]{2,0,1:T(4,128)(2,1)} collective-permute-done((bf16[4,180,640]{2,0,1:T(4,128)(2,1)}, bf16[4,180,640]{2,0,1:T(4,128)(2,1)}, u32[]{:S(2)}, u32[]{:S(2)}) %collective-permute-start.7) | collective-permute-done | bytes 921632 | tf_op jit(solution)/shard_map/ppermute | solution.py:205
  191.8 1.3 collective-permute-start.4
  193.1 2.6 collective-permute-done.12
  195.7 0.9 collective-permute-start.13
  196.7 3.0 collective-permute-start.14
  199.6 15.9 %collective-permute-done.18 = bf16[4,180,640]{2,0,1:T(4,128)(2,1)} collective-permute-done((bf16[4,180,640]{2,0,1:T(4,128)(2,1)S(1)}, bf16[4,180,640]{2,0,1:T(4,128)(2,1)}, u32[]{:S(2)}, u32[]{:S(2)}) %collective-permute-start.18) | collective-permute-done | bytes 921632 | tf_op jit(solution)/shard_map/ppermute | solution.py:204
  215.5 3.4 %collective-permute-start.20 = (bf16[4,180,640]{2,0,1:T(4,128)(2,1)}, bf16[4,180,640]{2,0,1:T(4,128)(2,1)}, u32[]{:S(2)}, u32[]{:S(2)}) collective-permute-start(bf16[4,180,640]{2,0,1:T(4,128)(2,1)} %collective-permute-done.18), channel_id=1, source_target_pairs={{0,2},{6,4},{8,10},{14,12},{16,18},{22,20},{24,26},{30,28},{1,3},{... | collective-permute-start | bytes 2764808 | tf_op jit(solution)/shard_map/ppermute | solution.py:206
  218.9 1.3 collective-permute-start.9
  220.4 0.7 collective-permute-done.13
  221.2 1.3 collective-permute-start.15
  222.6 18.3 %collective-permute-done.19 = bf16[4,180,640]{2,0,1:T(4,128)(2,1)} collective-permute-done((bf16[4,180,640]{2,0,1:T(4,128)(2,1)}, bf16[4,180,640]{2,0,1:T(4,128)(2,1)}, u32[]{:S(2)}, u32[]{:S(2)}) %collective-permute-start.19) | collective-permute-done | bytes 921632 | tf_op jit(solution)/shard_map/ppermute | solution.py:205
  240.9 1.5 collective-permute-start.21
  242.9 0.5 stack.51.refs_0_
  243.4 0.1 copy.22.refs_3_
  243.5 1.4 copy.29.refs_3_
  245.0 0.1 copy.34.refs_1_
  245.2 0.1 copy.41.refs_1_
  245.3 0.1 copy.21.refs_2_
  245.4 0.1 copy.28.refs_2_
  245.5 0.7 copy-done.17
  246.2 0.1 copy.23.refs_4_
  246.3 2.4 copy.30.refs_4_
  248.7 1.4 copy.36.refs_3_
  250.1 1.4 copy.43.refs_3_
  251.5 0.1 copy.24.refs_5_
  251.6 1.1 copy.31.refs_5_
  252.7 0.1 copy.35.refs_2_
  252.8 0.1 copy.42.refs_2_
  252.9 2.3 copy.37.refs_4_
  255.2 1.3 copy.44.refs_4_
  256.5 0.1 copy.25.refs_6_
  256.7 2.3 copy.32.refs_6_
  259.0 2.3 copy.38.refs_5_
  261.3 2.3 copy.45.refs_5_
  263.6 5.8 %filter_rows.4.before_ref = bf16[16,180,640]{2,1,0:T(8,128)(2,1)} custom-call(s32[16]{0:T(128)S(1)} %copy-done.8, s32[16]{0:T(128)S(1)} %copy-done.9, s32[6]{0:T(128)S(1)} %stack.45.sector_ref, f32[32,5,384]{2,1,0:T(8,128)S(1)} %stack.51.refs_0_, bf16[4,180,640]{2,1,0:T(8,128)(2,1)S(1)} %copy-done.1, bf16[4,180,640]{2,1,0:T(8,128)(2,1)S(1)} %copy.21.refs_2_, ...), custom_call_target="tpu_custom_call" | custom-call | flops 2013265920 | bytes 6451200 | tf_op jit(solution)/shard_map/filter_rows/pallas_call | solution.py:150
  269.4 1.2 copy-done.4
  270.6 1.2 copy-done.5
  271.8 1.2 copy-done.7
  273.0 5.8 %filter_rows.5.before_ref = bf16[16,180,640]{2,1,0:T(8,128)(2,1)} custom-call(s32[16]{0:T(128)S(1)} %copy-done.8, s32[16]{0:T(128)S(1)} %copy-done.9, s32[6]{0:T(128)S(1)} %stack.45.sector_ref, bf16[16,180,640]{2,1,0:T(8,128)(2,1)} %filter_rows.4.before_ref, f32[32,5,384]{2,1,0:T(8,128)S(1)} %stack.51.refs_0_, ...), custom_call_target="tpu_custom_call", output_to_operand_aliasing={{}: (3, {})} | custom-call | flops 2013265920 | bytes 6451200 | tf_op jit(solution)/shard_map/filter_rows/pallas_call | solution.py:150
  278.8 1.3 copy.39.refs_6_
  280.1 5.9 %filter_rows.6.before_ref = bf16[16,180,640]{2,1,0:T(8,128)(2,1)} custom-call(s32[16]{0:T(128)S(1)} %copy-done.8, s32[16]{0:T(128)S(1)} %copy-done.9, s32[6]{0:T(128)S(1)} %stack.45.sector_ref, bf16[16,180,640]{2,1,0:T(8,128)(2,1)} %filter_rows.5.before_ref, f32[32,5,384]{2,1,0:T(8,128)S(1)} %stack.51.refs_0_, ...), custom_call_target="tpu_custom_call", output_to_operand_aliasing={{}: (3, {})} | custom-call | flops 2013265920 | bytes 6451200 | tf_op jit(solution)/shard_map/filter_rows/pallas_call | solution.py:150
  286.0 1.3 copy.46.refs_6_
  287.3 5.9 %filter_rows.7 = bf16[16,180,640]{2,1,0:T(8,128)(2,1)} custom-call(s32[16]{0:T(128)S(1)} %copy-done.8, s32[16]{0:T(128)S(1)} %copy-done.9, s32[6]{0:T(128)S(1)} %stack.45.sector_ref, bf16[16,180,640]{2,1,0:T(8,128)(2,1)} %filter_rows.6.before_ref, f32[32,5,384]{2,1,0:T(8,128)S(1)} %stack.51.refs_0_, ...), custom_call_target="tpu_custom_call", output_to_operand_aliasing={{}: (3, {})} | custom-call | flops 2013265920 | bytes 6451200 | tf_op jit(solution)/shard_map/filter_rows/pallas_call | solution.py:150
  293.2 4.4 %copy.47 = bf16[16,180,640]{2,0,1:T(8,128)(2,1)} copy(bf16[16,180,640]{2,1,0:T(8,128)(2,1)} %filter_rows.7) | data formatting | bytes 7372800 | tf_op jit(solution)/shard_map/filter_rows/pallas_call | solution.py:150
  (90 shorter events, 1.1 us)
Async XLA Ops:
  121.7 7.0 %copy-start.11 = (bf16[4,180,640]{2,1,0:T(8,128)(2,1)S(1)}, bf16[4,180,640]{2,1,0:T(8,128)(2,1)}, u32[]{:S(2)}) copy-start(bf16[4,180,640]{2,1,0:T(8,128)(2,1)} %get-tuple-element.15) | copy-start | bytes 2764804
  121.7 9.1 %copy-start.10 = (bf16[4,180,640]{2,1,0:T(8,128)(2,1)S(1)}, bf16[4,180,640]{2,1,0:T(8,128)(2,1)}, u32[]{:S(2)}) copy-start(bf16[4,180,640]{2,1,0:T(8,128)(2,1)} %get-tuple-element.16) | copy-start | bytes 2764804
  121.7 98.5 %copy-start.28 = (bf16[32,2880]{1,0:T(8,128)(2,1)S(1)}, bf16[32,2880]{1,0:T(8,128)(2,1)}, u32[]{:S(2)}) copy-start(bf16[32,2880]{1,0:T(8,128)(2,1)} %param.7) | copy-start | bytes 552964
  121.7 98.5 %copy-start.30 = (s32[32]{0:T(128)S(1)}, s32[32]{0:T(128)}, u32[]{:S(2)}) copy-start(s32[32]{0:T(128)} %param.6) | copy-start | bytes 388
  123.4 24.3 %collective-permute-start.1 = (bf16[4,180,640]{2,0,1:T(4,128)(2,1)S(1)}, bf16[4,180,640]{2,0,1:T(4,128)(2,1)S(1)}, u32[]{:S(2)}, u32[]{:S(2)}) collective-permute-start(bf16[4,180,640]{2,0,1:T(4,128)(2,1)S(1)} %copy.19), channel_id=1, source_target_pairs={{0,4},{2,6},{4,0},{6,2},{8,12},{10,14},{12,8},{14,10},{16,20},{18,... | collective-permute-start | bytes 2764808 | tf_op jit(solution)/shard_map/ppermute | solution.py:204
  126.4 23.4 %collective-permute-start = (bf16[4,180,640]{2,0,1:T(4,128)(2,1)S(1)}, bf16[4,180,640]{2,0,1:T(4,128)(2,1)S(1)}, u32[]{:S(2)}, u32[]{:S(2)}) collective-permute-start(bf16[4,180,640]{2,0,1:T(4,128)(2,1)S(1)} %copy.19), channel_id=1, source_target_pairs={{0,2},{2,0},{4,6},{6,4},{8,10},{10,8},{12,14},{14,12},{16,18},{18,... | collective-permute-start | bytes 2764808 | tf_op jit(solution)/shard_map/ppermute | solution.py:203
  126.4 116.4 %copy-start.29 = (pred[384]{0:T(512)(128)(4,1)S(1)}, pred[384]{0:T(512)(128)(4,1)}, u32[]{:S(2)}) copy-start(pred[384]{0:T(512)(128)(4,1)} %constant.50.clone.1) | copy-start | bytes 1156
  128.0 38.7 %collective-permute-start.6 = (bf16[4,180,640]{2,0,1:T(4,128)(2,1)S(1)}, bf16[4,180,640]{2,0,1:T(4,128)(2,1)}, u32[]{:S(2)}, u32[]{:S(2)}) collective-permute-start(bf16[4,180,640]{2,0,1:T(4,128)(2,1)S(1)} %copy.26), channel_id=1, source_target_pairs={{0,4},{2,6},{4,0},{6,2},{8,12},{10,14},{12,8},{14,10},{16,20},{18,... | collective-permute-start | bytes 2764808 | tf_op jit(solution)/shard_map/ppermute | solution.py:204
  128.1 39.9 %collective-permute-start.5 = (bf16[4,180,640]{2,0,1:T(4,128)(2,1)S(1)}, bf16[4,180,640]{2,0,1:T(4,128)(2,1)S(1)}, u32[]{:S(2)}, u32[]{:S(2)}) collective-permute-start(bf16[4,180,640]{2,0,1:T(4,128)(2,1)S(1)} %copy.26), channel_id=1, source_target_pairs={{0,2},{2,0},{4,6},{6,4},{8,10},{10,8},{12,14},{14,12},{16,18},{18,... | collective-permute-start | bytes 2764808 | tf_op jit(solution)/shard_map/ppermute | solution.py:203
  129.0 40.9 %collective-permute-start.10 = (bf16[4,180,640]{2,0,1:T(4,128)(2,1)S(1)}, bf16[4,180,640]{2,0,1:T(4,128)(2,1)S(1)}, u32[]{:S(2)}, u32[]{:S(2)}) collective-permute-start(bf16[4,180,640]{2,0,1:T(4,128)(2,1)S(1)} %copy.33), channel_id=1, source_target_pairs={{0,1},{1,0},{2,3},{3,2},{4,5},{5,4},{6,7},{7,6},{8,9},{9,8},{10,11... | collective-permute-start | bytes 2764808 | tf_op jit(solution)/shard_map/ppermute | solution.py:183
  147.7 23.7 %collective-permute-start.16 = (bf16[4,180,640]{2,0,1:T(4,128)(2,1)S(1)}, bf16[4,180,640]{2,0,1:T(4,128)(2,1)S(1)}, u32[]{:S(2)}, u32[]{:S(2)}) collective-permute-start(bf16[4,180,640]{2,0,1:T(4,128)(2,1)S(1)} %copy.40), channel_id=1, source_target_pairs={{0,1},{1,0},{2,3},{3,2},{4,5},{5,4},{6,7},{7,6},{8,9},{9,8},{10,11... | collective-permute-start | bytes 2764808 | tf_op jit(solution)/shard_map/ppermute | solution.py:183
  149.8 25.0 %collective-permute-start.2 = (bf16[4,180,640]{2,0,1:T(4,128)(2,1)S(1)}, bf16[4,180,640]{2,0,1:T(4,128)(2,1)S(1)}, u32[]{:S(2)}, u32[]{:S(2)}) collective-permute-start(bf16[4,180,640]{2,0,1:T(4,128)(2,1)S(1)} %collective-permute-done.1), channel_id=1, source_target_pairs={{0,8},{2,10},{4,28},{6,30},{8,16},{10,18},{12,4},{14,6},{16,24},{1... | collective-permute-start | bytes 2764808 | tf_op jit(solution)/shard_map/ppermute | solution.py:205
  166.7 9.0 %collective-permute-start.3 = (bf16[4,180,640]{2,0,1:T(4,128)(2,1)S(1)}, bf16[4,180,640]{2,0,1:T(4,128)(2,1)S(1)}, u32[]{:S(2)}, u32[]{:S(2)}) collective-permute-start(bf16[4,180,640]{2,0,1:T(4,128)(2,1)S(1)} %collective-permute-done.1), channel_id=1, source_target_pairs={{0,2},{6,4},{8,10},{14,12},{16,18},{22,20},{24,26},{30,28},{1,3},{... | collective-permute-start | bytes 2764808 | tf_op jit(solution)/shard_map/ppermute | solution.py:206
  168.0 23.7 %collective-permute-start.7 = (bf16[4,180,640]{2,0,1:T(4,128)(2,1)}, bf16[4,180,640]{2,0,1:T(4,128)(2,1)}, u32[]{:S(2)}, u32[]{:S(2)}) collective-permute-start(bf16[4,180,640]{2,0,1:T(4,128)(2,1)} %collective-permute-done.6), channel_id=1, source_target_pairs={{0,8},{2,10},{4,28},{6,30},{8,16},{10,18},{12,4},{14,6},{16,24},{1... | collective-permute-start | bytes 2764808 | tf_op jit(solution)/shard_map/ppermute | solution.py:205
  169.9 49.0 %copy-start.12 = (bf16[4,180,640]{2,0,1:T(4,128)(2,1)}, bf16[4,180,640]{2,0,1:T(4,128)(2,1)S(1)}, u32[]{:S(2)}) copy-start(bf16[4,180,640]{2,0,1:T(4,128)(2,1)S(1)} %collective-permute-done.10) | copy-start | bytes 2764804
  169.9 21.9 %collective-permute-start.8 = (bf16[4,180,640]{2,0,1:T(4,128)(2,1)}, bf16[4,180,640]{2,0,1:T(4,128)(2,1)S(1)}, u32[]{:S(2)}, u32[]{:S(2)}) collective-permute-start(bf16[4,180,640]{2,0,1:T(4,128)(2,1)} %collective-permute-done.6), channel_id=1, source_target_pairs={{0,2},{6,4},{8,10},{14,12},{16,18},{22,20},{24,26},{30,28},{1,3},{... | collective-permute-start | bytes 2764808 | tf_op jit(solution)/shard_map/ppermute | solution.py:206
  171.4 48.8 %copy-start.14 = (bf16[4,180,640]{2,0,1:T(4,128)(2,1)}, bf16[4,180,640]{2,0,1:T(4,128)(2,1)S(1)}, u32[]{:S(2)}) copy-start(bf16[4,180,640]{2,0,1:T(4,128)(2,1)S(1)} %collective-permute-done.16) | copy-start | bytes 2764804
  171.4 24.4 %collective-permute-start.12 = (bf16[4,180,640]{2,0,1:T(4,128)(2,1)S(1)}, bf16[4,180,640]{2,0,1:T(4,128)(2,1)}, u32[]{:S(2)}, u32[]{:S(2)}) collective-permute-start(bf16[4,180,640]{2,0,1:T(4,128)(2,1)S(1)} %collective-permute-done.10), channel_id=1, source_target_pairs={{0,4},{2,6},{4,0},{6,2},{8,12},{10,14},{12,8},{14,10},{16,20},{18,... | collective-permute-start | bytes 2764808 | tf_op jit(solution)/shard_map/ppermute | solution.py:204
  174.8 45.5 %copy-start.16 = (bf16[4,180,640]{2,0,1:T(4,128)(2,1)}, bf16[4,180,640]{2,0,1:T(4,128)(2,1)S(1)}, u32[]{:S(2)}) copy-start(bf16[4,180,640]{2,0,1:T(4,128)(2,1)S(1)} %collective-permute-done.2) | copy-start | bytes 2764804
  174.8 21.9 %collective-permute-start.11 = (bf16[4,180,640]{2,0,1:T(4,128)(2,1)S(1)}, bf16[4,180,640]{2,0,1:T(4,128)(2,1)S(1)}, u32[]{:S(2)}, u32[]{:S(2)}) collective-permute-start(bf16[4,180,640]{2,0,1:T(4,128)(2,1)S(1)} %collective-permute-done.10), channel_id=1, source_target_pairs={{0,2},{2,0},{4,6},{6,4},{8,10},{10,8},{12,14},{14,12},{16,18},{18,... | collective-permute-start | bytes 2764808 | tf_op jit(solution)/shard_map/ppermute | solution.py:203
  175.7 44.7 %copy-start.18 = (bf16[4,180,640]{2,0,1:T(4,128)(2,1)}, bf16[4,180,640]{2,0,1:T(4,128)(2,1)S(1)}, u32[]{:S(2)}) copy-start(bf16[4,180,640]{2,0,1:T(4,128)(2,1)S(1)} %collective-permute-done.3) | copy-start | bytes 2764804
  175.7 39.8 %collective-permute-start.18 = (bf16[4,180,640]{2,0,1:T(4,128)(2,1)S(1)}, bf16[4,180,640]{2,0,1:T(4,128)(2,1)}, u32[]{:S(2)}, u32[]{:S(2)}) collective-permute-start(bf16[4,180,640]{2,0,1:T(4,128)(2,1)S(1)} %collective-permute-done.16), channel_id=1, source_target_pairs={{0,4},{2,6},{4,0},{6,2},{8,12},{10,14},{12,8},{14,10},{16,20},{18,... | collective-permute-start | bytes 2764808 | tf_op jit(solution)/shard_map/ppermute | solution.py:204
  191.8 23.7 %collective-permute-start.17 = (bf16[4,180,640]{2,0,1:T(4,128)(2,1)S(1)}, bf16[4,180,640]{2,0,1:T(4,128)(2,1)S(1)}, u32[]{:S(2)}, u32[]{:S(2)}) collective-permute-start(bf16[4,180,640]{2,0,1:T(4,128)(2,1)S(1)} %collective-permute-done.16), channel_id=1, source_target_pairs={{0,2},{2,0},{4,6},{6,4},{8,10},{10,8},{12,14},{14,12},{16,18},{18,... | collective-permute-start | bytes 2764808 | tf_op jit(solution)/shard_map/ppermute | solution.py:203
  191.8 29.4 %copy-start.20 = (bf16[4,180,640]{2,0,1:T(4,128)(2,1)}, bf16[4,180,640]{2,0,1:T(4,128)(2,1)S(1)}, u32[]{:S(2)}) copy-start(bf16[4,180,640]{2,0,1:T(4,128)(2,1)S(1)} %collective-permute-done.8) | copy-start | bytes 2764804
  191.8 27.1 %collective-permute-start.4 = (bf16[4,180,640]{2,0,1:T(4,128)(2,1)S(1)}, bf16[4,180,640]{2,0,1:T(4,128)(2,1)S(1)}, u32[]{:S(2)}, u32[]{:S(2)}) collective-permute-start(bf16[4,180,640]{2,0,1:T(4,128)(2,1)S(1)} %collective-permute-done.2), channel_id=1, source_target_pairs={{2,0},{4,6},{10,8},{12,14},{18,16},{20,22},{26,24},{28,30},{3,1},{... | collective-permute-start | bytes 2764808 | tf_op jit(solution)/shard_map/ppermute | solution.py:207
  195.7 25.4 %collective-permute-start.13 = (bf16[4,180,640]{2,0,1:T(4,128)(2,1)}, bf16[4,180,640]{2,0,1:T(4,128)(2,1)}, u32[]{:S(2)}, u32[]{:S(2)}) collective-permute-start(bf16[4,180,640]{2,0,1:T(4,128)(2,1)} %collective-permute-done.12), channel_id=1, source_target_pairs={{0,8},{2,10},{4,28},{6,30},{8,16},{10,18},{12,4},{14,6},{16,24},{1... | collective-permute-start | bytes 2764808 | tf_op jit(solution)/shard_map/ppermute | solution.py:205
  196.7 25.8 %copy-start.22 = (bf16[4,180,640]{2,0,1:T(4,128)(2,1)}, bf16[4,180,640]{2,0,1:T(4,128)(2,1)S(1)}, u32[]{:S(2)}) copy-start(bf16[4,180,640]{2,0,1:T(4,128)(2,1)S(1)} %collective-permute-done.11) | copy-start | bytes 2764804
  196.7 62.3 %collective-permute-start.14 = (bf16[4,180,640]{2,0,1:T(4,128)(2,1)}, bf16[4,180,640]{2,0,1:T(4,128)(2,1)}, u32[]{:S(2)}, u32[]{:S(2)}) collective-permute-start(bf16[4,180,640]{2,0,1:T(4,128)(2,1)} %collective-permute-done.12), channel_id=1, source_target_pairs={{0,2},{6,4},{8,10},{14,12},{16,18},{22,20},{24,26},{30,28},{1,3},{... | collective-permute-start | bytes 2764808 | tf_op jit(solution)/shard_map/ppermute | solution.py:206
  215.5 25.4 %collective-permute-start.19 = (bf16[4,180,640]{2,0,1:T(4,128)(2,1)}, bf16[4,180,640]{2,0,1:T(4,128)(2,1)}, u32[]{:S(2)}, u32[]{:S(2)}) collective-permute-start(bf16[4,180,640]{2,0,1:T(4,128)(2,1)} %collective-permute-done.18), channel_id=1, source_target_pairs={{0,8},{2,10},{4,28},{6,30},{8,16},{10,18},{12,4},{14,6},{16,24},{1... | collective-permute-start | bytes 2764808 | tf_op jit(solution)/shard_map/ppermute | solution.py:205
  215.5 7.1 %copy-start.24 = (bf16[4,180,640]{2,0,1:T(4,128)(2,1)}, bf16[4,180,640]{2,0,1:T(4,128)(2,1)S(1)}, u32[]{:S(2)}) copy-start(bf16[4,180,640]{2,0,1:T(4,128)(2,1)S(1)} %collective-permute-done.17) | copy-start | bytes 2764804
  215.5 45.8 %collective-permute-start.20 = (bf16[4,180,640]{2,0,1:T(4,128)(2,1)}, bf16[4,180,640]{2,0,1:T(4,128)(2,1)}, u32[]{:S(2)}, u32[]{:S(2)}) collective-permute-start(bf16[4,180,640]{2,0,1:T(4,128)(2,1)} %collective-permute-done.18), channel_id=1, source_target_pairs={{0,2},{6,4},{8,10},{14,12},{16,18},{22,20},{24,26},{30,28},{1,3},{... | collective-permute-start | bytes 2764808 | tf_op jit(solution)/shard_map/ppermute | solution.py:206
  218.9 22.0 %copy-start.26 = (bf16[4,180,640]{2,0,1:T(4,128)(2,1)}, bf16[4,180,640]{2,0,1:T(4,128)(2,1)S(1)}, u32[]{:S(2)}) copy-start(bf16[4,180,640]{2,0,1:T(4,128)(2,1)S(1)} %collective-permute-done.4) | copy-start | bytes 2764804
  218.9 37.8 %collective-permute-start.9 = (bf16[4,180,640]{2,0,1:T(4,128)(2,1)}, bf16[4,180,640]{2,0,1:T(4,128)(2,1)}, u32[]{:S(2)}, u32[]{:S(2)}) collective-permute-start(bf16[4,180,640]{2,0,1:T(4,128)(2,1)} %collective-permute-done.7), channel_id=1, source_target_pairs={{2,0},{4,6},{10,8},{12,14},{18,16},{20,22},{26,24},{28,30},{3,1},{... | collective-permute-start | bytes 2764808 | tf_op jit(solution)/shard_map/ppermute | solution.py:207
  221.2 57.6 %collective-permute-start.15 = (bf16[4,180,640]{2,0,1:T(4,128)(2,1)}, bf16[4,180,640]{2,0,1:T(4,128)(2,1)}, u32[]{:S(2)}, u32[]{:S(2)}) collective-permute-start(bf16[4,180,640]{2,0,1:T(4,128)(2,1)} %collective-permute-done.13), channel_id=1, source_target_pairs={{2,0},{4,6},{10,8},{12,14},{18,16},{20,22},{26,24},{28,30},{3,1},{... | collective-permute-start | bytes 2764808 | tf_op jit(solution)/shard_map/ppermute | solution.py:207
  240.9 45.1 %collective-permute-start.21 = (bf16[4,180,640]{2,0,1:T(4,128)(2,1)}, bf16[4,180,640]{2,0,1:T(4,128)(2,1)}, u32[]{:S(2)}, u32[]{:S(2)}) collective-permute-start(bf16[4,180,640]{2,0,1:T(4,128)(2,1)} %collective-permute-done.19), channel_id=1, source_target_pairs={{2,0},{4,6},{10,8},{12,14},{18,16},{20,22},{26,24},{28,30},{3,1},{... | collective-permute-start | bytes 2764808 | tf_op jit(solution)/shard_map/ppermute | solution.py:207
  243.4 1.5 copy-start.13
  243.4 1.7 copy-start.15
  245.0 1.2 copy-start.17
  246.2 5.3 %copy-start.19 = (bf16[4,180,640]{2,0,1:T(4,128)(2,1)S(1)}, bf16[4,180,640]{2,0,1:T(4,128)(2,1)}, u32[]{:S(2)}) copy-start(bf16[4,180,640]{2,0,1:T(4,128)(2,1)} %copy-done.18) | copy-start | bytes 2764804
  246.3 5.3 %copy-start.21 = (bf16[4,180,640]{2,0,1:T(4,128)(2,1)S(1)}, bf16[4,180,640]{2,0,1:T(4,128)(2,1)}, u32[]{:S(2)}) copy-start(bf16[4,180,640]{2,0,1:T(4,128)(2,1)} %copy-done.20) | copy-start | bytes 2764804
  248.7 4.0 %copy-start.23 = (bf16[4,180,640]{2,0,1:T(4,128)(2,1)S(1)}, bf16[4,180,640]{2,0,1:T(4,128)(2,1)}, u32[]{:S(2)}) copy-start(bf16[4,180,640]{2,0,1:T(4,128)(2,1)} %copy-done.22) | copy-start | bytes 2764804
  250.1 2.7 copy-start.25
  252.7 3.8 %copy-start.27 = (bf16[4,180,640]{2,0,1:T(4,128)(2,1)S(1)}, bf16[4,180,640]{2,0,1:T(4,128)(2,1)}, u32[]{:S(2)}) copy-start(bf16[4,180,640]{2,0,1:T(4,128)(2,1)} %copy-done.26) | copy-start | bytes 2764804
  256.5 7.0 %copy-start.1 = (bf16[4,180,640]{2,1,0:T(8,128)(2,1)S(1)}, bf16[4,180,640]{2,1,0:T(8,128)(2,1)}, u32[]{:S(2)}) copy-start(bf16[4,180,640]{2,1,0:T(8,128)(2,1)} %get-tuple-element.13.refs_1_) | copy-start | bytes 2764804
  256.5 7.0 %copy-start.8 = (s32[16]{0:T(128)S(1)}, s32[16]{0:T(128)}, u32[]{:S(2)}) copy-start(s32[16]{0:T(128)} %get-tuple-element.11.rows_ref) | copy-start | bytes 196
  256.5 7.0 %copy-start.9 = (s32[16]{0:T(128)S(1)}, s32[16]{0:T(128)}, u32[]{:S(2)}) copy-start(s32[16]{0:T(128)} %get-tuple-element.12.slots_ref) | copy-start | bytes 196
  263.6 5.8 %copy-start = (bf16[4,180,640]{2,1,0:T(8,128)(2,1)S(1)}, bf16[4,180,640]{2,1,0:T(8,128)(2,1)}, u32[]{:S(2)}) copy-start(bf16[4,180,640]{2,1,0:T(8,128)(2,1)} %get-tuple-element.14.refs_1_) | copy-start | bytes 2764804
  269.4 1.2 copy-start.4
  270.6 1.2 copy-start.5
  271.8 1.2 copy-start.7
  273.0 7.1 %copy-start.2 = (bf16[4,180,640]{2,1,0:T(8,128)(2,1)S(1)}, bf16[4,180,640]{2,1,0:T(8,128)(2,1)}, u32[]{:S(2)}) copy-start(bf16[4,180,640]{2,1,0:T(8,128)(2,1)} %copy.37.refs_4_) | copy-start | bytes 2764804
  273.0 7.1 %copy-start.6 = (bf16[4,180,640]{2,1,0:T(8,128)(2,1)S(1)}, bf16[4,180,640]{2,1,0:T(8,128)(2,1)}, u32[]{:S(2)}) copy-start(bf16[4,180,640]{2,1,0:T(8,128)(2,1)} %copy.38.refs_5_) | copy-start | bytes 2764804
  280.1 7.2 %copy-start.3 = (bf16[4,180,640]{2,1,0:T(8,128)(2,1)S(1)}, bf16[4,180,640]{2,1,0:T(8,128)(2,1)}, u32[]{:S(2)}) copy-start(bf16[4,180,640]{2,1,0:T(8,128)(2,1)} %copy.45.refs_5_) | copy-start | bytes 2764804

commit v2 on v0

v2 whole, which is shorter than its diff:
```python
import functools

import jax
import jax.numpy as jnp
from jax import lax
from jax.experimental import pallas as pl
from jax.experimental.pallas import tpu as pltpu
from jax.sharding import PartitionSpec as P

VMEM_LIMIT = 48 * 1024 * 1024
SMEM_SPEC = pl.BlockSpec(memory_space=pltpu.SMEM)
STAY = (2, 2)
COME = (2, 2)


def up_to(value, multiple):
    return -(-value // multiple) * multiple


def shift_by(x, axis, by):
    count = lax.axis_size(axis)
    return lax.ppermute(x, axis, [(i, (i + by) % count) for i in range(count)])


def tap_windows(widths, tap_weights, lon_dev, reach):
    circle = tap_weights.shape[1]
    offset = jnp.arange(circle, dtype=jnp.int32)
    distance = jnp.minimum(offset, circle - offset)
    active = jnp.where(
        distance[None, :] <= widths[:, None],
        tap_weights.astype(jnp.float32),
        jnp.zeros((), jnp.float32),
    )
    behind = (reach + 1) * lon_dev
    line = jnp.concatenate([active[:, circle - behind :], active[:, :behind]], axis=1)
    lanes = up_to(2 * lon_dev, 128)
    return jnp.stack(
        [
            jnp.pad(line[:, s * lon_dev : (s + 2) * lon_dev], ((0, 0), (0, lanes - 2 * lon_dev)))
            for s in range(2 * reach + 1)
        ],
        axis=1,
    )


def toeplitz(taps, lon_dev, width):
    lanes = taps.shape[1]
    step = min(up_to(lon_dev, 16), 96)
    bands = []
    for start in range(0, up_to(lon_dev, step), step):
        band = jnp.broadcast_to(taps, (step, lanes))
        band = pltpu.roll(band, (lanes - lon_dev + start) % lanes, 1)
        band = pltpu.roll(band, 0, 1, stride=1, stride_axis=0)
        bands.append(band[:, :width].astype(jnp.bfloat16))
    return jnp.concatenate(bands, axis=0)


def take_kernel(chunks, lat_dev, lon_dev, block, slot_ref, place_ref, fields_ref, *refs):
    outs = refs[: len(chunks)]
    rows_ref, slots_ref, home_ref, take_ref = refs[len(chunks) :]
    half, quarter = lat_dev // 2, lat_dev // 4

    @pl.when(pl.program_id(0) == 0)
    def _():
        band, core = place_ref[0], place_ref[1]

        def at(n):
            mine = n // quarter == core
            return n % quarter + jnp.where(mine, 0, quarter)

        stay, leave, come = jnp.int32(0), jnp.int32(0), jnp.int32(0)
        for j in range(lat_dev):
            here = band * lat_dev + j
            there = (1 - band) * lat_dev + j
            stays = slot_ref[here] // lat_dev == band
            comes = slot_ref[there] // lat_dev == band
            home_ref[jnp.where(stays, at(stay), half + at(leave))] = jnp.int32(j)

            @pl.when(stays)
            def _():
                spot = at(stay)
                spot = spot + jnp.where(spot >= quarter, quarter, 0)
                rows_ref[spot] = here
                slots_ref[spot] = slot_ref[here] % lat_dev

            @pl.when(comes)
            def _():
                spot = at(come)
                spot = spot + jnp.where(spot >= quarter, half, quarter)
                rows_ref[spot] = there
                slots_ref[spot] = slot_ref[there] % lat_dev

            stay = stay + stays.astype(jnp.int32)
            leave = leave + 1 - stays.astype(jnp.int32)
            come = come + comes.astype(jnp.int32)
        lon_out = lax.broadcasted_iota(jnp.int32, (block, block * lat_dev), 0)
        column = lax.broadcasted_iota(jnp.int32, (block, block * lat_dev), 1)
        for place in range(lat_dev):
            wanted = lon_out * lat_dev + home_ref[place]
            take_ref[pl.ds(place * block, block), :] = jnp.where(column == wanted, 1.0, 0.0).astype(jnp.bfloat16)

    channels = fields_ref.shape[2]
    lon = pl.program_id(0) * block + lax.broadcasted_iota(jnp.int32, (block * lat_dev, channels), 0) // lat_dev
    panel = fields_ref[...].reshape(block * lat_dev, channels)
    panel = jnp.where(lon < lon_dev, panel.astype(jnp.float32), 0.0).astype(jnp.bfloat16)
    taken = jnp.dot(take_ref[...], panel, preferred_element_type=jnp.float32).astype(jnp.bfloat16)
    place = 0
    for out, count in zip(outs, chunks):
        out[...] = taken[place * block : (place + count) * block].reshape(count, block, channels)
        place += count


def take_rows(fields, owner_slot, place, chunks):
    lon_dev, lat_dev, channels = fields.shape
    block = 16
    padded = up_to(lon_dev, 8)
    ints = jax.ShapeDtypeStruct((lat_dev,), jnp.int32)
    result = pl.pallas_call(
        functools.partial(take_kernel, chunks, lat_dev, lon_dev, block),
        out_shape=[jax.ShapeDtypeStruct((n, padded, channels), fields.dtype) for n in chunks] + [ints, ints],
        grid=(pl.cdiv(lon_dev, block),),
        in_specs=[SMEM_SPEC, SMEM_SPEC, pl.BlockSpec((block, lat_dev, channels), lambda i: (i, 0, 0))],
        out_specs=[pl.BlockSpec((n, block, channels), lambda i: (0, i, 0)) for n in chunks] + [SMEM_SPEC, SMEM_SPEC],
        scratch_shapes=[
            pltpu.SMEM((lat_dev,), jnp.int32),
            pltpu.VMEM((block * lat_dev, block * lat_dev), jnp.bfloat16),
        ],
        compiler_params=pltpu.CompilerParams(vmem_limit_bytes=VMEM_LIMIT),
        cost_estimate=pl.CostEstimate(
            flops=2 * fields.size * block * lat_dev, bytes_accessed=4 * fields.size, transcendentals=0
        ),
        name="take_rows",
    )(owner_slot, place, fields)
    return result[:-2], result[-2], result[-1]


def put_kernel(counts, lat_dev, padded, block, slots_ref, *refs):
    ins, (out_ref, put_ref) = refs[:-2], refs[-2:]

    @pl.when(pl.program_id(0) == 0)
    def _():
        row = lax.broadcasted_iota(jnp.int32, (block * lat_dev, block), 0)
        lon_in = lax.broadcasted_iota(jnp.int32, (block * lat_dev, block), 1)
        strips = []
        for place in range(lat_dev):
            wanted = lon_in * lat_dev + slots_ref[place]
            strips.append(jnp.where(row == wanted, 1.0, 0.0))
        put_ref[...] = jnp.concatenate(strips, axis=1).astype(jnp.bfloat16)

    channels = out_ref.shape[2]
    panel = jnp.concatenate([r[...].reshape(n * block, channels) for r, n in zip(ins, counts)], axis=0)
    lon = lax.broadcasted_iota(jnp.int32, (block * lat_dev, channels), 0) % block + pl.program_id(0) * block
    panel = jnp.where(lon < padded, panel.astype(jnp.float32), 0.0).astype(jnp.bfloat16)
    spread = jnp.dot(put_ref[...], panel, preferred_element_type=jnp.float32).astype(jnp.bfloat16)
    out_ref[...] = spread.reshape(block, lat_dev, channels)


def put_rows(panels, slots, lon_dev, lat_dev):
    padded, channels = panels[0].shape[1:]
    block = 16
    counts = tuple(p.shape[0] for p in panels)
    return pl.pallas_call(
        functools.partial(put_kernel, counts, lat_dev, padded, block),
        out_shape=jax.ShapeDtypeStruct((lon_dev, lat_dev, channels), panels[0].dtype),
        grid=(pl.cdiv(lon_dev, block),),
        in_specs=[SMEM_SPEC] + [pl.BlockSpec((n, block, channels), lambda i: (0, i, 0)) for n in counts],
        out_specs=pl.BlockSpec((block, lat_dev, channels), lambda i: (i, 0, 0)),
        scratch_shapes=[pltpu.VMEM((block * lat_dev, block * lat_dev), jnp.bfloat16)],
        compiler_params=pltpu.CompilerParams(vmem_limit_bytes=VMEM_LIMIT),
        cost_estimate=pl.CostEstimate(
            flops=2 * lon_dev * lat_dev * channels * block * lat_dev,
            bytes_accessed=4 * lon_dev * lat_dev * channels,
            transcendentals=0,
        ),
        name="put_rows",
    )(slots, *panels)


def pair_kernel(lon_dev, rows_ref, sign_ref, win_ref, own, other, x_own, x_other, z_own, z_other,
                out_own, out_other, block_ref, total_ref):
    padded, channels = own.shape[1:]
    for s in range(5):
        block_ref[s] = toeplitz(win_ref[0, s : s + 1, :], lon_dev, padded)
    side, along = sign_ref[0], sign_ref[1]

    def times(offset, panel):
        return jnp.dot(block_ref[2 + offset], panel, preferred_element_type=jnp.float32)[:padded]

    def both(first, second):
        return jnp.concatenate([first[0], second[0]], axis=1)

    here = both(own, other)
    total = here.astype(jnp.float32) + times(0, here)
    total += times(2 * along, both(x_own, x_other))
    total += times(-2 * along, both(z_own, z_other))
    total += jnp.concatenate([times(side, other[0]), times(-side, own[0])], axis=1)
    total_ref[...] = total

    @pl.when(side == along)
    def _():
        total_ref[...] += jnp.concatenate([times(-along, z_other[0]), times(along, x_own[0])], axis=1)

    @pl.when(side != along)
    def _():
        total_ref[...] += jnp.concatenate([times(along, x_other[0]), times(-along, z_own[0])], axis=1)

    out_own[0] = total_ref[:, :channels].astype(out_own.dtype)
    out_other[0] = total_ref[:, channels:].astype(out_other.dtype)


def filter_pair(rows, signs, windows, panels, base, lon_dev):
    count, padded, channels = panels[0].shape
    row_spec = pl.BlockSpec((1, padded, channels), lambda i, rows, signs: (i, 0, 0))
    win_spec = pl.BlockSpec((1,) + windows.shape[1:], lambda i, rows, signs: (rows[base + i], 0, 0))
    out = jax.ShapeDtypeStruct((count, padded, channels), panels[0].dtype)
    tall = up_to(lon_dev, 96)
    return pl.pallas_call(
        functools.partial(pair_kernel, lon_dev),
        out_shape=[out, out],
        grid_spec=pltpu.PrefetchScalarGridSpec(
            num_scalar_prefetch=2,
            grid=(count,),
            in_specs=[win_spec] + [row_spec] * len(panels),
            out_specs=[row_spec, row_spec],
            scratch_shapes=[
                pltpu.VMEM((5, tall, padded), jnp.bfloat16),
                pltpu.VMEM((padded, 2 * channels), jnp.float32),
            ],
        ),
        compiler_params=pltpu.CompilerParams(vmem_limit_bytes=VMEM_LIMIT),
        cost_estimate=pl.CostEstimate(
            flops=2 * count * 10 * 256 * 256 * 768,
            bytes_accessed=2 * 8 * panels[0].size,
            transcendentals=0,
        ),
        name="filter_pair",
    )(rows, signs, windows, *panels)


def chip_aware(fields, owner_slot, widths, tap_weights):
    lat_dev, lon_dev, channels = fields.shape
    n_lon = lax.axis_size("lon")
    at = lax.axis_index("lon")
    band = lax.axis_index("lat")
    core, x = at % 2, at // 2 % 2
    place = jnp.stack([band, core]).astype(jnp.int32)
    signs = jnp.stack([1 - 2 * core, 1 - 2 * x]).astype(jnp.int32)
    chunks = STAY + STAY + COME + COME
    taken, rows, slots = take_rows(jnp.transpose(fields, (1, 0, 2)), owner_slot, place, chunks)
    n_stay, n_come = len(STAY), len(COME)
    keep, give = taken[:n_stay], taken[n_stay : 2 * n_stay]
    straight, cross = taken[2 * n_stay : 2 * n_stay + n_come], taken[2 * n_stay + n_come :]

    across_core = [(i, i ^ 1) for i in range(n_lon)]
    across_x = [(i, i ^ 2) for i in range(n_lon)]
    across_z = [(i, (i + (4 if i // 2 % 2 == 0 else -4)) % n_lon) for i in range(n_lon)]
    across_y = [(i, i ^ 1) for i in range(2 * n_lon)]
    across_both = [(i, i ^ 3) for i in range(2 * n_lon)]

    own = list(keep)
    other = [lax.ppermute(g, "lon", across_core) for g in give]
    own += [lax.ppermute(s, ("lon", "lat"), across_y) for s in straight]
    other += [lax.ppermute(s, ("lon", "lat"), across_both) for s in cross]
    windows = tap_windows(widths, tap_weights, lon_dev, 2)
    mine, theirs = [], []
    base = 0
    for part in zip(own, other):
        by_x = [lax.ppermute(p, "lon", across_x) for p in part]
        by_z = [lax.ppermute(p, "lon", across_z) for p in by_x]
        out_own, out_other = filter_pair(rows, signs, windows, list(part) + by_x + by_z, base, lon_dev)
        mine.append(out_own)
        theirs.append(lax.ppermute(out_other, "lon", across_core))
        base += part[0].shape[0]
    out = put_rows(mine + theirs, slots, lon_dev, lat_dev)
    return jnp.transpose(out, (1, 0, 2))


def filter_kernel(rows_ref, slots_ref, sector_ref, win_ref, *refs):
    ins, out_ref = refs[:-1], refs[-1]
    lon_dev, channels = out_ref.shape[1:]
    total = ins[0][0].astype(jnp.float32)
    for group, ref in enumerate(ins):
        block = toeplitz(win_ref[0, pl.ds(sector_ref[group], 1), :], lon_dev, lon_dev)
        total += jnp.dot(block, ref[0], preferred_element_type=jnp.float32)[:lon_dev]
    out_ref[0] = total.astype(out_ref.dtype)


def filter_rows(rows, slots, sectors, windows, arrays):
    lat_dev, lon_dev, channels = arrays[0].shape
    row_spec = pl.BlockSpec((1, lon_dev, channels), lambda i, rows, slots, sectors: (i, 0, 0))
    win_spec = pl.BlockSpec((1,) + windows.shape[1:], lambda i, rows, slots, sectors: (rows[i], 0, 0))
    out_spec = pl.BlockSpec((1, lon_dev, channels), lambda i, rows, slots, sectors: (slots[i], 0, 0))
    return pl.pallas_call(
        filter_kernel,
        out_shape=jax.ShapeDtypeStruct(arrays[0].shape, arrays[0].dtype),
        grid_spec=pltpu.PrefetchScalarGridSpec(
            num_scalar_prefetch=3,
            grid=(lat_dev,),
            in_specs=[win_spec] + [row_spec] * len(arrays),
            out_specs=out_spec,
        ),
        compiler_params=pltpu.CompilerParams(vmem_limit_bytes=VMEM_LIMIT),
        name="filter_rows",
    )(rows, slots, sectors, windows, *arrays)


def any_mesh(fields, owner_slot, widths, tap_weights):
    lat_dev, lon_dev, channels = fields.shape
    n_lon = lax.axis_size("lon")
    n_lat = lax.axis_size("lat")
    reach = n_lon // 8
    band = lax.axis_index("lat")
    dest_band = owner_slot // lat_dev
    home_rows = band * lat_dev + jnp.arange(lat_dev, dtype=jnp.int32)
    ordering = jnp.argsort(dest_band[home_rows], stable=True)
    rows = jnp.argsort((dest_band != band).astype(jnp.int32), stable=True)[:lat_dev].astype(jnp.int32)
    slots = (owner_slot[rows] % lat_dev).astype(jnp.int32)
    outgoing = fields[ordering].reshape(n_lat, lat_dev // n_lat, lon_dev, channels)
    incoming = lax.all_to_all(outgoing, "lat", split_axis=0, concat_axis=0, tiled=True)
    own = incoming.reshape(lat_dev, lon_dev, channels)
    windows = tap_windows(widths, tap_weights, lon_dev, reach)
    arrays, order = [own], [reach]
    ahead = behind = own
    for step in range(1, reach + 1):
        ahead = shift_by(ahead, "lon", -1)
        behind = shift_by(behind, "lon", 1)
        arrays += [ahead, behind]
        order += [reach + step, reach - step]
    sectors = jnp.array(order, jnp.int32)
    return filter_rows(rows, slots, sectors, windows, arrays)


def solution(mesh):
    in_specs = (P("lat", "lon", None), P(), P(), P())
    out_specs = P("lat", "lon", None)
    body = chip_aware if (mesh.shape["lon"], mesh.shape["lat"]) == (16, 2) else any_mesh
    return jax.shard_map(body, mesh=mesh, in_specs=in_specs, out_specs=out_specs, check_vma=False)
```

time: 539 us -> 180 us (0.33)
  local copies, waits for them, and re-layouts: 427 us -> 6.6 us
  waiting for transfers between devices: 40.4 us -> 107 us
  matrix products: 45.6 us -> 0 us
  Pallas kernels: 0 us -> 36.7 us
  starting transfers between devices: 11.5 us -> 28.4 us
  other arithmetic: 11.8 us -> 0.35 us
    gather x23 -> x0, local copies, waits for them, and re-layouts: 398 us -> none  [the longest x15 374 us: sector_term(): tap_block = jnp.take(active, tap_index, axis=1)]
    ppermute x5 -> x26, waiting for transfers between devices: 0.5 us -> 107 us  [the longest x8 47.1 us: chip_aware(): by_x = [lax.ppermute(p, 'lon', across_x) for p in part]]
    dot_general x5 -> x0, matrix products: 45.6 us -> none  [sector_term(): jnp.einsum('sim,smc->sic', tap_block, sector, preferred_element_type=jnp....]
    all_to_all x1 -> x0, waiting for transfers between devices: 39.9 us -> none  [body(): lax.all_to_all(outgoing, 'lat', split_axis=0, concat_axis=0, tiled=True)]
    pallas_call x0 -> x6, Pallas kernels: none -> 36.7 us  [the longest x4 17 us: filter_pair(): pl.pallas_call(functools.partial(pair_kernel, lon_dev), out_shape=[out, o...]
    ppermute x5 -> x26, starting transfers between devices: 5.96 us -> 28.4 us  [the longest x8 11 us: chip_aware(): by_x = [lax.ppermute(p, 'lon', across_x) for p in part]]
    while x4 -> x0, local copies, waits for them, and re-layouts: 16.9 us -> none
    convert_element_type x2 -> x0, other arithmetic: 5.71 us -> none  [the longest x1 5.01 us: body(): return (panel_rows.astype(jnp.float32) + summed).astype(jnp.bfloat16)]
  transfers between devices with their start and end apart: 6 -> 26, of which waited for: 2 -> 14; matrix products, arithmetic and copies ran while one was open for 71% -> 1% of each run, Pallas kernels for 0% -> 9%
where the time goes in v2:
time: 180 us; the launch traced here: 179 us
  waiting for transfers between devices  107 us (59%)
  Pallas kernels  36.7 us (20%)
  starting transfers between devices  28.4 us (16%)
  local copies, waits for them, and re-layouts  6.6 us (4%)
    ppermute x8, waiting for transfers between devices, chip_aware(): by_x = [lax.ppermute(p, 'lon', across_x) for p in part]  47.1 us
    ppermute x8, waiting for transfers between devices, chip_aware(): by_z = [lax.ppermute(p, 'lon', across_z) for p in by_x]  24.6 us
    ppermute x2, waiting for transfers between devices, chip_aware(): own += [lax.ppermute(s, ('lon', 'lat'), across_y) for s in straight]  19.4 us
    pallas_call x4, Pallas kernels, filter_pair(): pl.pallas_call(functools.partial(pair_kernel, lon_dev), out_shape=[out, o...  17 us
    ppermute x2, waiting for transfers between devices, chip_aware(): other += [lax.ppermute(s, ('lon', 'lat'), across_both) for s in cross]  14.1 us
    pallas_call x1, Pallas kernels, take_rows(): pl.pallas_call(functools.partial(take_kernel, chunks, lat_dev, lon_dev, b...  11.3 us
    ppermute x8, starting transfers between devices, chip_aware(): by_x = [lax.ppermute(p, 'lon', across_x) for p in part]  11 us
    ppermute x8, starting transfers between devices, chip_aware(): by_z = [lax.ppermute(p, 'lon', across_z) for p in by_x]  10.8 us
  transfers between devices with their start and end apart: 26, of which 14 were waited for; matrix products, arithmetic and copies ran while one was open for 1% of the time, Pallas kernels for 9%

profile of v2, /device:TPU:0, one launch (start us, length us, event | category | flops | bytes accessed | tf_op | source)
XLA Modules:
  0.0 179.3 jit_solution(5099319952703939292)
XLA Ops:
  0.0 0.1 pad_add_fusion.place_ref
  0.1 0.7 copy-done
  0.7 11.3 %take_rows.1 = (bf16[2,184,640]{2,1,0:T(8,128)(2,1)S(1)}, bf16[2,184,640]{2,1,0:T(8,128)(2,1)S(1)}, bf16[2,184,640]{2,1,0:T(8,128)(2,1)S(1)}, bf16[2,184,640]{2,...) custom-call(s32[32]{0:T(128)S(1)} %copy-done, ...), custom_call_target="tpu_custom_call" | custom-call | flops 943718400 | bytes 7372800 | tf_op jit(solution)/shard_map/take_rows/pallas_call | solution.py:118
  12.1 3.0 %collective-permute-start.16 = (bf16[2,184,640]{2,1,0:T(8,128)(2,1)S(1)}, bf16[2,184,640]{2,1,0:T(8,128)(2,1)S(1)}, u32[]{:S(2)}, u32[]{:S(2)}) collective-permute-start(bf16[2,184,640]{2,1,0:T(8,128)(2,1)S(1)} %get-tuple-element.34), channel_id=1, source_target_pairs={{0,1},{1,0},{2,3},{3,2},{4,5},{5,4},{6,7},{7,6},{8,9},{9,8},{10,11... | collective-permute-start | bytes 1413128 | tf_op jit(solution)/shard_map/ppermute | solution.py:262
  15.1 0.0 collective-permute-start.17
  15.1 1.2 collective-permute-start.10
  16.3 0.6 collective-permute-start.11
  16.9 0.4 collective-permute-start.5
  17.3 9.4 %collective-permute-done.16.own = bf16[2,184,640]{2,1,0:T(8,128)(2,1)S(1)} collective-permute-done((bf16[2,184,640]{2,1,0:T(8,128)(2,1)S(1)}, bf16[2,184,640]{2,1,0:T(8,128)(2,1)S(1)}, u32[]{:S(2)}, u32[]{:S(2)}) %collective-permute-start.16) | collective-permute-done | bytes 471072 | tf_op jit(solution)/shard_map/ppermute | solution.py:262
  26.7 2.0 %collective-permute-start.6 = (bf16[2,184,640]{2,1,0:T(8,128)(2,1)S(1)}, bf16[2,184,640]{2,1,0:T(8,128)(2,1)S(1)}, u32[]{:S(2)}, u32[]{:S(2)}) collective-permute-start(bf16[2,184,640]{2,1,0:T(8,128)(2,1)S(1)} %get-tuple-element.28.own), channel_id=1, source_target_pairs={{0,4},{2,6},{4,0},{6,2},{8,12},{10,14},{12,8},{14,10},{16,20},{18,... | collective-permute-start | bytes 1413128 | tf_op jit(solution)/shard_map/ppermute | solution.py:268
  28.7 7.6 %collective-permute-done.17.other = bf16[2,184,640]{2,1,0:T(8,128)(2,1)S(1)} collective-permute-done((bf16[2,184,640]{2,1,0:T(8,128)(2,1)S(1)}, bf16[2,184,640]{2,1,0:T(8,128)(2,1)S(1)}, u32[]{:S(2)}, u32[]{:S(2)}) %collective-permute-start.17) | collective-permute-done | bytes 471072 | tf_op jit(solution)/shard_map/ppermute | solution.py:263
  36.4 0.5 collective-permute-start
  36.9 10.0 %collective-permute-done.10.own = bf16[2,184,640]{2,1,0:T(8,128)(2,1)S(1)} collective-permute-done((bf16[2,184,640]{2,1,0:T(8,128)(2,1)S(1)}, bf16[2,184,640]{2,1,0:T(8,128)(2,1)S(1)}, u32[]{:S(2)}, u32[]{:S(2)}) %collective-permute-start.10) | collective-permute-done | bytes 471072 | tf_op jit(solution)/shard_map/ppermute | solution.py:262
  46.9 2.0 %collective-permute-start.1 = (bf16[2,184,640]{2,1,0:T(8,128)(2,1)S(1)}, bf16[2,184,640]{2,1,0:T(8,128)(2,1)S(1)}, u32[]{:S(2)}, u32[]{:S(2)}) collective-permute-start(bf16[2,184,640]{2,1,0:T(8,128)(2,1)S(1)} %get-tuple-element.25.own), channel_id=1, source_target_pairs={{0,4},{2,6},{4,0},{6,2},{8,12},{10,14},{12,8},{14,10},{16,20},{18,... | collective-permute-start | bytes 1413128 | tf_op jit(solution)/shard_map/ppermute | solution.py:268
  48.9 6.5 %collective-permute-done.11.other = bf16[2,184,640]{2,1,0:T(8,128)(2,1)S(1)} collective-permute-done((bf16[2,184,640]{2,1,0:T(8,128)(2,1)S(1)}, bf16[2,184,640]{2,1,0:T(8,128)(2,1)S(1)}, u32[]{:S(2)}, u32[]{:S(2)}) %collective-permute-start.11) | collective-permute-done | bytes 471072 | tf_op jit(solution)/shard_map/ppermute | solution.py:263
  55.4 1.5 collective-permute-start.18
  56.9 0.8 copy-done.5
  57.7 0.0 collective-permute-done.5.other
  57.7 0.5 collective-permute-start.19
  58.2 0.8 copy-done.7
  59.0 1.5 collective-permute-start.12
  60.5 0.5 collective-permute-start.13
  61.1 0.1 convert_select_fusion
  61.2 1.6 collective-permute-start.7
  62.7 0.1 fusion.3
  62.8 6.3 %collective-permute-done.18.x_own = bf16[2,184,640]{2,1,0:T(8,128)(2,1)} collective-permute-done((bf16[2,184,640]{2,1,0:T(8,128)(2,1)S(1)}, bf16[2,184,640]{2,1,0:T(8,128)(2,1)}, u32[]{:S(2)}, u32[]{:S(2)}) %collective-permute-start.18) | collective-permute-done | bytes 471072 | tf_op jit(solution)/shard_map/ppermute | solution.py:268
  69.2 1.4 collective-permute-start.2
  70.6 8.7 %collective-permute-done.19.x_other = bf16[2,184,640]{2,1,0:T(8,128)(2,1)} collective-permute-done((bf16[2,184,640]{2,1,0:T(8,128)(2,1)S(1)}, bf16[2,184,640]{2,1,0:T(8,128)(2,1)}, u32[]{:S(2)}, u32[]{:S(2)}) %collective-permute-start.19) | collective-permute-done | bytes 471072 | tf_op jit(solution)/shard_map/ppermute | solution.py:268
  79.3 1.5 collective-permute-start.20
  80.7 0.1 fusion.2
  80.8 8.5 %collective-permute-done.12.x_own = bf16[2,184,640]{2,1,0:T(8,128)(2,1)} collective-permute-done((bf16[2,184,640]{2,1,0:T(8,128)(2,1)S(1)}, bf16[2,184,640]{2,1,0:T(8,128)(2,1)}, u32[]{:S(2)}, u32[]{:S(2)}) %collective-permute-start.12) | collective-permute-done | bytes 471072 | tf_op jit(solution)/shard_map/ppermute | solution.py:268
  89.4 1.5 collective-permute-start.21
  90.8 8.6 %collective-permute-done.13.x_other = bf16[2,184,640]{2,1,0:T(8,128)(2,1)} collective-permute-done((bf16[2,184,640]{2,1,0:T(8,128)(2,1)S(1)}, bf16[2,184,640]{2,1,0:T(8,128)(2,1)}, u32[]{:S(2)}, u32[]{:S(2)}) %collective-permute-start.13) | collective-permute-done | bytes 471072 | tf_op jit(solution)/shard_map/ppermute | solution.py:268
  99.5 1.5 collective-permute-start.14
  100.9 0.6 pad_bitcast_fusion
  101.6 0.1 copy.5
  101.6 0.9 copy.6
  102.5 0.1 fusion.1
  102.6 0.1 copy.7
  102.7 6.9 %collective-permute-done.7.x_other = bf16[2,184,640]{2,1,0:T(8,128)(2,1)} collective-permute-done((bf16[2,184,640]{2,1,0:T(8,128)(2,1)S(1)}, bf16[2,184,640]{2,1,0:T(8,128)(2,1)}, u32[]{:S(2)}, u32[]{:S(2)}) %collective-permute-start.7) | collective-permute-done | bytes 471072 | tf_op jit(solution)/shard_map/ppermute | solution.py:268
  109.6 1.5 collective-permute-start.15
  111.0 0.1 copy.8
  111.1 0.5 stack.47.win_ref
  111.6 8.0 %collective-permute-done.2.x_other = bf16[2,184,640]{2,1,0:T(8,128)(2,1)} collective-permute-done((bf16[2,184,640]{2,1,0:T(8,128)(2,1)S(1)}, bf16[2,184,640]{2,1,0:T(8,128)(2,1)}, u32[]{:S(2)}, u32[]{:S(2)}) %collective-permute-start.2) | collective-permute-done | bytes 471072 | tf_op jit(solution)/shard_map/ppermute | solution.py:268
  119.5 1.6 collective-permute-start.8
  121.1 1.6 collective-permute-start.9
  122.7 0.1 pad_add_fusion.1.sign_ref
  122.8 1.6 collective-permute-start.3
  124.4 0.2 collective-permute-start.4
  124.6 1.0 copy-done.6
  125.6 1.0 copy-done.8
  126.6 4.4 %filter_pair.7 = (bf16[2,184,640]{2,1,0:T(8,128)(2,1)S(1)}, bf16[2,184,640]{2,1,0:T(8,128)(2,1)S(1)}) custom-call(s32[16]{0:T(128)S(1)} %get-tuple-element.24.rows_ref, s32[2]{0:T(128)S(1)} %pad_add_fusion.1.sign_ref, f32[32,5,384]{2,1,0:T(8,128)S(1)} %stack.47.win_ref, bf16[2,184,640]{2,1,0:T(8,128)(2,1)S(1)} %copy-done.6, ...), custom_call_target="tpu_custom_call" | custom-call | flops 2013265920 | bytes 3768320 | tf_op jit(solution)/shard_map/filter_pair/pallas_call | solution.py:217
  131.1 0.1 collective-permute-start.25
  131.2 4.4 %filter_pair.6 = (bf16[2,184,640]{2,1,0:T(8,128)(2,1)S(1)}, bf16[2,184,640]{2,1,0:T(8,128)(2,1)S(1)}) custom-call(s32[16]{0:T(128)S(1)} %get-tuple-element.24.rows_ref, s32[2]{0:T(128)S(1)} %pad_add_fusion.1.sign_ref, f32[32,5,384]{2,1,0:T(8,128)S(1)} %stack.47.win_ref, bf16[2,184,640]{2,1,0:T(8,128)(2,1)S(1)} %copy-done.2, ...), custom_call_target="tpu_custom_call" | custom-call | flops 2013265920 | bytes 3768320 | tf_op jit(solution)/shard_map/filter_pair/pallas_call | solution.py:217
  135.6 0.5 collective-permute-start.24
  136.2 8.9 %collective-permute-done.9.z_other = bf16[2,184,640]{2,1,0:T(8,128)(2,1)S(1)} collective-permute-done((bf16[2,184,640]{2,1,0:T(8,128)(2,1)}, bf16[2,184,640]{2,1,0:T(8,128)(2,1)S(1)}, u32[]{:S(2)}, u32[]{:S(2)}) %collective-permute-start.9) | collective-permute-done | bytes 471072 | tf_op jit(solution)/shard_map/ppermute | solution.py:269
  145.0 4.1 %filter_pair.5 = (bf16[2,184,640]{2,1,0:T(8,128)(2,1)S(1)}, bf16[2,184,640]{2,1,0:T(8,128)(2,1)S(1)}) custom-call(s32[16]{0:T(128)S(1)} %get-tuple-element.24.rows_ref, s32[2]{0:T(128)S(1)} %pad_add_fusion.1.sign_ref, f32[32,5,384]{2,1,0:T(8,128)S(1)} %stack.47.win_ref, bf16[2,184,640]{2,1,0:T(8,128)(2,1)S(1)} %get-tuple-element.28.own, ...), custom_call_target="tpu_custom_call" | custom-call | flops 2013265920 | bytes 3768320 | tf_op jit(solution)/shard_map/filter_pair/pallas_call | solution.py:217
  149.1 0.1 collective-permute-start.23
  149.2 5.9 %collective-permute-done.3.z_own = bf16[2,184,640]{2,1,0:T(8,128)(2,1)S(1)} collective-permute-done((bf16[2,184,640]{2,1,0:T(8,128)(2,1)S(1)}, bf16[2,184,640]{2,1,0:T(8,128)(2,1)S(1)}, u32[]{:S(2)}, u32[]{:S(2)}) %collective-permute-start.3) | collective-permute-done | bytes 471072 | tf_op jit(solution)/shard_map/ppermute | solution.py:269
  155.1 9.8 %collective-permute-done.4.z_other = bf16[2,184,640]{2,1,0:T(8,128)(2,1)S(1)} collective-permute-done((bf16[2,184,640]{2,1,0:T(8,128)(2,1)}, bf16[2,184,640]{2,1,0:T(8,128)(2,1)S(1)}, u32[]{:S(2)}, u32[]{:S(2)}) %collective-permute-start.4) | collective-permute-done | bytes 471072 | tf_op jit(solution)/shard_map/ppermute | solution.py:269
  164.9 4.1 %filter_pair.4 = (bf16[2,184,640]{2,1,0:T(8,128)(2,1)S(1)}, bf16[2,184,640]{2,1,0:T(8,128)(2,1)S(1)}) custom-call(s32[16]{0:T(128)S(1)} %get-tuple-element.24.rows_ref, s32[2]{0:T(128)S(1)} %pad_add_fusion.1.sign_ref, f32[32,5,384]{2,1,0:T(8,128)S(1)} %stack.47.win_ref, bf16[2,184,640]{2,1,0:T(8,128)(2,1)S(1)} %get-tuple-element.25.own, ...), custom_call_target="tpu_custom_call" | custom-call | flops 2013265920 | bytes 3768320 | tf_op jit(solution)/shard_map/filter_pair/pallas_call | solution.py:217
  169.0 0.1 collective-permute-start.22
  169.1 1.8 collective-permute-done.22.refs_4_
  170.9 8.4 %put_rows.1 = bf16[180,16,640]{2,1,0:T(8,128)(2,1)} custom-call(s32[16]{0:T(128)S(1)} %get-tuple-element.23.slots_ref, bf16[2,184,640]{2,1,0:T(8,128)(2,1)S(1)} %get-tuple-element.27.refs_0_, bf16[2,184,640]{2,1,0:T(8,128)(2,1)S(1)} %get-tuple-element.30.refs_1_, bf16[2,184,640]{2,1,0:T(8,128)(2,1)S(1)} %get-tuple-element.33.refs_2_, ...), custom_call_target="tpu_custom_call" | custom-call | flops 943718400 | bytes 7372800 | tf_op jit(solution)/shard_map/put_rows/pallas_call | solution.py:162
  (34 shorter events, 0.1 us)
Async XLA Ops:
  0.0 111.0 %copy-start.10 = (pred[384]{0:T(512)(128)(4,1)S(1)}, pred[384]{0:T(512)(128)(4,1)}, u32[]{:S(2)}) copy-start(pred[384]{0:T(512)(128)(4,1)} %constant.44.clone.1) | copy-start | bytes 1156
  0.0 61.1 %copy-start.11 = (s32[32]{0:T(128)S(1)}, s32[32]{0:T(128)}, u32[]{:S(2)}) copy-start(s32[32]{0:T(128)} %param.6) | copy-start | bytes 388
  0.1 0.7 copy-start
  0.7 60.3 %copy-start.9 = (bf16[32,2880]{1,0:T(8,128)(2,1)S(1)}, bf16[32,2880]{1,0:T(8,128)(2,1)}, u32[]{:S(2)}) copy-start(bf16[32,2880]{1,0:T(8,128)(2,1)} %param.7) | copy-start | bytes 552964
  12.1 14.6 %collective-permute-start.16 = (bf16[2,184,640]{2,1,0:T(8,128)(2,1)S(1)}, bf16[2,184,640]{2,1,0:T(8,128)(2,1)S(1)}, u32[]{:S(2)}, u32[]{:S(2)}) collective-permute-start(bf16[2,184,640]{2,1,0:T(8,128)(2,1)S(1)} %get-tuple-element.34), channel_id=1, source_target_pairs={{0,1},{1,0},{2,3},{3,2},{4,5},{5,4},{6,7},{7,6},{8,9},{9,8},{10,11... | collective-permute-start | bytes 1413128 | tf_op jit(solution)/shard_map/ppermute | solution.py:262
  15.1 21.3 %collective-permute-start.17 = (bf16[2,184,640]{2,1,0:T(8,128)(2,1)S(1)}, bf16[2,184,640]{2,1,0:T(8,128)(2,1)S(1)}, u32[]{:S(2)}, u32[]{:S(2)}) collective-permute-start(bf16[2,184,640]{2,1,0:T(8,128)(2,1)S(1)} %get-tuple-element.35), channel_id=1, source_target_pairs={{0,3},{1,2},{2,1},{3,0},{4,7},{5,6},{6,5},{7,4},{8,11},{9,10},{10,... | collective-permute-start | bytes 1413128 | tf_op jit(solution)/shard_map/ppermute | solution.py:263
  15.1 31.8 %collective-permute-start.10 = (bf16[2,184,640]{2,1,0:T(8,128)(2,1)S(1)}, bf16[2,184,640]{2,1,0:T(8,128)(2,1)S(1)}, u32[]{:S(2)}, u32[]{:S(2)}) collective-permute-start(bf16[2,184,640]{2,1,0:T(8,128)(2,1)S(1)} %get-tuple-element.31), channel_id=1, source_target_pairs={{0,1},{1,0},{2,3},{3,2},{4,5},{5,4},{6,7},{7,6},{8,9},{9,8},{10,11... | collective-permute-start | bytes 1413128 | tf_op jit(solution)/shard_map/ppermute | solution.py:262
  16.3 39.1 %collective-permute-start.11 = (bf16[2,184,640]{2,1,0:T(8,128)(2,1)S(1)}, bf16[2,184,640]{2,1,0:T(8,128)(2,1)S(1)}, u32[]{:S(2)}, u32[]{:S(2)}) collective-permute-start(bf16[2,184,640]{2,1,0:T(8,128)(2,1)S(1)} %get-tuple-element.32), channel_id=1, source_target_pairs={{0,3},{1,2},{2,1},{3,0},{4,7},{5,6},{6,5},{7,4},{8,11},{9,10},{10,... | collective-permute-start | bytes 1413128 | tf_op jit(solution)/shard_map/ppermute | solution.py:263
  16.9 40.8 %collective-permute-start.5 = (bf16[2,184,640]{2,1,0:T(8,128)(2,1)S(1)}, bf16[2,184,640]{2,1,0:T(8,128)(2,1)S(1)}, u32[]{:S(2)}, u32[]{:S(2)}) collective-permute-start(bf16[2,184,640]{2,1,0:T(8,128)(2,1)S(1)} %get-tuple-element.29), channel_id=1, source_target_pairs={{0,2},{2,0},{4,6},{6,4},{8,10},{10,8},{12,14},{14,12},{16,18},{18,... | collective-permute-start | bytes 1413128 | tf_op jit(solution)/shard_map/ppermute | solution.py:261
  26.7 32.3 %collective-permute-start.6 = (bf16[2,184,640]{2,1,0:T(8,128)(2,1)S(1)}, bf16[2,184,640]{2,1,0:T(8,128)(2,1)S(1)}, u32[]{:S(2)}, u32[]{:S(2)}) collective-permute-start(bf16[2,184,640]{2,1,0:T(8,128)(2,1)S(1)} %get-tuple-element.28.own), channel_id=1, source_target_pairs={{0,4},{2,6},{4,0},{6,2},{8,12},{10,14},{12,8},{14,10},{16,20},{18,... | collective-permute-start | bytes 1413128 | tf_op jit(solution)/shard_map/ppermute | solution.py:268
  36.4 24.1 %collective-permute-start = (bf16[2,184,640]{2,1,0:T(8,128)(2,1)S(1)}, bf16[2,184,640]{2,1,0:T(8,128)(2,1)S(1)}, u32[]{:S(2)}, u32[]{:S(2)}) collective-permute-start(bf16[2,184,640]{2,1,0:T(8,128)(2,1)S(1)} %get-tuple-element.26), channel_id=1, source_target_pairs={{0,2},{2,0},{4,6},{6,4},{8,10},{10,8},{12,14},{14,12},{16,18},{18,... | collective-permute-start | bytes 1413128 | tf_op jit(solution)/shard_map/ppermute | solution.py:261
  46.9 15.9 %copy-start.1 = (bf16[2,184,640]{2,1,0:T(8,128)(2,1)}, bf16[2,184,640]{2,1,0:T(8,128)(2,1)S(1)}, u32[]{:S(2)}) copy-start(bf16[2,184,640]{2,1,0:T(8,128)(2,1)S(1)} %collective-permute-done.10.own) | copy-start | bytes 1413124
  46.9 14.3 %collective-permute-start.1 = (bf16[2,184,640]{2,1,0:T(8,128)(2,1)S(1)}, bf16[2,184,640]{2,1,0:T(8,128)(2,1)S(1)}, u32[]{:S(2)}, u32[]{:S(2)}) collective-permute-start(bf16[2,184,640]{2,1,0:T(8,128)(2,1)S(1)} %get-tuple-element.25.own), channel_id=1, source_target_pairs={{0,4},{2,6},{4,0},{6,2},{8,12},{10,14},{12,8},{14,10},{16,20},{18,... | collective-permute-start | bytes 1413128 | tf_op jit(solution)/shard_map/ppermute | solution.py:268
  55.4 34.0 %copy-start.3 = (bf16[2,184,640]{2,1,0:T(8,128)(2,1)}, bf16[2,184,640]{2,1,0:T(8,128)(2,1)S(1)}, u32[]{:S(2)}) copy-start(bf16[2,184,640]{2,1,0:T(8,128)(2,1)S(1)} %collective-permute-done.11.other) | copy-start | bytes 1413124
  55.4 13.8 %collective-permute-start.18 = (bf16[2,184,640]{2,1,0:T(8,128)(2,1)S(1)}, bf16[2,184,640]{2,1,0:T(8,128)(2,1)}, u32[]{:S(2)}, u32[]{:S(2)}) collective-permute-start(bf16[2,184,640]{2,1,0:T(8,128)(2,1)S(1)} %collective-permute-done.16.own), channel_id=1, source_target_pairs={{0,4},{2,6},{4,0},{6,2},{8,12},{10,14},{12,8},{14,10},{16,20},{18,... | collective-permute-start | bytes 1413128 | tf_op jit(solution)/shard_map/ppermute | solution.py:268
  56.9 0.8 copy-start.5
  57.7 21.6 %collective-permute-start.19 = (bf16[2,184,640]{2,1,0:T(8,128)(2,1)S(1)}, bf16[2,184,640]{2,1,0:T(8,128)(2,1)}, u32[]{:S(2)}, u32[]{:S(2)}) collective-permute-start(bf16[2,184,640]{2,1,0:T(8,128)(2,1)S(1)} %collective-permute-done.17.other), channel_id=1, source_target_pairs={{0,4},{2,6},{4,0},{6,2},{8,12},{10,14},{12,8},{14,10},{16,20},{18,... | collective-permute-start | bytes 1413128 | tf_op jit(solution)/shard_map/ppermute | solution.py:268
  58.2 0.8 copy-start.7
  59.0 30.3 %collective-permute-start.12 = (bf16[2,184,640]{2,1,0:T(8,128)(2,1)S(1)}, bf16[2,184,640]{2,1,0:T(8,128)(2,1)}, u32[]{:S(2)}, u32[]{:S(2)}) collective-permute-start(bf16[2,184,640]{2,1,0:T(8,128)(2,1)S(1)} %collective-permute-done.10.own), channel_id=1, source_target_pairs={{0,4},{2,6},{4,0},{6,2},{8,12},{10,14},{12,8},{14,10},{16,20},{18,... | collective-permute-start | bytes 1413128 | tf_op jit(solution)/shard_map/ppermute | solution.py:268
  60.5 38.9 %collective-permute-start.13 = (bf16[2,184,640]{2,1,0:T(8,128)(2,1)S(1)}, bf16[2,184,640]{2,1,0:T(8,128)(2,1)}, u32[]{:S(2)}, u32[]{:S(2)}) collective-permute-start(bf16[2,184,640]{2,1,0:T(8,128)(2,1)S(1)} %collective-permute-done.11.other), channel_id=1, source_target_pairs={{0,4},{2,6},{4,0},{6,2},{8,12},{10,14},{12,8},{14,10},{16,20},{18,... | collective-permute-start | bytes 1413128 | tf_op jit(solution)/shard_map/ppermute | solution.py:268
  61.2 48.4 %collective-permute-start.7 = (bf16[2,184,640]{2,1,0:T(8,128)(2,1)S(1)}, bf16[2,184,640]{2,1,0:T(8,128)(2,1)}, u32[]{:S(2)}, u32[]{:S(2)}) collective-permute-start(bf16[2,184,640]{2,1,0:T(8,128)(2,1)S(1)} %collective-permute-done.5.other), channel_id=1, source_target_pairs={{0,4},{2,6},{4,0},{6,2},{8,12},{10,14},{12,8},{14,10},{16,20},{18,... | collective-permute-start | bytes 1413128 | tf_op jit(solution)/shard_map/ppermute | solution.py:268
  69.2 50.4 %collective-permute-start.2 = (bf16[2,184,640]{2,1,0:T(8,128)(2,1)S(1)}, bf16[2,184,640]{2,1,0:T(8,128)(2,1)}, u32[]{:S(2)}, u32[]{:S(2)}) collective-permute-start(bf16[2,184,640]{2,1,0:T(8,128)(2,1)S(1)} %collective-permute-done.other), channel_id=1, source_target_pairs={{0,4},{2,6},{4,0},{6,2},{8,12},{10,14},{12,8},{14,10},{16,20},{18,... | collective-permute-start | bytes 1413128 | tf_op jit(solution)/shard_map/ppermute | solution.py:268
  79.3 41.9 %collective-permute-start.20 = (bf16[2,184,640]{2,1,0:T(8,128)(2,1)}, bf16[2,184,640]{2,1,0:T(8,128)(2,1)}, u32[]{:S(2)}, u32[]{:S(2)}) collective-permute-start(bf16[2,184,640]{2,1,0:T(8,128)(2,1)} %collective-permute-done.18.x_own), channel_id=1, source_target_pairs={{0,8},{2,10},{4,28},{6,30},{8,16},{10,18},{12,4},{14,6},{16,24},{1... | collective-permute-start | bytes 1413128 | tf_op jit(solution)/shard_map/ppermute | solution.py:269
  89.4 33.4 %collective-permute-start.21 = (bf16[2,184,640]{2,1,0:T(8,128)(2,1)}, bf16[2,184,640]{2,1,0:T(8,128)(2,1)}, u32[]{:S(2)}, u32[]{:S(2)}) collective-permute-start(bf16[2,184,640]{2,1,0:T(8,128)(2,1)} %collective-permute-done.19.x_other), channel_id=1, source_target_pairs={{0,8},{2,10},{4,28},{6,30},{8,16},{10,18},{12,4},{14,6},{16,24},{1... | collective-permute-start | bytes 1413128 | tf_op jit(solution)/shard_map/ppermute | solution.py:269
  99.5 24.9 %collective-permute-start.14 = (bf16[2,184,640]{2,1,0:T(8,128)(2,1)}, bf16[2,184,640]{2,1,0:T(8,128)(2,1)}, u32[]{:S(2)}, u32[]{:S(2)}) collective-permute-start(bf16[2,184,640]{2,1,0:T(8,128)(2,1)} %collective-permute-done.12.x_own), channel_id=1, source_target_pairs={{0,8},{2,10},{4,28},{6,30},{8,16},{10,18},{12,4},{14,6},{16,24},{1... | collective-permute-start | bytes 1413128 | tf_op jit(solution)/shard_map/ppermute | solution.py:269
  109.6 21.5 %collective-permute-start.15 = (bf16[2,184,640]{2,1,0:T(8,128)(2,1)}, bf16[2,184,640]{2,1,0:T(8,128)(2,1)}, u32[]{:S(2)}, u32[]{:S(2)}) collective-permute-start(bf16[2,184,640]{2,1,0:T(8,128)(2,1)} %collective-permute-done.13.x_other), channel_id=1, source_target_pairs={{0,8},{2,10},{4,28},{6,30},{8,16},{10,18},{12,4},{14,6},{16,24},{1... | collective-permute-start | bytes 1413128 | tf_op jit(solution)/shard_map/ppermute | solution.py:269
  119.5 16.1 %collective-permute-start.8 = (bf16[2,184,640]{2,1,0:T(8,128)(2,1)S(1)}, bf16[2,184,640]{2,1,0:T(8,128)(2,1)S(1)}, u32[]{:S(2)}, u32[]{:S(2)}) collective-permute-start(bf16[2,184,640]{2,1,0:T(8,128)(2,1)S(1)} %collective-permute-done.6.x_own), channel_id=1, source_target_pairs={{0,8},{2,10},{4,28},{6,30},{8,16},{10,18},{12,4},{14,6},{16,24},{1... | collective-permute-start | bytes 1413128 | tf_op jit(solution)/shard_map/ppermute | solution.py:269
  121.1 23.9 %collective-permute-start.9 = (bf16[2,184,640]{2,1,0:T(8,128)(2,1)}, bf16[2,184,640]{2,1,0:T(8,128)(2,1)S(1)}, u32[]{:S(2)}, u32[]{:S(2)}) collective-permute-start(bf16[2,184,640]{2,1,0:T(8,128)(2,1)} %collective-permute-done.7.x_other), channel_id=1, source_target_pairs={{0,8},{2,10},{4,28},{6,30},{8,16},{10,18},{12,4},{14,6},{16,24},{1... | collective-permute-start | bytes 1413128 | tf_op jit(solution)/shard_map/ppermute | solution.py:269
  122.8 32.4 %collective-permute-start.3 = (bf16[2,184,640]{2,1,0:T(8,128)(2,1)S(1)}, bf16[2,184,640]{2,1,0:T(8,128)(2,1)S(1)}, u32[]{:S(2)}, u32[]{:S(2)}) collective-permute-start(bf16[2,184,640]{2,1,0:T(8,128)(2,1)S(1)} %collective-permute-done.1.x_own), channel_id=1, source_target_pairs={{0,8},{2,10},{4,28},{6,30},{8,16},{10,18},{12,4},{14,6},{16,24},{1... | collective-permute-start | bytes 1413128 | tf_op jit(solution)/shard_map/ppermute | solution.py:269
  124.4 40.6 %collective-permute-start.4 = (bf16[2,184,640]{2,1,0:T(8,128)(2,1)}, bf16[2,184,640]{2,1,0:T(8,128)(2,1)S(1)}, u32[]{:S(2)}, u32[]{:S(2)}) collective-permute-start(bf16[2,184,640]{2,1,0:T(8,128)(2,1)} %collective-permute-done.2.x_other), channel_id=1, source_target_pairs={{0,8},{2,10},{4,28},{6,30},{8,16},{10,18},{12,4},{14,6},{16,24},{1... | collective-permute-start | bytes 1413128 | tf_op jit(solution)/shard_map/ppermute | solution.py:269
  124.6 1.0 copy-start.6
  125.6 1.0 copy-start.8
  126.6 4.5 %copy-start.2 = (bf16[2,184,640]{2,1,0:T(8,128)(2,1)S(1)}, bf16[2,184,640]{2,1,0:T(8,128)(2,1)}, u32[]{:S(2)}) copy-start(bf16[2,184,640]{2,1,0:T(8,128)(2,1)} %copy-done.1) | copy-start | bytes 1413124
  126.6 4.5 %copy-start.4 = (bf16[2,184,640]{2,1,0:T(8,128)(2,1)S(1)}, bf16[2,184,640]{2,1,0:T(8,128)(2,1)}, u32[]{:S(2)}) copy-start(bf16[2,184,640]{2,1,0:T(8,128)(2,1)} %copy-done.3) | copy-start | bytes 1413124
  131.1 38.0 %collective-permute-start.25 = (bf16[2,184,640]{2,1,0:T(8,128)(2,1)S(1)}, bf16[2,184,640]{2,1,0:T(8,128)(2,1)S(1)}, u32[]{:S(2)}, u32[]{:S(2)}) collective-permute-start(bf16[2,184,640]{2,1,0:T(8,128)(2,1)S(1)} %get-tuple-element.40), channel_id=1, source_target_pairs={{0,2},{2,0},{4,6},{6,4},{8,10},{10,8},{12,14},{14,12},{16,18},{18,... | collective-permute-start | bytes 1413128 | tf_op jit(solution)/shard_map/ppermute | solution.py:272
  135.6 33.5 %collective-permute-start.24 = (bf16[2,184,640]{2,1,0:T(8,128)(2,1)S(1)}, bf16[2,184,640]{2,1,0:T(8,128)(2,1)S(1)}, u32[]{:S(2)}, u32[]{:S(2)}) collective-permute-start(bf16[2,184,640]{2,1,0:T(8,128)(2,1)S(1)} %get-tuple-element.39), channel_id=1, source_target_pairs={{0,2},{2,0},{4,6},{6,4},{8,10},{10,8},{12,14},{14,12},{16,18},{18,... | collective-permute-start | bytes 1413128 | tf_op jit(solution)/shard_map/ppermute | solution.py:272
  149.1 20.0 %collective-permute-start.23 = (bf16[2,184,640]{2,1,0:T(8,128)(2,1)S(1)}, bf16[2,184,640]{2,1,0:T(8,128)(2,1)S(1)}, u32[]{:S(2)}, u32[]{:S(2)}) collective-permute-start(bf16[2,184,640]{2,1,0:T(8,128)(2,1)S(1)} %get-tuple-element.38), channel_id=1, source_target_pairs={{0,2},{2,0},{4,6},{6,4},{8,10},{10,8},{12,14},{14,12},{16,18},{18,... | collective-permute-start | bytes 1413128 | tf_op jit(solution)/shard_map/ppermute | solution.py:272
  169.0 1.9 %collective-permute-start.22 = (bf16[2,184,640]{2,1,0:T(8,128)(2,1)S(1)}, bf16[2,184,640]{2,1,0:T(8,128)(2,1)S(1)}, u32[]{:S(2)}, u32[]{:S(2)}) collective-permute-start(bf16[2,184,640]{2,1,0:T(8,128)(2,1)S(1)} %get-tuple-element.37), channel_id=1, source_target_pairs={{0,2},{2,0},{4,6},{6,4},{8,10},{10,8},{12,14},{14,12},{16,18},{18,... | collective-permute-start | bytes 1413128 | tf_op jit(solution)/shard_map/ppermute | solution.py:272

commit v3 on v2

--- a/solution.py
+++ b/solution.py
@@ -9,6 +9,8 @@
 
 VMEM_LIMIT = 48 * 1024 * 1024
 SMEM_SPEC = pl.BlockSpec(memory_space=pltpu.SMEM)
+VMEM_SPEC = pl.BlockSpec(memory_space=pltpu.VMEM)
+ANY_SPEC = pl.BlockSpec(memory_space=pl.ANY)
 STAY = (2, 2)
 COME = (2, 2)
 
@@ -55,59 +57,68 @@
     return jnp.concatenate(bands, axis=0)
 
 
-def take_kernel(chunks, lat_dev, lon_dev, block, slot_ref, place_ref, fields_ref, *refs):
+def take_kernel(chunks, lat_dev, block, slot_ref, place_ref, fields_ref, *refs):
     outs = refs[: len(chunks)]
-    rows_ref, slots_ref, home_ref, take_ref = refs[len(chunks) :]
+    rows_ref, slots_ref, home_ref, take_ref, panel_ref, sems = refs[len(chunks) :]
+    lon_dev, _, channels = fields_ref.shape
     half, quarter = lat_dev // 2, lat_dev // 4
-
-    @pl.when(pl.program_id(0) == 0)
-    def _():
-        band, core = place_ref[0], place_ref[1]
-
-        def at(n):
-            mine = n // quarter == core
-            return n % quarter + jnp.where(mine, 0, quarter)
-
-        stay, leave, come = jnp.int32(0), jnp.int32(0), jnp.int32(0)
-        for j in range(lat_dev):
-            here = band * lat_dev + j
-            there = (1 - band) * lat_dev + j
-            stays = slot_ref[here] // lat_dev == band
-            comes = slot_ref[there] // lat_dev == band
-            home_ref[jnp.where(stays, at(stay), half + at(leave))] = jnp.int32(j)
-
-            @pl.when(stays)
-            def _():
-                spot = at(stay)
-                spot = spot + jnp.where(spot >= quarter, quarter, 0)
-                rows_ref[spot] = here
-                slots_ref[spot] = slot_ref[here] % lat_dev
-
-            @pl.when(comes)
-            def _():
-                spot = at(come)
-                spot = spot + jnp.where(spot >= quarter, half, quarter)
-                rows_ref[spot] = there
-                slots_ref[spot] = slot_ref[there] % lat_dev
-
-            stay = stay + stays.astype(jnp.int32)
-            leave = leave + 1 - stays.astype(jnp.int32)
-            come = come + comes.astype(jnp.int32)
-        lon_out = lax.broadcasted_iota(jnp.int32, (block, block * lat_dev), 0)
-        column = lax.broadcasted_iota(jnp.int32, (block, block * lat_dev), 1)
-        for place in range(lat_dev):
-            wanted = lon_out * lat_dev + home_ref[place]
-            take_ref[pl.ds(place * block, block), :] = jnp.where(column == wanted, 1.0, 0.0).astype(jnp.bfloat16)
-
-    channels = fields_ref.shape[2]
-    lon = pl.program_id(0) * block + lax.broadcasted_iota(jnp.int32, (block * lat_dev, channels), 0) // lat_dev
-    panel = fields_ref[...].reshape(block * lat_dev, channels)
-    panel = jnp.where(lon < lon_dev, panel.astype(jnp.float32), 0.0).astype(jnp.bfloat16)
-    taken = jnp.dot(take_ref[...], panel, preferred_element_type=jnp.float32).astype(jnp.bfloat16)
-    place = 0
-    for out, count in zip(outs, chunks):
-        out[...] = taken[place * block : (place + count) * block].reshape(count, block, channels)
-        place += count
+    starts = list(range(0, lon_dev, block))
+    copies = []
+    for n, start in enumerate(starts):
+        window = pl.ds(start, min(block, lon_dev - start))
+        copies.append(pltpu.make_async_copy(fields_ref.at[window], panel_ref.at[window], sems.at[n]))
+        copies[-1].start()
+
+    band, core = place_ref[0], place_ref[1]
+
+    def at(n):
+        return n % quarter + jnp.where(n // quarter == core, 0, quarter)
+
+    stay, leave, come = jnp.int32(0), jnp.int32(0), jnp.int32(0)
+    for j in range(lat_dev):
+        here = band * lat_dev + j
+        there = (1 - band) * lat_dev + j
+        stays = slot_ref[here] // lat_dev == band
+        comes = slot_ref[there] // lat_dev == band
+        home_ref[jnp.where(stays, at(stay), half + at(leave))] = jnp.int32(j)
+
+        @pl.when(stays)
+        def _():
+            spot = at(stay)
+            spot = spot + jnp.where(spot >= quarter, quarter, 0)
+            rows_ref[spot] = here
+            slots_ref[spot] = slot_ref[here] % lat_dev
+
+        @pl.when(comes)
+        def _():
+            spot = at(come)
+            spot = spot + jnp.where(spot >= quarter, half, quarter)
+            rows_ref[spot] = there
+            slots_ref[spot] = slot_ref[there] % lat_dev
+
+        stay = stay + stays.astype(jnp.int32)
+        leave = leave + 1 - stays.astype(jnp.int32)
+        come = come + comes.astype(jnp.int32)
+
+    def selector(lon_in, lon_out):
+        lon = lax.broadcasted_iota(jnp.int32, (lon_out, lon_in * lat_dev), 0)
+        column = lax.broadcasted_iota(jnp.int32, (lon_out, lon_in * lat_dev), 1)
+        strips = [jnp.where(column == lon * lat_dev + home_ref[p], 1.0, 0.0) for p in range(lat_dev)]
+        return jnp.concatenate(strips, axis=0).astype(jnp.bfloat16)
+
+    take_ref[...] = selector(block, block)
+    for n, start in enumerate(starts):
+        copies[n].wait()
+        lon_in = min(block, lon_dev - start)
+        lon_out = min(block, outs[0].shape[1] - start)
+        panel = panel_ref[start : start + lon_in].reshape(lon_in * lat_dev, channels)
+        take = take_ref[...] if (lon_in, lon_out) == (block, block) else selector(lon_in, lon_out)
+        taken = jnp.dot(take, panel, preferred_element_type=jnp.float32).astype(jnp.bfloat16)
+        place = 0
+        for out, count in zip(outs, chunks):
+            for i in range(count):
+                out[i, start : start + lon_out, :] = taken[place * lon_out : (place + 1) * lon_out]
+                place += 1
 
 
 def take_rows(fields, owner_slot, place, chunks):
@@ -116,14 +127,15 @@
     padded = up_to(lon_dev, 8)
     ints = jax.ShapeDtypeStruct((lat_dev,), jnp.int32)
     result = pl.pallas_call(
-        functools.partial(take_kernel, chunks, lat_dev, lon_dev, block),
+        functools.partial(take_kernel, chunks, lat_dev, block),
         out_shape=[jax.ShapeDtypeStruct((n, padded, channels), fields.dtype) for n in chunks] + [ints, ints],
-        grid=(pl.cdiv(lon_dev, block),),
-        in_specs=[SMEM_SPEC, SMEM_SPEC, pl.BlockSpec((block, lat_dev, channels), lambda i: (i, 0, 0))],
-        out_specs=[pl.BlockSpec((n, block, channels), lambda i: (0, i, 0)) for n in chunks] + [SMEM_SPEC, SMEM_SPEC],
+        in_specs=[SMEM_SPEC, SMEM_SPEC, ANY_SPEC],
+        out_specs=[VMEM_SPEC] * len(chunks) + [SMEM_SPEC, SMEM_SPEC],
         scratch_shapes=[
             pltpu.SMEM((lat_dev,), jnp.int32),
             pltpu.VMEM((block * lat_dev, block * lat_dev), jnp.bfloat16),
+            pltpu.VMEM(fields.shape, fields.dtype),
+            pltpu.SemaphoreType.DMA((pl.cdiv(lon_dev, block),)),
         ],
         compiler_params=pltpu.CompilerParams(vmem_limit_bytes=VMEM_LIMIT),
         cost_estimate=pl.CostEstimate(
@@ -134,38 +146,49 @@
     return result[:-2], result[-2], result[-1]
 
 
-def put_kernel(counts, lat_dev, padded, block, slots_ref, *refs):
-    ins, (out_ref, put_ref) = refs[:-2], refs[-2:]
-
-    @pl.when(pl.program_id(0) == 0)
-    def _():
-        row = lax.broadcasted_iota(jnp.int32, (block * lat_dev, block), 0)
-        lon_in = lax.broadcasted_iota(jnp.int32, (block * lat_dev, block), 1)
-        strips = []
-        for place in range(lat_dev):
-            wanted = lon_in * lat_dev + slots_ref[place]
-            strips.append(jnp.where(row == wanted, 1.0, 0.0))
-        put_ref[...] = jnp.concatenate(strips, axis=1).astype(jnp.bfloat16)
-
-    channels = out_ref.shape[2]
-    panel = jnp.concatenate([r[...].reshape(n * block, channels) for r, n in zip(ins, counts)], axis=0)
-    lon = lax.broadcasted_iota(jnp.int32, (block * lat_dev, channels), 0) % block + pl.program_id(0) * block
-    panel = jnp.where(lon < padded, panel.astype(jnp.float32), 0.0).astype(jnp.bfloat16)
-    spread = jnp.dot(put_ref[...], panel, preferred_element_type=jnp.float32).astype(jnp.bfloat16)
-    out_ref[...] = spread.reshape(block, lat_dev, channels)
+def put_kernel(counts, lat_dev, block, slots_ref, *refs):
+    ins, (out_ref, panel_ref, sems) = refs[:-3], refs[-3:]
+    lon_dev, _, channels = out_ref.shape
+
+    def selector(lon_in, lon_out):
+        shape = (lon_out * lat_dev, lat_dev * lon_in)
+        row = lax.broadcasted_iota(jnp.int32, shape, 0)
+        column = lax.broadcasted_iota(jnp.int32, (8, lat_dev * lon_in), 1)
+        wanted = column % lon_in * lat_dev
+        for p in range(lat_dev):
+            wanted += jnp.where(column // lon_in == p, slots_ref[p], 0)
+        return jnp.where(row == wanted[:1], 1.0, 0.0).astype(jnp.bfloat16)
+
+    whole = selector(block, block)
+    copies = []
+    for n, start in enumerate(range(0, lon_dev, block)):
+        lon_out = min(block, lon_dev - start)
+        lon_in = min(block, ins[0].shape[1] - start)
+        pieces = [r[i, start : start + lon_in, :] for r, count in zip(ins, counts) for i in range(count)]
+        put = whole if (lon_in, lon_out) == (block, block) else selector(lon_in, lon_out)
+        spread = jnp.dot(put, jnp.concatenate(pieces, axis=0), preferred_element_type=jnp.float32)
+        window = pl.ds(start, lon_out)
+        panel_ref[window] = spread.astype(jnp.bfloat16).reshape(lon_out, lat_dev, channels)
+        copies.append(pltpu.make_async_copy(panel_ref.at[window], out_ref.at[window], sems.at[n]))
+        copies[-1].start()
+    for copy in copies:
+        copy.wait()
 
 
 def put_rows(panels, slots, lon_dev, lat_dev):
     padded, channels = panels[0].shape[1:]
     block = 16
     counts = tuple(p.shape[0] for p in panels)
+    shape = (lon_dev, lat_dev, channels)
     return pl.pallas_call(
-        functools.partial(put_kernel, counts, lat_dev, padded, block),
-        out_shape=jax.ShapeDtypeStruct((lon_dev, lat_dev, channels), panels[0].dtype),
-        grid=(pl.cdiv(lon_dev, block),),
-        in_specs=[SMEM_SPEC] + [pl.BlockSpec((n, block, channels), lambda i: (0, i, 0)) for n in counts],
-        out_specs=pl.BlockSpec((block, lat_dev, channels), lambda i: (i, 0, 0)),
-        scratch_shapes=[pltpu.VMEM((block * lat_dev, block * lat_dev), jnp.bfloat16)],
+        functools.partial(put_kernel, counts, lat_dev, block),
+        out_shape=jax.ShapeDtypeStruct(shape, panels[0].dtype),
+        in_specs=[SMEM_SPEC] + [VMEM_SPEC] * len(panels),
+        out_specs=ANY_SPEC,
+        scratch_shapes=[
+            pltpu.VMEM(shape, panels[0].dtype),
+            pltpu.SemaphoreType.DMA((pl.cdiv(lon_dev, block),)),
+        ],
         compiler_params=pltpu.CompilerParams(vmem_limit_bytes=VMEM_LIMIT),
         cost_estimate=pl.CostEstimate(
             flops=2 * lon_dev * lat_dev * channels * block * lat_dev,
@@ -257,20 +280,36 @@
     across_y = [(i, i ^ 1) for i in range(2 * n_lon)]
     across_both = [(i, i ^ 3) for i in range(2 * n_lon)]
 
+    def over_core(p):
+        return lax.ppermute(p, "lon", across_core)
+
+    def after(operand, *done):
+        return lax.optimization_barrier((operand,) + done)[0]
+
     own = list(keep)
-    other = [lax.ppermute(g, "lon", across_core) for g in give]
-    own += [lax.ppermute(s, ("lon", "lat"), across_y) for s in straight]
-    other += [lax.ppermute(s, ("lon", "lat"), across_both) for s in cross]
+    other = [over_core(g) for g in give]
+    for i in range(n_come):
+        s, c = straight[i], cross[i]
+        if i > 0:
+            s, c = after(s, own[-1]), after(c, other[-1])
+        own.append(lax.ppermute(s, ("lon", "lat"), across_y))
+        other.append(lax.ppermute(c, ("lon", "lat"), across_both))
     windows = tap_windows(widths, tap_weights, lon_dev, 2)
+    parts = [p for pair in zip(own, other) for p in pair]
+    by_x, by_z = [], []
+    for i, part in enumerate(parts):
+        if i >= 2:
+            part = after(part, by_x[i - 2], *by_z[max(i - 3, 0) : i - 2])
+        by_x.append(lax.ppermute(part, "lon", across_x))
+        by_z.append(lax.ppermute(by_x[i], "lon", across_z))
     mine, theirs = [], []
     base = 0
-    for part in zip(own, other):
-        by_x = [lax.ppermute(p, "lon", across_x) for p in part]
-        by_z = [lax.ppermute(p, "lon", across_z) for p in by_x]
-        out_own, out_other = filter_pair(rows, signs, windows, list(part) + by_x + by_z, base, lon_dev)
+    for i in range(0, len(parts), 2):
+        panels = parts[i : i + 2] + by_x[i : i + 2] + by_z[i : i + 2]
+        out_own, out_other = filter_pair(rows, signs, windows, panels, base, lon_dev)
         mine.append(out_own)
-        theirs.append(lax.ppermute(out_other, "lon", across_core))
-        base += part[0].shape[0]
+        theirs.append(over_core(out_other))
+        base += out_own.shape[0]
     out = put_rows(mine + theirs, slots, lon_dev, lat_dev)
     return jnp.transpose(out, (1, 0, 2))
 

time: 180 us -> 126 us (0.70)
  waiting for transfers between devices: 107 us -> 61.5 us
  Pallas kernels: 36.7 us -> 22.1 us
  local copies, waits for them, and re-layouts: 6.6 us -> 13.1 us
    ppermute x26, waiting for transfers between devices: 107 us -> 61.5 us  [the longest x8 32.9 us: chip_aware(): by_z.append(lax.ppermute(by_x[i], 'lon', across_z))]
    pallas_call x2, Pallas kernels: 19.7 us -> 8.32 us  [the longest x1 5.55 us: take_rows(): pl.pallas_call(functools.partial(take_kernel, chunks, lat_dev, block), ou...]
    unnamed x24 -> x52, local copies, waits for them, and re-layouts: 4.29 us -> 10.8 us
    pallas_call x4, Pallas kernels: 17 us -> 13.8 us  [filter_pair(): pl.pallas_call(functools.partial(pair_kernel, lon_dev), out_shape=[out, o...]
  transfers between devices with their start and end apart: 26 -> 26, of which waited for: 14 -> 15; matrix products, arithmetic and copies ran while one was open for 1% -> 2% of each run, Pallas kernels for 9% -> 11%
where the time goes in v3:
time: 126 us
  waiting for transfers between devices  61.5 us (49%)
  starting transfers between devices  28.2 us (22%)
  Pallas kernels  22.1 us (18%)
  local copies, waits for them, and re-layouts  13.1 us (10%)
    ppermute x8, waiting for transfers between devices, chip_aware(): by_z.append(lax.ppermute(by_x[i], 'lon', across_z))  32.9 us
    ppermute x8, waiting for transfers between devices, chip_aware(): by_x.append(lax.ppermute(part, 'lon', across_x))  26.8 us
    pallas_call x4, Pallas kernels, filter_pair(): pl.pallas_call(functools.partial(pair_kernel, lon_dev), out_shape=[out, o...  13.8 us
    ppermute x8, starting transfers between devices, chip_aware(): by_x.append(lax.ppermute(part, 'lon', across_x))  13.1 us
    unnamed x52, local copies, waits for them, and re-layouts  10.8 us
    ppermute x8, starting transfers between devices, chip_aware(): by_z.append(lax.ppermute(by_x[i], 'lon', across_z))  10.7 us
    pallas_call x1, Pallas kernels, take_rows(): pl.pallas_call(functools.partial(take_kernel, chunks, lat_dev, block), ou...  5.55 us
    ppermute x2, starting transfers between devices, chip_aware(): own.append(lax.ppermute(s, ('lon', 'lat'), across_y))  3.04 us
  transfers between devices with their start and end apart: 26, of which 15 were waited for; matrix products, arithmetic and copies ran while one was open for 2% of the time, Pallas kernels for 11%

profile of v3, /device:TPU:0, one launch (start us, length us, event | category | flops | bytes accessed | tf_op | source)
XLA Modules:
  0.0 125.8 jit_solution(5131773439116525457)
XLA Ops:
  0.0 0.1 pad_add_fusion.place_ref
  0.1 0.7 copy-done
  0.7 5.5 %take_rows.1 = (bf16[2,184,640]{2,1,0:T(8,128)(2,1)S(1)}, bf16[2,184,640]{2,1,0:T(8,128)(2,1)S(1)}, bf16[2,184,640]{2,1,0:T(8,128)(2,1)S(1)}, bf16[2,184,640]{2,...) custom-call(s32[32]{0:T(128)S(1)} %copy-done, ...), custom_call_target="tpu_custom_call" | custom-call | flops 943718400 | bytes 7372800 | tf_op jit(solution)/shard_map/take_rows/pallas_call | solution.py:129
  6.3 0.5 collective-permute-start
  6.8 2.6 %collective-permute-start.1 = (bf16[2,184,640]{2,1,0:T(8,128)(2,1)S(1)}, bf16[2,184,640]{2,1,0:T(8,128)(2,1)S(1)}, u32[]{:S(2)}, u32[]{:S(2)}) collective-permute-start(bf16[2,184,640]{2,1,0:T(8,128)(2,1)S(1)} %get-tuple-element.33.own), channel_id=1, source_target_pairs={{0,4},{2,6},{4,0},{6,2},{8,12},{10,14},{12,8},{14,10},{16,20},{18,... | collective-permute-start | bytes 1413128 | tf_op jit(solution)/shard_map/ppermute | solution.py:303
  9.4 1.8 %collective-permute-start.2 = (bf16[2,184,640]{2,1,0:T(8,128)(2,1)S(1)}, bf16[2,184,640]{2,1,0:T(8,128)(2,1)S(1)}, u32[]{:S(2)}, u32[]{:S(2)}) collective-permute-start(bf16[2,184,640]{2,1,0:T(8,128)(2,1)S(1)} %collective-permute-done.other), channel_id=1, source_target_pairs={{0,4},{2,6},{4,0},{6,2},{8,12},{10,14},{12,8},{14,10},{16,20},{18,... | collective-permute-start | bytes 1413128 | tf_op jit(solution)/shard_map/ppermute | solution.py:303
  11.1 9.9 %collective-permute-done.1.x_own = bf16[2,184,640]{2,1,0:T(8,128)(2,1)S(1)} collective-permute-done((bf16[2,184,640]{2,1,0:T(8,128)(2,1)S(1)}, bf16[2,184,640]{2,1,0:T(8,128)(2,1)S(1)}, u32[]{:S(2)}, u32[]{:S(2)}) %collective-permute-start.1) | collective-permute-done | bytes 471072 | tf_op jit(solution)/shard_map/ppermute | solution.py:303
  21.0 2.0 %collective-permute-start.3 = (bf16[2,184,640]{2,1,0:T(8,128)(2,1)S(1)}, bf16[2,184,640]{2,1,0:T(8,128)(2,1)S(1)}, u32[]{:S(2)}, u32[]{:S(2)}) collective-permute-start(bf16[2,184,640]{2,1,0:T(8,128)(2,1)S(1)} %collective-permute-done.1.x_own), channel_id=1, source_target_pairs={{0,8},{2,10},{4,28},{6,30},{8,16},{10,18},{12,4},{14,6},{16,24},{1... | collective-permute-start | bytes 1413128 | tf_op jit(solution)/shard_map/ppermute | solution.py:304
  23.1 3.5 %collective-permute-start.6 = (bf16[2,184,640]{2,1,0:T(8,128)(2,1)S(1)}, bf16[2,184,640]{2,1,0:T(8,128)(2,1)S(1)}, u32[]{:S(2)}, u32[]{:S(2)}) collective-permute-start(bf16[2,184,640]{2,1,0:T(8,128)(2,1)S(1)} %get-tuple-element.38.own), channel_id=1, source_target_pairs={{0,4},{2,6},{4,0},{6,2},{8,12},{10,14},{12,8},{14,10},{16,20},{18,... | collective-permute-start | bytes 1413128 | tf_op jit(solution)/shard_map/ppermute | solution.py:303
  26.6 1.5 %collective-permute-start.10 = (bf16[2,184,640]{2,1,0:T(8,128)(2,1)S(1)}, bf16[2,184,640]{2,1,0:T(8,128)(2,1)S(1)}, u32[]{:S(2)}, u32[]{:S(2)}) collective-permute-start(bf16[2,184,640]{2,1,0:T(8,128)(2,1)S(1)} %get-tuple-element.41), channel_id=1, source_target_pairs={{0,1},{1,0},{2,3},{3,2},{4,5},{5,4},{6,7},{7,6},{8,9},{9,8},{10,11... | collective-permute-start | bytes 1413128 | tf_op jit(solution)/shard_map/ppermute | solution.py:295
  28.1 3.0 %collective-permute-done.2.x_other = bf16[2,184,640]{2,1,0:T(8,128)(2,1)S(1)} collective-permute-done((bf16[2,184,640]{2,1,0:T(8,128)(2,1)S(1)}, bf16[2,184,640]{2,1,0:T(8,128)(2,1)S(1)}, u32[]{:S(2)}, u32[]{:S(2)}) %collective-permute-start.2) | collective-permute-done | bytes 471072 | tf_op jit(solution)/shard_map/ppermute | solution.py:303
  31.1 2.0 %collective-permute-start.4 = (bf16[2,184,640]{2,1,0:T(8,128)(2,1)S(1)}, bf16[2,184,640]{2,1,0:T(8,128)(2,1)S(1)}, u32[]{:S(2)}, u32[]{:S(2)}) collective-permute-start(bf16[2,184,640]{2,1,0:T(8,128)(2,1)S(1)} %collective-permute-done.2.x_other), channel_id=1, source_target_pairs={{0,8},{2,10},{4,28},{6,30},{8,16},{10,18},{12,4},{14,6},{16,24},{1... | collective-permute-start | bytes 1413128 | tf_op jit(solution)/shard_map/ppermute | solution.py:304
  33.1 0.8 copy-done.1
  33.9 0.1 collective-permute-start.11
  34.0 1.3 collective-permute-done.3.z_own
  35.2 0.8 copy-done.7
  36.0 2.3 %collective-permute-start.7 = (bf16[2,184,640]{2,1,0:T(8,128)(2,1)S(1)}, bf16[2,184,640]{2,1,0:T(8,128)(2,1)S(1)}, u32[]{:S(2)}, u32[]{:S(2)}) collective-permute-start(bf16[2,184,640]{2,1,0:T(8,128)(2,1)S(1)} %collective-permute-done.5.other), channel_id=1, source_target_pairs={{0,4},{2,6},{4,0},{6,2},{8,12},{10,14},{12,8},{14,10},{16,20},{18,... | collective-permute-start | bytes 1413128 | tf_op jit(solution)/shard_map/ppermute | solution.py:303
  38.3 2.8 %collective-permute-done.6.x_own = bf16[2,184,640]{2,1,0:T(8,128)(2,1)S(1)} collective-permute-done((bf16[2,184,640]{2,1,0:T(8,128)(2,1)S(1)}, bf16[2,184,640]{2,1,0:T(8,128)(2,1)S(1)}, u32[]{:S(2)}, u32[]{:S(2)}) %collective-permute-start.6) | collective-permute-done | bytes 471072 | tf_op jit(solution)/shard_map/ppermute | solution.py:303
  41.1 2.1 %collective-permute-start.8 = (bf16[2,184,640]{2,1,0:T(8,128)(2,1)S(1)}, bf16[2,184,640]{2,1,0:T(8,128)(2,1)S(1)}, u32[]{:S(2)}, u32[]{:S(2)}) collective-permute-start(bf16[2,184,640]{2,1,0:T(8,128)(2,1)S(1)} %collective-permute-done.6.x_own), channel_id=1, source_target_pairs={{0,8},{2,10},{4,28},{6,30},{8,16},{10,18},{12,4},{14,6},{16,24},{1... | collective-permute-start | bytes 1413128 | tf_op jit(solution)/shard_map/ppermute | solution.py:304
  43.2 0.8 copy-done.3
  44.0 1.3 %collective-permute-done.4.z_other = bf16[2,184,640]{2,1,0:T(8,128)(2,1)S(1)} collective-permute-done((bf16[2,184,640]{2,1,0:T(8,128)(2,1)S(1)}, bf16[2,184,640]{2,1,0:T(8,128)(2,1)S(1)}, u32[]{:S(2)}, u32[]{:S(2)}) %collective-permute-start.4) | collective-permute-done | bytes 471072 | tf_op jit(solution)/shard_map/ppermute | solution.py:304
  45.3 0.8 copy-done.9
  46.1 2.2 %collective-permute-start.12 = (bf16[2,184,640]{2,1,0:T(8,128)(2,1)S(1)}, bf16[2,184,640]{2,1,0:T(8,128)(2,1)S(1)}, u32[]{:S(2)}, u32[]{:S(2)}) collective-permute-start(bf16[2,184,640]{2,1,0:T(8,128)(2,1)S(1)} %collective-permute-done.10.own), channel_id=1, source_target_pairs={{0,4},{2,6},{4,0},{6,2},{8,12},{10,14},{12,8},{14,10},{16,20},{18,... | collective-permute-start | bytes 1413128 | tf_op jit(solution)/shard_map/ppermute | solution.py:303
  48.3 1.5 %collective-permute-start.16 = (bf16[2,184,640]{2,1,0:T(8,128)(2,1)S(1)}, bf16[2,184,640]{2,1,0:T(8,128)(2,1)}, u32[]{:S(2)}, u32[]{:S(2)}) collective-permute-start(bf16[2,184,640]{2,1,0:T(8,128)(2,1)S(1)} %get-tuple-element.47), channel_id=1, source_target_pairs={{0,1},{1,0},{2,3},{3,2},{4,5},{5,4},{6,7},{7,6},{8,9},{9,8},{10,11... | collective-permute-start | bytes 1413128 | tf_op jit(solution)/shard_map/ppermute | solution.py:295
  49.8 1.4 %collective-permute-done.7.x_other = bf16[2,184,640]{2,1,0:T(8,128)(2,1)S(1)} collective-permute-done((bf16[2,184,640]{2,1,0:T(8,128)(2,1)S(1)}, bf16[2,184,640]{2,1,0:T(8,128)(2,1)S(1)}, u32[]{:S(2)}, u32[]{:S(2)}) %collective-permute-start.7) | collective-permute-done | bytes 471072 | tf_op jit(solution)/shard_map/ppermute | solution.py:303
  51.2 4.2 %collective-permute-done.8.z_own = bf16[2,184,640]{2,1,0:T(8,128)(2,1)S(1)} collective-permute-done((bf16[2,184,640]{2,1,0:T(8,128)(2,1)S(1)}, bf16[2,184,640]{2,1,0:T(8,128)(2,1)S(1)}, u32[]{:S(2)}, u32[]{:S(2)}) %collective-permute-start.8) | collective-permute-done | bytes 471072 | tf_op jit(solution)/shard_map/ppermute | solution.py:304
  55.4 0.8 copy-done.15
  56.2 0.8 collective-permute-start.13
  57.0 0.8 copy-done.5
  57.8 0.5 collective-permute-start.9
  58.2 0.8 copy-done.11
  59.0 2.3 %collective-permute-done.12.x_own = bf16[2,184,640]{2,1,0:T(8,128)(2,1)S(1)} collective-permute-done((bf16[2,184,640]{2,1,0:T(8,128)(2,1)S(1)}, bf16[2,184,640]{2,1,0:T(8,128)(2,1)S(1)}, u32[]{:S(2)}, u32[]{:S(2)}) %collective-permute-start.12) | collective-permute-done | bytes 471072 | tf_op jit(solution)/shard_map/ppermute | solution.py:303
  61.3 2.1 %collective-permute-start.14 = (bf16[2,184,640]{2,1,0:T(8,128)(2,1)S(1)}, bf16[2,184,640]{2,1,0:T(8,128)(2,1)S(1)}, u32[]{:S(2)}, u32[]{:S(2)}) collective-permute-start(bf16[2,184,640]{2,1,0:T(8,128)(2,1)S(1)} %collective-permute-done.12.x_own), channel_id=1, source_target_pairs={{0,8},{2,10},{4,28},{6,30},{8,16},{10,18},{12,4},{14,6},{16,24},{1... | collective-permute-start | bytes 1413128 | tf_op jit(solution)/shard_map/ppermute | solution.py:304
  63.4 0.1 convert_select_fusion
  63.5 0.1 fusion.2
  63.6 0.1 fusion.3
  63.7 10.0 %collective-permute-done.9.z_other = bf16[2,184,640]{2,1,0:T(8,128)(2,1)S(1)} collective-permute-done((bf16[2,184,640]{2,1,0:T(8,128)(2,1)S(1)}, bf16[2,184,640]{2,1,0:T(8,128)(2,1)S(1)}, u32[]{:S(2)}, u32[]{:S(2)}) %collective-permute-start.9) | collective-permute-done | bytes 471072 | tf_op jit(solution)/shard_map/ppermute | solution.py:304
  73.7 0.8 copy-done.21
  74.5 6.5 %collective-permute-done.14.z_own = bf16[2,184,640]{2,1,0:T(8,128)(2,1)S(1)} collective-permute-done((bf16[2,184,640]{2,1,0:T(8,128)(2,1)S(1)}, bf16[2,184,640]{2,1,0:T(8,128)(2,1)S(1)}, u32[]{:S(2)}, u32[]{:S(2)}) %collective-permute-start.14) | collective-permute-done | bytes 471072 | tf_op jit(solution)/shard_map/ppermute | solution.py:304
  81.1 0.8 copy-done.19
  81.9 0.6 pad_bitcast_fusion
  82.5 0.9 copy.6
  83.4 0.1 fusion.1
  83.7 0.5 stack.47.win_ref
  84.2 0.1 collective-permute-start.15
  84.2 0.1 pad_add_fusion.1.sign_ref
  84.3 0.3 collective-permute-done.18.x_own
  84.6 1.8 %collective-permute-start.20 = (bf16[2,184,640]{2,1,0:T(8,128)(2,1)}, bf16[2,184,640]{2,1,0:T(8,128)(2,1)S(1)}, u32[]{:S(2)}, u32[]{:S(2)}) collective-permute-start(bf16[2,184,640]{2,1,0:T(8,128)(2,1)} %collective-permute-done.18.x_own), channel_id=1, source_target_pairs={{0,8},{2,10},{4,28},{6,30},{8,16},{10,18},{12,4},{14,6},{16,24},{1... | collective-permute-start | bytes 1413128 | tf_op jit(solution)/shard_map/ppermute | solution.py:304
  86.5 7.0 %collective-permute-done.19.x_other = bf16[2,184,640]{2,1,0:T(8,128)(2,1)} collective-permute-done((bf16[2,184,640]{2,1,0:T(8,128)(2,1)}, bf16[2,184,640]{2,1,0:T(8,128)(2,1)}, u32[]{:S(2)}, u32[]{:S(2)}) %collective-permute-start.19) | collective-permute-done | bytes 471072 | tf_op jit(solution)/shard_map/ppermute | solution.py:303
  93.5 1.0 copy-done.2
  94.5 1.0 copy-done.8
  95.6 1.0 copy-done.10
  96.6 3.1 %filter_pair.4 = (bf16[2,184,640]{2,1,0:T(8,128)(2,1)S(1)}, bf16[2,184,640]{2,1,0:T(8,128)(2,1)S(1)}) custom-call(s32[16]{0:T(128)S(1)} %get-tuple-element.32.rows_ref, s32[2]{0:T(128)S(1)} %pad_add_fusion.1.sign_ref, f32[32,5,384]{2,1,0:T(8,128)S(1)} %stack.47.win_ref, bf16[2,184,640]{2,1,0:T(8,128)(2,1)S(1)} %get-tuple-element.33.own, ...), custom_call_target="tpu_custom_call" | custom-call | flops 2013265920 | bytes 3768320 | tf_op jit(solution)/shard_map/filter_pair/pallas_call | solution.py:240
  99.8 0.1 collective-permute-start.22
  99.9 3.1 %filter_pair.5 = (bf16[2,184,640]{2,1,0:T(8,128)(2,1)S(1)}, bf16[2,184,640]{2,1,0:T(8,128)(2,1)S(1)}) custom-call(s32[16]{0:T(128)S(1)} %get-tuple-element.32.rows_ref, s32[2]{0:T(128)S(1)} %pad_add_fusion.1.sign_ref, f32[32,5,384]{2,1,0:T(8,128)S(1)} %stack.47.win_ref, bf16[2,184,640]{2,1,0:T(8,128)(2,1)S(1)} %get-tuple-element.38.own, ...), custom_call_target="tpu_custom_call" | custom-call | flops 2013265920 | bytes 3768320 | tf_op jit(solution)/shard_map/filter_pair/pallas_call | solution.py:240
  103.0 0.6 collective-permute-start.23
  103.6 3.1 %filter_pair.6 = (bf16[2,184,640]{2,1,0:T(8,128)(2,1)S(1)}, bf16[2,184,640]{2,1,0:T(8,128)(2,1)S(1)}) custom-call(s32[16]{0:T(128)S(1)} %get-tuple-element.32.rows_ref, s32[2]{0:T(128)S(1)} %pad_add_fusion.1.sign_ref, f32[32,5,384]{2,1,0:T(8,128)S(1)} %stack.47.win_ref, bf16[2,184,640]{2,1,0:T(8,128)(2,1)S(1)} %collective-permute-done.10.own, ...), custom_call_target="tpu_custom_call" | custom-call | flops 2013265920 | bytes 3768320 | tf_op jit(solution)/shard_map/filter_pair/pallas_call | solution.py:240
  106.7 0.1 collective-permute-start.24
  106.8 3.2 %collective-permute-done.20.z_own = bf16[2,184,640]{2,1,0:T(8,128)(2,1)S(1)} collective-permute-done((bf16[2,184,640]{2,1,0:T(8,128)(2,1)}, bf16[2,184,640]{2,1,0:T(8,128)(2,1)S(1)}, u32[]{:S(2)}, u32[]{:S(2)}) %collective-permute-start.20) | collective-permute-done | bytes 471072 | tf_op jit(solution)/shard_map/ppermute | solution.py:304
  110.1 6.4 %collective-permute-done.21.z_other = bf16[2,184,640]{2,1,0:T(8,128)(2,1)S(1)} collective-permute-done((bf16[2,184,640]{2,1,0:T(8,128)(2,1)}, bf16[2,184,640]{2,1,0:T(8,128)(2,1)S(1)}, u32[]{:S(2)}, u32[]{:S(2)}) %collective-permute-start.21) | collective-permute-done | bytes 471072 | tf_op jit(solution)/shard_map/ppermute | solution.py:304
  116.5 4.4 %filter_pair.7 = (bf16[2,184,640]{2,1,0:T(8,128)(2,1)S(1)}, bf16[2,184,640]{2,1,0:T(8,128)(2,1)S(1)}) custom-call(s32[16]{0:T(128)S(1)} %get-tuple-element.32.rows_ref, s32[2]{0:T(128)S(1)} %pad_add_fusion.1.sign_ref, f32[32,5,384]{2,1,0:T(8,128)S(1)} %stack.47.win_ref, bf16[2,184,640]{2,1,0:T(8,128)(2,1)} %collective-permute-done.16.own, ...), custom_call_target="tpu_custom_call" | custom-call | flops 2013265920 | bytes 3768320 | tf_op jit(solution)/shard_map/filter_pair/pallas_call | solution.py:240
  120.9 0.1 collective-permute-start.25
  121.0 1.8 %collective-permute-done.25.refs_7_ = bf16[2,184,640]{2,1,0:T(8,128)(2,1)S(1)} collective-permute-done((bf16[2,184,640]{2,1,0:T(8,128)(2,1)S(1)}, bf16[2,184,640]{2,1,0:T(8,128)(2,1)S(1)}, u32[]{:S(2)}, u32[]{:S(2)}) %collective-permute-start.25) | collective-permute-done | bytes 471072 | tf_op jit(solution)/shard_map/ppermute | solution.py:284
  122.8 2.8 %put_rows.1 = bf16[180,16,640]{2,1,0:T(8,128)(2,1)} custom-call(s32[16]{0:T(128)S(1)} %get-tuple-element.31.slots_ref, bf16[2,184,640]{2,1,0:T(8,128)(2,1)S(1)} %get-tuple-element.35.refs_0_, bf16[2,184,640]{2,1,0:T(8,128)(2,1)S(1)} %get-tuple-element.40.refs_1_, bf16[2,184,640]{2,1,0:T(8,128)(2,1)S(1)} %get-tuple-element.45.refs_2_, ...), custom_call_target="tpu_custom_call" | custom-call | flops 943718400 | bytes 7372800 | tf_op jit(solution)/shard_map/put_rows/pallas_call | solution.py:183
  (62 shorter events, 0.3 us)
Async XLA Ops:
  0.0 83.6 %copy-start.24 = (pred[384]{0:T(512)(128)(4,1)S(1)}, pred[384]{0:T(512)(128)(4,1)}, u32[]{:S(2)}) copy-start(pred[384]{0:T(512)(128)(4,1)} %constant.44.clone.1) | copy-start | bytes 1156
  0.0 63.4 %copy-start.25 = (s32[32]{0:T(128)S(1)}, s32[32]{0:T(128)}, u32[]{:S(2)}) copy-start(s32[32]{0:T(128)} %param.6) | copy-start | bytes 388
  0.1 0.7 copy-start
  0.7 62.7 %copy-start.23 = (bf16[32,2880]{1,0:T(8,128)(2,1)S(1)}, bf16[32,2880]{1,0:T(8,128)(2,1)}, u32[]{:S(2)}) copy-start(bf16[32,2880]{1,0:T(8,128)(2,1)} %param.7) | copy-start | bytes 552964
  6.3 3.1 %collective-permute-start = (bf16[2,184,640]{2,1,0:T(8,128)(2,1)S(1)}, bf16[2,184,640]{2,1,0:T(8,128)(2,1)S(1)}, u32[]{:S(2)}, u32[]{:S(2)}) collective-permute-start(bf16[2,184,640]{2,1,0:T(8,128)(2,1)S(1)} %get-tuple-element.34), channel_id=1, source_target_pairs={{0,2},{2,0},{4,6},{6,4},{8,10},{10,8},{12,14},{14,12},{16,18},{18,... | collective-permute-start | bytes 1413128 | tf_op jit(solution)/shard_map/ppermute | solution.py:284
  6.8 14.2 %collective-permute-start.1 = (bf16[2,184,640]{2,1,0:T(8,128)(2,1)S(1)}, bf16[2,184,640]{2,1,0:T(8,128)(2,1)S(1)}, u32[]{:S(2)}, u32[]{:S(2)}) collective-permute-start(bf16[2,184,640]{2,1,0:T(8,128)(2,1)S(1)} %get-tuple-element.33.own), channel_id=1, source_target_pairs={{0,4},{2,6},{4,0},{6,2},{8,12},{10,14},{12,8},{14,10},{16,20},{18,... | collective-permute-start | bytes 1413128 | tf_op jit(solution)/shard_map/ppermute | solution.py:303
  9.4 21.7 %collective-permute-start.2 = (bf16[2,184,640]{2,1,0:T(8,128)(2,1)S(1)}, bf16[2,184,640]{2,1,0:T(8,128)(2,1)S(1)}, u32[]{:S(2)}, u32[]{:S(2)}) collective-permute-start(bf16[2,184,640]{2,1,0:T(8,128)(2,1)S(1)} %collective-permute-done.other), channel_id=1, source_target_pairs={{0,4},{2,6},{4,0},{6,2},{8,12},{10,14},{12,8},{14,10},{16,20},{18,... | collective-permute-start | bytes 1413128 | tf_op jit(solution)/shard_map/ppermute | solution.py:303
  11.1 22.8 %collective-permute-start.5 = (bf16[2,184,640]{2,1,0:T(8,128)(2,1)S(1)}, bf16[2,184,640]{2,1,0:T(8,128)(2,1)S(1)}, u32[]{:S(2)}, u32[]{:S(2)}) collective-permute-start(bf16[2,184,640]{2,1,0:T(8,128)(2,1)S(1)} %get-tuple-element.37), channel_id=1, source_target_pairs={{0,2},{2,0},{4,6},{6,4},{8,10},{10,8},{12,14},{14,12},{16,18},{18,... | collective-permute-start | bytes 1413128 | tf_op jit(solution)/shard_map/ppermute | solution.py:284
  21.0 14.2 %collective-permute-start.3 = (bf16[2,184,640]{2,1,0:T(8,128)(2,1)S(1)}, bf16[2,184,640]{2,1,0:T(8,128)(2,1)S(1)}, u32[]{:S(2)}, u32[]{:S(2)}) collective-permute-start(bf16[2,184,640]{2,1,0:T(8,128)(2,1)S(1)} %collective-permute-done.1.x_own), channel_id=1, source_target_pairs={{0,8},{2,10},{4,28},{6,30},{8,16},{10,18},{12,4},{14,6},{16,24},{1... | collective-permute-start | bytes 1413128 | tf_op jit(solution)/shard_map/ppermute | solution.py:304
  23.1 18.1 %collective-permute-start.6 = (bf16[2,184,640]{2,1,0:T(8,128)(2,1)S(1)}, bf16[2,184,640]{2,1,0:T(8,128)(2,1)S(1)}, u32[]{:S(2)}, u32[]{:S(2)}) collective-permute-start(bf16[2,184,640]{2,1,0:T(8,128)(2,1)S(1)} %get-tuple-element.38.own), channel_id=1, source_target_pairs={{0,4},{2,6},{4,0},{6,2},{8,12},{10,14},{12,8},{14,10},{16,20},{18,... | collective-permute-start | bytes 1413128 | tf_op jit(solution)/shard_map/ppermute | solution.py:303
  26.6 17.5 %collective-permute-start.10 = (bf16[2,184,640]{2,1,0:T(8,128)(2,1)S(1)}, bf16[2,184,640]{2,1,0:T(8,128)(2,1)S(1)}, u32[]{:S(2)}, u32[]{:S(2)}) collective-permute-start(bf16[2,184,640]{2,1,0:T(8,128)(2,1)S(1)} %get-tuple-element.41), channel_id=1, source_target_pairs={{0,1},{1,0},{2,3},{3,2},{4,5},{5,4},{6,7},{7,6},{8,9},{9,8},{10,11... | collective-permute-start | bytes 1413128 | tf_op jit(solution)/shard_map/ppermute | solution.py:295
  31.1 14.2 %collective-permute-start.4 = (bf16[2,184,640]{2,1,0:T(8,128)(2,1)S(1)}, bf16[2,184,640]{2,1,0:T(8,128)(2,1)S(1)}, u32[]{:S(2)}, u32[]{:S(2)}) collective-permute-start(bf16[2,184,640]{2,1,0:T(8,128)(2,1)S(1)} %collective-permute-done.2.x_other), channel_id=1, source_target_pairs={{0,8},{2,10},{4,28},{6,30},{8,16},{10,18},{12,4},{14,6},{16,24},{1... | collective-permute-start | bytes 1413128 | tf_op jit(solution)/shard_map/ppermute | solution.py:304
  33.1 0.8 copy-start.1
  33.9 15.9 %collective-permute-start.11 = (bf16[2,184,640]{2,1,0:T(8,128)(2,1)S(1)}, bf16[2,184,640]{2,1,0:T(8,128)(2,1)S(1)}, u32[]{:S(2)}, u32[]{:S(2)}) collective-permute-start(bf16[2,184,640]{2,1,0:T(8,128)(2,1)S(1)} %get-tuple-element.42), channel_id=1, source_target_pairs={{0,3},{1,2},{2,1},{3,0},{4,7},{5,6},{6,5},{7,4},{8,11},{9,10},{10,... | collective-permute-start | bytes 1413128 | tf_op jit(solution)/shard_map/ppermute | solution.py:296
  35.2 0.8 copy-start.7
  36.0 15.2 %collective-permute-start.7 = (bf16[2,184,640]{2,1,0:T(8,128)(2,1)S(1)}, bf16[2,184,640]{2,1,0:T(8,128)(2,1)S(1)}, u32[]{:S(2)}, u32[]{:S(2)}) collective-permute-start(bf16[2,184,640]{2,1,0:T(8,128)(2,1)S(1)} %collective-permute-done.5.other), channel_id=1, source_target_pairs={{0,4},{2,6},{4,0},{6,2},{8,12},{10,14},{12,8},{14,10},{16,20},{18,... | collective-permute-start | bytes 1413128 | tf_op jit(solution)/shard_map/ppermute | solution.py:303
  41.1 14.3 %collective-permute-start.8 = (bf16[2,184,640]{2,1,0:T(8,128)(2,1)S(1)}, bf16[2,184,640]{2,1,0:T(8,128)(2,1)S(1)}, u32[]{:S(2)}, u32[]{:S(2)}) collective-permute-start(bf16[2,184,640]{2,1,0:T(8,128)(2,1)S(1)} %collective-permute-done.6.x_own), channel_id=1, source_target_pairs={{0,8},{2,10},{4,28},{6,30},{8,16},{10,18},{12,4},{14,6},{16,24},{1... | collective-permute-start | bytes 1413128 | tf_op jit(solution)/shard_map/ppermute | solution.py:304
  43.2 0.8 copy-start.3
  45.3 0.8 copy-start.9
  46.1 15.2 %collective-permute-start.12 = (bf16[2,184,640]{2,1,0:T(8,128)(2,1)S(1)}, bf16[2,184,640]{2,1,0:T(8,128)(2,1)S(1)}, u32[]{:S(2)}, u32[]{:S(2)}) collective-permute-start(bf16[2,184,640]{2,1,0:T(8,128)(2,1)S(1)} %collective-permute-done.10.own), channel_id=1, source_target_pairs={{0,4},{2,6},{4,0},{6,2},{8,12},{10,14},{12,8},{14,10},{16,20},{18,... | collective-permute-start | bytes 1413128 | tf_op jit(solution)/shard_map/ppermute | solution.py:303
  48.3 15.4 %collective-permute-start.16 = (bf16[2,184,640]{2,1,0:T(8,128)(2,1)S(1)}, bf16[2,184,640]{2,1,0:T(8,128)(2,1)}, u32[]{:S(2)}, u32[]{:S(2)}) collective-permute-start(bf16[2,184,640]{2,1,0:T(8,128)(2,1)S(1)} %get-tuple-element.47), channel_id=1, source_target_pairs={{0,1},{1,0},{2,3},{3,2},{4,5},{5,4},{6,7},{7,6},{8,9},{9,8},{10,11... | collective-permute-start | bytes 1413128 | tf_op jit(solution)/shard_map/ppermute | solution.py:295
  49.8 24.7 %collective-permute-start.17 = (bf16[2,184,640]{2,1,0:T(8,128)(2,1)S(1)}, bf16[2,184,640]{2,1,0:T(8,128)(2,1)}, u32[]{:S(2)}, u32[]{:S(2)}) collective-permute-start(bf16[2,184,640]{2,1,0:T(8,128)(2,1)S(1)} %get-tuple-element.49), channel_id=1, source_target_pairs={{0,3},{1,2},{2,1},{3,0},{4,7},{5,6},{6,5},{7,4},{8,11},{9,10},{10,... | collective-permute-start | bytes 1413128 | tf_op jit(solution)/shard_map/ppermute | solution.py:296
  55.4 0.8 copy-start.15
  56.2 18.3 %collective-permute-start.13 = (bf16[2,184,640]{2,1,0:T(8,128)(2,1)S(1)}, bf16[2,184,640]{2,1,0:T(8,128)(2,1)S(1)}, u32[]{:S(2)}, u32[]{:S(2)}) collective-permute-start(bf16[2,184,640]{2,1,0:T(8,128)(2,1)S(1)} %collective-permute-done.11.other), channel_id=1, source_target_pairs={{0,4},{2,6},{4,0},{6,2},{8,12},{10,14},{12,8},{14,10},{16,20},{18,... | collective-permute-start | bytes 1413128 | tf_op jit(solution)/shard_map/ppermute | solution.py:303
  57.0 0.8 copy-start.5
  57.8 16.0 %collective-permute-start.9 = (bf16[2,184,640]{2,1,0:T(8,128)(2,1)S(1)}, bf16[2,184,640]{2,1,0:T(8,128)(2,1)S(1)}, u32[]{:S(2)}, u32[]{:S(2)}) collective-permute-start(bf16[2,184,640]{2,1,0:T(8,128)(2,1)S(1)} %collective-permute-done.7.x_other), channel_id=1, source_target_pairs={{0,8},{2,10},{4,28},{6,30},{8,16},{10,18},{12,4},{14,6},{16,24},{1... | collective-permute-start | bytes 1413128 | tf_op jit(solution)/shard_map/ppermute | solution.py:304
  58.2 0.8 copy-start.11
  61.3 13.2 %copy-start.13 = (bf16[2,184,640]{2,1,0:T(8,128)(2,1)}, bf16[2,184,640]{2,1,0:T(8,128)(2,1)S(1)}, u32[]{:S(2)}) copy-start(bf16[2,184,640]{2,1,0:T(8,128)(2,1)S(1)} %collective-permute-done.12.x_own) | copy-start | bytes 1413124
  61.3 19.8 %collective-permute-start.14 = (bf16[2,184,640]{2,1,0:T(8,128)(2,1)S(1)}, bf16[2,184,640]{2,1,0:T(8,128)(2,1)S(1)}, u32[]{:S(2)}, u32[]{:S(2)}) collective-permute-start(bf16[2,184,640]{2,1,0:T(8,128)(2,1)S(1)} %collective-permute-done.12.x_own), channel_id=1, source_target_pairs={{0,8},{2,10},{4,28},{6,30},{8,16},{10,18},{12,4},{14,6},{16,24},{1... | collective-permute-start | bytes 1413128 | tf_op jit(solution)/shard_map/ppermute | solution.py:304
  73.7 0.8 copy-start.21
  74.5 10.1 %collective-permute-start.18 = (bf16[2,184,640]{2,1,0:T(8,128)(2,1)}, bf16[2,184,640]{2,1,0:T(8,128)(2,1)}, u32[]{:S(2)}, u32[]{:S(2)}) collective-permute-start(bf16[2,184,640]{2,1,0:T(8,128)(2,1)} %collective-permute-done.16.own), channel_id=1, source_target_pairs={{0,4},{2,6},{4,0},{6,2},{8,12},{10,14},{12,8},{14,10},{16,20},{18,... | collective-permute-start | bytes 1413128 | tf_op jit(solution)/shard_map/ppermute | solution.py:303
  74.5 6.6 %copy-start.17 = (bf16[2,184,640]{2,1,0:T(8,128)(2,1)}, bf16[2,184,640]{2,1,0:T(8,128)(2,1)S(1)}, u32[]{:S(2)}) copy-start(bf16[2,184,640]{2,1,0:T(8,128)(2,1)S(1)} %collective-permute-done.13.x_other) | copy-start | bytes 1413124
  81.1 0.8 copy-start.19
  81.9 11.6 %collective-permute-start.19 = (bf16[2,184,640]{2,1,0:T(8,128)(2,1)}, bf16[2,184,640]{2,1,0:T(8,128)(2,1)}, u32[]{:S(2)}, u32[]{:S(2)}) collective-permute-start(bf16[2,184,640]{2,1,0:T(8,128)(2,1)} %collective-permute-done.17.other), channel_id=1, source_target_pairs={{0,4},{2,6},{4,0},{6,2},{8,12},{10,14},{12,8},{14,10},{16,20},{18,... | collective-permute-start | bytes 1413128 | tf_op jit(solution)/shard_map/ppermute | solution.py:303
  84.2 19.4 %collective-permute-start.15 = (bf16[2,184,640]{2,1,0:T(8,128)(2,1)}, bf16[2,184,640]{2,1,0:T(8,128)(2,1)S(1)}, u32[]{:S(2)}, u32[]{:S(2)}) collective-permute-start(bf16[2,184,640]{2,1,0:T(8,128)(2,1)} %copy-done.17), channel_id=1, source_target_pairs={{0,8},{2,10},{4,28},{6,30},{8,16},{10,18},{12,4},{14,6},{16,24},{1... | collective-permute-start | bytes 1413128 | tf_op jit(solution)/shard_map/ppermute | solution.py:304
  84.6 25.4 %collective-permute-start.20 = (bf16[2,184,640]{2,1,0:T(8,128)(2,1)}, bf16[2,184,640]{2,1,0:T(8,128)(2,1)S(1)}, u32[]{:S(2)}, u32[]{:S(2)}) collective-permute-start(bf16[2,184,640]{2,1,0:T(8,128)(2,1)} %collective-permute-done.18.x_own), channel_id=1, source_target_pairs={{0,8},{2,10},{4,28},{6,30},{8,16},{10,18},{12,4},{14,6},{16,24},{1... | collective-permute-start | bytes 1413128 | tf_op jit(solution)/shard_map/ppermute | solution.py:304
  93.5 23.0 %collective-permute-start.21 = (bf16[2,184,640]{2,1,0:T(8,128)(2,1)}, bf16[2,184,640]{2,1,0:T(8,128)(2,1)S(1)}, u32[]{:S(2)}, u32[]{:S(2)}) collective-permute-start(bf16[2,184,640]{2,1,0:T(8,128)(2,1)} %collective-permute-done.19.x_other), channel_id=1, source_target_pairs={{0,8},{2,10},{4,28},{6,30},{8,16},{10,18},{12,4},{14,6},{16,24},{1... | collective-permute-start | bytes 1413128 | tf_op jit(solution)/shard_map/ppermute | solution.py:304
  93.5 1.0 copy-start.2
  94.5 1.0 copy-start.8
  95.6 1.0 copy-start.10
  96.6 3.3 %copy-start.4 = (bf16[2,184,640]{2,1,0:T(8,128)(2,1)S(1)}, bf16[2,184,640]{2,1,0:T(8,128)(2,1)}, u32[]{:S(2)}) copy-start(bf16[2,184,640]{2,1,0:T(8,128)(2,1)} %copy-done.3) | copy-start | bytes 1413124
  96.6 3.3 %copy-start.12 = (bf16[2,184,640]{2,1,0:T(8,128)(2,1)S(1)}, bf16[2,184,640]{2,1,0:T(8,128)(2,1)}, u32[]{:S(2)}) copy-start(bf16[2,184,640]{2,1,0:T(8,128)(2,1)} %copy-done.11) | copy-start | bytes 1413124
  96.6 3.3 %copy-start.16 = (bf16[2,184,640]{2,1,0:T(8,128)(2,1)S(1)}, bf16[2,184,640]{2,1,0:T(8,128)(2,1)}, u32[]{:S(2)}) copy-start(bf16[2,184,640]{2,1,0:T(8,128)(2,1)} %copy-done.15) | copy-start | bytes 1413124
  96.6 3.3 %copy-start.22 = (bf16[2,184,640]{2,1,0:T(8,128)(2,1)S(1)}, bf16[2,184,640]{2,1,0:T(8,128)(2,1)}, u32[]{:S(2)}) copy-start(bf16[2,184,640]{2,1,0:T(8,128)(2,1)} %copy-done.21) | copy-start | bytes 1413124
  99.7 3.8 %copy-start.6 = (bf16[2,184,640]{2,1,0:T(8,128)(2,1)S(1)}, bf16[2,184,640]{2,1,0:T(8,128)(2,1)}, u32[]{:S(2)}) copy-start(bf16[2,184,640]{2,1,0:T(8,128)(2,1)} %copy-done.5) | copy-start | bytes 1413124
  99.7 3.8 %copy-start.14 = (bf16[2,184,640]{2,1,0:T(8,128)(2,1)S(1)}, bf16[2,184,640]{2,1,0:T(8,128)(2,1)}, u32[]{:S(2)}) copy-start(bf16[2,184,640]{2,1,0:T(8,128)(2,1)} %copy-done.13) | copy-start | bytes 1413124
  99.7 3.8 %copy-start.18 = (bf16[2,184,640]{2,1,0:T(8,128)(2,1)S(1)}, bf16[2,184,640]{2,1,0:T(8,128)(2,1)}, u32[]{:S(2)}) copy-start(bf16[2,184,640]{2,1,0:T(8,128)(2,1)} %copy-done.17) | copy-start | bytes 1413124
  99.8 3.8 %copy-start.20 = (bf16[2,184,640]{2,1,0:T(8,128)(2,1)S(1)}, bf16[2,184,640]{2,1,0:T(8,128)(2,1)}, u32[]{:S(2)}) copy-start(bf16[2,184,640]{2,1,0:T(8,128)(2,1)} %copy-done.19) | copy-start | bytes 1413124
  99.8 21.2 %collective-permute-start.22 = (bf16[2,184,640]{2,1,0:T(8,128)(2,1)S(1)}, bf16[2,184,640]{2,1,0:T(8,128)(2,1)S(1)}, u32[]{:S(2)}, u32[]{:S(2)}) collective-permute-start(bf16[2,184,640]{2,1,0:T(8,128)(2,1)S(1)} %get-tuple-element.53), channel_id=1, source_target_pairs={{0,2},{2,0},{4,6},{6,4},{8,10},{10,8},{12,14},{14,12},{16,18},{18,... | collective-permute-start | bytes 1413128 | tf_op jit(solution)/shard_map/ppermute | solution.py:284
  103.0 18.0 %collective-permute-start.23 = (bf16[2,184,640]{2,1,0:T(8,128)(2,1)S(1)}, bf16[2,184,640]{2,1,0:T(8,128)(2,1)S(1)}, u32[]{:S(2)}, u32[]{:S(2)}) collective-permute-start(bf16[2,184,640]{2,1,0:T(8,128)(2,1)S(1)} %get-tuple-element.54), channel_id=1, source_target_pairs={{0,2},{2,0},{4,6},{6,4},{8,10},{10,8},{12,14},{14,12},{16,18},{18,... | collective-permute-start | bytes 1413128 | tf_op jit(solution)/shard_map/ppermute | solution.py:284
  106.7 14.3 %collective-permute-start.24 = (bf16[2,184,640]{2,1,0:T(8,128)(2,1)S(1)}, bf16[2,184,640]{2,1,0:T(8,128)(2,1)S(1)}, u32[]{:S(2)}, u32[]{:S(2)}) collective-permute-start(bf16[2,184,640]{2,1,0:T(8,128)(2,1)S(1)} %get-tuple-element.55), channel_id=1, source_target_pairs={{0,2},{2,0},{4,6},{6,4},{8,10},{10,8},{12,14},{14,12},{16,18},{18,... | collective-permute-start | bytes 1413128 | tf_op jit(solution)/shard_map/ppermute | solution.py:284
  120.9 1.9 %collective-permute-start.25 = (bf16[2,184,640]{2,1,0:T(8,128)(2,1)S(1)}, bf16[2,184,640]{2,1,0:T(8,128)(2,1)S(1)}, u32[]{:S(2)}, u32[]{:S(2)}) collective-permute-start(bf16[2,184,640]{2,1,0:T(8,128)(2,1)S(1)} %get-tuple-element.56), channel_id=1, source_target_pairs={{0,2},{2,0},{4,6},{6,4},{8,10},{10,8},{12,14},{14,12},{16,18},{18,... | collective-permute-start | bytes 1413128 | tf_op jit(solution)/shard_map/ppermute | solution.py:284

commit v4 on v3

--- a/solution.py
+++ b/solution.py
@@ -7,10 +7,10 @@
 from jax.experimental.pallas import tpu as pltpu
 from jax.sharding import PartitionSpec as P
 
-VMEM_LIMIT = 48 * 1024 * 1024
+VMEM_LIMIT = 16 * 1024 * 1024
 SMEM_SPEC = pl.BlockSpec(memory_space=pltpu.SMEM)
 VMEM_SPEC = pl.BlockSpec(memory_space=pltpu.VMEM)
-ANY_SPEC = pl.BlockSpec(memory_space=pl.ANY)
+HBM_SPEC = pl.BlockSpec(memory_space=pltpu.HBM)
 STAY = (2, 2)
 COME = (2, 2)
 
@@ -59,16 +59,10 @@
 
 def take_kernel(chunks, lat_dev, block, slot_ref, place_ref, fields_ref, *refs):
     outs = refs[: len(chunks)]
-    rows_ref, slots_ref, home_ref, take_ref, panel_ref, sems = refs[len(chunks) :]
+    rows_ref, slots_ref, home_ref, take_ref = refs[len(chunks) :]
     lon_dev, _, channels = fields_ref.shape
     half, quarter = lat_dev // 2, lat_dev // 4
     starts = list(range(0, lon_dev, block))
-    copies = []
-    for n, start in enumerate(starts):
-        window = pl.ds(start, min(block, lon_dev - start))
-        copies.append(pltpu.make_async_copy(fields_ref.at[window], panel_ref.at[window], sems.at[n]))
-        copies[-1].start()
-
     band, core = place_ref[0], place_ref[1]
 
     def at(n):
@@ -107,11 +101,10 @@
         return jnp.concatenate(strips, axis=0).astype(jnp.bfloat16)
 
     take_ref[...] = selector(block, block)
-    for n, start in enumerate(starts):
-        copies[n].wait()
+    for start in starts:
         lon_in = min(block, lon_dev - start)
         lon_out = min(block, outs[0].shape[1] - start)
-        panel = panel_ref[start : start + lon_in].reshape(lon_in * lat_dev, channels)
+        panel = fields_ref[start : start + lon_in].reshape(lon_in * lat_dev, channels)
         take = take_ref[...] if (lon_in, lon_out) == (block, block) else selector(lon_in, lon_out)
         taken = jnp.dot(take, panel, preferred_element_type=jnp.float32).astype(jnp.bfloat16)
         place = 0
@@ -129,13 +122,11 @@
     result = pl.pallas_call(
         functools.partial(take_kernel, chunks, lat_dev, block),
         out_shape=[jax.ShapeDtypeStruct((n, padded, channels), fields.dtype) for n in chunks] + [ints, ints],
-        in_specs=[SMEM_SPEC, SMEM_SPEC, ANY_SPEC],
+        in_specs=[SMEM_SPEC, SMEM_SPEC, VMEM_SPEC],
         out_specs=[VMEM_SPEC] * len(chunks) + [SMEM_SPEC, SMEM_SPEC],
         scratch_shapes=[
             pltpu.SMEM((lat_dev,), jnp.int32),
             pltpu.VMEM((block * lat_dev, block * lat_dev), jnp.bfloat16),
-            pltpu.VMEM(fields.shape, fields.dtype),
-            pltpu.SemaphoreType.DMA((pl.cdiv(lon_dev, block),)),
         ],
         compiler_params=pltpu.CompilerParams(vmem_limit_bytes=VMEM_LIMIT),
         cost_estimate=pl.CostEstimate(
@@ -184,7 +175,7 @@
         functools.partial(put_kernel, counts, lat_dev, block),
         out_shape=jax.ShapeDtypeStruct(shape, panels[0].dtype),
         in_specs=[SMEM_SPEC] + [VMEM_SPEC] * len(panels),
-        out_specs=ANY_SPEC,
+        out_specs=HBM_SPEC,
         scratch_shapes=[
             pltpu.VMEM(shape, panels[0].dtype),
             pltpu.SemaphoreType.DMA((pl.cdiv(lon_dev, block),)),
@@ -288,20 +279,21 @@
 
     own = list(keep)
     other = [over_core(g) for g in give]
+    over_y = []
     for i in range(n_come):
-        s, c = straight[i], cross[i]
-        if i > 0:
-            s, c = after(s, own[-1]), after(c, other[-1])
-        own.append(lax.ppermute(s, ("lon", "lat"), across_y))
-        other.append(lax.ppermute(c, ("lon", "lat"), across_both))
+        for operand, pairs in ((straight[i], across_y), (cross[i], across_both)):
+            operand = after(operand, *over_y[-2:-1])
+            over_y.append(lax.ppermute(operand, ("lon", "lat"), pairs))
+    own += over_y[0::2]
+    other += over_y[1::2]
     windows = tap_windows(widths, tap_weights, lon_dev, 2)
     parts = [p for pair in zip(own, other) for p in pair]
     by_x, by_z = [], []
     for i, part in enumerate(parts):
         if i >= 2:
-            part = after(part, by_x[i - 2], *by_z[max(i - 3, 0) : i - 2])
+            part = after(part, by_x[i - 2], *over_y[i - 2 : i - 1])
         by_x.append(lax.ppermute(part, "lon", across_x))
-        by_z.append(lax.ppermute(by_x[i], "lon", across_z))
+        by_z.append(lax.ppermute(after(by_x[i], *by_z[max(i - 2, 0) : max(i - 1, 0)]), "lon", across_z))
     mine, theirs = [], []
     base = 0
     for i in range(0, len(parts), 2):

time: 126 us -> 119 us (0.944)
  waiting for transfers between devices: 61.5 us -> 35.9 us
  starting transfers between devices: 28.2 us -> 45.7 us
  local copies, waits for them, and re-layouts: 13.1 us -> 14.6 us
  Pallas kernels: 22.1 us -> 20.7 us
    ppermute x12, waiting for transfers between devices: 33 us -> 5.74 us  [the longest x8 5 us: chip_aware(): lax.ppermute(after(by_x[i], *by_z[max(i - 2, 0):max(i - 1, 0)]), 'lon', a...]
    ppermute x8, starting transfers between devices: 13.1 us -> 23.5 us  [chip_aware(): by_x.append(lax.ppermute(part, 'lon', across_x))]
    ppermute x12, starting transfers between devices: 13.8 us -> 20.5 us  [the longest x8 15.6 us: chip_aware(): lax.ppermute(after(by_x[i], *by_z[max(i - 2, 0):max(i - 1, 0)]), 'lon', a...]
    pallas_call x1, Pallas kernels: 5.55 us -> 3 us  [take_rows(): pl.pallas_call(functools.partial(take_kernel, chunks, lat_dev, block), ou...]
    ppermute x8, waiting for transfers between devices: 26.8 us -> 28.7 us  [chip_aware(): by_x.append(lax.ppermute(part, 'lon', across_x))]
    unnamed x52 -> x46, local copies, waits for them, and re-layouts: 10.8 us -> 12.3 us
  transfers between devices with their start and end apart: 26 -> 26, of which waited for: 15 -> 13; matrix products, arithmetic and copies ran while one was open for 2% -> 2% of each run, Pallas kernels for 11% -> 13%
where the time goes in v4:
time: 119 us; the launch traced here: 118 us
  starting transfers between devices  45.7 us (38%)
  waiting for transfers between devices  35.9 us (30%)
  Pallas kernels  20.7 us (17%)
  local copies, waits for them, and re-layouts  14.6 us (12%)
    ppermute x8, waiting for transfers between devices, chip_aware(): by_x.append(lax.ppermute(part, 'lon', across_x))  28.7 us
    ppermute x8, starting transfers between devices, chip_aware(): by_x.append(lax.ppermute(part, 'lon', across_x))  23.5 us
    ppermute x8, starting transfers between devices, chip_aware(): lax.ppermute(after(by_x[i], *by_z[max(i - 2, 0):max(i - 1, 0)]), 'lon', a...  15.6 us
    pallas_call x4, Pallas kernels, filter_pair(): pl.pallas_call(functools.partial(pair_kernel, lon_dev), out_shape=[out, o...  14.9 us
    unnamed x46, local copies, waits for them, and re-layouts  12.3 us
    ppermute x8, waiting for transfers between devices, chip_aware(): lax.ppermute(after(by_x[i], *by_z[max(i - 2, 0):max(i - 1, 0)]), 'lon', a...  5 us
    ppermute x4, starting transfers between devices, chip_aware(): over_y.append(lax.ppermute(operand, ('lon', 'lat'), pairs))  4.83 us
    pallas_call x1, Pallas kernels, take_rows(): pl.pallas_call(functools.partial(take_kernel, chunks, lat_dev, block), ou...  3 us
  transfers between devices with their start and end apart: 26, of which 13 were waited for; matrix products, arithmetic and copies ran while one was open for 2% of the time, Pallas kernels for 13%

profile of v4, /device:TPU:0, one launch (start us, length us, event | category | flops | bytes accessed | tf_op | source)
XLA Modules:
  0.0 117.5 jit_solution(14220871860776183185)
XLA Ops:
  0.0 0.1 pad_add_fusion.place_ref
  0.1 2.0 %copy-done = bf16[16,180,640]{2,0,1:T(8,128)(2,1)S(1)} copy-done((bf16[16,180,640]{2,0,1:T(8,128)(2,1)S(1)}, bf16[16,180,640]{2,0,1:T(8,128)(2,1)}, u32[]{:S(2)}) %copy-start) | copy-done | bytes 3686424
  2.1 0.7 copy-done.1
  2.8 3.0 %take_rows.1 = (bf16[2,184,640]{2,1,0:T(8,128)(2,1)S(1)}, bf16[2,184,640]{2,1,0:T(8,128)(2,1)S(1)}, bf16[2,184,640]{2,1,0:T(8,128)(2,1)S(1)}, bf16[2,184,640]{2,...) custom-call(s32[32]{0:T(128)S(1)} %copy-done.1, ...), custom_call_target="tpu_custom_call" | custom-call | flops 943718400 | bytes 7372800 | tf_op jit(solution)/shard_map/take_rows/pallas_call | solution.py:122
  5.8 0.5 collective-permute-start
  6.3 2.6 %collective-permute-start.1 = (bf16[2,184,640]{2,1,0:T(8,128)(2,1)S(1)}, bf16[2,184,640]{2,1,0:T(8,128)(2,1)S(1)}, u32[]{:S(2)}, u32[]{:S(2)}) collective-permute-start(bf16[2,184,640]{2,1,0:T(8,128)(2,1)S(1)} %get-tuple-element.39.own), channel_id=1, source_target_pairs={{0,4},{2,6},{4,0},{6,2},{8,12},{10,14},{12,8},{14,10},{16,20},{18,... | collective-permute-start | bytes 1413128 | tf_op jit(solution)/shard_map/ppermute | solution.py:295
  8.9 1.5 %collective-permute-start.6 = (bf16[2,184,640]{2,1,0:T(8,128)(2,1)S(1)}, bf16[2,184,640]{2,1,0:T(8,128)(2,1)S(1)}, u32[]{:S(2)}, u32[]{:S(2)}) collective-permute-start(bf16[2,184,640]{2,1,0:T(8,128)(2,1)S(1)} %get-tuple-element.44), channel_id=1, source_target_pairs={{0,1},{1,0},{2,3},{3,2},{4,5},{5,4},{6,7},{7,6},{8,9},{9,8},{10,11... | collective-permute-start | bytes 1413128 | tf_op jit(solution)/shard_map/ppermute | solution.py:286
  10.4 0.5 collective-permute-start.2
  10.9 1.3 %collective-permute-start.8 = (bf16[2,184,640]{2,1,0:T(8,128)(2,1)S(1)}, bf16[2,184,640]{2,1,0:T(8,128)(2,1)S(1)}, u32[]{:S(2)}, u32[]{:S(2)}) collective-permute-start(bf16[2,184,640]{2,1,0:T(8,128)(2,1)S(1)} %get-tuple-element.46), channel_id=1, source_target_pairs={{0,3},{1,2},{2,1},{3,0},{4,7},{5,6},{6,5},{7,4},{8,11},{9,10},{10,... | collective-permute-start | bytes 1413128 | tf_op jit(solution)/shard_map/ppermute | solution.py:286
  12.3 8.2 %collective-permute-done.1.x_own = bf16[2,184,640]{2,1,0:T(8,128)(2,1)S(1)} collective-permute-done((bf16[2,184,640]{2,1,0:T(8,128)(2,1)S(1)}, bf16[2,184,640]{2,1,0:T(8,128)(2,1)S(1)}, u32[]{:S(2)}, u32[]{:S(2)}) %collective-permute-start.1) | collective-permute-done | bytes 471072 | tf_op jit(solution)/shard_map/ppermute | solution.py:295
  20.5 2.0 %collective-permute-start.3 = (bf16[2,184,640]{2,1,0:T(8,128)(2,1)S(1)}, bf16[2,184,640]{2,1,0:T(8,128)(2,1)S(1)}, u32[]{:S(2)}, u32[]{:S(2)}) collective-permute-start(bf16[2,184,640]{2,1,0:T(8,128)(2,1)S(1)} %collective-permute-done.1.x_own), channel_id=1, source_target_pairs={{0,8},{2,10},{4,28},{6,30},{8,16},{10,18},{12,4},{14,6},{16,24},{1... | collective-permute-start | bytes 1413128 | tf_op jit(solution)/shard_map/ppermute | solution.py:296
  22.5 0.8 copy-done.2
  23.3 3.5 %collective-permute-start.7 = (bf16[2,184,640]{2,1,0:T(8,128)(2,1)S(1)}, bf16[2,184,640]{2,1,0:T(8,128)(2,1)S(1)}, u32[]{:S(2)}, u32[]{:S(2)}) collective-permute-start(bf16[2,184,640]{2,1,0:T(8,128)(2,1)S(1)} %get-tuple-element.45.own), channel_id=1, source_target_pairs={{0,4},{2,6},{4,0},{6,2},{8,12},{10,14},{12,8},{14,10},{16,20},{18,... | collective-permute-start | bytes 1413128 | tf_op jit(solution)/shard_map/ppermute | solution.py:295
  26.8 3.8 %collective-permute-done.2.x_other = bf16[2,184,640]{2,1,0:T(8,128)(2,1)S(1)} collective-permute-done((bf16[2,184,640]{2,1,0:T(8,128)(2,1)S(1)}, bf16[2,184,640]{2,1,0:T(8,128)(2,1)S(1)}, u32[]{:S(2)}, u32[]{:S(2)}) %collective-permute-start.2) | collective-permute-done | bytes 471072 | tf_op jit(solution)/shard_map/ppermute | solution.py:295
  30.6 2.0 %collective-permute-start.12 = (bf16[2,184,640]{2,1,0:T(8,128)(2,1)S(1)}, bf16[2,184,640]{2,1,0:T(8,128)(2,1)S(1)}, u32[]{:S(2)}, u32[]{:S(2)}) collective-permute-start(bf16[2,184,640]{2,1,0:T(8,128)(2,1)S(1)} %get-tuple-element.52), channel_id=1, source_target_pairs={{0,1},{1,0},{2,3},{3,2},{4,5},{5,4},{6,7},{7,6},{8,9},{9,8},{10,11... | collective-permute-start | bytes 1413128 | tf_op jit(solution)/shard_map/ppermute | solution.py:286
  32.6 1.6 %collective-permute-start.4 = (bf16[2,184,640]{2,1,0:T(8,128)(2,1)S(1)}, bf16[2,184,640]{2,1,0:T(8,128)(2,1)S(1)}, u32[]{:S(2)}, u32[]{:S(2)}) collective-permute-start(bf16[2,184,640]{2,1,0:T(8,128)(2,1)S(1)} %collective-permute-done.2.x_other), channel_id=1, source_target_pairs={{0,8},{2,10},{4,28},{6,30},{8,16},{10,18},{12,4},{14,6},{16,24},{1... | collective-permute-start | bytes 1413128 | tf_op jit(solution)/shard_map/ppermute | solution.py:296
  34.2 3.5 %collective-permute-start.9 = (bf16[2,184,640]{2,1,0:T(8,128)(2,1)S(1)}, bf16[2,184,640]{2,1,0:T(8,128)(2,1)S(1)}, u32[]{:S(2)}, u32[]{:S(2)}) collective-permute-start(bf16[2,184,640]{2,1,0:T(8,128)(2,1)S(1)} %collective-permute-done.5.other), channel_id=1, source_target_pairs={{0,4},{2,6},{4,0},{6,2},{8,12},{10,14},{12,8},{14,10},{16,20},{18,... | collective-permute-start | bytes 1413128 | tf_op jit(solution)/shard_map/ppermute | solution.py:295
  37.7 0.8 copy-done.10
  38.5 2.2 %collective-permute-done.7.x_own = bf16[2,184,640]{2,1,0:T(8,128)(2,1)S(1)} collective-permute-done((bf16[2,184,640]{2,1,0:T(8,128)(2,1)S(1)}, bf16[2,184,640]{2,1,0:T(8,128)(2,1)S(1)}, u32[]{:S(2)}, u32[]{:S(2)}) %collective-permute-start.7) | collective-permute-done | bytes 471072 | tf_op jit(solution)/shard_map/ppermute | solution.py:295
  40.7 2.0 %collective-permute-start.10 = (bf16[2,184,640]{2,1,0:T(8,128)(2,1)S(1)}, bf16[2,184,640]{2,1,0:T(8,128)(2,1)S(1)}, u32[]{:S(2)}, u32[]{:S(2)}) collective-permute-start(bf16[2,184,640]{2,1,0:T(8,128)(2,1)S(1)} %collective-permute-done.7.x_own), channel_id=1, source_target_pairs={{0,8},{2,10},{4,28},{6,30},{8,16},{10,18},{12,4},{14,6},{16,24},{1... | collective-permute-start | bytes 1413128 | tf_op jit(solution)/shard_map/ppermute | solution.py:296
  42.7 0.8 copy-done.8
  43.5 0.7 collective-permute-done.12.own
  44.2 2.8 %collective-permute-start.13 = (bf16[2,184,640]{2,1,0:T(8,128)(2,1)S(1)}, bf16[2,184,640]{2,1,0:T(8,128)(2,1)}, u32[]{:S(2)}, u32[]{:S(2)}) collective-permute-start(bf16[2,184,640]{2,1,0:T(8,128)(2,1)S(1)} %collective-permute-done.6.own), channel_id=1, source_target_pairs={{0,4},{2,6},{4,0},{6,2},{8,12},{10,14},{12,8},{14,10},{16,20},{18,... | collective-permute-start | bytes 1413128 | tf_op jit(solution)/shard_map/ppermute | solution.py:295
  47.0 0.2 collective-permute-done.4.z_other
  47.3 0.8 copy-done.14
  48.0 2.8 %collective-permute-done.9.x_other = bf16[2,184,640]{2,1,0:T(8,128)(2,1)S(1)} collective-permute-done((bf16[2,184,640]{2,1,0:T(8,128)(2,1)S(1)}, bf16[2,184,640]{2,1,0:T(8,128)(2,1)S(1)}, u32[]{:S(2)}, u32[]{:S(2)}) %collective-permute-start.9) | collective-permute-done | bytes 471072 | tf_op jit(solution)/shard_map/ppermute | solution.py:295
  50.8 2.0 %collective-permute-start.11 = (bf16[2,184,640]{2,1,0:T(8,128)(2,1)S(1)}, bf16[2,184,640]{2,1,0:T(8,128)(2,1)S(1)}, u32[]{:S(2)}, u32[]{:S(2)}) collective-permute-start(bf16[2,184,640]{2,1,0:T(8,128)(2,1)S(1)} %collective-permute-done.9.x_other), channel_id=1, source_target_pairs={{0,8},{2,10},{4,28},{6,30},{8,16},{10,18},{12,4},{14,6},{16,24},{1... | collective-permute-start | bytes 1413128 | tf_op jit(solution)/shard_map/ppermute | solution.py:296
  52.8 0.8 copy-done.12
  53.6 3.5 %collective-permute-start.15 = (bf16[2,184,640]{2,1,0:T(8,128)(2,1)S(1)}, bf16[2,184,640]{2,1,0:T(8,128)(2,1)}, u32[]{:S(2)}, u32[]{:S(2)}) collective-permute-start(bf16[2,184,640]{2,1,0:T(8,128)(2,1)S(1)} %collective-permute-done.8.other), channel_id=1, source_target_pairs={{0,4},{2,6},{4,0},{6,2},{8,12},{10,14},{12,8},{14,10},{16,20},{18,... | collective-permute-start | bytes 1413128 | tf_op jit(solution)/shard_map/ppermute | solution.py:295
  57.1 0.1 convert_select_fusion
  57.2 0.1 fusion.2
  57.3 0.1 fusion.3
  57.5 0.8 copy-done.16
  58.2 2.8 %collective-permute-done.13.x_own = bf16[2,184,640]{2,1,0:T(8,128)(2,1)} collective-permute-done((bf16[2,184,640]{2,1,0:T(8,128)(2,1)S(1)}, bf16[2,184,640]{2,1,0:T(8,128)(2,1)}, u32[]{:S(2)}, u32[]{:S(2)}) %collective-permute-start.13) | collective-permute-done | bytes 471072 | tf_op jit(solution)/shard_map/ppermute | solution.py:295
  61.0 2.0 %collective-permute-start.16 = (bf16[2,184,640]{2,1,0:T(8,128)(2,1)}, bf16[2,184,640]{2,1,0:T(8,128)(2,1)}, u32[]{:S(2)}, u32[]{:S(2)}) collective-permute-start(bf16[2,184,640]{2,1,0:T(8,128)(2,1)} %collective-permute-done.13.x_own), channel_id=1, source_target_pairs={{0,8},{2,10},{4,28},{6,30},{8,16},{10,18},{12,4},{14,6},{16,24},{1... | collective-permute-start | bytes 1413128 | tf_op jit(solution)/shard_map/ppermute | solution.py:296
  63.0 3.5 %collective-permute-start.18 = (bf16[2,184,640]{2,1,0:T(8,128)(2,1)S(1)}, bf16[2,184,640]{2,1,0:T(8,128)(2,1)}, u32[]{:S(2)}, u32[]{:S(2)}) collective-permute-start(bf16[2,184,640]{2,1,0:T(8,128)(2,1)S(1)} %collective-permute-done.12.own), channel_id=1, source_target_pairs={{0,4},{2,6},{4,0},{6,2},{8,12},{10,14},{12,8},{14,10},{16,20},{18,... | collective-permute-start | bytes 1413128 | tf_op jit(solution)/shard_map/ppermute | solution.py:295
  66.5 0.6 collective-permute-done.11.z_other
  67.1 0.8 copy-done.18
  67.9 3.2 %collective-permute-done.15.x_other = bf16[2,184,640]{2,1,0:T(8,128)(2,1)} collective-permute-done((bf16[2,184,640]{2,1,0:T(8,128)(2,1)S(1)}, bf16[2,184,640]{2,1,0:T(8,128)(2,1)}, u32[]{:S(2)}, u32[]{:S(2)}) %collective-permute-start.15) | collective-permute-done | bytes 471072 | tf_op jit(solution)/shard_map/ppermute | solution.py:295
  71.1 2.0 %collective-permute-start.17 = (bf16[2,184,640]{2,1,0:T(8,128)(2,1)}, bf16[2,184,640]{2,1,0:T(8,128)(2,1)}, u32[]{:S(2)}, u32[]{:S(2)}) collective-permute-start(bf16[2,184,640]{2,1,0:T(8,128)(2,1)} %collective-permute-done.15.x_other), channel_id=1, source_target_pairs={{0,8},{2,10},{4,28},{6,30},{8,16},{10,18},{12,4},{14,6},{16,24},{1... | collective-permute-start | bytes 1413128 | tf_op jit(solution)/shard_map/ppermute | solution.py:296
  73.1 3.5 %collective-permute-start.19 = (bf16[2,184,640]{2,1,0:T(8,128)(2,1)}, bf16[2,184,640]{2,1,0:T(8,128)(2,1)}, u32[]{:S(2)}, u32[]{:S(2)}) collective-permute-start(bf16[2,184,640]{2,1,0:T(8,128)(2,1)} %collective-permute-done.14.other), channel_id=1, source_target_pairs={{0,4},{2,6},{4,0},{6,2},{8,12},{10,14},{12,8},{14,10},{16,20},{18,... | collective-permute-start | bytes 1413128 | tf_op jit(solution)/shard_map/ppermute | solution.py:295
  76.6 0.6 pad_bitcast_fusion
  77.3 0.9 copy.6
  78.2 0.1 fusion.1
  78.5 0.5 stack.47.win_ref
  78.9 0.1 pad_add_fusion.1.sign_ref
  79.0 2.2 %collective-permute-done.18.x_own = bf16[2,184,640]{2,1,0:T(8,128)(2,1)} collective-permute-done((bf16[2,184,640]{2,1,0:T(8,128)(2,1)S(1)}, bf16[2,184,640]{2,1,0:T(8,128)(2,1)}, u32[]{:S(2)}, u32[]{:S(2)}) %collective-permute-start.18) | collective-permute-done | bytes 471072 | tf_op jit(solution)/shard_map/ppermute | solution.py:295
  81.2 2.0 %collective-permute-start.20 = (bf16[2,184,640]{2,1,0:T(8,128)(2,1)}, bf16[2,184,640]{2,1,0:T(8,128)(2,1)S(1)}, u32[]{:S(2)}, u32[]{:S(2)}) collective-permute-start(bf16[2,184,640]{2,1,0:T(8,128)(2,1)} %collective-permute-done.18.x_own), channel_id=1, source_target_pairs={{0,8},{2,10},{4,28},{6,30},{8,16},{10,18},{12,4},{14,6},{16,24},{1... | collective-permute-start | bytes 1413128 | tf_op jit(solution)/shard_map/ppermute | solution.py:296
  83.2 4.2 %collective-permute-done.17.z_other = bf16[2,184,640]{2,1,0:T(8,128)(2,1)} collective-permute-done((bf16[2,184,640]{2,1,0:T(8,128)(2,1)}, bf16[2,184,640]{2,1,0:T(8,128)(2,1)}, u32[]{:S(2)}, u32[]{:S(2)}) %collective-permute-start.17) | collective-permute-done | bytes 471072 | tf_op jit(solution)/shard_map/ppermute | solution.py:296
  87.4 3.6 %collective-permute-done.19.x_other = bf16[2,184,640]{2,1,0:T(8,128)(2,1)} collective-permute-done((bf16[2,184,640]{2,1,0:T(8,128)(2,1)}, bf16[2,184,640]{2,1,0:T(8,128)(2,1)}, u32[]{:S(2)}, u32[]{:S(2)}) %collective-permute-start.19) | collective-permute-done | bytes 471072 | tf_op jit(solution)/shard_map/ppermute | solution.py:295
  91.0 1.8 %collective-permute-start.21 = (bf16[2,184,640]{2,1,0:T(8,128)(2,1)}, bf16[2,184,640]{2,1,0:T(8,128)(2,1)S(1)}, u32[]{:S(2)}, u32[]{:S(2)}) collective-permute-start(bf16[2,184,640]{2,1,0:T(8,128)(2,1)} %collective-permute-done.19.x_other), channel_id=1, source_target_pairs={{0,8},{2,10},{4,28},{6,30},{8,16},{10,18},{12,4},{14,6},{16,24},{1... | collective-permute-start | bytes 1413128 | tf_op jit(solution)/shard_map/ppermute | solution.py:296
  92.9 1.0 copy-done.3
  93.9 1.0 copy-done.7
  94.9 1.0 copy-done.11
  95.9 1.0 copy-done.15
  97.0 3.1 %filter_pair.4 = (bf16[2,184,640]{2,1,0:T(8,128)(2,1)S(1)}, bf16[2,184,640]{2,1,0:T(8,128)(2,1)S(1)}) custom-call(s32[16]{0:T(128)S(1)} %get-tuple-element.38.rows_ref, s32[2]{0:T(128)S(1)} %pad_add_fusion.1.sign_ref, f32[32,5,384]{2,1,0:T(8,128)S(1)} %stack.47.win_ref, bf16[2,184,640]{2,1,0:T(8,128)(2,1)S(1)} %get-tuple-element.39.own, ...), custom_call_target="tpu_custom_call" | custom-call | flops 2013265920 | bytes 3768320 | tf_op jit(solution)/shard_map/filter_pair/pallas_call | solution.py:231
  100.2 3.1 %filter_pair.5 = (bf16[2,184,640]{2,1,0:T(8,128)(2,1)S(1)}, bf16[2,184,640]{2,1,0:T(8,128)(2,1)S(1)}) custom-call(s32[16]{0:T(128)S(1)} %get-tuple-element.38.rows_ref, s32[2]{0:T(128)S(1)} %pad_add_fusion.1.sign_ref, f32[32,5,384]{2,1,0:T(8,128)S(1)} %stack.47.win_ref, bf16[2,184,640]{2,1,0:T(8,128)(2,1)S(1)} %get-tuple-element.45.own, ...), custom_call_target="tpu_custom_call" | custom-call | flops 2013265920 | bytes 3768320 | tf_op jit(solution)/shard_map/filter_pair/pallas_call | solution.py:231
  103.4 0.5 collective-permute-start.23
  103.9 4.4 %filter_pair.6 = (bf16[2,184,640]{2,1,0:T(8,128)(2,1)S(1)}, bf16[2,184,640]{2,1,0:T(8,128)(2,1)S(1)}) custom-call(s32[16]{0:T(128)S(1)} %get-tuple-element.38.rows_ref, s32[2]{0:T(128)S(1)} %pad_add_fusion.1.sign_ref, f32[32,5,384]{2,1,0:T(8,128)S(1)} %stack.47.win_ref, bf16[2,184,640]{2,1,0:T(8,128)(2,1)S(1)} %collective-permute-done.6.own, ...), custom_call_target="tpu_custom_call" | custom-call | flops 2013265920 | bytes 3768320 | tf_op jit(solution)/shard_map/filter_pair/pallas_call | solution.py:231
  108.3 0.1 collective-permute-start.24
  108.4 4.3 %filter_pair.7 = (bf16[2,184,640]{2,1,0:T(8,128)(2,1)S(1)}, bf16[2,184,640]{2,1,0:T(8,128)(2,1)S(1)}) custom-call(s32[16]{0:T(128)S(1)} %get-tuple-element.38.rows_ref, s32[2]{0:T(128)S(1)} %pad_add_fusion.1.sign_ref, f32[32,5,384]{2,1,0:T(8,128)S(1)} %stack.47.win_ref, bf16[2,184,640]{2,1,0:T(8,128)(2,1)S(1)} %collective-permute-done.12.own, ...), custom_call_target="tpu_custom_call" | custom-call | flops 2013265920 | bytes 3768320 | tf_op jit(solution)/shard_map/filter_pair/pallas_call | solution.py:231
  112.7 0.6 collective-permute-start.25
  113.3 1.4 %collective-permute-done.25.refs_7_ = bf16[2,184,640]{2,1,0:T(8,128)(2,1)S(1)} collective-permute-done((bf16[2,184,640]{2,1,0:T(8,128)(2,1)S(1)}, bf16[2,184,640]{2,1,0:T(8,128)(2,1)S(1)}, u32[]{:S(2)}, u32[]{:S(2)}) %collective-permute-start.25) | collective-permute-done | bytes 471072 | tf_op jit(solution)/shard_map/ppermute | solution.py:275
  114.7 2.8 %put_rows.1 = bf16[180,16,640]{2,1,0:T(8,128)(2,1)} custom-call(s32[16]{0:T(128)S(1)} %get-tuple-element.37.slots_ref, bf16[2,184,640]{2,1,0:T(8,128)(2,1)S(1)} %get-tuple-element.41.refs_0_, bf16[2,184,640]{2,1,0:T(8,128)(2,1)S(1)} %get-tuple-element.50.refs_1_, bf16[2,184,640]{2,1,0:T(8,128)(2,1)S(1)} %get-tuple-element.59.refs_2_, ...), custom_call_target="tpu_custom_call" | custom-call | flops 943718400 | bytes 7372800 | tf_op jit(solution)/shard_map/put_rows/pallas_call | solution.py:174
  (56 shorter events, 0.4 us)
Async XLA Ops:
  0.0 78.3 %copy-start.21 = (pred[384]{0:T(512)(128)(4,1)S(1)}, pred[384]{0:T(512)(128)(4,1)}, u32[]{:S(2)}) copy-start(pred[384]{0:T(512)(128)(4,1)} %constant.44.clone.1) | copy-start | bytes 1156
  0.0 57.1 %copy-start.22 = (s32[32]{0:T(128)S(1)}, s32[32]{0:T(128)}, u32[]{:S(2)}) copy-start(s32[32]{0:T(128)} %param.6) | copy-start | bytes 388
  0.1 2.0 %copy-start = (bf16[16,180,640]{2,0,1:T(8,128)(2,1)S(1)}, bf16[16,180,640]{2,0,1:T(8,128)(2,1)}, u32[]{:S(2)}) copy-start(bf16[16,180,640]{2,0,1:T(8,128)(2,1)} %param.4) | copy-start | bytes 11059204
  2.1 0.7 copy-start.1
  2.8 54.4 %copy-start.20 = (bf16[32,2880]{1,0:T(8,128)(2,1)S(1)}, bf16[32,2880]{1,0:T(8,128)(2,1)}, u32[]{:S(2)}) copy-start(bf16[32,2880]{1,0:T(8,128)(2,1)} %param.7) | copy-start | bytes 552964
  5.8 4.6 %collective-permute-start = (bf16[2,184,640]{2,1,0:T(8,128)(2,1)S(1)}, bf16[2,184,640]{2,1,0:T(8,128)(2,1)S(1)}, u32[]{:S(2)}, u32[]{:S(2)}) collective-permute-start(bf16[2,184,640]{2,1,0:T(8,128)(2,1)S(1)} %get-tuple-element.40), channel_id=1, source_target_pairs={{0,2},{2,0},{4,6},{6,4},{8,10},{10,8},{12,14},{14,12},{16,18},{18,... | collective-permute-start | bytes 1413128 | tf_op jit(solution)/shard_map/ppermute | solution.py:275
  6.3 14.2 %collective-permute-start.1 = (bf16[2,184,640]{2,1,0:T(8,128)(2,1)S(1)}, bf16[2,184,640]{2,1,0:T(8,128)(2,1)S(1)}, u32[]{:S(2)}, u32[]{:S(2)}) collective-permute-start(bf16[2,184,640]{2,1,0:T(8,128)(2,1)S(1)} %get-tuple-element.39.own), channel_id=1, source_target_pairs={{0,4},{2,6},{4,0},{6,2},{8,12},{10,14},{12,8},{14,10},{16,20},{18,... | collective-permute-start | bytes 1413128 | tf_op jit(solution)/shard_map/ppermute | solution.py:295
  8.9 14.4 %collective-permute-start.6 = (bf16[2,184,640]{2,1,0:T(8,128)(2,1)S(1)}, bf16[2,184,640]{2,1,0:T(8,128)(2,1)S(1)}, u32[]{:S(2)}, u32[]{:S(2)}) collective-permute-start(bf16[2,184,640]{2,1,0:T(8,128)(2,1)S(1)} %get-tuple-element.44), channel_id=1, source_target_pairs={{0,1},{1,0},{2,3},{3,2},{4,5},{5,4},{6,7},{7,6},{8,9},{9,8},{10,11... | collective-permute-start | bytes 1413128 | tf_op jit(solution)/shard_map/ppermute | solution.py:286
  10.4 20.2 %collective-permute-start.2 = (bf16[2,184,640]{2,1,0:T(8,128)(2,1)S(1)}, bf16[2,184,640]{2,1,0:T(8,128)(2,1)S(1)}, u32[]{:S(2)}, u32[]{:S(2)}) collective-permute-start(bf16[2,184,640]{2,1,0:T(8,128)(2,1)S(1)} %collective-permute-done.other), channel_id=1, source_target_pairs={{0,4},{2,6},{4,0},{6,2},{8,12},{10,14},{12,8},{14,10},{16,20},{18,... | collective-permute-start | bytes 1413128 | tf_op jit(solution)/shard_map/ppermute | solution.py:295
  10.9 21.7 %collective-permute-start.5 = (bf16[2,184,640]{2,1,0:T(8,128)(2,1)S(1)}, bf16[2,184,640]{2,1,0:T(8,128)(2,1)S(1)}, u32[]{:S(2)}, u32[]{:S(2)}) collective-permute-start(bf16[2,184,640]{2,1,0:T(8,128)(2,1)S(1)} %get-tuple-element.43), channel_id=1, source_target_pairs={{0,2},{2,0},{4,6},{6,4},{8,10},{10,8},{12,14},{14,12},{16,18},{18,... | collective-permute-start | bytes 1413128 | tf_op jit(solution)/shard_map/ppermute | solution.py:275
  10.9 23.2 %collective-permute-start.8 = (bf16[2,184,640]{2,1,0:T(8,128)(2,1)S(1)}, bf16[2,184,640]{2,1,0:T(8,128)(2,1)S(1)}, u32[]{:S(2)}, u32[]{:S(2)}) collective-permute-start(bf16[2,184,640]{2,1,0:T(8,128)(2,1)S(1)} %get-tuple-element.46), channel_id=1, source_target_pairs={{0,3},{1,2},{2,1},{3,0},{4,7},{5,6},{6,5},{7,4},{8,11},{9,10},{10,... | collective-permute-start | bytes 1413128 | tf_op jit(solution)/shard_map/ppermute | solution.py:286
  20.5 17.2 %collective-permute-start.3 = (bf16[2,184,640]{2,1,0:T(8,128)(2,1)S(1)}, bf16[2,184,640]{2,1,0:T(8,128)(2,1)S(1)}, u32[]{:S(2)}, u32[]{:S(2)}) collective-permute-start(bf16[2,184,640]{2,1,0:T(8,128)(2,1)S(1)} %collective-permute-done.1.x_own), channel_id=1, source_target_pairs={{0,8},{2,10},{4,28},{6,30},{8,16},{10,18},{12,4},{14,6},{16,24},{1... | collective-permute-start | bytes 1413128 | tf_op jit(solution)/shard_map/ppermute | solution.py:296
  22.5 0.8 copy-start.2
  23.3 17.4 %collective-permute-start.7 = (bf16[2,184,640]{2,1,0:T(8,128)(2,1)S(1)}, bf16[2,184,640]{2,1,0:T(8,128)(2,1)S(1)}, u32[]{:S(2)}, u32[]{:S(2)}) collective-permute-start(bf16[2,184,640]{2,1,0:T(8,128)(2,1)S(1)} %get-tuple-element.45.own), channel_id=1, source_target_pairs={{0,4},{2,6},{4,0},{6,2},{8,12},{10,14},{12,8},{14,10},{16,20},{18,... | collective-permute-start | bytes 1413128 | tf_op jit(solution)/shard_map/ppermute | solution.py:295
  30.6 42.5 %copy-start.6 = (bf16[2,184,640]{2,1,0:T(8,128)(2,1)}, bf16[2,184,640]{2,1,0:T(8,128)(2,1)S(1)}, u32[]{:S(2)}) copy-start(bf16[2,184,640]{2,1,0:T(8,128)(2,1)S(1)} %collective-permute-done.2.x_other) | copy-start | bytes 1413124
  30.6 13.6 %collective-permute-start.12 = (bf16[2,184,640]{2,1,0:T(8,128)(2,1)S(1)}, bf16[2,184,640]{2,1,0:T(8,128)(2,1)S(1)}, u32[]{:S(2)}, u32[]{:S(2)}) collective-permute-start(bf16[2,184,640]{2,1,0:T(8,128)(2,1)S(1)} %get-tuple-element.52), channel_id=1, source_target_pairs={{0,1},{1,0},{2,3},{3,2},{4,5},{5,4},{6,7},{7,6},{8,9},{9,8},{10,11... | collective-permute-start | bytes 1413128 | tf_op jit(solution)/shard_map/ppermute | solution.py:286
  32.6 38.5 %copy-start.4 = (bf16[2,184,640]{2,1,0:T(8,128)(2,1)}, bf16[2,184,640]{2,1,0:T(8,128)(2,1)S(1)}, u32[]{:S(2)}) copy-start(bf16[2,184,640]{2,1,0:T(8,128)(2,1)S(1)} %collective-permute-done.5.other) | copy-start | bytes 1413124
  32.6 14.7 %collective-permute-start.4 = (bf16[2,184,640]{2,1,0:T(8,128)(2,1)S(1)}, bf16[2,184,640]{2,1,0:T(8,128)(2,1)S(1)}, u32[]{:S(2)}, u32[]{:S(2)}) collective-permute-start(bf16[2,184,640]{2,1,0:T(8,128)(2,1)S(1)} %collective-permute-done.2.x_other), channel_id=1, source_target_pairs={{0,8},{2,10},{4,28},{6,30},{8,16},{10,18},{12,4},{14,6},{16,24},{1... | collective-permute-start | bytes 1413128 | tf_op jit(solution)/shard_map/ppermute | solution.py:296
  34.2 16.6 %collective-permute-start.9 = (bf16[2,184,640]{2,1,0:T(8,128)(2,1)S(1)}, bf16[2,184,640]{2,1,0:T(8,128)(2,1)S(1)}, u32[]{:S(2)}, u32[]{:S(2)}) collective-permute-start(bf16[2,184,640]{2,1,0:T(8,128)(2,1)S(1)} %collective-permute-done.5.other), channel_id=1, source_target_pairs={{0,4},{2,6},{4,0},{6,2},{8,12},{10,14},{12,8},{14,10},{16,20},{18,... | collective-permute-start | bytes 1413128 | tf_op jit(solution)/shard_map/ppermute | solution.py:295
  37.7 0.8 copy-start.10
  38.5 15.1 %collective-permute-start.14 = (bf16[2,184,640]{2,1,0:T(8,128)(2,1)S(1)}, bf16[2,184,640]{2,1,0:T(8,128)(2,1)}, u32[]{:S(2)}, u32[]{:S(2)}) collective-permute-start(bf16[2,184,640]{2,1,0:T(8,128)(2,1)S(1)} %get-tuple-element.55), channel_id=1, source_target_pairs={{0,3},{1,2},{2,1},{3,0},{4,7},{5,6},{6,5},{7,4},{8,11},{9,10},{10,... | collective-permute-start | bytes 1413128 | tf_op jit(solution)/shard_map/ppermute | solution.py:286
  40.7 16.7 %collective-permute-start.10 = (bf16[2,184,640]{2,1,0:T(8,128)(2,1)S(1)}, bf16[2,184,640]{2,1,0:T(8,128)(2,1)S(1)}, u32[]{:S(2)}, u32[]{:S(2)}) collective-permute-start(bf16[2,184,640]{2,1,0:T(8,128)(2,1)S(1)} %collective-permute-done.7.x_own), channel_id=1, source_target_pairs={{0,8},{2,10},{4,28},{6,30},{8,16},{10,18},{12,4},{14,6},{16,24},{1... | collective-permute-start | bytes 1413128 | tf_op jit(solution)/shard_map/ppermute | solution.py:296
  42.7 0.8 copy-start.8
  44.2 16.7 %collective-permute-start.13 = (bf16[2,184,640]{2,1,0:T(8,128)(2,1)S(1)}, bf16[2,184,640]{2,1,0:T(8,128)(2,1)}, u32[]{:S(2)}, u32[]{:S(2)}) collective-permute-start(bf16[2,184,640]{2,1,0:T(8,128)(2,1)S(1)} %collective-permute-done.6.own), channel_id=1, source_target_pairs={{0,4},{2,6},{4,0},{6,2},{8,12},{10,14},{12,8},{14,10},{16,20},{18,... | collective-permute-start | bytes 1413128 | tf_op jit(solution)/shard_map/ppermute | solution.py:295
  47.2 0.8 copy-start.14
  50.8 16.3 %collective-permute-start.11 = (bf16[2,184,640]{2,1,0:T(8,128)(2,1)S(1)}, bf16[2,184,640]{2,1,0:T(8,128)(2,1)S(1)}, u32[]{:S(2)}, u32[]{:S(2)}) collective-permute-start(bf16[2,184,640]{2,1,0:T(8,128)(2,1)S(1)} %collective-permute-done.9.x_other), channel_id=1, source_target_pairs={{0,8},{2,10},{4,28},{6,30},{8,16},{10,18},{12,4},{14,6},{16,24},{1... | collective-permute-start | bytes 1413128 | tf_op jit(solution)/shard_map/ppermute | solution.py:296
  52.8 0.8 copy-start.12
  53.6 17.5 %collective-permute-start.15 = (bf16[2,184,640]{2,1,0:T(8,128)(2,1)S(1)}, bf16[2,184,640]{2,1,0:T(8,128)(2,1)}, u32[]{:S(2)}, u32[]{:S(2)}) collective-permute-start(bf16[2,184,640]{2,1,0:T(8,128)(2,1)S(1)} %collective-permute-done.8.other), channel_id=1, source_target_pairs={{0,4},{2,6},{4,0},{6,2},{8,12},{10,14},{12,8},{14,10},{16,20},{18,... | collective-permute-start | bytes 1413128 | tf_op jit(solution)/shard_map/ppermute | solution.py:295
  57.4 0.8 copy-start.16
  61.0 18.0 %collective-permute-start.16 = (bf16[2,184,640]{2,1,0:T(8,128)(2,1)}, bf16[2,184,640]{2,1,0:T(8,128)(2,1)}, u32[]{:S(2)}, u32[]{:S(2)}) collective-permute-start(bf16[2,184,640]{2,1,0:T(8,128)(2,1)} %collective-permute-done.13.x_own), channel_id=1, source_target_pairs={{0,8},{2,10},{4,28},{6,30},{8,16},{10,18},{12,4},{14,6},{16,24},{1... | collective-permute-start | bytes 1413128 | tf_op jit(solution)/shard_map/ppermute | solution.py:296
  63.0 18.2 %collective-permute-start.18 = (bf16[2,184,640]{2,1,0:T(8,128)(2,1)S(1)}, bf16[2,184,640]{2,1,0:T(8,128)(2,1)}, u32[]{:S(2)}, u32[]{:S(2)}) collective-permute-start(bf16[2,184,640]{2,1,0:T(8,128)(2,1)S(1)} %collective-permute-done.12.own), channel_id=1, source_target_pairs={{0,4},{2,6},{4,0},{6,2},{8,12},{10,14},{12,8},{14,10},{16,20},{18,... | collective-permute-start | bytes 1413128 | tf_op jit(solution)/shard_map/ppermute | solution.py:295
  67.1 0.8 copy-start.18
  71.1 16.3 %collective-permute-start.17 = (bf16[2,184,640]{2,1,0:T(8,128)(2,1)}, bf16[2,184,640]{2,1,0:T(8,128)(2,1)}, u32[]{:S(2)}, u32[]{:S(2)}) collective-permute-start(bf16[2,184,640]{2,1,0:T(8,128)(2,1)} %collective-permute-done.15.x_other), channel_id=1, source_target_pairs={{0,8},{2,10},{4,28},{6,30},{8,16},{10,18},{12,4},{14,6},{16,24},{1... | collective-permute-start | bytes 1413128 | tf_op jit(solution)/shard_map/ppermute | solution.py:296
  73.1 17.9 %collective-permute-start.19 = (bf16[2,184,640]{2,1,0:T(8,128)(2,1)}, bf16[2,184,640]{2,1,0:T(8,128)(2,1)}, u32[]{:S(2)}, u32[]{:S(2)}) collective-permute-start(bf16[2,184,640]{2,1,0:T(8,128)(2,1)} %collective-permute-done.14.other), channel_id=1, source_target_pairs={{0,4},{2,6},{4,0},{6,2},{8,12},{10,14},{12,8},{14,10},{16,20},{18,... | collective-permute-start | bytes 1413128 | tf_op jit(solution)/shard_map/ppermute | solution.py:295
  81.2 27.2 %collective-permute-start.20 = (bf16[2,184,640]{2,1,0:T(8,128)(2,1)}, bf16[2,184,640]{2,1,0:T(8,128)(2,1)S(1)}, u32[]{:S(2)}, u32[]{:S(2)}) collective-permute-start(bf16[2,184,640]{2,1,0:T(8,128)(2,1)} %collective-permute-done.18.x_own), channel_id=1, source_target_pairs={{0,8},{2,10},{4,28},{6,30},{8,16},{10,18},{12,4},{14,6},{16,24},{1... | collective-permute-start | bytes 1413128 | tf_op jit(solution)/shard_map/ppermute | solution.py:296
  91.0 17.4 %collective-permute-start.21 = (bf16[2,184,640]{2,1,0:T(8,128)(2,1)}, bf16[2,184,640]{2,1,0:T(8,128)(2,1)S(1)}, u32[]{:S(2)}, u32[]{:S(2)}) collective-permute-start(bf16[2,184,640]{2,1,0:T(8,128)(2,1)} %collective-permute-done.19.x_other), channel_id=1, source_target_pairs={{0,8},{2,10},{4,28},{6,30},{8,16},{10,18},{12,4},{14,6},{16,24},{1... | collective-permute-start | bytes 1413128 | tf_op jit(solution)/shard_map/ppermute | solution.py:296
  92.9 1.0 copy-start.3
  93.9 1.0 copy-start.7
  94.9 1.0 copy-start.11
  95.9 1.0 copy-start.15
  97.0 3.2 %copy-start.5 = (bf16[2,184,640]{2,1,0:T(8,128)(2,1)S(1)}, bf16[2,184,640]{2,1,0:T(8,128)(2,1)}, u32[]{:S(2)}) copy-start(bf16[2,184,640]{2,1,0:T(8,128)(2,1)} %copy-done.4) | copy-start | bytes 1413124
  97.0 3.2 %copy-start.9 = (bf16[2,184,640]{2,1,0:T(8,128)(2,1)S(1)}, bf16[2,184,640]{2,1,0:T(8,128)(2,1)}, u32[]{:S(2)}) copy-start(bf16[2,184,640]{2,1,0:T(8,128)(2,1)} %copy-done.8) | copy-start | bytes 1413124
  97.0 3.2 %copy-start.13 = (bf16[2,184,640]{2,1,0:T(8,128)(2,1)S(1)}, bf16[2,184,640]{2,1,0:T(8,128)(2,1)}, u32[]{:S(2)}) copy-start(bf16[2,184,640]{2,1,0:T(8,128)(2,1)} %copy-done.12) | copy-start | bytes 1413124
  97.0 3.3 %copy-start.17 = (bf16[2,184,640]{2,1,0:T(8,128)(2,1)S(1)}, bf16[2,184,640]{2,1,0:T(8,128)(2,1)}, u32[]{:S(2)}) copy-start(bf16[2,184,640]{2,1,0:T(8,128)(2,1)} %copy-done.16) | copy-start | bytes 1413124
  97.0 3.3 %copy-start.19 = (bf16[2,184,640]{2,1,0:T(8,128)(2,1)S(1)}, bf16[2,184,640]{2,1,0:T(8,128)(2,1)}, u32[]{:S(2)}) copy-start(bf16[2,184,640]{2,1,0:T(8,128)(2,1)} %copy-done.18) | copy-start | bytes 1413124
  100.1 13.2 %collective-permute-start.22 = (bf16[2,184,640]{2,1,0:T(8,128)(2,1)S(1)}, bf16[2,184,640]{2,1,0:T(8,128)(2,1)S(1)}, u32[]{:S(2)}, u32[]{:S(2)}) collective-permute-start(bf16[2,184,640]{2,1,0:T(8,128)(2,1)S(1)} %get-tuple-element.65), channel_id=1, source_target_pairs={{0,2},{2,0},{4,6},{6,4},{8,10},{10,8},{12,14},{14,12},{16,18},{18,... | collective-permute-start | bytes 1413128 | tf_op jit(solution)/shard_map/ppermute | solution.py:275
  103.4 9.9 %collective-permute-start.23 = (bf16[2,184,640]{2,1,0:T(8,128)(2,1)S(1)}, bf16[2,184,640]{2,1,0:T(8,128)(2,1)S(1)}, u32[]{:S(2)}, u32[]{:S(2)}) collective-permute-start(bf16[2,184,640]{2,1,0:T(8,128)(2,1)S(1)} %get-tuple-element.66), channel_id=1, source_target_pairs={{0,2},{2,0},{4,6},{6,4},{8,10},{10,8},{12,14},{14,12},{16,18},{18,... | collective-permute-start | bytes 1413128 | tf_op jit(solution)/shard_map/ppermute | solution.py:275
  108.3 5.0 %collective-permute-start.24 = (bf16[2,184,640]{2,1,0:T(8,128)(2,1)S(1)}, bf16[2,184,640]{2,1,0:T(8,128)(2,1)S(1)}, u32[]{:S(2)}, u32[]{:S(2)}) collective-permute-start(bf16[2,184,640]{2,1,0:T(8,128)(2,1)S(1)} %get-tuple-element.67), channel_id=1, source_target_pairs={{0,2},{2,0},{4,6},{6,4},{8,10},{10,8},{12,14},{14,12},{16,18},{18,... | collective-permute-start | bytes 1413128 | tf_op jit(solution)/shard_map/ppermute | solution.py:275
  112.7 2.0 %collective-permute-start.25 = (bf16[2,184,640]{2,1,0:T(8,128)(2,1)S(1)}, bf16[2,184,640]{2,1,0:T(8,128)(2,1)S(1)}, u32[]{:S(2)}, u32[]{:S(2)}) collective-permute-start(bf16[2,184,640]{2,1,0:T(8,128)(2,1)S(1)} %get-tuple-element.68), channel_id=1, source_target_pairs={{0,2},{2,0},{4,6},{6,4},{8,10},{10,8},{12,14},{14,12},{16,18},{18,... | collective-permute-start | bytes 1413128 | tf_op jit(solution)/shard_map/ppermute | solution.py:275

commit v5 on v4

--- a/solution.py
+++ b/solution.py
@@ -11,8 +11,27 @@
 SMEM_SPEC = pl.BlockSpec(memory_space=pltpu.SMEM)
 VMEM_SPEC = pl.BlockSpec(memory_space=pltpu.VMEM)
 HBM_SPEC = pl.BlockSpec(memory_space=pltpu.HBM)
-STAY = (2, 2)
+STAY = (1, 1, 2)
 COME = (2, 2)
+PARTS = [("k", 2), ("c", 2), ("y", 0), ("y", 1), ("y", 2), ("y", 3)]
+FILTERS = ((2, 3), (4, 5), (6, 7))
+WAITS = {
+    ("x", 1): [("p", 1), ("q", 0)],
+    ("x", 2): [("x", 0), ("q", 1), ("q", 0)],
+    ("x", 3): [("x", 1), ("q", 2)],
+    ("x", 4): [("x", 2), ("q", 3), ("q", 2)],
+    ("x", 5): [("x", 3), ("z", 0), ("f", 0)],
+    ("q", 3): [("q", 1)],
+    ("z", 0): [("q", 2)],
+    ("z", 1): [("q", 3)],
+    ("z", 2): [("z", 0)],
+    ("z", 3): [("z", 1)],
+    ("z", 4): [("z", 2)],
+    ("z", 5): [("z", 3)],
+    ("y", 2): [("y", 0)],
+    ("y", 3): [("y", 1)],
+}
+FLOPS = 6
 
 
 def up_to(value, multiple):
@@ -63,10 +82,15 @@
     lon_dev, _, channels = fields_ref.shape
     half, quarter = lat_dev // 2, lat_dev // 4
     starts = list(range(0, lon_dev, block))
-    band, core = place_ref[0], place_ref[1]
+    band, core, x = place_ref[0], place_ref[1], place_ref[2]
 
     def at(n):
-        return n % quarter + jnp.where(n // quarter == core, 0, quarter)
+        within = n % quarter
+        return within + jnp.where(n // quarter == core, 0, quarter)
+
+    def traded(n):
+        within = n % quarter
+        return n + jnp.where(within < 2, (within + x) % 2 - within, 0)
 
     stay, leave, come = jnp.int32(0), jnp.int32(0), jnp.int32(0)
     for j in range(lat_dev):
@@ -74,11 +98,11 @@
         there = (1 - band) * lat_dev + j
         stays = slot_ref[here] // lat_dev == band
         comes = slot_ref[there] // lat_dev == band
-        home_ref[jnp.where(stays, at(stay), half + at(leave))] = jnp.int32(j)
+        home_ref[jnp.where(stays, traded(at(stay)), half + at(leave))] = jnp.int32(j)
 
         @pl.when(stays)
         def _():
-            spot = at(stay)
+            spot = traded(at(stay))
             spot = spot + jnp.where(spot >= quarter, quarter, 0)
             rows_ref[spot] = here
             slots_ref[spot] = slot_ref[here] % lat_dev
@@ -190,65 +214,72 @@
     )(slots, *panels)
 
 
-def pair_kernel(lon_dev, rows_ref, sign_ref, win_ref, own, other, x_own, x_other, z_own, z_other,
-                out_own, out_other, block_ref, total_ref):
-    padded, channels = own.shape[1:]
-    for s in range(5):
-        block_ref[s] = toeplitz(win_ref[0, s : s + 1, :], lon_dev, padded)
+def pair_kernel(lon_dev, base, plan, rows_ref, sign_ref, win_ref, *refs):
+    ins, (out_own, out_other, block_ref, total_ref) = refs[:-4], refs[-4:]
+    padded, channels = out_own.shape[1:]
     side, along = sign_ref[0], sign_ref[1]
-
-    def times(offset, panel):
-        return jnp.dot(block_ref[2 + offset], panel, preferred_element_type=jnp.float32)[:padded]
-
-    def both(first, second):
-        return jnp.concatenate([first[0], second[0]], axis=1)
-
-    here = both(own, other)
-    total = here.astype(jnp.float32) + times(0, here)
-    total += times(2 * along, both(x_own, x_other))
-    total += times(-2 * along, both(z_own, z_other))
-    total += jnp.concatenate([times(side, other[0]), times(-side, own[0])], axis=1)
-    total_ref[...] = total
-
-    @pl.when(side == along)
-    def _():
-        total_ref[...] += jnp.concatenate([times(-along, z_other[0]), times(along, x_own[0])], axis=1)
-
-    @pl.when(side != along)
-    def _():
-        total_ref[...] += jnp.concatenate([times(along, x_other[0]), times(-along, z_own[0])], axis=1)
-
-    out_own[0] = total_ref[:, :channels].astype(out_own.dtype)
-    out_other[0] = total_ref[:, channels:].astype(out_other.dtype)
-
-
-def filter_pair(rows, signs, windows, panels, base, lon_dev):
-    count, padded, channels = panels[0].shape
-    row_spec = pl.BlockSpec((1, padded, channels), lambda i, rows, signs: (i, 0, 0))
-    win_spec = pl.BlockSpec((1,) + windows.shape[1:], lambda i, rows, signs: (rows[base + i], 0, 0))
-    out = jax.ShapeDtypeStruct((count, padded, channels), panels[0].dtype)
-    tall = up_to(lon_dev, 96)
+    for n, places in enumerate(plan):
+        taps = win_ref[rows_ref[base + n]]
+        for s in range(5):
+            block_ref[n, s] = toeplitz(taps[s : s + 1], lon_dev, padded)
+        own, other, x_own, x_other, z_own, z_other = [ins[array].at[i] for array, i in places]
+
+        def times(offset, panel):
+            return jnp.dot(block_ref[n, 2 + offset], panel, preferred_element_type=jnp.float32)[:padded]
+
+        def both(first, second):
+            return jnp.concatenate([first[...], second[...]], axis=1)
+
+        here = both(own, other)
+        total = here.astype(jnp.float32) + times(0, here)
+        total += times(2 * along, both(x_own, x_other))
+        total += times(-2 * along, both(z_own, z_other))
+        total += jnp.concatenate([times(side, other[...]), times(-side, own[...])], axis=1)
+        total_ref[n] = total
+
+        @pl.when(side == along)
+        def _():
+            total_ref[n] += jnp.concatenate([times(-along, z_other[...]), times(along, x_own[...])], axis=1)
+
+        @pl.when(side != along)
+        def _():
+            total_ref[n] += jnp.concatenate([times(along, x_other[...]), times(-along, z_own[...])], axis=1)
+
+        out_own[n] = total_ref[n, :, :channels].astype(out_own.dtype)
+        out_other[n] = total_ref[n, :, channels:].astype(out_other.dtype)
+
+
+def filter_pair(rows, signs, windows, places, base, lon_dev):
+    arrays = []
+    plan = []
+    for row in places:
+        found = []
+        for array, i in row:
+            at = next((n for n, a in enumerate(arrays) if a is array), len(arrays))
+            if at == len(arrays):
+                arrays.append(array)
+            found.append((at, i))
+        plan.append(tuple(found))
+    count = len(plan)
+    padded, channels = arrays[0].shape[1:]
+    out = jax.ShapeDtypeStruct((count, padded, channels), arrays[0].dtype)
     return pl.pallas_call(
-        functools.partial(pair_kernel, lon_dev),
+        functools.partial(pair_kernel, lon_dev, base, tuple(plan)),
         out_shape=[out, out],
-        grid_spec=pltpu.PrefetchScalarGridSpec(
-            num_scalar_prefetch=2,
-            grid=(count,),
-            in_specs=[win_spec] + [row_spec] * len(panels),
-            out_specs=[row_spec, row_spec],
-            scratch_shapes=[
-                pltpu.VMEM((5, tall, padded), jnp.bfloat16),
-                pltpu.VMEM((padded, 2 * channels), jnp.float32),
-            ],
-        ),
+        in_specs=[SMEM_SPEC, SMEM_SPEC] + [VMEM_SPEC] * (1 + len(arrays)),
+        out_specs=[VMEM_SPEC, VMEM_SPEC],
+        scratch_shapes=[
+            pltpu.VMEM((count, 5, up_to(lon_dev, 96), padded), jnp.bfloat16),
+            pltpu.VMEM((count, padded, 2 * channels), jnp.float32),
+        ],
         compiler_params=pltpu.CompilerParams(vmem_limit_bytes=VMEM_LIMIT),
         cost_estimate=pl.CostEstimate(
-            flops=2 * count * 10 * 256 * 256 * 768,
-            bytes_accessed=2 * 8 * panels[0].size,
+            flops=FLOPS * count * 10 * 256 * 256 * 768,
+            bytes_accessed=16 * count * padded * channels,
             transcendentals=0,
         ),
         name="filter_pair",
-    )(rows, signs, windows, *panels)
+    )(rows, signs, windows, *arrays)
 
 
 def chip_aware(fields, owner_slot, widths, tap_weights):
@@ -257,7 +288,7 @@
     at = lax.axis_index("lon")
     band = lax.axis_index("lat")
     core, x = at % 2, at // 2 % 2
-    place = jnp.stack([band, core]).astype(jnp.int32)
+    place = jnp.stack([band, core, x]).astype(jnp.int32)
     signs = jnp.stack([1 - 2 * core, 1 - 2 * x]).astype(jnp.int32)
     chunks = STAY + STAY + COME + COME
     taken, rows, slots = take_rows(jnp.transpose(fields, (1, 0, 2)), owner_slot, place, chunks)
@@ -267,41 +298,74 @@
 
     across_core = [(i, i ^ 1) for i in range(n_lon)]
     across_x = [(i, i ^ 2) for i in range(n_lon)]
+    across_x_core = [(i, i ^ 3) for i in range(n_lon)]
     across_z = [(i, (i + (4 if i // 2 % 2 == 0 else -4)) % n_lon) for i in range(n_lon)]
+    back_z = [(i, (i + (-4 if i // 2 % 2 == 0 else 4)) % n_lon) for i in range(n_lon)]
     across_y = [(i, i ^ 1) for i in range(2 * n_lon)]
     across_both = [(i, i ^ 3) for i in range(2 * n_lon)]
 
-    def over_core(p):
-        return lax.ppermute(p, "lon", across_core)
-
-    def after(operand, *done):
-        return lax.optimization_barrier((operand,) + done)[0]
-
-    own = list(keep)
-    other = [over_core(g) for g in give]
-    over_y = []
-    for i in range(n_come):
-        for operand, pairs in ((straight[i], across_y), (cross[i], across_both)):
-            operand = after(operand, *over_y[-2:-1])
-            over_y.append(lax.ppermute(operand, ("lon", "lat"), pairs))
-    own += over_y[0::2]
-    other += over_y[1::2]
     windows = tap_windows(widths, tap_weights, lon_dev, 2)
-    parts = [p for pair in zip(own, other) for p in pair]
-    by_x, by_z = [], []
-    for i, part in enumerate(parts):
-        if i >= 2:
-            part = after(part, by_x[i - 2], *over_y[i - 2 : i - 1])
-        by_x.append(lax.ppermute(part, "lon", across_x))
-        by_z.append(lax.ppermute(after(by_x[i], *by_z[max(i - 2, 0) : max(i - 1, 0)]), "lon", across_z))
-    mine, theirs = [], []
-    base = 0
-    for i in range(0, len(parts), 2):
-        panels = parts[i : i + 2] + by_x[i : i + 2] + by_z[i : i + 2]
-        out_own, out_other = filter_pair(rows, signs, windows, panels, base, lon_dev)
-        mine.append(out_own)
-        theirs.append(over_core(out_other))
-        base += out_own.shape[0]
+    sizes = STAY + COME
+    starts = [sum(sizes[:c]) for c in range(len(sizes))]
+    done = {}
+
+    def get(kind, i):
+        if (kind, i) in done:
+            return done[kind, i]
+
+        def moved(operand, axes, pairs):
+            first = [get(*g)[0] if g[0] in "ft" else get(*g) for g in WAITS.get((kind, i), ())]
+            if first:
+                operand = lax.optimization_barrier((operand, *first))[0]
+            return lax.ppermute(operand, axes, pairs)
+
+        if kind == "k":
+            result = keep[i]
+        elif kind == "c":
+            result = moved(give[i], "lon", across_core)
+        elif kind == "y":
+            operand, pairs = ((straight, across_y), (cross, across_both))[i % 2]
+            result = moved(operand[i // 2], ("lon", "lat"), pairs)
+        elif kind == "x":
+            result = moved(get(*PARTS[i]), "lon", across_x)
+        elif kind == "z":
+            result = moved(get("x", i), "lon", across_z)
+        elif kind == "p":
+            operand, pairs = ((keep[1], across_x), (give[1], across_x_core))[i]
+            result = moved(operand, "lon", pairs)
+        elif kind == "q":
+            operand = get(*(("k", 0), ("c", 0), ("p", 0), ("p", 1))[i])
+            result = moved(operand, "lon", back_z if i < 2 else across_z)
+        elif kind == "t":
+            here = [get("k", 0), get("c", 0)]
+            beside = [get("p", 0), get("p", 1)]
+            if i == 0:
+                panels = here + beside + [get("q", 2), get("q", 3)]
+            else:
+                panels = beside + [get("q", 0), get("q", 1)] + here
+            result = filter_pair(rows, signs, windows, [[(p, 0) for p in panels]], 0, lon_dev)
+        elif kind == "b":
+            operand, pairs = ((get("t", 0)[1], across_core), (get("t", 1)[0], across_x), (get("t", 1)[1], across_x_core))[i]
+            result = moved(operand, "lon", pairs)
+        elif kind == "f":
+            places = []
+            for row in FILTERS[i]:
+                chunk, index = next((c, row - at) for c, at in enumerate(starts) if at <= row < at + sizes[c])
+                if chunk < n_stay:
+                    pair = ("k", chunk), ("c", chunk)
+                else:
+                    pair = ("y", 2 * (chunk - n_stay)), ("y", 2 * (chunk - n_stay) + 1)
+                parts = [get(*p) for p in pair]
+                parts += [get(axis, PARTS.index(p)) for axis in "xz" for p in pair]
+                places.append([(p, index) for p in parts])
+            result = filter_pair(rows, signs, windows, places, FILTERS[i][0], lon_dev)
+        else:
+            result = moved(get("f", i)[1], "lon", across_core)
+        done[kind, i] = result
+        return result
+
+    mine = [get("t", 0)[0], get("b", 1)] + [get("f", i)[0] for i in range(len(FILTERS))]
+    theirs = [get("b", 0), get("b", 2)] + [get("o", i) for i in range(len(FILTERS))]
     out = put_rows(mine + theirs, slots, lon_dev, lat_dev)
     return jnp.transpose(out, (1, 0, 2))
 
@@ -364,5 +428,11 @@
 def solution(mesh):
     in_specs = (P("lat", "lon", None), P(), P(), P())
     out_specs = P("lat", "lon", None)
-    body = chip_aware if (mesh.shape["lon"], mesh.shape["lat"]) == (16, 2) else any_mesh
+    chips = (mesh.shape["lon"], mesh.shape["lat"]) == (16, 2)
+
+    def body(fields, owner_slot, widths, tap_weights):
+        fits = chips and fields.shape[0] == 4 * sum(STAY)
+        form = chip_aware if fits else any_mesh
+        return form(fields, owner_slot, widths, tap_weights)
+
     return jax.shard_map(body, mesh=mesh, in_specs=in_specs, out_specs=out_specs, check_vma=False)

time: 119 us -> 114 us (0.958)
  starting transfers between devices: 45.7 us -> 35.6 us
  waiting for transfers between devices: 35.9 us -> 42.5 us
  local copies, waits for them, and re-layouts: 14.6 us -> 13.1 us
    ppermute x26 -> x30, starting transfers between devices: 45.7 us -> 35.6 us  [moved(): return lax.ppermute(operand, axes, pairs)]
    unnamed x46 -> x38, local copies, waits for them, and re-layouts: 12.3 us -> 4.86 us
    ppermute x26 -> x30, waiting for transfers between devices: 35.9 us -> 42.5 us  [moved(): return lax.ppermute(operand, axes, pairs)]
    another operation x7, local copies, waits for them, and re-layouts: 2.13 us -> 6.13 us  [tap_windows(): jnp.stack([jnp.pad(line[:, s * lon_dev:(s + 2) * lon_dev], ((0, 0), (0, l...]
    pallas_call x4 -> x5, Pallas kernels: 14.9 us -> 15 us  [filter_pair(): pl.pallas_call(functools.partial(pair_kernel, lon_dev, base, tuple(plan))...]
  transfers between devices with their start and end apart: 26 -> 30, of which waited for: 13 -> 11; matrix products, arithmetic and copies ran while one was open for 2% -> 8% of each run, Pallas kernels for 13% -> 13%
where the time goes in v5:
time: 114 us
  waiting for transfers between devices  42.5 us (37%)
  starting transfers between devices  35.6 us (31%)
  Pallas kernels  20.9 us (18%)
  local copies, waits for them, and re-layouts  13.1 us (11%)
    ppermute x30, waiting for transfers between devices, moved(): return lax.ppermute(operand, axes, pairs)  42.5 us
    ppermute x30, starting transfers between devices, moved(): return lax.ppermute(operand, axes, pairs)  35.6 us
    pallas_call x5, Pallas kernels, filter_pair(): pl.pallas_call(functools.partial(pair_kernel, lon_dev, base, tuple(plan))...  15 us
    another operation x7, local copies, waits for them, and re-layouts, tap_windows(): jnp.stack([jnp.pad(line[:, s * lon_dev:(s + 2) * lon_dev], ((0, 0), (0, l...  6.13 us
    unnamed x38, local copies, waits for them, and re-layouts  4.86 us
    pallas_call x1, Pallas kernels, take_rows(): pl.pallas_call(functools.partial(take_kernel, chunks, lat_dev, block), ou...  3.11 us
    pallas_call x1, Pallas kernels, put_rows(): pl.pallas_call(functools.partial(put_kernel, counts, lat_dev, block), out...  2.78 us
  transfers between devices with their start and end apart: 30, of which 11 were waited for; matrix products, arithmetic and copies ran while one was open for 8% of the time, Pallas kernels for 13%

profile of v5, /device:TPU:0, one launch (start us, length us, event | category | flops | bytes accessed | tf_op | source)
XLA Modules:
  0.0 113.6 jit_solution(16454961822408097818)
XLA Ops:
  0.0 0.1 pad_add_fusion.place_ref
  0.1 2.0 %copy-done = bf16[16,180,640]{2,0,1:T(8,128)(2,1)S(1)} copy-done((bf16[16,180,640]{2,0,1:T(8,128)(2,1)S(1)}, bf16[16,180,640]{2,0,1:T(8,128)(2,1)}, u32[]{:S(2)}) %copy-start) | copy-done | bytes 3686424
  2.1 0.7 copy-done.1
  2.8 3.1 %take_rows.1 = (bf16[1,184,640]{2,1,0:T(8,128)(2,1)S(1)}, bf16[1,184,640]{2,1,0:T(8,128)(2,1)S(1)}, bf16[2,184,640]{2,1,0:T(8,128)(2,1)S(1)}, bf16[1,184,640]{2,...) custom-call(s32[32]{0:T(128)S(1)} %copy-done.1, ...), custom_call_target="tpu_custom_call" | custom-call | flops 943718400 | bytes 7372800 | tf_op jit(solution)/shard_map/take_rows/pallas_call | solution.py:146
  5.9 0.5 collective-permute-start.8
  6.4 0.1 collective-permute-start
  6.5 2.9 %collective-permute-start.1 = (bf16[1,184,640]{2,1,0:T(8,128)(2,1)S(1)}, bf16[1,184,640]{2,1,0:T(8,128)(2,1)S(1)}, u32[]{:S(2)}, u32[]{:S(2)}) collective-permute-start(bf16[1,184,640]{2,1,0:T(8,128)(2,1)S(1)} %get-tuple-element.45), channel_id=1, source_target_pairs={{0,4},{2,6},{4,0},{6,2},{8,12},{10,14},{12,8},{14,10},{16,20},{18,... | collective-permute-start | bytes 706568 | tf_op jit(solution)/shard_map/ppermute | solution.py:320
  9.4 3.6 %collective-permute-start.6 = (bf16[1,184,640]{2,1,0:T(8,128)(2,1)S(1)}, bf16[1,184,640]{2,1,0:T(8,128)(2,1)S(1)}, u32[]{:S(2)}, u32[]{:S(2)}) collective-permute-start(bf16[1,184,640]{2,1,0:T(8,128)(2,1)S(1)} %get-tuple-element.43.refs_0_.refs_4_), channel_id=1, source_target_pairs={{0,24},{2,26},{4,12},{6,14},{8,0},{10,2},{12,20},{14,22},{16,8},{1... | collective-permute-start | bytes 706568 | tf_op jit(solution)/shard_map/ppermute | solution.py:320
  13.0 0.5 collective-permute-start.4
  13.5 2.4 %collective-permute-done.1.refs_2_.refs_0_ = bf16[1,184,640]{2,1,0:T(8,128)(2,1)S(1)} collective-permute-done((bf16[1,184,640]{2,1,0:T(8,128)(2,1)S(1)}, bf16[1,184,640]{2,1,0:T(8,128)(2,1)S(1)}, u32[]{:S(2)}, u32[]{:S(2)}) %collective-permute-start.1) | collective-permute-done | bytes 235552 | tf_op jit(solution)/shard_map/ppermute | solution.py:320
  15.9 2.1 %collective-permute-start.9 = (bf16[2,184,640]{2,1,0:T(8,128)(2,1)S(1)}, bf16[2,184,640]{2,1,0:T(8,128)(2,1)}, u32[]{:S(2)}, u32[]{:S(2)}) collective-permute-start(bf16[2,184,640]{2,1,0:T(8,128)(2,1)S(1)} %get-tuple-element.50.refs_0_), channel_id=1, source_target_pairs={{0,4},{2,6},{4,0},{6,2},{8,12},{10,14},{12,8},{14,10},{16,20},{18,... | collective-permute-start | bytes 1413128 | tf_op jit(solution)/shard_map/ppermute | solution.py:320
  18.0 2.6 %collective-permute-done.2.refs_3_.refs_1_ = bf16[1,184,640]{2,1,0:T(8,128)(2,1)S(1)} collective-permute-done((bf16[1,184,640]{2,1,0:T(8,128)(2,1)S(1)}, bf16[1,184,640]{2,1,0:T(8,128)(2,1)S(1)}, u32[]{:S(2)}, u32[]{:S(2)}) %collective-permute-start.2) | collective-permute-done | bytes 235552 | tf_op jit(solution)/shard_map/ppermute | solution.py:320
  20.6 1.5 %collective-permute-start.13 = (bf16[2,184,640]{2,1,0:T(8,128)(2,1)S(1)}, bf16[2,184,640]{2,1,0:T(8,128)(2,1)S(1)}, u32[]{:S(2)}, u32[]{:S(2)}) collective-permute-start(bf16[2,184,640]{2,1,0:T(8,128)(2,1)S(1)} %get-tuple-element.56), channel_id=1, source_target_pairs={{0,1},{1,0},{2,3},{3,2},{4,5},{5,4},{6,7},{7,6},{8,9},{9,8},{10,11... | collective-permute-start | bytes 1413128 | tf_op jit(solution)/shard_map/ppermute | solution.py:320
  22.1 0.0 collective-permute-done.6.refs_2_
  22.1 0.7 copy-done.12
  22.8 0.8 collective-permute-start.14
  23.6 1.8 %collective-permute-start.3 = (bf16[1,184,640]{2,1,0:T(8,128)(2,1)S(1)}, bf16[1,184,640]{2,1,0:T(8,128)(2,1)S(1)}, u32[]{:S(2)}, u32[]{:S(2)}) collective-permute-start(bf16[1,184,640]{2,1,0:T(8,128)(2,1)S(1)} %collective-permute-done.1.refs_2_.refs_0_), channel_id=1, source_target_pairs={{0,8},{2,10},{4,28},{6,30},{8,16},{10,18},{12,4},{14,6},{16,24},{1... | collective-permute-start | bytes 706568 | tf_op jit(solution)/shard_map/ppermute | solution.py:320
  25.3 0.7 copy-done.14
  26.0 3.5 %collective-permute-start.10 = (bf16[2,184,640]{2,1,0:T(8,128)(2,1)S(1)}, bf16[2,184,640]{2,1,0:T(8,128)(2,1)}, u32[]{:S(2)}, u32[]{:S(2)}) collective-permute-start(bf16[2,184,640]{2,1,0:T(8,128)(2,1)S(1)} %collective-permute-done.8.refs_1_), channel_id=1, source_target_pairs={{0,4},{2,6},{4,0},{6,2},{8,12},{10,14},{12,8},{14,10},{16,20},{18,... | collective-permute-start | bytes 1413128 | tf_op jit(solution)/shard_map/ppermute | solution.py:320
  29.5 0.1 convert_select_fusion
  29.7 3.5 %collective-permute-done.3.refs_4_ = bf16[1,184,640]{2,1,0:T(8,128)(2,1)S(1)} collective-permute-done((bf16[1,184,640]{2,1,0:T(8,128)(2,1)S(1)}, bf16[1,184,640]{2,1,0:T(8,128)(2,1)S(1)}, u32[]{:S(2)}, u32[]{:S(2)}) %collective-permute-start.3) | collective-permute-done | bytes 235552 | tf_op jit(solution)/shard_map/ppermute | solution.py:320
  33.1 0.7 fusion.2
  33.8 0.6 fusion.3
  34.5 1.3 %collective-permute-start.11 = (bf16[2,184,640]{2,1,0:T(8,128)(2,1)}, bf16[2,184,640]{2,1,0:T(8,128)(2,1)}, u32[]{:S(2)}, u32[]{:S(2)}) collective-permute-start(bf16[2,184,640]{2,1,0:T(8,128)(2,1)} %collective-permute-done.9.refs_2_), channel_id=1, source_target_pairs={{0,8},{2,10},{4,28},{6,30},{8,16},{10,18},{12,4},{14,6},{16,24},{1... | collective-permute-start | bytes 1413128 | tf_op jit(solution)/shard_map/ppermute | solution.py:320
  35.8 3.8 %collective-permute-start.15 = (bf16[2,184,640]{2,1,0:T(8,128)(2,1)S(1)}, bf16[2,184,640]{2,1,0:T(8,128)(2,1)}, u32[]{:S(2)}, u32[]{:S(2)}) collective-permute-start(bf16[2,184,640]{2,1,0:T(8,128)(2,1)S(1)} %collective-permute-done.13.refs_0_), channel_id=1, source_target_pairs={{0,4},{2,6},{4,0},{6,2},{8,12},{10,14},{12,8},{14,10},{16,20},{18,... | collective-permute-start | bytes 1413128 | tf_op jit(solution)/shard_map/ppermute | solution.py:320
  39.6 4.0 %collective-permute-done.5.refs_5_ = bf16[1,184,640]{2,1,0:T(8,128)(2,1)S(1)} collective-permute-done((bf16[1,184,640]{2,1,0:T(8,128)(2,1)S(1)}, bf16[1,184,640]{2,1,0:T(8,128)(2,1)S(1)}, u32[]{:S(2)}, u32[]{:S(2)}) %collective-permute-start.5) | collective-permute-done | bytes 235552 | tf_op jit(solution)/shard_map/ppermute | solution.py:320
  43.6 0.7 copy-done.10
  44.3 1.3 %collective-permute-start.19 = (bf16[2,184,640]{2,1,0:T(8,128)(2,1)S(1)}, bf16[2,184,640]{2,1,0:T(8,128)(2,1)}, u32[]{:S(2)}, u32[]{:S(2)}) collective-permute-start(bf16[2,184,640]{2,1,0:T(8,128)(2,1)S(1)} %get-tuple-element.64), channel_id=1, source_target_pairs={{0,1},{1,0},{2,3},{3,2},{4,5},{5,4},{6,7},{7,6},{8,9},{9,8},{10,11... | collective-permute-start | bytes 1413128 | tf_op jit(solution)/shard_map/ppermute | solution.py:320
  45.6 4.3 %collective-permute-start.16 = (bf16[2,184,640]{2,1,0:T(8,128)(2,1)S(1)}, bf16[2,184,640]{2,1,0:T(8,128)(2,1)}, u32[]{:S(2)}, u32[]{:S(2)}) collective-permute-start(bf16[2,184,640]{2,1,0:T(8,128)(2,1)S(1)} %collective-permute-done.14.refs_1_), channel_id=1, source_target_pairs={{0,4},{2,6},{4,0},{6,2},{8,12},{10,14},{12,8},{14,10},{16,20},{18,... | collective-permute-start | bytes 1413128 | tf_op jit(solution)/shard_map/ppermute | solution.py:320
  49.9 0.7 pad_bitcast_fusion
  50.6 1.5 %copy.5 = f32[32,1,384]{2,1,0:T(1,128)} copy(f32[32,1,384]{2,0,1:T(8,128)} %get-tuple-element.83) | data formatting | bytes 98304 | tf_op jit(solution)/shard_map/stack | solution.py:58
  52.0 1.5 %copy.6 = f32[32,1,384]{2,1,0:T(1,128)} copy(f32[32,1,384]{2,0,1:T(8,128)} %get-tuple-element.82) | data formatting | bytes 98304 | tf_op jit(solution)/shard_map/stack | solution.py:58
  53.5 0.8 fusion.1
  54.4 0.1 copy.7
  54.4 0.7 copy.8
  55.1 0.8 pad.20
  55.9 0.6 stack.50
  56.6 1.2 %stack.51.win_ref = f32[32,5,384]{2,1,0:T(8,128)S(1)} concatenate(f32[32,1,384]{2,1,0:T(1,128)} %copy.5, f32[32,1,384]{2,1,0:T(1,128)} %copy.6, f32[32,1,384]{2,1,0:T(1,128)S(1)} %copy.7, f32[32,1,384]{2,1,0:T(1,128)} %copy.8, f32[32,1,384]{2,1,0:T(1,128)} %stack.50), dimensions={1} | concatenate | bytes 491520 | tf_op jit(solution)/shard_map/stack | solution.py:58
  57.7 0.1 pad_add_fusion.1.sign_ref
  57.8 0.0 collective-permute-start.20
  57.9 0.1 collective-permute-start.17
  57.9 1.6 %collective-permute-start.21 = (bf16[2,184,640]{2,1,0:T(8,128)(2,1)}, bf16[2,184,640]{2,1,0:T(8,128)(2,1)S(1)}, u32[]{:S(2)}, u32[]{:S(2)}) collective-permute-start(bf16[2,184,640]{2,1,0:T(8,128)(2,1)} %collective-permute-done.19.refs_0_), channel_id=1, source_target_pairs={{0,4},{2,6},{4,0},{6,2},{8,12},{10,14},{12,8},{14,10},{16,20},{18,... | collective-permute-start | bytes 1413128 | tf_op jit(solution)/shard_map/ppermute | solution.py:320
  59.5 2.7 %collective-permute-done.12.refs_5_ = bf16[2,184,640]{2,1,0:T(8,128)(2,1)} collective-permute-done((bf16[2,184,640]{2,1,0:T(8,128)(2,1)}, bf16[2,184,640]{2,1,0:T(8,128)(2,1)}, u32[]{:S(2)}, u32[]{:S(2)}) %collective-permute-start.12) | collective-permute-done | bytes 471072 | tf_op jit(solution)/shard_map/ppermute | solution.py:320
  62.2 0.9 collective-permute-start.18
  63.1 4.0 %filter_pair.7 = (bf16[2,184,640]{2,1,0:T(8,128)(2,1)S(1)}, bf16[2,184,640]{2,1,0:T(8,128)(2,1)S(1)}) custom-call(s32[16]{0:T(128)S(1)} %get-tuple-element.42.rows_ref, s32[2]{0:T(128)S(1)} %pad_add_fusion.1.sign_ref, f32[32,5,384]{2,1,0:T(8,128)S(1)} %stack.51.win_ref, bf16[2,184,640]{2,1,0:T(8,128)(2,1)S(1)} %get-tuple-element.50.refs_0_, ...), custom_call_target="tpu_custom_call" | custom-call | flops 6039797760 | bytes 3768320 | tf_op jit(solution)/shard_map/filter_pair/pallas_call | solution.py:266
  67.1 3.8 %collective-permute-done.20.refs_1_ = bf16[2,184,640]{2,1,0:T(8,128)(2,1)S(1)} collective-permute-done((bf16[2,184,640]{2,1,0:T(8,128)(2,1)S(1)}, bf16[2,184,640]{2,1,0:T(8,128)(2,1)S(1)}, u32[]{:S(2)}, u32[]{:S(2)}) %collective-permute-start.20) | collective-permute-done | bytes 471072 | tf_op jit(solution)/shard_map/ppermute | solution.py:320
  70.9 2.1 %collective-permute-start.22 = (bf16[2,184,640]{2,1,0:T(8,128)(2,1)S(1)}, bf16[2,184,640]{2,1,0:T(8,128)(2,1)S(1)}, u32[]{:S(2)}, u32[]{:S(2)}) collective-permute-start(bf16[2,184,640]{2,1,0:T(8,128)(2,1)S(1)} %collective-permute-done.20.refs_1_), channel_id=1, source_target_pairs={{0,4},{2,6},{4,0},{6,2},{8,12},{10,14},{12,8},{14,10},{16,20},{18,... | collective-permute-start | bytes 1413128 | tf_op jit(solution)/shard_map/ppermute | solution.py:320
  73.0 1.8 %filter_pair.6 = (bf16[1,184,640]{2,1,0:T(8,128)(2,1)S(1)}, bf16[1,184,640]{2,1,0:T(8,128)(2,1)S(1)}) custom-call(s32[16]{0:T(128)S(1)} %get-tuple-element.42.rows_ref, s32[2]{0:T(128)S(1)} %pad_add_fusion.1.sign_ref, f32[32,5,384]{2,1,0:T(8,128)S(1)} %stack.51.win_ref, bf16[1,184,640]{2,1,0:T(8,128)(2,1)S(1)} %copy-done.5, ...), custom_call_target="tpu_custom_call" | custom-call | flops 3019898880 | bytes 1884160 | tf_op jit(solution)/shard_map/filter_pair/pallas_call | solution.py:266
  74.8 0.1 collective-permute-start.7
  74.9 0.1 collective-permute-start.26
  75.0 0.1 collective-permute-start.23
  75.0 8.1 %collective-permute-done.18.refs_5_ = bf16[2,184,640]{2,1,0:T(8,128)(2,1)S(1)} collective-permute-done((bf16[2,184,640]{2,1,0:T(8,128)(2,1)}, bf16[2,184,640]{2,1,0:T(8,128)(2,1)S(1)}, u32[]{:S(2)}, u32[]{:S(2)}) %collective-permute-start.18) | collective-permute-done | bytes 471072 | tf_op jit(solution)/shard_map/ppermute | solution.py:320
  83.2 1.1 collective-permute-start.27
  84.3 0.3 collective-permute-done.22.refs_3_
  84.6 3.8 %filter_pair.8 = (bf16[2,184,640]{2,1,0:T(8,128)(2,1)S(1)}, bf16[2,184,640]{2,1,0:T(8,128)(2,1)S(1)}) custom-call(s32[16]{0:T(128)S(1)} %get-tuple-element.42.rows_ref, s32[2]{0:T(128)S(1)} %pad_add_fusion.1.sign_ref, f32[32,5,384]{2,1,0:T(8,128)S(1)} %stack.51.win_ref, bf16[2,184,640]{2,1,0:T(8,128)(2,1)S(1)} %collective-permute-done.13.refs_0_, ...), custom_call_target="tpu_custom_call" | custom-call | flops 6039797760 | bytes 3768320 | tf_op jit(solution)/shard_map/filter_pair/pallas_call | solution.py:266
  88.4 4.8 %collective-permute-done.23.refs_4_ = bf16[2,184,640]{2,1,0:T(8,128)(2,1)S(1)} collective-permute-done((bf16[2,184,640]{2,1,0:T(8,128)(2,1)S(1)}, bf16[2,184,640]{2,1,0:T(8,128)(2,1)S(1)}, u32[]{:S(2)}, u32[]{:S(2)}) %collective-permute-start.23) | collective-permute-done | bytes 471072 | tf_op jit(solution)/shard_map/ppermute | solution.py:320
  93.3 1.1 collective-permute-start.28
  94.4 9.0 %collective-permute-done.24.refs_5_ = bf16[2,184,640]{2,1,0:T(8,128)(2,1)S(1)} collective-permute-done((bf16[2,184,640]{2,1,0:T(8,128)(2,1)S(1)}, bf16[2,184,640]{2,1,0:T(8,128)(2,1)S(1)}, u32[]{:S(2)}, u32[]{:S(2)}) %collective-permute-start.24) | collective-permute-done | bytes 471072 | tf_op jit(solution)/shard_map/ppermute | solution.py:320
  103.4 3.5 %filter_pair.9 = (bf16[2,184,640]{2,1,0:T(8,128)(2,1)S(1)}, bf16[2,184,640]{2,1,0:T(8,128)(2,1)S(1)}) custom-call(s32[16]{0:T(128)S(1)} %get-tuple-element.42.rows_ref, s32[2]{0:T(128)S(1)} %pad_add_fusion.1.sign_ref, f32[32,5,384]{2,1,0:T(8,128)S(1)} %stack.51.win_ref, bf16[2,184,640]{2,1,0:T(8,128)(2,1)} %collective-permute-done.19.refs_0_, ...), custom_call_target="tpu_custom_call" | custom-call | flops 6039797760 | bytes 3768320 | tf_op jit(solution)/shard_map/filter_pair/pallas_call | solution.py:266
  106.9 0.4 collective-permute-start.29
  107.3 1.8 %filter_pair.5 = (bf16[1,184,640]{2,1,0:T(8,128)(2,1)S(1)}, bf16[1,184,640]{2,1,0:T(8,128)(2,1)S(1)}) custom-call(s32[16]{0:T(128)S(1)} %get-tuple-element.42.rows_ref, s32[2]{0:T(128)S(1)} %pad_add_fusion.1.sign_ref, f32[32,5,384]{2,1,0:T(8,128)S(1)} %stack.51.win_ref, bf16[1,184,640]{2,1,0:T(8,128)(2,1)S(1)} %get-tuple-element.43.refs_0_.refs_4_, ...), custom_call_target="tpu_custom_call" | custom-call | flops 3019898880 | bytes 1884160 | tf_op jit(solution)/shard_map/filter_pair/pallas_call | solution.py:266
  109.1 0.2 collective-permute-start.25
  109.3 1.3 %collective-permute-done.25.refs_5_ = bf16[1,184,640]{2,1,0:T(8,128)(2,1)S(1)} collective-permute-done((bf16[1,184,640]{2,1,0:T(8,128)(2,1)S(1)}, bf16[1,184,640]{2,1,0:T(8,128)(2,1)S(1)}, u32[]{:S(2)}, u32[]{:S(2)}) %collective-permute-start.25) | collective-permute-done | bytes 235552 | tf_op jit(solution)/shard_map/ppermute | solution.py:320
  110.7 2.8 %put_rows.1 = bf16[180,16,640]{2,1,0:T(8,128)(2,1)} custom-call(s32[16]{0:T(128)S(1)} %get-tuple-element.41.slots_ref, bf16[1,184,640]{2,1,0:T(8,128)(2,1)S(1)} %get-tuple-element.48.refs_0_, bf16[1,184,640]{2,1,0:T(8,128)(2,1)S(1)} %collective-permute-done.7.refs_1_, bf16[2,184,640]{2,1,0:T(8,128)(2,1)S(1)} %get-tuple-element.55.refs_2_, ...), custom_call_target="tpu_custom_call" | custom-call | flops 943718400 | bytes 7372800 | tf_op jit(solution)/shard_map/put_rows/pallas_call | solution.py:198
  (57 shorter events, 0.1 us)
Async XLA Ops:
  0.0 54.4 %copy-start.17 = (pred[384]{0:T(512)(128)(4,1)S(1)}, pred[384]{0:T(512)(128)(4,1)}, u32[]{:S(2)}) copy-start(pred[384]{0:T(512)(128)(4,1)} %constant.44.clone.1) | copy-start | bytes 1156
  0.0 29.5 %copy-start.18 = (s32[32]{0:T(128)S(1)}, s32[32]{0:T(128)}, u32[]{:S(2)}) copy-start(s32[32]{0:T(128)} %param.6) | copy-start | bytes 388
  0.1 2.0 %copy-start = (bf16[16,180,640]{2,0,1:T(8,128)(2,1)S(1)}, bf16[16,180,640]{2,0,1:T(8,128)(2,1)}, u32[]{:S(2)}) copy-start(bf16[16,180,640]{2,0,1:T(8,128)(2,1)} %param.4) | copy-start | bytes 11059204
  2.1 0.7 copy-start.1
  2.8 26.8 %copy-start.16 = (bf16[32,2880]{1,0:T(8,128)(2,1)S(1)}, bf16[32,2880]{1,0:T(8,128)(2,1)}, u32[]{:S(2)}) copy-start(bf16[32,2880]{1,0:T(8,128)(2,1)} %param.7) | copy-start | bytes 552964
  5.9 17.7 %collective-permute-start.8 = (bf16[2,184,640]{2,1,0:T(8,128)(2,1)S(1)}, bf16[2,184,640]{2,1,0:T(8,128)(2,1)S(1)}, u32[]{:S(2)}, u32[]{:S(2)}) collective-permute-start(bf16[2,184,640]{2,1,0:T(8,128)(2,1)S(1)} %get-tuple-element.51), channel_id=1, source_target_pairs={{0,2},{2,0},{4,6},{6,4},{8,10},{10,8},{12,14},{14,12},{16,18},{18,... | collective-permute-start | bytes 1413128 | tf_op jit(solution)/shard_map/ppermute | solution.py:320
  6.4 6.6 %collective-permute-start = (bf16[1,184,640]{2,1,0:T(8,128)(2,1)S(1)}, bf16[1,184,640]{2,1,0:T(8,128)(2,1)S(1)}, u32[]{:S(2)}, u32[]{:S(2)}) collective-permute-start(bf16[1,184,640]{2,1,0:T(8,128)(2,1)S(1)} %get-tuple-element.44), channel_id=1, source_target_pairs={{0,2},{2,0},{4,6},{6,4},{8,10},{10,8},{12,14},{14,12},{16,18},{18,... | collective-permute-start | bytes 706568 | tf_op jit(solution)/shard_map/ppermute | solution.py:320
  6.5 9.4 %collective-permute-start.1 = (bf16[1,184,640]{2,1,0:T(8,128)(2,1)S(1)}, bf16[1,184,640]{2,1,0:T(8,128)(2,1)S(1)}, u32[]{:S(2)}, u32[]{:S(2)}) collective-permute-start(bf16[1,184,640]{2,1,0:T(8,128)(2,1)S(1)} %get-tuple-element.45), channel_id=1, source_target_pairs={{0,4},{2,6},{4,0},{6,2},{8,12},{10,14},{12,8},{14,10},{16,20},{18,... | collective-permute-start | bytes 706568 | tf_op jit(solution)/shard_map/ppermute | solution.py:320
  9.4 11.2 %collective-permute-start.2 = (bf16[1,184,640]{2,1,0:T(8,128)(2,1)S(1)}, bf16[1,184,640]{2,1,0:T(8,128)(2,1)S(1)}, u32[]{:S(2)}, u32[]{:S(2)}) collective-permute-start(bf16[1,184,640]{2,1,0:T(8,128)(2,1)S(1)} %get-tuple-element.46), channel_id=1, source_target_pairs={{0,6},{2,4},{4,2},{6,0},{8,14},{10,12},{12,10},{14,8},{16,22},{18,... | collective-permute-start | bytes 706568 | tf_op jit(solution)/shard_map/ppermute | solution.py:320
  9.4 12.7 %collective-permute-start.6 = (bf16[1,184,640]{2,1,0:T(8,128)(2,1)S(1)}, bf16[1,184,640]{2,1,0:T(8,128)(2,1)S(1)}, u32[]{:S(2)}, u32[]{:S(2)}) collective-permute-start(bf16[1,184,640]{2,1,0:T(8,128)(2,1)S(1)} %get-tuple-element.43.refs_0_.refs_4_), channel_id=1, source_target_pairs={{0,24},{2,26},{4,12},{6,14},{8,0},{10,2},{12,20},{14,22},{16,8},{1... | collective-permute-start | bytes 706568 | tf_op jit(solution)/shard_map/ppermute | solution.py:320
  13.0 32.6 %copy-start.2 = (bf16[1,184,640]{2,1,0:T(8,128)(2,1)}, bf16[1,184,640]{2,1,0:T(8,128)(2,1)S(1)}, u32[]{:S(2)}) copy-start(bf16[1,184,640]{2,1,0:T(8,128)(2,1)S(1)} %collective-permute-done.refs_1_.refs_5_) | copy-start | bytes 706564
  13.0 12.3 %collective-permute-start.4 = (bf16[1,184,640]{2,1,0:T(8,128)(2,1)S(1)}, bf16[1,184,640]{2,1,0:T(8,128)(2,1)S(1)}, u32[]{:S(2)}, u32[]{:S(2)}) collective-permute-start(bf16[1,184,640]{2,1,0:T(8,128)(2,1)S(1)} %collective-permute-done.refs_1_.refs_5_), channel_id=1, source_target_pairs={{0,24},{2,26},{4,12},{6,14},{8,0},{10,2},{12,20},{14,22},{16,8},{1... | collective-permute-start | bytes 706568 | tf_op jit(solution)/shard_map/ppermute | solution.py:320
  15.9 34.0 %copy-start.4 = (bf16[1,184,640]{2,1,0:T(8,128)(2,1)}, bf16[1,184,640]{2,1,0:T(8,128)(2,1)S(1)}, u32[]{:S(2)}) copy-start(bf16[1,184,640]{2,1,0:T(8,128)(2,1)S(1)} %collective-permute-done.1.refs_2_.refs_0_) | copy-start | bytes 706564
  15.9 18.5 %collective-permute-start.9 = (bf16[2,184,640]{2,1,0:T(8,128)(2,1)S(1)}, bf16[2,184,640]{2,1,0:T(8,128)(2,1)}, u32[]{:S(2)}, u32[]{:S(2)}) collective-permute-start(bf16[2,184,640]{2,1,0:T(8,128)(2,1)S(1)} %get-tuple-element.50.refs_0_), channel_id=1, source_target_pairs={{0,4},{2,6},{4,0},{6,2},{8,12},{10,14},{12,8},{14,10},{16,20},{18,... | collective-permute-start | bytes 1413128 | tf_op jit(solution)/shard_map/ppermute | solution.py:320
  20.6 29.3 %copy-start.6 = (bf16[1,184,640]{2,1,0:T(8,128)(2,1)}, bf16[1,184,640]{2,1,0:T(8,128)(2,1)S(1)}, u32[]{:S(2)}) copy-start(bf16[1,184,640]{2,1,0:T(8,128)(2,1)S(1)} %collective-permute-done.2.refs_3_.refs_1_) | copy-start | bytes 706564
  20.6 15.2 %collective-permute-start.13 = (bf16[2,184,640]{2,1,0:T(8,128)(2,1)S(1)}, bf16[2,184,640]{2,1,0:T(8,128)(2,1)S(1)}, u32[]{:S(2)}, u32[]{:S(2)}) collective-permute-start(bf16[2,184,640]{2,1,0:T(8,128)(2,1)S(1)} %get-tuple-element.56), channel_id=1, source_target_pairs={{0,1},{1,0},{2,3},{3,2},{4,5},{5,4},{6,7},{7,6},{8,9},{9,8},{10,11... | collective-permute-start | bytes 1413128 | tf_op jit(solution)/shard_map/ppermute | solution.py:320
  22.1 0.7 copy-start.12
  22.8 22.8 %collective-permute-start.14 = (bf16[2,184,640]{2,1,0:T(8,128)(2,1)S(1)}, bf16[2,184,640]{2,1,0:T(8,128)(2,1)S(1)}, u32[]{:S(2)}, u32[]{:S(2)}) collective-permute-start(bf16[2,184,640]{2,1,0:T(8,128)(2,1)S(1)} %get-tuple-element.57), channel_id=1, source_target_pairs={{0,3},{1,2},{2,1},{3,0},{4,7},{5,6},{6,5},{7,4},{8,11},{9,10},{10,... | collective-permute-start | bytes 1413128 | tf_op jit(solution)/shard_map/ppermute | solution.py:320
  23.6 9.6 %collective-permute-start.3 = (bf16[1,184,640]{2,1,0:T(8,128)(2,1)S(1)}, bf16[1,184,640]{2,1,0:T(8,128)(2,1)S(1)}, u32[]{:S(2)}, u32[]{:S(2)}) collective-permute-start(bf16[1,184,640]{2,1,0:T(8,128)(2,1)S(1)} %collective-permute-done.1.refs_2_.refs_0_), channel_id=1, source_target_pairs={{0,8},{2,10},{4,28},{6,30},{8,16},{10,18},{12,4},{14,6},{16,24},{1... | collective-permute-start | bytes 706568 | tf_op jit(solution)/shard_map/ppermute | solution.py:320
  25.3 0.7 copy-start.14
  26.0 19.6 %collective-permute-start.10 = (bf16[2,184,640]{2,1,0:T(8,128)(2,1)S(1)}, bf16[2,184,640]{2,1,0:T(8,128)(2,1)}, u32[]{:S(2)}, u32[]{:S(2)}) collective-permute-start(bf16[2,184,640]{2,1,0:T(8,128)(2,1)S(1)} %collective-permute-done.8.refs_1_), channel_id=1, source_target_pairs={{0,4},{2,6},{4,0},{6,2},{8,12},{10,14},{12,8},{14,10},{16,20},{18,... | collective-permute-start | bytes 1413128 | tf_op jit(solution)/shard_map/ppermute | solution.py:320
  33.1 16.8 %copy-start.8 = (bf16[1,184,640]{2,1,0:T(8,128)(2,1)}, bf16[1,184,640]{2,1,0:T(8,128)(2,1)S(1)}, u32[]{:S(2)}) copy-start(bf16[1,184,640]{2,1,0:T(8,128)(2,1)S(1)} %collective-permute-done.3.refs_4_) | copy-start | bytes 706564
  33.1 10.5 %collective-permute-start.5 = (bf16[1,184,640]{2,1,0:T(8,128)(2,1)S(1)}, bf16[1,184,640]{2,1,0:T(8,128)(2,1)S(1)}, u32[]{:S(2)}, u32[]{:S(2)}) collective-permute-start(bf16[1,184,640]{2,1,0:T(8,128)(2,1)S(1)} %collective-permute-done.2.refs_3_.refs_1_), channel_id=1, source_target_pairs={{0,8},{2,10},{4,28},{6,30},{8,16},{10,18},{12,4},{14,6},{16,24},{1... | collective-permute-start | bytes 706568 | tf_op jit(solution)/shard_map/ppermute | solution.py:320
  34.5 23.3 %collective-permute-start.11 = (bf16[2,184,640]{2,1,0:T(8,128)(2,1)}, bf16[2,184,640]{2,1,0:T(8,128)(2,1)}, u32[]{:S(2)}, u32[]{:S(2)}) collective-permute-start(bf16[2,184,640]{2,1,0:T(8,128)(2,1)} %collective-permute-done.9.refs_2_), channel_id=1, source_target_pairs={{0,8},{2,10},{4,28},{6,30},{8,16},{10,18},{12,4},{14,6},{16,24},{1... | collective-permute-start | bytes 1413128 | tf_op jit(solution)/shard_map/ppermute | solution.py:320
  35.8 22.1 %collective-permute-start.15 = (bf16[2,184,640]{2,1,0:T(8,128)(2,1)S(1)}, bf16[2,184,640]{2,1,0:T(8,128)(2,1)}, u32[]{:S(2)}, u32[]{:S(2)}) collective-permute-start(bf16[2,184,640]{2,1,0:T(8,128)(2,1)S(1)} %collective-permute-done.13.refs_0_), channel_id=1, source_target_pairs={{0,4},{2,6},{4,0},{6,2},{8,12},{10,14},{12,8},{14,10},{16,20},{18,... | collective-permute-start | bytes 1413128 | tf_op jit(solution)/shard_map/ppermute | solution.py:320
  43.6 0.7 copy-start.10
  44.3 13.6 %collective-permute-start.19 = (bf16[2,184,640]{2,1,0:T(8,128)(2,1)S(1)}, bf16[2,184,640]{2,1,0:T(8,128)(2,1)}, u32[]{:S(2)}, u32[]{:S(2)}) collective-permute-start(bf16[2,184,640]{2,1,0:T(8,128)(2,1)S(1)} %get-tuple-element.64), channel_id=1, source_target_pairs={{0,1},{1,0},{2,3},{3,2},{4,5},{5,4},{6,7},{7,6},{8,9},{9,8},{10,11... | collective-permute-start | bytes 1413128 | tf_op jit(solution)/shard_map/ppermute | solution.py:320
  45.6 16.5 %collective-permute-start.12 = (bf16[2,184,640]{2,1,0:T(8,128)(2,1)}, bf16[2,184,640]{2,1,0:T(8,128)(2,1)}, u32[]{:S(2)}, u32[]{:S(2)}) collective-permute-start(bf16[2,184,640]{2,1,0:T(8,128)(2,1)} %collective-permute-done.10.refs_3_), channel_id=1, source_target_pairs={{0,8},{2,10},{4,28},{6,30},{8,16},{10,18},{12,4},{14,6},{16,24},{1... | collective-permute-start | bytes 1413128 | tf_op jit(solution)/shard_map/ppermute | solution.py:320
  45.6 16.5 %collective-permute-start.16 = (bf16[2,184,640]{2,1,0:T(8,128)(2,1)S(1)}, bf16[2,184,640]{2,1,0:T(8,128)(2,1)}, u32[]{:S(2)}, u32[]{:S(2)}) collective-permute-start(bf16[2,184,640]{2,1,0:T(8,128)(2,1)S(1)} %collective-permute-done.14.refs_1_), channel_id=1, source_target_pairs={{0,4},{2,6},{4,0},{6,2},{8,12},{10,14},{12,8},{14,10},{16,20},{18,... | collective-permute-start | bytes 1413128 | tf_op jit(solution)/shard_map/ppermute | solution.py:320
  57.8 13.0 %collective-permute-start.20 = (bf16[2,184,640]{2,1,0:T(8,128)(2,1)S(1)}, bf16[2,184,640]{2,1,0:T(8,128)(2,1)S(1)}, u32[]{:S(2)}, u32[]{:S(2)}) collective-permute-start(bf16[2,184,640]{2,1,0:T(8,128)(2,1)S(1)} %get-tuple-element.66), channel_id=1, source_target_pairs={{0,3},{1,2},{2,1},{3,0},{4,7},{5,6},{6,5},{7,4},{8,11},{9,10},{10,... | collective-permute-start | bytes 1413128 | tf_op jit(solution)/shard_map/ppermute | solution.py:320
  57.9 17.0 %collective-permute-start.17 = (bf16[2,184,640]{2,1,0:T(8,128)(2,1)}, bf16[2,184,640]{2,1,0:T(8,128)(2,1)S(1)}, u32[]{:S(2)}, u32[]{:S(2)}) collective-permute-start(bf16[2,184,640]{2,1,0:T(8,128)(2,1)} %collective-permute-done.15.refs_2_), channel_id=1, source_target_pairs={{0,8},{2,10},{4,28},{6,30},{8,16},{10,18},{12,4},{14,6},{16,24},{1... | collective-permute-start | bytes 1413128 | tf_op jit(solution)/shard_map/ppermute | solution.py:320
  57.9 17.0 %collective-permute-start.21 = (bf16[2,184,640]{2,1,0:T(8,128)(2,1)}, bf16[2,184,640]{2,1,0:T(8,128)(2,1)S(1)}, u32[]{:S(2)}, u32[]{:S(2)}) collective-permute-start(bf16[2,184,640]{2,1,0:T(8,128)(2,1)} %collective-permute-done.19.refs_0_), channel_id=1, source_target_pairs={{0,4},{2,6},{4,0},{6,2},{8,12},{10,14},{12,8},{14,10},{16,20},{18,... | collective-permute-start | bytes 1413128 | tf_op jit(solution)/shard_map/ppermute | solution.py:320
  62.2 21.0 %collective-permute-start.18 = (bf16[2,184,640]{2,1,0:T(8,128)(2,1)}, bf16[2,184,640]{2,1,0:T(8,128)(2,1)S(1)}, u32[]{:S(2)}, u32[]{:S(2)}) collective-permute-start(bf16[2,184,640]{2,1,0:T(8,128)(2,1)} %collective-permute-done.16.refs_3_), channel_id=1, source_target_pairs={{0,8},{2,10},{4,28},{6,30},{8,16},{10,18},{12,4},{14,6},{16,24},{1... | collective-permute-start | bytes 1413128 | tf_op jit(solution)/shard_map/ppermute | solution.py:320
  63.0 9.9 %copy-start.3 = (bf16[1,184,640]{2,1,0:T(8,128)(2,1)S(1)}, bf16[1,184,640]{2,1,0:T(8,128)(2,1)}, u32[]{:S(2)}) copy-start(bf16[1,184,640]{2,1,0:T(8,128)(2,1)} %copy-done.2) | copy-start | bytes 706564
  63.0 9.9 %copy-start.5 = (bf16[1,184,640]{2,1,0:T(8,128)(2,1)S(1)}, bf16[1,184,640]{2,1,0:T(8,128)(2,1)}, u32[]{:S(2)}) copy-start(bf16[1,184,640]{2,1,0:T(8,128)(2,1)} %copy-done.4) | copy-start | bytes 706564
  63.0 9.9 %copy-start.7 = (bf16[1,184,640]{2,1,0:T(8,128)(2,1)S(1)}, bf16[1,184,640]{2,1,0:T(8,128)(2,1)}, u32[]{:S(2)}) copy-start(bf16[1,184,640]{2,1,0:T(8,128)(2,1)} %copy-done.6) | copy-start | bytes 706564
  63.0 9.9 %copy-start.13 = (bf16[1,184,640]{2,1,0:T(8,128)(2,1)S(1)}, bf16[1,184,640]{2,1,0:T(8,128)(2,1)}, u32[]{:S(2)}) copy-start(bf16[1,184,640]{2,1,0:T(8,128)(2,1)} %copy-done.12) | copy-start | bytes 706564
  63.0 9.9 %copy-start.15 = (bf16[1,184,640]{2,1,0:T(8,128)(2,1)S(1)}, bf16[1,184,640]{2,1,0:T(8,128)(2,1)}, u32[]{:S(2)}) copy-start(bf16[1,184,640]{2,1,0:T(8,128)(2,1)} %copy-done.14) | copy-start | bytes 706564
  70.9 13.7 %collective-permute-start.22 = (bf16[2,184,640]{2,1,0:T(8,128)(2,1)S(1)}, bf16[2,184,640]{2,1,0:T(8,128)(2,1)S(1)}, u32[]{:S(2)}, u32[]{:S(2)}) collective-permute-start(bf16[2,184,640]{2,1,0:T(8,128)(2,1)S(1)} %collective-permute-done.20.refs_1_), channel_id=1, source_target_pairs={{0,4},{2,6},{4,0},{6,2},{8,12},{10,14},{12,8},{14,10},{16,20},{18,... | collective-permute-start | bytes 1413128 | tf_op jit(solution)/shard_map/ppermute | solution.py:320
  74.8 34.3 %collective-permute-start.7 = (bf16[1,184,640]{2,1,0:T(8,128)(2,1)S(1)}, bf16[1,184,640]{2,1,0:T(8,128)(2,1)S(1)}, u32[]{:S(2)}, u32[]{:S(2)}) collective-permute-start(bf16[1,184,640]{2,1,0:T(8,128)(2,1)S(1)} %get-tuple-element.49), channel_id=1, source_target_pairs={{0,4},{2,6},{4,0},{6,2},{8,12},{10,14},{12,8},{14,10},{16,20},{18,... | collective-permute-start | bytes 706568 | tf_op jit(solution)/shard_map/ppermute | solution.py:320
  74.9 34.4 %collective-permute-start.26 = (bf16[1,184,640]{2,1,0:T(8,128)(2,1)S(1)}, bf16[1,184,640]{2,1,0:T(8,128)(2,1)S(1)}, u32[]{:S(2)}, u32[]{:S(2)}) collective-permute-start(bf16[1,184,640]{2,1,0:T(8,128)(2,1)S(1)} %get-tuple-element.73), channel_id=1, source_target_pairs={{0,6},{2,4},{4,2},{6,0},{8,14},{10,12},{12,10},{14,8},{16,22},{18,... | collective-permute-start | bytes 706568 | tf_op jit(solution)/shard_map/ppermute | solution.py:320
  75.0 18.3 %collective-permute-start.23 = (bf16[2,184,640]{2,1,0:T(8,128)(2,1)S(1)}, bf16[2,184,640]{2,1,0:T(8,128)(2,1)S(1)}, u32[]{:S(2)}, u32[]{:S(2)}) collective-permute-start(bf16[2,184,640]{2,1,0:T(8,128)(2,1)S(1)} %collective-permute-done.21.refs_2_), channel_id=1, source_target_pairs={{0,8},{2,10},{4,28},{6,30},{8,16},{10,18},{12,4},{14,6},{16,24},{1... | collective-permute-start | bytes 1413128 | tf_op jit(solution)/shard_map/ppermute | solution.py:320
  83.2 27.5 %collective-permute-start.27 = (bf16[2,184,640]{2,1,0:T(8,128)(2,1)S(1)}, bf16[2,184,640]{2,1,0:T(8,128)(2,1)S(1)}, u32[]{:S(2)}, u32[]{:S(2)}) collective-permute-start(bf16[2,184,640]{2,1,0:T(8,128)(2,1)S(1)} %get-tuple-element.74), channel_id=1, source_target_pairs={{0,2},{2,0},{4,6},{6,4},{8,10},{10,8},{12,14},{14,12},{16,18},{18,... | collective-permute-start | bytes 1413128 | tf_op jit(solution)/shard_map/ppermute | solution.py:320
  84.6 18.8 %collective-permute-start.24 = (bf16[2,184,640]{2,1,0:T(8,128)(2,1)S(1)}, bf16[2,184,640]{2,1,0:T(8,128)(2,1)S(1)}, u32[]{:S(2)}, u32[]{:S(2)}) collective-permute-start(bf16[2,184,640]{2,1,0:T(8,128)(2,1)S(1)} %collective-permute-done.22.refs_3_), channel_id=1, source_target_pairs={{0,8},{2,10},{4,28},{6,30},{8,16},{10,18},{12,4},{14,6},{16,24},{1... | collective-permute-start | bytes 1413128 | tf_op jit(solution)/shard_map/ppermute | solution.py:320
  93.3 14.0 %copy-start.9 = (bf16[1,184,640]{2,1,0:T(8,128)(2,1)S(1)}, bf16[1,184,640]{2,1,0:T(8,128)(2,1)}, u32[]{:S(2)}) copy-start(bf16[1,184,640]{2,1,0:T(8,128)(2,1)} %copy-done.8) | copy-start | bytes 706564
  93.3 14.0 %copy-start.11 = (bf16[1,184,640]{2,1,0:T(8,128)(2,1)S(1)}, bf16[1,184,640]{2,1,0:T(8,128)(2,1)}, u32[]{:S(2)}) copy-start(bf16[1,184,640]{2,1,0:T(8,128)(2,1)} %copy-done.10) | copy-start | bytes 706564
  93.3 17.4 %collective-permute-start.28 = (bf16[2,184,640]{2,1,0:T(8,128)(2,1)S(1)}, bf16[2,184,640]{2,1,0:T(8,128)(2,1)S(1)}, u32[]{:S(2)}, u32[]{:S(2)}) collective-permute-start(bf16[2,184,640]{2,1,0:T(8,128)(2,1)S(1)} %get-tuple-element.75), channel_id=1, source_target_pairs={{0,2},{2,0},{4,6},{6,4},{8,10},{10,8},{12,14},{14,12},{16,18},{18,... | collective-permute-start | bytes 1413128 | tf_op jit(solution)/shard_map/ppermute | solution.py:320
  106.9 3.8 %collective-permute-start.29 = (bf16[2,184,640]{2,1,0:T(8,128)(2,1)S(1)}, bf16[2,184,640]{2,1,0:T(8,128)(2,1)S(1)}, u32[]{:S(2)}, u32[]{:S(2)}) collective-permute-start(bf16[2,184,640]{2,1,0:T(8,128)(2,1)S(1)} %get-tuple-element.76), channel_id=1, source_target_pairs={{0,2},{2,0},{4,6},{6,4},{8,10},{10,8},{12,14},{14,12},{16,18},{18,... | collective-permute-start | bytes 1413128 | tf_op jit(solution)/shard_map/ppermute | solution.py:320
  109.1 1.6 %collective-permute-start.25 = (bf16[1,184,640]{2,1,0:T(8,128)(2,1)S(1)}, bf16[1,184,640]{2,1,0:T(8,128)(2,1)S(1)}, u32[]{:S(2)}, u32[]{:S(2)}) collective-permute-start(bf16[1,184,640]{2,1,0:T(8,128)(2,1)S(1)} %get-tuple-element.72), channel_id=1, source_target_pairs={{0,2},{2,0},{4,6},{6,4},{8,10},{10,8},{12,14},{14,12},{16,18},{18,... | collective-permute-start | bytes 706568 | tf_op jit(solution)/shard_map/ppermute | solution.py:320

commit v6 on v5

--- a/solution.py
+++ b/solution.py
@@ -8,6 +8,8 @@
 from jax.sharding import PartitionSpec as P
 
 VMEM_LIMIT = 16 * 1024 * 1024
+TAKE_VMEM_LIMIT = 50 * 1024 * 1024
+AHEAD = 4
 SMEM_SPEC = pl.BlockSpec(memory_space=pltpu.SMEM)
 VMEM_SPEC = pl.BlockSpec(memory_space=pltpu.VMEM)
 HBM_SPEC = pl.BlockSpec(memory_space=pltpu.HBM)
@@ -43,45 +45,40 @@
     return lax.ppermute(x, axis, [(i, (i + by) % count) for i in range(count)])
 
 
-def tap_windows(widths, tap_weights, lon_dev, reach):
+def tap_lines(widths, tap_weights, lon_dev, reach):
     circle = tap_weights.shape[1]
-    offset = jnp.arange(circle, dtype=jnp.int32)
+    behind = (reach + 1) * lon_dev
+    line = jnp.concatenate([tap_weights[:, circle - behind :], tap_weights[:, :behind]], axis=1)
+    offset = jnp.arange(circle - behind, circle + behind, dtype=jnp.int32) % circle
     distance = jnp.minimum(offset, circle - offset)
-    active = jnp.where(
-        distance[None, :] <= widths[:, None],
-        tap_weights.astype(jnp.float32),
-        jnp.zeros((), jnp.float32),
-    )
-    behind = (reach + 1) * lon_dev
-    line = jnp.concatenate([active[:, circle - behind :], active[:, :behind]], axis=1)
-    lanes = up_to(2 * lon_dev, 128)
-    return jnp.stack(
-        [
-            jnp.pad(line[:, s * lon_dev : (s + 2) * lon_dev], ((0, 0), (0, lanes - 2 * lon_dev)))
-            for s in range(2 * reach + 1)
-        ],
-        axis=1,
-    )
-
-
-def toeplitz(taps, lon_dev, width):
-    lanes = taps.shape[1]
+    line = jnp.where(distance[None, :] <= widths[:, None], line.astype(jnp.float32), jnp.zeros((), jnp.float32))
+    return jnp.pad(line, ((0, 0), (0, up_to(2 * behind, 128) - 2 * behind)))
+
+
+def toeplitz(line, at, lon_dev, width):
+    lanes = up_to(width, 128) + 128
     step = min(up_to(lon_dev, 16), 96)
     bands = []
     for start in range(0, up_to(lon_dev, step), step):
-        band = jnp.broadcast_to(taps, (step, lanes))
-        band = pltpu.roll(band, (lanes - lon_dev + start) % lanes, 1)
-        band = pltpu.roll(band, 0, 1, stride=1, stride_axis=0)
+        taps = pltpu.roll(line, line.shape[1] + start - at, 1)
+        taps = jnp.concatenate([taps[:, : lanes - 128], taps[:, -128:]], axis=1)[:1]
+        band = pltpu.roll(jnp.broadcast_to(taps, (step, lanes)), 0, 1, stride=1, stride_axis=0)
         bands.append(band[:, :width].astype(jnp.bfloat16))
     return jnp.concatenate(bands, axis=0)
 
 
 def take_kernel(chunks, lat_dev, block, slot_ref, place_ref, fields_ref, *refs):
     outs = refs[: len(chunks)]
-    rows_ref, slots_ref, home_ref, take_ref = refs[len(chunks) :]
+    rows_ref, slots_ref, home_ref, take_ref, panel_ref, sems = refs[len(chunks) :]
     lon_dev, _, channels = fields_ref.shape
     half, quarter = lat_dev // 2, lat_dev // 4
     starts = list(range(0, lon_dev, block))
+    copies = []
+    for n, start in enumerate(starts):
+        window = pl.ds(start, min(block, lon_dev - start))
+        copies.append(pltpu.make_async_copy(fields_ref.at[window], panel_ref.at[window], sems.at[n]))
+    for copy in copies[:AHEAD]:
+        copy.start()
     band, core, x = place_ref[0], place_ref[1], place_ref[2]
 
     def at(n):
@@ -125,10 +122,13 @@
         return jnp.concatenate(strips, axis=0).astype(jnp.bfloat16)
 
     take_ref[...] = selector(block, block)
-    for start in starts:
+    for n, start in enumerate(starts):
+        copies[n].wait()
+        if n + AHEAD < len(copies):
+            copies[n + AHEAD].start()
         lon_in = min(block, lon_dev - start)
         lon_out = min(block, outs[0].shape[1] - start)
-        panel = fields_ref[start : start + lon_in].reshape(lon_in * lat_dev, channels)
+        panel = panel_ref[start : start + lon_in].reshape(lon_in * lat_dev, channels)
         take = take_ref[...] if (lon_in, lon_out) == (block, block) else selector(lon_in, lon_out)
         taken = jnp.dot(take, panel, preferred_element_type=jnp.float32).astype(jnp.bfloat16)
         place = 0
@@ -146,13 +146,15 @@
     result = pl.pallas_call(
         functools.partial(take_kernel, chunks, lat_dev, block),
         out_shape=[jax.ShapeDtypeStruct((n, padded, channels), fields.dtype) for n in chunks] + [ints, ints],
-        in_specs=[SMEM_SPEC, SMEM_SPEC, VMEM_SPEC],
+        in_specs=[SMEM_SPEC, SMEM_SPEC, HBM_SPEC],
         out_specs=[VMEM_SPEC] * len(chunks) + [SMEM_SPEC, SMEM_SPEC],
         scratch_shapes=[
             pltpu.SMEM((lat_dev,), jnp.int32),
             pltpu.VMEM((block * lat_dev, block * lat_dev), jnp.bfloat16),
+            pltpu.VMEM(fields.shape, fields.dtype),
+            pltpu.SemaphoreType.DMA((pl.cdiv(lon_dev, block),)),
         ],
-        compiler_params=pltpu.CompilerParams(vmem_limit_bytes=VMEM_LIMIT),
+        compiler_params=pltpu.CompilerParams(vmem_limit_bytes=TAKE_VMEM_LIMIT),
         cost_estimate=pl.CostEstimate(
             flops=2 * fields.size * block * lat_dev, bytes_accessed=4 * fields.size, transcendentals=0
         ),
@@ -214,42 +216,57 @@
     )(slots, *panels)
 
 
-def pair_kernel(lon_dev, base, plan, rows_ref, sign_ref, win_ref, *refs):
-    ins, (out_own, out_other, block_ref, total_ref) = refs[:-4], refs[-4:]
-    padded, channels = out_own.shape[1:]
+def pair_kernel(lon_dev, base, plan, phase, rows_ref, sign_ref, *refs):
+    count = len(plan)
     side, along = sign_ref[0], sign_ref[1]
+    if phase == "late":
+        (total_in, block_ref), refs = refs[:2], refs[2:]
+    else:
+        line_ref, refs = refs[0], refs[1:]
+    if phase == "early":
+        ins, (total_ref, block_ref) = refs[:-2], refs[-2:]
+    elif phase == "late":
+        ins, (out_own, out_other, total_ref) = refs[:-3], refs[-3:]
+    else:
+        ins, (out_own, out_other, total_ref, block_ref) = refs[:-4], refs[-4:]
+    padded, channels = ins[0].shape[1:]
+
+    def both(first, second):
+        return jnp.concatenate([first[...], second[...]], axis=1)
+
     for n, places in enumerate(plan):
-        taps = win_ref[rows_ref[base + n]]
-        for s in range(5):
-            block_ref[n, s] = toeplitz(taps[s : s + 1], lon_dev, padded)
-        own, other, x_own, x_other, z_own, z_other = [ins[array].at[i] for array, i in places]
+        panels = [ins[array].at[i] for array, i in places]
 
         def times(offset, panel):
             return jnp.dot(block_ref[n, 2 + offset], panel, preferred_element_type=jnp.float32)[:padded]
 
-        def both(first, second):
-            return jnp.concatenate([first[...], second[...]], axis=1)
-
-        here = both(own, other)
-        total = here.astype(jnp.float32) + times(0, here)
-        total += times(2 * along, both(x_own, x_other))
-        total += times(-2 * along, both(z_own, z_other))
-        total += jnp.concatenate([times(side, other[...]), times(-side, own[...])], axis=1)
-        total_ref[n] = total
-
-        @pl.when(side == along)
-        def _():
-            total_ref[n] += jnp.concatenate([times(-along, z_other[...]), times(along, x_own[...])], axis=1)
-
-        @pl.when(side != along)
-        def _():
-            total_ref[n] += jnp.concatenate([times(along, x_other[...]), times(-along, z_own[...])], axis=1)
-
-        out_own[n] = total_ref[n, :, :channels].astype(out_own.dtype)
-        out_other[n] = total_ref[n, :, channels:].astype(out_other.dtype)
-
-
-def filter_pair(rows, signs, windows, places, base, lon_dev):
+        def add(which, offset, panel):
+            lanes = pl.ds(which * channels, channels)
+            total_ref[n, :, lanes] += times(offset, panel[...])
+
+        if phase != "late":
+            own, other, x_own, x_other = panels[:4]
+            line = jnp.broadcast_to(line_ref[pl.ds(rows_ref[base + n], 1), :], (8, line_ref.shape[1]))
+            for s in range(5):
+                block_ref[n, s] = toeplitz(line, (s + 1) * lon_dev, lon_dev, padded)
+            here = both(own, other)
+            total = here.astype(jnp.float32) + times(0, here)
+            total += times(2 * along, both(x_own, x_other))
+            total += jnp.concatenate([times(side, other[...]), times(-side, own[...])], axis=1)
+            total_ref[n] = total
+            pl.when(side == along)(functools.partial(add, 1, along, x_own))
+            pl.when(side != along)(functools.partial(add, 0, along, x_other))
+        if phase != "early":
+            z_own, z_other = panels[-2:]
+            before = total_in[n] if phase == "late" else total_ref[n]
+            total_ref[n] = before + times(-2 * along, both(z_own, z_other))
+            pl.when(side == along)(functools.partial(add, 0, -along, z_other))
+            pl.when(side != along)(functools.partial(add, 1, -along, z_own))
+            out_own[n] = total_ref[n, :, :channels].astype(out_own.dtype)
+            out_other[n] = total_ref[n, :, channels:].astype(out_other.dtype)
+
+
+def filter_pair(rows, signs, lines, places, base, lon_dev, phase="whole", early=()):
     arrays = []
     plan = []
     for row in places:
@@ -262,24 +279,31 @@
         plan.append(tuple(found))
     count = len(plan)
     padded, channels = arrays[0].shape[1:]
+    total = (count, padded, 2 * channels), jnp.float32
+    block = (count, 5, up_to(lon_dev, 96), padded), jnp.bfloat16
     out = jax.ShapeDtypeStruct((count, padded, channels), arrays[0].dtype)
+    first = [lines] if phase != "late" else list(early)
+    if phase == "early":
+        outs, scratch = [jax.ShapeDtypeStruct(*total), jax.ShapeDtypeStruct(*block)], []
+    elif phase == "late":
+        outs, scratch = [out, out], [pltpu.VMEM(*total)]
+    else:
+        outs, scratch = [out, out], [pltpu.VMEM(*total), pltpu.VMEM(*block)]
+    weight = {"whole": 10, "early": 7, "late": 3}[phase]
     return pl.pallas_call(
-        functools.partial(pair_kernel, lon_dev, base, tuple(plan)),
-        out_shape=[out, out],
-        in_specs=[SMEM_SPEC, SMEM_SPEC] + [VMEM_SPEC] * (1 + len(arrays)),
-        out_specs=[VMEM_SPEC, VMEM_SPEC],
-        scratch_shapes=[
-            pltpu.VMEM((count, 5, up_to(lon_dev, 96), padded), jnp.bfloat16),
-            pltpu.VMEM((count, padded, 2 * channels), jnp.float32),
-        ],
+        functools.partial(pair_kernel, lon_dev, base, tuple(plan), phase),
+        out_shape=outs,
+        in_specs=[SMEM_SPEC, SMEM_SPEC] + [VMEM_SPEC] * (len(first) + len(arrays)),
+        out_specs=[VMEM_SPEC] * len(outs),
+        scratch_shapes=scratch,
         compiler_params=pltpu.CompilerParams(vmem_limit_bytes=VMEM_LIMIT),
         cost_estimate=pl.CostEstimate(
-            flops=FLOPS * count * 10 * 256 * 256 * 768,
+            flops=FLOPS * count * weight * 256 * 256 * 768,
             bytes_accessed=16 * count * padded * channels,
             transcendentals=0,
         ),
-        name="filter_pair",
-    )(rows, signs, windows, *arrays)
+        name="filter_" + phase,
+    )(rows, signs, *first, *arrays)
 
 
 def chip_aware(fields, owner_slot, widths, tap_weights):
@@ -304,7 +328,7 @@
     across_y = [(i, i ^ 1) for i in range(2 * n_lon)]
     across_both = [(i, i ^ 3) for i in range(2 * n_lon)]
 
-    windows = tap_windows(widths, tap_weights, lon_dev, 2)
+    lines = tap_lines(widths, tap_weights, lon_dev, 2)
     sizes = STAY + COME
     starts = [sum(sizes[:c]) for c in range(len(sizes))]
     done = {}
@@ -343,7 +367,7 @@
                 panels = here + beside + [get("q", 2), get("q", 3)]
             else:
                 panels = beside + [get("q", 0), get("q", 1)] + here
-            result = filter_pair(rows, signs, windows, [[(p, 0) for p in panels]], 0, lon_dev)
+            result = filter_pair(rows, signs, lines, [[(p, 0) for p in panels]], 0, lon_dev)
         elif kind == "b":
             operand, pairs = ((get("t", 0)[1], across_core), (get("t", 1)[0], across_x), (get("t", 1)[1], across_x_core))[i]
             result = moved(operand, "lon", pairs)
@@ -358,7 +382,12 @@
                 parts = [get(*p) for p in pair]
                 parts += [get(axis, PARTS.index(p)) for axis in "xz" for p in pair]
                 places.append([(p, index) for p in parts])
-            result = filter_pair(rows, signs, windows, places, FILTERS[i][0], lon_dev)
+            base = FILTERS[i][0]
+            if i < len(FILTERS) - 1:
+                result = filter_pair(rows, signs, lines, places, base, lon_dev)
+            else:
+                early = filter_pair(rows, signs, lines, [p[:4] for p in places], base, lon_dev, "early")
+                result = filter_pair(rows, signs, lines, [p[4:] for p in places], base, lon_dev, "late", early)
         else:
             result = moved(get("f", i)[1], "lon", across_core)
         done[kind, i] = result
@@ -370,20 +399,22 @@
     return jnp.transpose(out, (1, 0, 2))
 
 
-def filter_kernel(rows_ref, slots_ref, sector_ref, win_ref, *refs):
+def filter_kernel(rows_ref, slots_ref, sector_ref, line_ref, *refs):
     ins, out_ref = refs[:-1], refs[-1]
     lon_dev, channels = out_ref.shape[1:]
+    row = rows_ref[pl.program_id(0)]
+    line = jnp.broadcast_to(line_ref[pl.ds(row, 1), :], (8, line_ref.shape[1]))
     total = ins[0][0].astype(jnp.float32)
     for group, ref in enumerate(ins):
-        block = toeplitz(win_ref[0, pl.ds(sector_ref[group], 1), :], lon_dev, lon_dev)
+        block = toeplitz(line, (sector_ref[group] + 1) * lon_dev, lon_dev, lon_dev)
         total += jnp.dot(block, ref[0], preferred_element_type=jnp.float32)[:lon_dev]
     out_ref[0] = total.astype(out_ref.dtype)
 
 
-def filter_rows(rows, slots, sectors, windows, arrays):
+def filter_rows(rows, slots, sectors, lines, arrays):
     lat_dev, lon_dev, channels = arrays[0].shape
     row_spec = pl.BlockSpec((1, lon_dev, channels), lambda i, rows, slots, sectors: (i, 0, 0))
-    win_spec = pl.BlockSpec((1,) + windows.shape[1:], lambda i, rows, slots, sectors: (rows[i], 0, 0))
+    line_spec = pl.BlockSpec(lines.shape, lambda i, rows, slots, sectors: (0, 0))
     out_spec = pl.BlockSpec((1, lon_dev, channels), lambda i, rows, slots, sectors: (slots[i], 0, 0))
     return pl.pallas_call(
         filter_kernel,
@@ -391,12 +422,12 @@
         grid_spec=pltpu.PrefetchScalarGridSpec(
             num_scalar_prefetch=3,
             grid=(lat_dev,),
-            in_specs=[win_spec] + [row_spec] * len(arrays),
+            in_specs=[line_spec] + [row_spec] * len(arrays),
             out_specs=out_spec,
         ),
         compiler_params=pltpu.CompilerParams(vmem_limit_bytes=VMEM_LIMIT),
         name="filter_rows",
-    )(rows, slots, sectors, windows, *arrays)
+    )(rows, slots, sectors, lines, *arrays)
 
 
 def any_mesh(fields, owner_slot, widths, tap_weights):
@@ -413,7 +444,7 @@
     outgoing = fields[ordering].reshape(n_lat, lat_dev // n_lat, lon_dev, channels)
     incoming = lax.all_to_all(outgoing, "lat", split_axis=0, concat_axis=0, tiled=True)
     own = incoming.reshape(lat_dev, lon_dev, channels)
-    windows = tap_windows(widths, tap_weights, lon_dev, reach)
+    lines = tap_lines(widths, tap_weights, lon_dev, reach)
     arrays, order = [own], [reach]
     ahead = behind = own
     for step in range(1, reach + 1):
@@ -422,7 +453,7 @@
         arrays += [ahead, behind]
         order += [reach + step, reach - step]
     sectors = jnp.array(order, jnp.int32)
-    return filter_rows(rows, slots, sectors, windows, arrays)
+    return filter_rows(rows, slots, sectors, lines, arrays)
 
 
 def solution(mesh):

time: 114 us -> 115 us (level)
  local copies, waits for them, and re-layouts: 13.1 us -> 3.63 us
  waiting for transfers between devices: 42.5 us -> 51.4 us
  Pallas kernels: 20.9 us -> 26.6 us
  starting transfers between devices: 35.6 us -> 32.5 us
    ppermute x30, waiting for transfers between devices: 42.5 us -> 51.4 us  [moved(): return lax.ppermute(operand, axes, pairs)]
    another operation x7 -> x0, local copies, waits for them, and re-layouts: 6.13 us -> none  [tap_windows(): jnp.stack([jnp.pad(line[:, s * lon_dev:(s + 2) * lon_dev], ((0, 0), (0, l...]
    ppermute x30, starting transfers between devices: 35.6 us -> 32.5 us  [moved(): return lax.ppermute(operand, axes, pairs)]
    pallas_call x5 -> x6, Pallas kernels: 15 us -> 17.9 us  [filter_pair(): pl.pallas_call(functools.partial(pair_kernel, lon_dev, base, tuple(plan),...]
    pallas_call x1, Pallas kernels: 3.11 us -> 5.92 us  [take_rows(): pl.pallas_call(functools.partial(take_kernel, chunks, lat_dev, block), ou...]
    unnamed x38 -> x16, local copies, waits for them, and re-layouts: 4.86 us -> 2.73 us
  transfers between devices with their start and end apart: 30 -> 30, of which waited for: 11 -> 14; matrix products, arithmetic and copies ran while one was open for 8% -> 1% of each run, Pallas kernels for 13% -> 16%
where the time goes in v6:
time: 115 us
  waiting for transfers between devices  51.4 us (45%)
  starting transfers between devices  32.5 us (28%)
  Pallas kernels  26.6 us (23%)
  local copies, waits for them, and re-layouts  3.63 us (3%)
    ppermute x30, waiting for transfers between devices, moved(): return lax.ppermute(operand, axes, pairs)  51.4 us
    ppermute x30, starting transfers between devices, moved(): return lax.ppermute(operand, axes, pairs)  32.5 us
    pallas_call x6, Pallas kernels, filter_pair(): pl.pallas_call(functools.partial(pair_kernel, lon_dev, base, tuple(plan),...  17.9 us
    pallas_call x1, Pallas kernels, take_rows(): pl.pallas_call(functools.partial(take_kernel, chunks, lat_dev, block), ou...  5.92 us
    pallas_call x1, Pallas kernels, put_rows(): pl.pallas_call(functools.partial(put_kernel, counts, lat_dev, block), out...  2.77 us
    unnamed x16, local copies, waits for them, and re-layouts  2.73 us
  transfers between devices with their start and end apart: 30, of which 14 were waited for; matrix products, arithmetic and copies ran while one was open for 1% of the time, Pallas kernels for 16%

profile of v6, /device:TPU:0, one launch (start us, length us, event | category | flops | bytes accessed | tf_op | source)
XLA Modules:
  0.0 114.7 jit_solution(1636069676109769235)
XLA Ops:
  0.0 0.1 pad_add_fusion.place_ref
  0.1 0.7 copy-done
  0.7 5.9 %take_rows.1 = (bf16[1,184,640]{2,1,0:T(8,128)(2,1)S(1)}, bf16[1,184,640]{2,1,0:T(8,128)(2,1)S(1)}, bf16[2,184,640]{2,1,0:T(8,128)(2,1)S(1)}, bf16[1,184,640]{2,...) custom-call(s32[32]{0:T(128)S(1)} %copy-done, ...), custom_call_target="tpu_custom_call" | custom-call | flops 943718400 | bytes 7372800 | tf_op jit(solution)/shard_map/take_rows/pallas_call | solution.py:146
  6.7 0.5 collective-permute-start.8
  7.2 0.1 collective-permute-start
  7.3 2.6 %collective-permute-start.2 = (bf16[1,184,640]{2,1,0:T(8,128)(2,1)S(1)}, bf16[1,184,640]{2,1,0:T(8,128)(2,1)}, u32[]{:S(2)}, u32[]{:S(2)}) collective-permute-start(bf16[1,184,640]{2,1,0:T(8,128)(2,1)S(1)} %get-tuple-element.48), channel_id=1, source_target_pairs={{0,6},{2,4},{4,2},{6,0},{8,14},{10,12},{12,10},{14,8},{16,22},{18,... | collective-permute-start | bytes 706568 | tf_op jit(solution)/shard_map/ppermute | solution.py:344
  9.9 1.5 %collective-permute-start.13 = (bf16[2,184,640]{2,1,0:T(8,128)(2,1)S(1)}, bf16[2,184,640]{2,1,0:T(8,128)(2,1)S(1)}, u32[]{:S(2)}, u32[]{:S(2)}) collective-permute-start(bf16[2,184,640]{2,1,0:T(8,128)(2,1)S(1)} %get-tuple-element.58), channel_id=1, source_target_pairs={{0,1},{1,0},{2,3},{3,2},{4,5},{5,4},{6,7},{7,6},{8,9},{9,8},{10,11... | collective-permute-start | bytes 1413128 | tf_op jit(solution)/shard_map/ppermute | solution.py:344
  11.4 3.6 %collective-permute-start.6 = (bf16[1,184,640]{2,1,0:T(8,128)(2,1)S(1)}, bf16[1,184,640]{2,1,0:T(8,128)(2,1)S(1)}, u32[]{:S(2)}, u32[]{:S(2)}) collective-permute-start(bf16[1,184,640]{2,1,0:T(8,128)(2,1)S(1)} %get-tuple-element.45.refs_1_.refs_5_), channel_id=1, source_target_pairs={{0,24},{2,26},{4,12},{6,14},{8,0},{10,2},{12,20},{14,22},{16,8},{1... | collective-permute-start | bytes 706568 | tf_op jit(solution)/shard_map/ppermute | solution.py:344
  15.0 0.0 collective-permute-done.refs_2_.refs_6_
  15.0 0.0 collective-permute-start.1
  15.0 1.0 collective-permute-done.2.refs_4_.refs_2_
  16.0 4.2 %collective-permute-start.4 = (bf16[1,184,640]{2,1,0:T(8,128)(2,1)S(1)}, bf16[1,184,640]{2,1,0:T(8,128)(2,1)S(1)}, u32[]{:S(2)}, u32[]{:S(2)}) collective-permute-start(bf16[1,184,640]{2,1,0:T(8,128)(2,1)S(1)} %collective-permute-done.refs_2_.refs_6_), channel_id=1, source_target_pairs={{0,24},{2,26},{4,12},{6,14},{8,0},{10,2},{12,20},{14,22},{16,8},{1... | collective-permute-start | bytes 706568 | tf_op jit(solution)/shard_map/ppermute | solution.py:344
  20.2 0.7 copy-done.1
  20.9 0.0 collective-permute-done.6.refs_3_
  20.9 0.7 copy-done.3
  21.5 0.7 collective-permute-start.9
  22.3 1.3 %collective-permute-start.10 = (bf16[2,184,640]{2,1,0:T(8,128)(2,1)S(1)}, bf16[2,184,640]{2,1,0:T(8,128)(2,1)}, u32[]{:S(2)}, u32[]{:S(2)}) collective-permute-start(bf16[2,184,640]{2,1,0:T(8,128)(2,1)S(1)} %collective-permute-done.8.refs_2_), channel_id=1, source_target_pairs={{0,4},{2,6},{4,0},{6,2},{8,12},{10,14},{12,8},{14,10},{16,20},{18,... | collective-permute-start | bytes 1413128 | tf_op jit(solution)/shard_map/ppermute | solution.py:344
  23.6 0.8 collective-permute-start.14
  24.4 1.5 %collective-permute-done.4.refs_4_ = bf16[1,184,640]{2,1,0:T(8,128)(2,1)S(1)} collective-permute-done((bf16[1,184,640]{2,1,0:T(8,128)(2,1)S(1)}, bf16[1,184,640]{2,1,0:T(8,128)(2,1)S(1)}, u32[]{:S(2)}, u32[]{:S(2)}) %collective-permute-start.4) | collective-permute-done | bytes 235552 | tf_op jit(solution)/shard_map/ppermute | solution.py:344
  25.9 0.7 copy-done.5
  26.6 0.5 collective-permute-start.3
  27.0 1.6 %collective-permute-start.5 = (bf16[1,184,640]{2,1,0:T(8,128)(2,1)}, bf16[1,184,640]{2,1,0:T(8,128)(2,1)}, u32[]{:S(2)}, u32[]{:S(2)}) collective-permute-start(bf16[1,184,640]{2,1,0:T(8,128)(2,1)} %collective-permute-done.2.refs_4_.refs_2_), channel_id=1, source_target_pairs={{0,8},{2,10},{4,28},{6,30},{8,16},{10,18},{12,4},{14,6},{16,24},{1... | collective-permute-start | bytes 706568 | tf_op jit(solution)/shard_map/ppermute | solution.py:344
  28.6 0.9 fusion.3
  29.5 5.7 %collective-permute-done.9.refs_3_ = bf16[2,184,640]{2,1,0:T(8,128)(2,1)S(1)} collective-permute-done((bf16[2,184,640]{2,1,0:T(8,128)(2,1)S(1)}, bf16[2,184,640]{2,1,0:T(8,128)(2,1)S(1)}, u32[]{:S(2)}, u32[]{:S(2)}) %collective-permute-start.9) | collective-permute-done | bytes 471072 | tf_op jit(solution)/shard_map/ppermute | solution.py:344
  35.2 1.5 %collective-permute-start.19 = (bf16[2,184,640]{2,1,0:T(8,128)(2,1)S(1)}, bf16[2,184,640]{2,1,0:T(8,128)(2,1)S(1)}, u32[]{:S(2)}, u32[]{:S(2)}) collective-permute-start(bf16[2,184,640]{2,1,0:T(8,128)(2,1)S(1)} %get-tuple-element.66), channel_id=1, source_target_pairs={{0,1},{1,0},{2,3},{3,2},{4,5},{5,4},{6,7},{7,6},{8,9},{9,8},{10,11... | collective-permute-start | bytes 1413128 | tf_op jit(solution)/shard_map/ppermute | solution.py:344
  36.7 1.0 collective-permute-done.3.refs_5_
  37.7 5.0 %collective-permute-done.5.refs_6_ = bf16[1,184,640]{2,1,0:T(8,128)(2,1)} collective-permute-done((bf16[1,184,640]{2,1,0:T(8,128)(2,1)}, bf16[1,184,640]{2,1,0:T(8,128)(2,1)}, u32[]{:S(2)}, u32[]{:S(2)}) %collective-permute-start.5) | collective-permute-done | bytes 235552 | tf_op jit(solution)/shard_map/ppermute | solution.py:344
  42.8 0.0 collective-permute-start.15
  42.8 2.6 %collective-permute-done.10.refs_4_ = bf16[2,184,640]{2,1,0:T(8,128)(2,1)} collective-permute-done((bf16[2,184,640]{2,1,0:T(8,128)(2,1)S(1)}, bf16[2,184,640]{2,1,0:T(8,128)(2,1)}, u32[]{:S(2)}, u32[]{:S(2)}) %collective-permute-start.10) | collective-permute-done | bytes 471072 | tf_op jit(solution)/shard_map/ppermute | solution.py:344
  45.4 0.0 collective-permute-start.12
  45.4 0.0 collective-permute-done.14.refs_2_
  45.4 3.5 %collective-permute-start.16 = (bf16[2,184,640]{2,1,0:T(8,128)(2,1)S(1)}, bf16[2,184,640]{2,1,0:T(8,128)(2,1)S(1)}, u32[]{:S(2)}, u32[]{:S(2)}) collective-permute-start(bf16[2,184,640]{2,1,0:T(8,128)(2,1)S(1)} %collective-permute-done.14.refs_2_), channel_id=1, source_target_pairs={{0,4},{2,6},{4,0},{6,2},{8,12},{10,14},{12,8},{14,10},{16,20},{18,... | collective-permute-start | bytes 1413128 | tf_op jit(solution)/shard_map/ppermute | solution.py:344
  48.8 0.1 convert_select_fusion
  48.9 0.1 pad_add_fusion.1.sign_ref
  49.0 0.0 collective-permute-start.20
  49.1 7.4 %collective-permute-done.15.refs_3_ = bf16[2,184,640]{2,1,0:T(8,128)(2,1)S(1)} collective-permute-done((bf16[2,184,640]{2,1,0:T(8,128)(2,1)S(1)}, bf16[2,184,640]{2,1,0:T(8,128)(2,1)S(1)}, u32[]{:S(2)}, u32[]{:S(2)}) %collective-permute-start.15) | collective-permute-done | bytes 471072 | tf_op jit(solution)/shard_map/ppermute | solution.py:344
  56.5 0.0 collective-permute-done.11.refs_5_
  56.5 3.6 %collective-permute-start.21 = (bf16[2,184,640]{2,1,0:T(8,128)(2,1)S(1)}, bf16[2,184,640]{2,1,0:T(8,128)(2,1)S(1)}, u32[]{:S(2)}, u32[]{:S(2)}) collective-permute-start(bf16[2,184,640]{2,1,0:T(8,128)(2,1)S(1)} %collective-permute-done.19.refs_1_), channel_id=1, source_target_pairs={{0,4},{2,6},{4,0},{6,2},{8,12},{10,14},{12,8},{14,10},{16,20},{18,... | collective-permute-start | bytes 1413128 | tf_op jit(solution)/shard_map/ppermute | solution.py:344
  60.1 3.3 %collective-permute-done.12.refs_6_ = bf16[2,184,640]{2,1,0:T(8,128)(2,1)S(1)} collective-permute-done((bf16[2,184,640]{2,1,0:T(8,128)(2,1)}, bf16[2,184,640]{2,1,0:T(8,128)(2,1)S(1)}, u32[]{:S(2)}, u32[]{:S(2)}) %collective-permute-start.12) | collective-permute-done | bytes 471072 | tf_op jit(solution)/shard_map/ppermute | solution.py:344
  63.3 3.2 %collective-permute-done.16.refs_4_ = bf16[2,184,640]{2,1,0:T(8,128)(2,1)S(1)} collective-permute-done((bf16[2,184,640]{2,1,0:T(8,128)(2,1)S(1)}, bf16[2,184,640]{2,1,0:T(8,128)(2,1)S(1)}, u32[]{:S(2)}, u32[]{:S(2)}) %collective-permute-start.16) | collective-permute-done | bytes 471072 | tf_op jit(solution)/shard_map/ppermute | solution.py:344
  66.6 0.0 collective-permute-start.18
  66.6 4.3 %filter_whole.6 = (bf16[2,184,640]{2,1,0:T(8,128)(2,1)S(1)}, bf16[2,184,640]{2,1,0:T(8,128)(2,1)S(1)}) custom-call(s32[16]{0:T(128)S(1)} %get-tuple-element.44.rows_ref, s32[2]{0:T(128)S(1)} %pad_add_fusion.1.sign_ref, f32[32,1152]{1,0:T(8,128)S(1)} %pad.4.refs_0_, bf16[2,184,640]{2,1,0:T(8,128)(2,1)S(1)} %get-tuple-element.52.refs_1_, ...), custom_call_target="tpu_custom_call" | custom-call | flops 6039797760 | bytes 3768320 | tf_op jit(solution)/shard_map/filter_whole/pallas_call | solution.py:293
  70.9 0.0 collective-permute-done.20.refs_2_
  70.9 3.7 %collective-permute-start.22 = (bf16[2,184,640]{2,1,0:T(8,128)(2,1)S(1)}, bf16[2,184,640]{2,1,0:T(8,128)(2,1)S(1)}, u32[]{:S(2)}, u32[]{:S(2)}) collective-permute-start(bf16[2,184,640]{2,1,0:T(8,128)(2,1)S(1)} %collective-permute-done.20.refs_2_), channel_id=1, source_target_pairs={{0,4},{2,6},{4,0},{6,2},{8,12},{10,14},{12,8},{14,10},{16,20},{18,... | collective-permute-start | bytes 1413128 | tf_op jit(solution)/shard_map/ppermute | solution.py:344
  74.6 2.7 %filter_whole.5 = (bf16[1,184,640]{2,1,0:T(8,128)(2,1)S(1)}, bf16[1,184,640]{2,1,0:T(8,128)(2,1)S(1)}) custom-call(s32[16]{0:T(128)S(1)} %get-tuple-element.44.rows_ref, s32[2]{0:T(128)S(1)} %pad_add_fusion.1.sign_ref, f32[32,1152]{1,0:T(8,128)S(1)} %pad.4.refs_0_, bf16[1,184,640]{2,1,0:T(8,128)(2,1)} %collective-permute-done.1.refs_3_.refs_1_, ...), custom_call_target="tpu_custom_call" | custom-call | flops 3019898880 | bytes 1884160 | tf_op jit(solution)/shard_map/filter_whole/pallas_call | solution.py:293
  77.2 0.1 collective-permute-start.7
  77.4 0.0 collective-permute-done.17.refs_5_
  77.4 0.0 collective-permute-start.26
  77.4 2.0 %collective-permute-start.27 = (bf16[2,184,640]{2,1,0:T(8,128)(2,1)S(1)}, bf16[2,184,640]{2,1,0:T(8,128)(2,1)S(1)}, u32[]{:S(2)}, u32[]{:S(2)}) collective-permute-start(bf16[2,184,640]{2,1,0:T(8,128)(2,1)S(1)} %get-tuple-element.78), channel_id=1, source_target_pairs={{0,2},{2,0},{4,6},{6,4},{8,10},{10,8},{12,14},{14,12},{16,18},{18,... | collective-permute-start | bytes 1413128 | tf_op jit(solution)/shard_map/ppermute | solution.py:344
  79.4 2.7 %collective-permute-done.18.refs_6_ = bf16[2,184,640]{2,1,0:T(8,128)(2,1)S(1)} collective-permute-done((bf16[2,184,640]{2,1,0:T(8,128)(2,1)S(1)}, bf16[2,184,640]{2,1,0:T(8,128)(2,1)S(1)}, u32[]{:S(2)}, u32[]{:S(2)}) %collective-permute-start.18) | collective-permute-done | bytes 471072 | tf_op jit(solution)/shard_map/ppermute | solution.py:344
  82.1 0.0 collective-permute-start.23
  82.1 4.6 %collective-permute-done.22.refs_4_ = bf16[2,184,640]{2,1,0:T(8,128)(2,1)S(1)} collective-permute-done((bf16[2,184,640]{2,1,0:T(8,128)(2,1)S(1)}, bf16[2,184,640]{2,1,0:T(8,128)(2,1)S(1)}, u32[]{:S(2)}, u32[]{:S(2)}) %collective-permute-start.22) | collective-permute-done | bytes 471072 | tf_op jit(solution)/shard_map/ppermute | solution.py:344
  86.8 3.8 %filter_whole.7 = (bf16[2,184,640]{2,1,0:T(8,128)(2,1)S(1)}, bf16[2,184,640]{2,1,0:T(8,128)(2,1)S(1)}) custom-call(s32[16]{0:T(128)S(1)} %get-tuple-element.44.rows_ref, s32[2]{0:T(128)S(1)} %pad_add_fusion.1.sign_ref, f32[32,1152]{1,0:T(8,128)S(1)} %pad.4.refs_0_, bf16[2,184,640]{2,1,0:T(8,128)(2,1)S(1)} %collective-permute-done.13.refs_1_, ...), custom_call_target="tpu_custom_call" | custom-call | flops 6039797760 | bytes 3768320 | tf_op jit(solution)/shard_map/filter_whole/pallas_call | solution.py:293
  90.6 2.6 %filter_early.1 = (f32[2,184,1280]{2,1,0:T(8,128)S(1)}, bf16[2,5,192,184]{3,2,1,0:T(8,128)(2,1)S(1)}) custom-call(s32[16]{0:T(128)S(1)} %get-tuple-element.44.rows_ref, s32[2]{0:T(128)S(1)} %pad_add_fusion.1.sign_ref, f32[32,1152]{1,0:T(8,128)S(1)} %pad.4.refs_0_, bf16[2,184,640]{2,1,0:T(8,128)(2,1)S(1)} %collective-permute-done.19.refs_1_, ...), custom_call_target="tpu_custom_call" | custom-call | flops 4227858432 | bytes 3768320 | tf_op jit(solution)/shard_map/filter_early/pallas_call | solution.py:293
  93.3 4.4 %collective-permute-done.23.refs_2_ = bf16[2,184,640]{2,1,0:T(8,128)(2,1)S(1)} collective-permute-done((bf16[2,184,640]{2,1,0:T(8,128)(2,1)S(1)}, bf16[2,184,640]{2,1,0:T(8,128)(2,1)S(1)}, u32[]{:S(2)}, u32[]{:S(2)}) %collective-permute-start.23) | collective-permute-done | bytes 471072 | tf_op jit(solution)/shard_map/ppermute | solution.py:344
  97.6 0.0 collective-permute-start.28
  97.6 7.8 %collective-permute-done.24.refs_3_ = bf16[2,184,640]{2,1,0:T(8,128)(2,1)S(1)} collective-permute-done((bf16[2,184,640]{2,1,0:T(8,128)(2,1)S(1)}, bf16[2,184,640]{2,1,0:T(8,128)(2,1)S(1)}, u32[]{:S(2)}, u32[]{:S(2)}) %collective-permute-start.24) | collective-permute-done | bytes 471072 | tf_op jit(solution)/shard_map/ppermute | solution.py:344
  105.4 1.7 %filter_late.1 = (bf16[2,184,640]{2,1,0:T(8,128)(2,1)S(1)}, bf16[2,184,640]{2,1,0:T(8,128)(2,1)S(1)}) custom-call(s32[16]{0:T(128)S(1)} %get-tuple-element.44.rows_ref, s32[2]{0:T(128)S(1)} %pad_add_fusion.1.sign_ref, f32[2,184,1280]{2,1,0:T(8,128)S(1)} %get-tuple-element.71.refs_0_, bf16[2,5,192,184]{3,2,1,0:T(8,128)(2,1)S(1)} %get-tuple-element.72.refs_1_, ...), custom_call_target="tpu_custom_call" | custom-call | flops 1811939328 | bytes 3768320 | tf_op jit(solution)/shard_map/filter_late/pallas_call | solution.py:293
  107.1 0.1 collective-permute-start.29
  107.2 2.9 %filter_whole.4 = (bf16[1,184,640]{2,1,0:T(8,128)(2,1)S(1)}, bf16[1,184,640]{2,1,0:T(8,128)(2,1)S(1)}) custom-call(s32[16]{0:T(128)S(1)} %get-tuple-element.44.rows_ref, s32[2]{0:T(128)S(1)} %pad_add_fusion.1.sign_ref, f32[32,1152]{1,0:T(8,128)S(1)} %pad.4.refs_0_, bf16[1,184,640]{2,1,0:T(8,128)(2,1)S(1)} %get-tuple-element.45.refs_1_.refs_5_, ...), custom_call_target="tpu_custom_call" | custom-call | flops 3019898880 | bytes 1884160 | tf_op jit(solution)/shard_map/filter_whole/pallas_call | solution.py:293
  110.1 0.6 collective-permute-start.25
  110.7 1.1 collective-permute-done.25.refs_5_
  111.8 0.0 collective-permute-done.27.refs_7_
  111.8 2.8 %put_rows.1 = bf16[180,16,640]{2,1,0:T(8,128)(2,1)} custom-call(s32[16]{0:T(128)S(1)} %get-tuple-element.43.slots_ref, bf16[1,184,640]{2,1,0:T(8,128)(2,1)S(1)} %get-tuple-element.50.refs_0_, bf16[1,184,640]{2,1,0:T(8,128)(2,1)S(1)} %collective-permute-done.7.refs_1_, bf16[2,184,640]{2,1,0:T(8,128)(2,1)S(1)} %get-tuple-element.57.refs_2_, ...), custom_call_target="tpu_custom_call" | custom-call | flops 943718400 | bytes 7372800 | tf_op jit(solution)/shard_map/put_rows/pallas_call | solution.py:200
  (26 shorter events, 0.1 us)
Async XLA Ops:
  0.0 48.8 %copy-start.7 = (s32[32]{0:T(128)S(1)}, s32[32]{0:T(128)}, u32[]{:S(2)}) copy-start(s32[32]{0:T(128)} %param.6) | copy-start | bytes 388
  0.1 0.7 copy-start
  6.7 15.6 %collective-permute-start.8 = (bf16[2,184,640]{2,1,0:T(8,128)(2,1)S(1)}, bf16[2,184,640]{2,1,0:T(8,128)(2,1)S(1)}, u32[]{:S(2)}, u32[]{:S(2)}) collective-permute-start(bf16[2,184,640]{2,1,0:T(8,128)(2,1)S(1)} %get-tuple-element.53), channel_id=1, source_target_pairs={{0,2},{2,0},{4,6},{6,4},{8,10},{10,8},{12,14},{14,12},{16,18},{18,... | collective-permute-start | bytes 1413128 | tf_op jit(solution)/shard_map/ppermute | solution.py:344
  7.2 7.8 %collective-permute-start = (bf16[1,184,640]{2,1,0:T(8,128)(2,1)S(1)}, bf16[1,184,640]{2,1,0:T(8,128)(2,1)S(1)}, u32[]{:S(2)}, u32[]{:S(2)}) collective-permute-start(bf16[1,184,640]{2,1,0:T(8,128)(2,1)S(1)} %get-tuple-element.46), channel_id=1, source_target_pairs={{0,2},{2,0},{4,6},{6,4},{8,10},{10,8},{12,14},{14,12},{16,18},{18,... | collective-permute-start | bytes 706568 | tf_op jit(solution)/shard_map/ppermute | solution.py:344
  7.3 8.7 %collective-permute-start.2 = (bf16[1,184,640]{2,1,0:T(8,128)(2,1)S(1)}, bf16[1,184,640]{2,1,0:T(8,128)(2,1)}, u32[]{:S(2)}, u32[]{:S(2)}) collective-permute-start(bf16[1,184,640]{2,1,0:T(8,128)(2,1)S(1)} %get-tuple-element.48), channel_id=1, source_target_pairs={{0,6},{2,4},{4,2},{6,0},{8,14},{10,12},{12,10},{14,8},{16,22},{18,... | collective-permute-start | bytes 706568 | tf_op jit(solution)/shard_map/ppermute | solution.py:344
  9.9 17.2 %collective-permute-start.13 = (bf16[2,184,640]{2,1,0:T(8,128)(2,1)S(1)}, bf16[2,184,640]{2,1,0:T(8,128)(2,1)S(1)}, u32[]{:S(2)}, u32[]{:S(2)}) collective-permute-start(bf16[2,184,640]{2,1,0:T(8,128)(2,1)S(1)} %get-tuple-element.58), channel_id=1, source_target_pairs={{0,1},{1,0},{2,3},{3,2},{4,5},{5,4},{6,7},{7,6},{8,9},{9,8},{10,11... | collective-permute-start | bytes 1413128 | tf_op jit(solution)/shard_map/ppermute | solution.py:344
  11.4 9.5 %collective-permute-start.6 = (bf16[1,184,640]{2,1,0:T(8,128)(2,1)S(1)}, bf16[1,184,640]{2,1,0:T(8,128)(2,1)S(1)}, u32[]{:S(2)}, u32[]{:S(2)}) collective-permute-start(bf16[1,184,640]{2,1,0:T(8,128)(2,1)S(1)} %get-tuple-element.45.refs_1_.refs_5_), channel_id=1, source_target_pairs={{0,24},{2,26},{4,12},{6,14},{8,0},{10,2},{12,20},{14,22},{16,8},{1... | collective-permute-start | bytes 706568 | tf_op jit(solution)/shard_map/ppermute | solution.py:344
  15.0 8.6 %collective-permute-start.1 = (bf16[1,184,640]{2,1,0:T(8,128)(2,1)S(1)}, bf16[1,184,640]{2,1,0:T(8,128)(2,1)}, u32[]{:S(2)}, u32[]{:S(2)}) collective-permute-start(bf16[1,184,640]{2,1,0:T(8,128)(2,1)S(1)} %get-tuple-element.47), channel_id=1, source_target_pairs={{0,4},{2,6},{4,0},{6,2},{8,12},{10,14},{12,8},{14,10},{16,20},{18,... | collective-permute-start | bytes 706568 | tf_op jit(solution)/shard_map/ppermute | solution.py:344
  16.0 9.9 %collective-permute-start.4 = (bf16[1,184,640]{2,1,0:T(8,128)(2,1)S(1)}, bf16[1,184,640]{2,1,0:T(8,128)(2,1)S(1)}, u32[]{:S(2)}, u32[]{:S(2)}) collective-permute-start(bf16[1,184,640]{2,1,0:T(8,128)(2,1)S(1)} %collective-permute-done.refs_2_.refs_6_), channel_id=1, source_target_pairs={{0,24},{2,26},{4,12},{6,14},{8,0},{10,2},{12,20},{14,22},{16,8},{1... | collective-permute-start | bytes 706568 | tf_op jit(solution)/shard_map/ppermute | solution.py:344
  20.2 0.7 copy-start.1
  20.9 0.7 copy-start.3
  21.5 13.6 %collective-permute-start.9 = (bf16[2,184,640]{2,1,0:T(8,128)(2,1)S(1)}, bf16[2,184,640]{2,1,0:T(8,128)(2,1)S(1)}, u32[]{:S(2)}, u32[]{:S(2)}) collective-permute-start(bf16[2,184,640]{2,1,0:T(8,128)(2,1)S(1)} %get-tuple-element.52.refs_1_), channel_id=1, source_target_pairs={{0,4},{2,6},{4,0},{6,2},{8,12},{10,14},{12,8},{14,10},{16,20},{18,... | collective-permute-start | bytes 1413128 | tf_op jit(solution)/shard_map/ppermute | solution.py:344
  22.3 23.1 %collective-permute-start.10 = (bf16[2,184,640]{2,1,0:T(8,128)(2,1)S(1)}, bf16[2,184,640]{2,1,0:T(8,128)(2,1)}, u32[]{:S(2)}, u32[]{:S(2)}) collective-permute-start(bf16[2,184,640]{2,1,0:T(8,128)(2,1)S(1)} %collective-permute-done.8.refs_2_), channel_id=1, source_target_pairs={{0,4},{2,6},{4,0},{6,2},{8,12},{10,14},{12,8},{14,10},{16,20},{18,... | collective-permute-start | bytes 1413128 | tf_op jit(solution)/shard_map/ppermute | solution.py:344
  23.6 21.8 %collective-permute-start.14 = (bf16[2,184,640]{2,1,0:T(8,128)(2,1)}, bf16[2,184,640]{2,1,0:T(8,128)(2,1)S(1)}, u32[]{:S(2)}, u32[]{:S(2)}) collective-permute-start(bf16[2,184,640]{2,1,0:T(8,128)(2,1)} %get-tuple-element.59), channel_id=1, source_target_pairs={{0,3},{1,2},{2,1},{3,0},{4,7},{5,6},{6,5},{7,4},{8,11},{9,10},{10,... | collective-permute-start | bytes 1413128 | tf_op jit(solution)/shard_map/ppermute | solution.py:344
  25.9 0.7 copy-start.5
  26.6 11.2 %collective-permute-start.3 = (bf16[1,184,640]{2,1,0:T(8,128)(2,1)}, bf16[1,184,640]{2,1,0:T(8,128)(2,1)}, u32[]{:S(2)}, u32[]{:S(2)}) collective-permute-start(bf16[1,184,640]{2,1,0:T(8,128)(2,1)} %collective-permute-done.1.refs_3_.refs_1_), channel_id=1, source_target_pairs={{0,8},{2,10},{4,28},{6,30},{8,16},{10,18},{12,4},{14,6},{16,24},{1... | collective-permute-start | bytes 706568 | tf_op jit(solution)/shard_map/ppermute | solution.py:344
  27.0 15.7 %collective-permute-start.5 = (bf16[1,184,640]{2,1,0:T(8,128)(2,1)}, bf16[1,184,640]{2,1,0:T(8,128)(2,1)}, u32[]{:S(2)}, u32[]{:S(2)}) collective-permute-start(bf16[1,184,640]{2,1,0:T(8,128)(2,1)} %collective-permute-done.2.refs_4_.refs_2_), channel_id=1, source_target_pairs={{0,8},{2,10},{4,28},{6,30},{8,16},{10,18},{12,4},{14,6},{16,24},{1... | collective-permute-start | bytes 706568 | tf_op jit(solution)/shard_map/ppermute | solution.py:344
  35.2 13.9 %collective-permute-start.19 = (bf16[2,184,640]{2,1,0:T(8,128)(2,1)S(1)}, bf16[2,184,640]{2,1,0:T(8,128)(2,1)S(1)}, u32[]{:S(2)}, u32[]{:S(2)}) collective-permute-start(bf16[2,184,640]{2,1,0:T(8,128)(2,1)S(1)} %get-tuple-element.66), channel_id=1, source_target_pairs={{0,1},{1,0},{2,3},{3,2},{4,5},{5,4},{6,7},{7,6},{8,9},{9,8},{10,11... | collective-permute-start | bytes 1413128 | tf_op jit(solution)/shard_map/ppermute | solution.py:344
  37.7 18.8 %collective-permute-start.11 = (bf16[2,184,640]{2,1,0:T(8,128)(2,1)S(1)}, bf16[2,184,640]{2,1,0:T(8,128)(2,1)S(1)}, u32[]{:S(2)}, u32[]{:S(2)}) collective-permute-start(bf16[2,184,640]{2,1,0:T(8,128)(2,1)S(1)} %collective-permute-done.9.refs_3_), channel_id=1, source_target_pairs={{0,8},{2,10},{4,28},{6,30},{8,16},{10,18},{12,4},{14,6},{16,24},{1... | collective-permute-start | bytes 1413128 | tf_op jit(solution)/shard_map/ppermute | solution.py:344
  42.8 13.7 %collective-permute-start.15 = (bf16[2,184,640]{2,1,0:T(8,128)(2,1)S(1)}, bf16[2,184,640]{2,1,0:T(8,128)(2,1)S(1)}, u32[]{:S(2)}, u32[]{:S(2)}) collective-permute-start(bf16[2,184,640]{2,1,0:T(8,128)(2,1)S(1)} %collective-permute-done.13.refs_1_), channel_id=1, source_target_pairs={{0,4},{2,6},{4,0},{6,2},{8,12},{10,14},{12,8},{14,10},{16,20},{18,... | collective-permute-start | bytes 1413128 | tf_op jit(solution)/shard_map/ppermute | solution.py:344
  45.4 18.0 %collective-permute-start.12 = (bf16[2,184,640]{2,1,0:T(8,128)(2,1)}, bf16[2,184,640]{2,1,0:T(8,128)(2,1)S(1)}, u32[]{:S(2)}, u32[]{:S(2)}) collective-permute-start(bf16[2,184,640]{2,1,0:T(8,128)(2,1)} %collective-permute-done.10.refs_4_), channel_id=1, source_target_pairs={{0,8},{2,10},{4,28},{6,30},{8,16},{10,18},{12,4},{14,6},{16,24},{1... | collective-permute-start | bytes 1413128 | tf_op jit(solution)/shard_map/ppermute | solution.py:344
  45.4 21.2 %collective-permute-start.16 = (bf16[2,184,640]{2,1,0:T(8,128)(2,1)S(1)}, bf16[2,184,640]{2,1,0:T(8,128)(2,1)S(1)}, u32[]{:S(2)}, u32[]{:S(2)}) collective-permute-start(bf16[2,184,640]{2,1,0:T(8,128)(2,1)S(1)} %collective-permute-done.14.refs_2_), channel_id=1, source_target_pairs={{0,4},{2,6},{4,0},{6,2},{8,12},{10,14},{12,8},{14,10},{16,20},{18,... | collective-permute-start | bytes 1413128 | tf_op jit(solution)/shard_map/ppermute | solution.py:344
  49.0 21.8 %collective-permute-start.20 = (bf16[2,184,640]{2,1,0:T(8,128)(2,1)S(1)}, bf16[2,184,640]{2,1,0:T(8,128)(2,1)S(1)}, u32[]{:S(2)}, u32[]{:S(2)}) collective-permute-start(bf16[2,184,640]{2,1,0:T(8,128)(2,1)S(1)} %get-tuple-element.68), channel_id=1, source_target_pairs={{0,3},{1,2},{2,1},{3,0},{4,7},{5,6},{6,5},{7,4},{8,11},{9,10},{10,... | collective-permute-start | bytes 1413128 | tf_op jit(solution)/shard_map/ppermute | solution.py:344
  56.5 20.9 %collective-permute-start.17 = (bf16[2,184,640]{2,1,0:T(8,128)(2,1)S(1)}, bf16[2,184,640]{2,1,0:T(8,128)(2,1)S(1)}, u32[]{:S(2)}, u32[]{:S(2)}) collective-permute-start(bf16[2,184,640]{2,1,0:T(8,128)(2,1)S(1)} %collective-permute-done.15.refs_3_), channel_id=1, source_target_pairs={{0,8},{2,10},{4,28},{6,30},{8,16},{10,18},{12,4},{14,6},{16,24},{1... | collective-permute-start | bytes 1413128 | tf_op jit(solution)/shard_map/ppermute | solution.py:344
  56.5 20.9 %collective-permute-start.21 = (bf16[2,184,640]{2,1,0:T(8,128)(2,1)S(1)}, bf16[2,184,640]{2,1,0:T(8,128)(2,1)S(1)}, u32[]{:S(2)}, u32[]{:S(2)}) collective-permute-start(bf16[2,184,640]{2,1,0:T(8,128)(2,1)S(1)} %collective-permute-done.19.refs_1_), channel_id=1, source_target_pairs={{0,4},{2,6},{4,0},{6,2},{8,12},{10,14},{12,8},{14,10},{16,20},{18,... | collective-permute-start | bytes 1413128 | tf_op jit(solution)/shard_map/ppermute | solution.py:344
  66.6 15.5 %collective-permute-start.18 = (bf16[2,184,640]{2,1,0:T(8,128)(2,1)S(1)}, bf16[2,184,640]{2,1,0:T(8,128)(2,1)S(1)}, u32[]{:S(2)}, u32[]{:S(2)}) collective-permute-start(bf16[2,184,640]{2,1,0:T(8,128)(2,1)S(1)} %collective-permute-done.16.refs_4_), channel_id=1, source_target_pairs={{0,8},{2,10},{4,28},{6,30},{8,16},{10,18},{12,4},{14,6},{16,24},{1... | collective-permute-start | bytes 1413128 | tf_op jit(solution)/shard_map/ppermute | solution.py:344
  66.6 8.0 %copy-start.2 = (bf16[1,184,640]{2,1,0:T(8,128)(2,1)S(1)}, bf16[1,184,640]{2,1,0:T(8,128)(2,1)}, u32[]{:S(2)}) copy-start(bf16[1,184,640]{2,1,0:T(8,128)(2,1)} %copy-done.1) | copy-start | bytes 706564
  66.6 8.0 %copy-start.4 = (bf16[1,184,640]{2,1,0:T(8,128)(2,1)S(1)}, bf16[1,184,640]{2,1,0:T(8,128)(2,1)}, u32[]{:S(2)}) copy-start(bf16[1,184,640]{2,1,0:T(8,128)(2,1)} %copy-done.3) | copy-start | bytes 706564
  66.6 8.0 %copy-start.6 = (bf16[1,184,640]{2,1,0:T(8,128)(2,1)S(1)}, bf16[1,184,640]{2,1,0:T(8,128)(2,1)}, u32[]{:S(2)}) copy-start(bf16[1,184,640]{2,1,0:T(8,128)(2,1)} %copy-done.5) | copy-start | bytes 706564
  70.9 15.9 %collective-permute-start.22 = (bf16[2,184,640]{2,1,0:T(8,128)(2,1)S(1)}, bf16[2,184,640]{2,1,0:T(8,128)(2,1)S(1)}, u32[]{:S(2)}, u32[]{:S(2)}) collective-permute-start(bf16[2,184,640]{2,1,0:T(8,128)(2,1)S(1)} %collective-permute-done.20.refs_2_), channel_id=1, source_target_pairs={{0,4},{2,6},{4,0},{6,2},{8,12},{10,14},{12,8},{14,10},{16,20},{18,... | collective-permute-start | bytes 1413128 | tf_op jit(solution)/shard_map/ppermute | solution.py:344
  77.2 32.9 %collective-permute-start.7 = (bf16[1,184,640]{2,1,0:T(8,128)(2,1)S(1)}, bf16[1,184,640]{2,1,0:T(8,128)(2,1)S(1)}, u32[]{:S(2)}, u32[]{:S(2)}) collective-permute-start(bf16[1,184,640]{2,1,0:T(8,128)(2,1)S(1)} %get-tuple-element.51), channel_id=1, source_target_pairs={{0,4},{2,6},{4,0},{6,2},{8,12},{10,14},{12,8},{14,10},{16,20},{18,... | collective-permute-start | bytes 706568 | tf_op jit(solution)/shard_map/ppermute | solution.py:344
  77.4 33.3 %collective-permute-start.26 = (bf16[1,184,640]{2,1,0:T(8,128)(2,1)S(1)}, bf16[1,184,640]{2,1,0:T(8,128)(2,1)S(1)}, u32[]{:S(2)}, u32[]{:S(2)}) collective-permute-start(bf16[1,184,640]{2,1,0:T(8,128)(2,1)S(1)} %get-tuple-element.77), channel_id=1, source_target_pairs={{0,6},{2,4},{4,2},{6,0},{8,14},{10,12},{12,10},{14,8},{16,22},{18,... | collective-permute-start | bytes 706568 | tf_op jit(solution)/shard_map/ppermute | solution.py:344
  77.4 34.4 %collective-permute-start.27 = (bf16[2,184,640]{2,1,0:T(8,128)(2,1)S(1)}, bf16[2,184,640]{2,1,0:T(8,128)(2,1)S(1)}, u32[]{:S(2)}, u32[]{:S(2)}) collective-permute-start(bf16[2,184,640]{2,1,0:T(8,128)(2,1)S(1)} %get-tuple-element.78), channel_id=1, source_target_pairs={{0,2},{2,0},{4,6},{6,4},{8,10},{10,8},{12,14},{14,12},{16,18},{18,... | collective-permute-start | bytes 1413128 | tf_op jit(solution)/shard_map/ppermute | solution.py:344
  82.1 15.5 %collective-permute-start.23 = (bf16[2,184,640]{2,1,0:T(8,128)(2,1)S(1)}, bf16[2,184,640]{2,1,0:T(8,128)(2,1)S(1)}, u32[]{:S(2)}, u32[]{:S(2)}) collective-permute-start(bf16[2,184,640]{2,1,0:T(8,128)(2,1)S(1)} %collective-permute-done.21.refs_3_), channel_id=1, source_target_pairs={{0,8},{2,10},{4,28},{6,30},{8,16},{10,18},{12,4},{14,6},{16,24},{1... | collective-permute-start | bytes 1413128 | tf_op jit(solution)/shard_map/ppermute | solution.py:344
  86.8 18.6 %collective-permute-start.24 = (bf16[2,184,640]{2,1,0:T(8,128)(2,1)S(1)}, bf16[2,184,640]{2,1,0:T(8,128)(2,1)S(1)}, u32[]{:S(2)}, u32[]{:S(2)}) collective-permute-start(bf16[2,184,640]{2,1,0:T(8,128)(2,1)S(1)} %collective-permute-done.22.refs_4_), channel_id=1, source_target_pairs={{0,8},{2,10},{4,28},{6,30},{8,16},{10,18},{12,4},{14,6},{16,24},{1... | collective-permute-start | bytes 1413128 | tf_op jit(solution)/shard_map/ppermute | solution.py:344
  97.6 14.2 %collective-permute-start.28 = (bf16[2,184,640]{2,1,0:T(8,128)(2,1)S(1)}, bf16[2,184,640]{2,1,0:T(8,128)(2,1)S(1)}, u32[]{:S(2)}, u32[]{:S(2)}) collective-permute-start(bf16[2,184,640]{2,1,0:T(8,128)(2,1)S(1)} %get-tuple-element.79), channel_id=1, source_target_pairs={{0,2},{2,0},{4,6},{6,4},{8,10},{10,8},{12,14},{14,12},{16,18},{18,... | collective-permute-start | bytes 1413128 | tf_op jit(solution)/shard_map/ppermute | solution.py:344
  107.1 4.7 %collective-permute-start.29 = (bf16[2,184,640]{2,1,0:T(8,128)(2,1)S(1)}, bf16[2,184,640]{2,1,0:T(8,128)(2,1)S(1)}, u32[]{:S(2)}, u32[]{:S(2)}) collective-permute-start(bf16[2,184,640]{2,1,0:T(8,128)(2,1)S(1)} %get-tuple-element.80), channel_id=1, source_target_pairs={{0,2},{2,0},{4,6},{6,4},{8,10},{10,8},{12,14},{14,12},{16,18},{18,... | collective-permute-start | bytes 1413128 | tf_op jit(solution)/shard_map/ppermute | solution.py:344
  110.1 1.7 %collective-permute-start.25 = (bf16[1,184,640]{2,1,0:T(8,128)(2,1)S(1)}, bf16[1,184,640]{2,1,0:T(8,128)(2,1)S(1)}, u32[]{:S(2)}, u32[]{:S(2)}) collective-permute-start(bf16[1,184,640]{2,1,0:T(8,128)(2,1)S(1)} %get-tuple-element.76), channel_id=1, source_target_pairs={{0,2},{2,0},{4,6},{6,4},{8,10},{10,8},{12,14},{14,12},{16,18},{18,... | collective-permute-start | bytes 706568 | tf_op jit(solution)/shard_map/ppermute | solution.py:344

commit v7 on v6

--- a/solution.py
+++ b/solution.py
@@ -8,8 +8,6 @@
 from jax.sharding import PartitionSpec as P
 
 VMEM_LIMIT = 16 * 1024 * 1024
-TAKE_VMEM_LIMIT = 50 * 1024 * 1024
-AHEAD = 4
 SMEM_SPEC = pl.BlockSpec(memory_space=pltpu.SMEM)
 VMEM_SPEC = pl.BlockSpec(memory_space=pltpu.VMEM)
 HBM_SPEC = pl.BlockSpec(memory_space=pltpu.HBM)
@@ -18,10 +16,10 @@
 PARTS = [("k", 2), ("c", 2), ("y", 0), ("y", 1), ("y", 2), ("y", 3)]
 FILTERS = ((2, 3), (4, 5), (6, 7))
 WAITS = {
-    ("x", 1): [("p", 1), ("q", 0)],
-    ("x", 2): [("x", 0), ("q", 1), ("q", 0)],
+    ("x", 1): [("q", 0)],
+    ("x", 2): [("x", 0), ("q", 1)],
     ("x", 3): [("x", 1), ("q", 2)],
-    ("x", 4): [("x", 2), ("q", 3), ("q", 2)],
+    ("x", 4): [("x", 2), ("q", 3), ("x", 1), ("t", 1)],
     ("x", 5): [("x", 3), ("z", 0), ("f", 0)],
     ("q", 3): [("q", 1)],
     ("z", 0): [("q", 2)],
@@ -29,7 +27,6 @@
     ("z", 2): [("z", 0)],
     ("z", 3): [("z", 1)],
     ("z", 4): [("z", 2)],
-    ("z", 5): [("z", 3)],
     ("y", 2): [("y", 0)],
     ("y", 3): [("y", 1)],
 }
@@ -61,24 +58,18 @@
     bands = []
     for start in range(0, up_to(lon_dev, step), step):
         taps = pltpu.roll(line, line.shape[1] + start - at, 1)
-        taps = jnp.concatenate([taps[:, : lanes - 128], taps[:, -128:]], axis=1)[:1]
-        band = pltpu.roll(jnp.broadcast_to(taps, (step, lanes)), 0, 1, stride=1, stride_axis=0)
+        taps = jnp.concatenate([taps[:, : lanes - 128], taps[:, -128:]], axis=1)
+        band = pltpu.roll(jnp.concatenate([taps] * (step // 8), axis=0), 0, 1, stride=1, stride_axis=0)
         bands.append(band[:, :width].astype(jnp.bfloat16))
     return jnp.concatenate(bands, axis=0)
 
 
 def take_kernel(chunks, lat_dev, block, slot_ref, place_ref, fields_ref, *refs):
     outs = refs[: len(chunks)]
-    rows_ref, slots_ref, home_ref, take_ref, panel_ref, sems = refs[len(chunks) :]
+    rows_ref, slots_ref, home_ref, take_ref = refs[len(chunks) :]
     lon_dev, _, channels = fields_ref.shape
     half, quarter = lat_dev // 2, lat_dev // 4
     starts = list(range(0, lon_dev, block))
-    copies = []
-    for n, start in enumerate(starts):
-        window = pl.ds(start, min(block, lon_dev - start))
-        copies.append(pltpu.make_async_copy(fields_ref.at[window], panel_ref.at[window], sems.at[n]))
-    for copy in copies[:AHEAD]:
-        copy.start()
     band, core, x = place_ref[0], place_ref[1], place_ref[2]
 
     def at(n):
@@ -122,13 +113,10 @@
         return jnp.concatenate(strips, axis=0).astype(jnp.bfloat16)
 
     take_ref[...] = selector(block, block)
-    for n, start in enumerate(starts):
-        copies[n].wait()
-        if n + AHEAD < len(copies):
-            copies[n + AHEAD].start()
+    for start in starts:
         lon_in = min(block, lon_dev - start)
         lon_out = min(block, outs[0].shape[1] - start)
-        panel = panel_ref[start : start + lon_in].reshape(lon_in * lat_dev, channels)
+        panel = fields_ref[start : start + lon_in].reshape(lon_in * lat_dev, channels)
         take = take_ref[...] if (lon_in, lon_out) == (block, block) else selector(lon_in, lon_out)
         taken = jnp.dot(take, panel, preferred_element_type=jnp.float32).astype(jnp.bfloat16)
         place = 0
@@ -146,15 +134,13 @@
     result = pl.pallas_call(
         functools.partial(take_kernel, chunks, lat_dev, block),
         out_shape=[jax.ShapeDtypeStruct((n, padded, channels), fields.dtype) for n in chunks] + [ints, ints],
-        in_specs=[SMEM_SPEC, SMEM_SPEC, HBM_SPEC],
+        in_specs=[SMEM_SPEC, SMEM_SPEC, VMEM_SPEC],
         out_specs=[VMEM_SPEC] * len(chunks) + [SMEM_SPEC, SMEM_SPEC],
         scratch_shapes=[
             pltpu.SMEM((lat_dev,), jnp.int32),
             pltpu.VMEM((block * lat_dev, block * lat_dev), jnp.bfloat16),
-            pltpu.VMEM(fields.shape, fields.dtype),
-            pltpu.SemaphoreType.DMA((pl.cdiv(lon_dev, block),)),
         ],
-        compiler_params=pltpu.CompilerParams(vmem_limit_bytes=TAKE_VMEM_LIMIT),
+        compiler_params=pltpu.CompilerParams(vmem_limit_bytes=VMEM_LIMIT),
         cost_estimate=pl.CostEstimate(
             flops=2 * fields.size * block * lat_dev, bytes_accessed=4 * fields.size, transcendentals=0
         ),
@@ -226,9 +212,9 @@
     if phase == "early":
         ins, (total_ref, block_ref) = refs[:-2], refs[-2:]
     elif phase == "late":
-        ins, (out_own, out_other, total_ref) = refs[:-3], refs[-3:]
+        ins, (out_own, out_other) = refs[:-2], refs[-2:]
     else:
-        ins, (out_own, out_other, total_ref, block_ref) = refs[:-4], refs[-4:]
+        ins, (out_own, out_other, block_ref) = refs[:-3], refs[-3:]
     padded, channels = ins[0].shape[1:]
 
     def both(first, second):
@@ -240,10 +226,11 @@
         def times(offset, panel):
             return jnp.dot(block_ref[n, 2 + offset], panel, preferred_element_type=jnp.float32)[:padded]
 
-        def add(which, offset, panel):
-            lanes = pl.ds(which * channels, channels)
-            total_ref[n, :, lanes] += times(offset, panel[...])
-
+        def halves(first, second):
+            return jnp.concatenate([first, second], axis=1)
+
+        nothing = jnp.zeros((padded, channels), jnp.float32)
+        same = side == along
         if phase != "late":
             own, other, x_own, x_other = panels[:4]
             line = jnp.broadcast_to(line_ref[pl.ds(rows_ref[base + n], 1), :], (8, line_ref.shape[1]))
@@ -253,17 +240,19 @@
             total = here.astype(jnp.float32) + times(0, here)
             total += times(2 * along, both(x_own, x_other))
             total += jnp.concatenate([times(side, other[...]), times(-side, own[...])], axis=1)
-            total_ref[n] = total
-            pl.when(side == along)(functools.partial(add, 1, along, x_own))
-            pl.when(side != along)(functools.partial(add, 0, along, x_other))
+            more = times(along, jnp.where(same, x_own[...], x_other[...]))
+            total += halves(jnp.where(same, nothing, more), jnp.where(same, more, nothing))
+            if phase == "early":
+                total_ref[n] = total
         if phase != "early":
             z_own, z_other = panels[-2:]
-            before = total_in[n] if phase == "late" else total_ref[n]
-            total_ref[n] = before + times(-2 * along, both(z_own, z_other))
-            pl.when(side == along)(functools.partial(add, 0, -along, z_other))
-            pl.when(side != along)(functools.partial(add, 1, -along, z_own))
-            out_own[n] = total_ref[n, :, :channels].astype(out_own.dtype)
-            out_other[n] = total_ref[n, :, channels:].astype(out_other.dtype)
+            if phase == "late":
+                total = total_in[n]
+            total += times(-2 * along, both(z_own, z_other))
+            more = times(-along, jnp.where(same, z_other[...], z_own[...]))
+            total += halves(jnp.where(same, more, nothing), jnp.where(same, nothing, more))
+            out_own[n] = total[:, :channels].astype(out_own.dtype)
+            out_other[n] = total[:, channels:].astype(out_other.dtype)
 
 
 def filter_pair(rows, signs, lines, places, base, lon_dev, phase="whole", early=()):
@@ -286,9 +275,9 @@
     if phase == "early":
         outs, scratch = [jax.ShapeDtypeStruct(*total), jax.ShapeDtypeStruct(*block)], []
     elif phase == "late":
-        outs, scratch = [out, out], [pltpu.VMEM(*total)]
+        outs, scratch = [out, out], []
     else:
-        outs, scratch = [out, out], [pltpu.VMEM(*total), pltpu.VMEM(*block)]
+        outs, scratch = [out, out], [pltpu.VMEM(*block)]
     weight = {"whole": 10, "early": 7, "late": 3}[phase]
     return pl.pallas_call(
         functools.partial(pair_kernel, lon_dev, base, tuple(plan), phase),

time: 115 us -> 110 us (0.957)
  local copies, waits for them, and re-layouts: 3.63 us -> 14.1 us
  waiting for transfers between devices: 51.4 us -> 43.1 us
  Pallas kernels: 26.6 us -> 19.5 us
    unnamed x16 -> x40, local copies, waits for them, and re-layouts: 2.73 us -> 12.2 us
    ppermute x30, waiting for transfers between devices: 51.4 us -> 43.1 us  [moved(): return lax.ppermute(operand, axes, pairs)]
    pallas_call x6, Pallas kernels: 17.9 us -> 13.7 us  [filter_pair(): pl.pallas_call(functools.partial(pair_kernel, lon_dev, base, tuple(plan),...]
    pallas_call x1, Pallas kernels: 5.92 us -> 3.11 us  [take_rows(): pl.pallas_call(functools.partial(take_kernel, chunks, lat_dev, block), ou...]
  transfers between devices with their start and end apart: 30 -> 30, of which waited for: 14 -> 16; matrix products, arithmetic and copies ran while one was open for 1% -> 2% of each run, Pallas kernels for 16% -> 12%
where the time goes in v7:
time: 110 us
  waiting for transfers between devices  43.1 us (39%)
  starting transfers between devices  31.6 us (29%)
  Pallas kernels  19.5 us (18%)
  local copies, waits for them, and re-layouts  14.1 us (13%)
    ppermute x30, waiting for transfers between devices, moved(): return lax.ppermute(operand, axes, pairs)  43.1 us
    ppermute x30, starting transfers between devices, moved(): return lax.ppermute(operand, axes, pairs)  31.6 us
    pallas_call x6, Pallas kernels, filter_pair(): pl.pallas_call(functools.partial(pair_kernel, lon_dev, base, tuple(plan),...  13.7 us
    unnamed x40, local copies, waits for them, and re-layouts  12.2 us
    pallas_call x1, Pallas kernels, take_rows(): pl.pallas_call(functools.partial(take_kernel, chunks, lat_dev, block), ou...  3.11 us
    pallas_call x1, Pallas kernels, put_rows(): pl.pallas_call(functools.partial(put_kernel, counts, lat_dev, block), out...  2.78 us
  transfers between devices with their start and end apart: 30, of which 16 were waited for; matrix products, arithmetic and copies ran while one was open for 2% of the time, Pallas kernels for 12%

profile of v7, /device:TPU:0, one launch (start us, length us, event | category | flops | bytes accessed | tf_op | source)
XLA Modules:
  0.0 109.6 jit_solution(9790385240373614019)
XLA Ops:
  0.1 2.0 %copy-done = bf16[16,180,640]{2,0,1:T(8,128)(2,1)S(1)} copy-done((bf16[16,180,640]{2,0,1:T(8,128)(2,1)S(1)}, bf16[16,180,640]{2,0,1:T(8,128)(2,1)}, u32[]{:S(2)}) %copy-start) | copy-done | bytes 3686424
  2.1 0.7 copy-done.1
  2.8 3.1 %take_rows.1 = (bf16[1,184,640]{2,1,0:T(8,128)(2,1)S(1)}, bf16[1,184,640]{2,1,0:T(8,128)(2,1)S(1)}, bf16[2,184,640]{2,1,0:T(8,128)(2,1)S(1)}, bf16[1,184,640]{2,...) custom-call(s32[32]{0:T(128)S(1)} %copy-done.1, ...), custom_call_target="tpu_custom_call" | custom-call | flops 943718400 | bytes 7372800 | tf_op jit(solution)/shard_map/take_rows/pallas_call | solution.py:134
  5.9 0.5 collective-permute-start.8
  6.5 2.9 %collective-permute-start.1 = (bf16[1,184,640]{2,1,0:T(8,128)(2,1)S(1)}, bf16[1,184,640]{2,1,0:T(8,128)(2,1)S(1)}, u32[]{:S(2)}, u32[]{:S(2)}) collective-permute-start(bf16[1,184,640]{2,1,0:T(8,128)(2,1)S(1)} %get-tuple-element.46), channel_id=1, source_target_pairs={{0,4},{2,6},{4,0},{6,2},{8,12},{10,14},{12,8},{14,10},{16,20},{18,... | collective-permute-start | bytes 706568 | tf_op jit(solution)/shard_map/ppermute | solution.py:333
  9.4 3.6 %collective-permute-start.6 = (bf16[1,184,640]{2,1,0:T(8,128)(2,1)S(1)}, bf16[1,184,640]{2,1,0:T(8,128)(2,1)S(1)}, u32[]{:S(2)}, u32[]{:S(2)}) collective-permute-start(bf16[1,184,640]{2,1,0:T(8,128)(2,1)S(1)} %get-tuple-element.44.refs_1_.refs_5_), channel_id=1, source_target_pairs={{0,24},{2,26},{4,12},{6,14},{8,0},{10,2},{12,20},{14,22},{16,8},{1... | collective-permute-start | bytes 706568 | tf_op jit(solution)/shard_map/ppermute | solution.py:333
  13.0 0.5 collective-permute-start.4
  13.5 0.7 copy-done.2
  14.2 1.4 %collective-permute-done.1.refs_3_.refs_1_ = bf16[1,184,640]{2,1,0:T(8,128)(2,1)S(1)} collective-permute-done((bf16[1,184,640]{2,1,0:T(8,128)(2,1)S(1)}, bf16[1,184,640]{2,1,0:T(8,128)(2,1)S(1)}, u32[]{:S(2)}, u32[]{:S(2)}) %collective-permute-start.1) | collective-permute-done | bytes 235552 | tf_op jit(solution)/shard_map/ppermute | solution.py:333
  15.5 2.6 %collective-permute-start.3 = (bf16[1,184,640]{2,1,0:T(8,128)(2,1)S(1)}, bf16[1,184,640]{2,1,0:T(8,128)(2,1)S(1)}, u32[]{:S(2)}, u32[]{:S(2)}) collective-permute-start(bf16[1,184,640]{2,1,0:T(8,128)(2,1)S(1)} %collective-permute-done.1.refs_3_.refs_1_), channel_id=1, source_target_pairs={{0,8},{2,10},{4,28},{6,30},{8,16},{10,18},{12,4},{14,6},{16,24},{1... | collective-permute-start | bytes 706568 | tf_op jit(solution)/shard_map/ppermute | solution.py:333
  18.1 0.7 copy-done.5
  18.8 0.4 collective-permute-done.6.refs_3_
  19.2 0.7 copy-done.15
  19.9 3.1 %collective-permute-start.9 = (bf16[2,184,640]{2,1,0:T(8,128)(2,1)S(1)}, bf16[2,184,640]{2,1,0:T(8,128)(2,1)}, u32[]{:S(2)}, u32[]{:S(2)}) collective-permute-start(bf16[2,184,640]{2,1,0:T(8,128)(2,1)S(1)} %get-tuple-element.51.refs_1_), channel_id=1, source_target_pairs={{0,4},{2,6},{4,0},{6,2},{8,12},{10,14},{12,8},{14,10},{16,20},{18,... | collective-permute-start | bytes 1413128 | tf_op jit(solution)/shard_map/ppermute | solution.py:333
  23.0 1.5 %collective-permute-start.13 = (bf16[2,184,640]{2,1,0:T(8,128)(2,1)S(1)}, bf16[2,184,640]{2,1,0:T(8,128)(2,1)S(1)}, u32[]{:S(2)}, u32[]{:S(2)}) collective-permute-start(bf16[2,184,640]{2,1,0:T(8,128)(2,1)S(1)} %get-tuple-element.57), channel_id=1, source_target_pairs={{0,1},{1,0},{2,3},{3,2},{4,5},{5,4},{6,7},{7,6},{8,9},{9,8},{10,11... | collective-permute-start | bytes 1413128 | tf_op jit(solution)/shard_map/ppermute | solution.py:333
  24.5 0.7 copy-done.17
  25.2 3.7 %collective-permute-done.3.refs_5_ = bf16[1,184,640]{2,1,0:T(8,128)(2,1)S(1)} collective-permute-done((bf16[1,184,640]{2,1,0:T(8,128)(2,1)S(1)}, bf16[1,184,640]{2,1,0:T(8,128)(2,1)S(1)}, u32[]{:S(2)}, u32[]{:S(2)}) %collective-permute-start.3) | collective-permute-done | bytes 235552 | tf_op jit(solution)/shard_map/ppermute | solution.py:333
  29.0 0.7 copy-done.11
  29.7 1.6 %collective-permute-start.5 = (bf16[1,184,640]{2,1,0:T(8,128)(2,1)S(1)}, bf16[1,184,640]{2,1,0:T(8,128)(2,1)S(1)}, u32[]{:S(2)}, u32[]{:S(2)}) collective-permute-start(bf16[1,184,640]{2,1,0:T(8,128)(2,1)S(1)} %collective-permute-done.2.refs_4_.refs_2_), channel_id=1, source_target_pairs={{0,8},{2,10},{4,28},{6,30},{8,16},{10,18},{12,4},{14,6},{16,24},{1... | collective-permute-start | bytes 706568 | tf_op jit(solution)/shard_map/ppermute | solution.py:333
  31.3 0.7 copy-done.8
  32.0 0.9 fusion.3
  32.9 1.9 %collective-permute-done.9.refs_3_ = bf16[2,184,640]{2,1,0:T(8,128)(2,1)} collective-permute-done((bf16[2,184,640]{2,1,0:T(8,128)(2,1)S(1)}, bf16[2,184,640]{2,1,0:T(8,128)(2,1)}, u32[]{:S(2)}, u32[]{:S(2)}) %collective-permute-start.9) | collective-permute-done | bytes 471072 | tf_op jit(solution)/shard_map/ppermute | solution.py:333
  34.8 0.1 collective-permute-start.11
  34.9 1.8 %collective-permute-done.13.refs_1_ = bf16[2,184,640]{2,1,0:T(8,128)(2,1)S(1)} collective-permute-done((bf16[2,184,640]{2,1,0:T(8,128)(2,1)S(1)}, bf16[2,184,640]{2,1,0:T(8,128)(2,1)S(1)}, u32[]{:S(2)}, u32[]{:S(2)}) %collective-permute-start.13) | collective-permute-done | bytes 471072 | tf_op jit(solution)/shard_map/ppermute | solution.py:333
  36.7 1.4 %collective-permute-start.15 = (bf16[2,184,640]{2,1,0:T(8,128)(2,1)S(1)}, bf16[2,184,640]{2,1,0:T(8,128)(2,1)S(1)}, u32[]{:S(2)}, u32[]{:S(2)}) collective-permute-start(bf16[2,184,640]{2,1,0:T(8,128)(2,1)S(1)} %collective-permute-done.13.refs_1_), channel_id=1, source_target_pairs={{0,4},{2,6},{4,0},{6,2},{8,12},{10,14},{12,8},{14,10},{16,20},{18,... | collective-permute-start | bytes 1413128 | tf_op jit(solution)/shard_map/ppermute | solution.py:333
  38.1 2.0 %collective-permute-done.5.refs_6_ = bf16[1,184,640]{2,1,0:T(8,128)(2,1)S(1)} collective-permute-done((bf16[1,184,640]{2,1,0:T(8,128)(2,1)S(1)}, bf16[1,184,640]{2,1,0:T(8,128)(2,1)S(1)}, u32[]{:S(2)}, u32[]{:S(2)}) %collective-permute-start.5) | collective-permute-done | bytes 235552 | tf_op jit(solution)/shard_map/ppermute | solution.py:333
  40.1 0.7 copy-done.13
  40.8 1.5 %collective-permute-start.19 = (bf16[2,184,640]{2,1,0:T(8,128)(2,1)S(1)}, bf16[2,184,640]{2,1,0:T(8,128)(2,1)}, u32[]{:S(2)}, u32[]{:S(2)}) collective-permute-start(bf16[2,184,640]{2,1,0:T(8,128)(2,1)S(1)} %get-tuple-element.65), channel_id=1, source_target_pairs={{0,1},{1,0},{2,3},{3,2},{4,5},{5,4},{6,7},{7,6},{8,9},{9,8},{10,11... | collective-permute-start | bytes 1413128 | tf_op jit(solution)/shard_map/ppermute | solution.py:333
  42.3 2.6 %collective-permute-done.10.refs_4_ = bf16[2,184,640]{2,1,0:T(8,128)(2,1)} collective-permute-done((bf16[2,184,640]{2,1,0:T(8,128)(2,1)S(1)}, bf16[2,184,640]{2,1,0:T(8,128)(2,1)}, u32[]{:S(2)}, u32[]{:S(2)}) %collective-permute-start.10) | collective-permute-done | bytes 471072 | tf_op jit(solution)/shard_map/ppermute | solution.py:333
  45.0 3.2 %collective-permute-start.16 = (bf16[2,184,640]{2,1,0:T(8,128)(2,1)S(1)}, bf16[2,184,640]{2,1,0:T(8,128)(2,1)}, u32[]{:S(2)}, u32[]{:S(2)}) collective-permute-start(bf16[2,184,640]{2,1,0:T(8,128)(2,1)S(1)} %collective-permute-done.14.refs_2_), channel_id=1, source_target_pairs={{0,4},{2,6},{4,0},{6,2},{8,12},{10,14},{12,8},{14,10},{16,20},{18,... | collective-permute-start | bytes 1413128 | tf_op jit(solution)/shard_map/ppermute | solution.py:333
  48.2 0.7 convert_select_fusion
  49.0 0.9 pad.4.refs_0_
  50.0 0.9 copy-done.3
  50.9 0.9 copy-done.6
  51.8 0.9 copy-done.9
  52.8 0.9 copy-done.16
  53.7 0.9 copy-done.18
  54.7 1.7 %filter_whole.5 = (bf16[1,184,640]{2,1,0:T(8,128)(2,1)S(1)}, bf16[1,184,640]{2,1,0:T(8,128)(2,1)S(1)}) custom-call(s32[16]{0:T(128)S(1)} %get-tuple-element.43.rows_ref, s32[2]{0:T(128)S(1)} %pad_add_fusion.1.sign_ref, f32[32,1152]{1,0:T(8,128)S(1)} %pad.4.refs_0_, bf16[1,184,640]{2,1,0:T(8,128)(2,1)S(1)} %copy-done.6, bf16[1,184,640]{2,1,0:T(8,128)(2,1)S(1)} %copy-done.9, ...), custom_call_target="tpu_custom_call" | custom-call | flops 3019898880 | bytes 1884160 | tf_op jit(solution)/shard_map/filter_whole/pallas_call | solution.py:282
  56.4 0.8 collective-permute-start.17
  57.2 1.8 %collective-permute-start.21 = (bf16[2,184,640]{2,1,0:T(8,128)(2,1)}, bf16[2,184,640]{2,1,0:T(8,128)(2,1)S(1)}, u32[]{:S(2)}, u32[]{:S(2)}) collective-permute-start(bf16[2,184,640]{2,1,0:T(8,128)(2,1)} %collective-permute-done.19.refs_1_), channel_id=1, source_target_pairs={{0,4},{2,6},{4,0},{6,2},{8,12},{10,14},{12,8},{14,10},{16,20},{18,... | collective-permute-start | bytes 1413128 | tf_op jit(solution)/shard_map/ppermute | solution.py:333
  59.0 0.3 collective-permute-done.12.refs_6_
  59.3 4.0 %collective-permute-done.16.refs_4_ = bf16[2,184,640]{2,1,0:T(8,128)(2,1)} collective-permute-done((bf16[2,184,640]{2,1,0:T(8,128)(2,1)S(1)}, bf16[2,184,640]{2,1,0:T(8,128)(2,1)}, u32[]{:S(2)}, u32[]{:S(2)}) %collective-permute-start.16) | collective-permute-done | bytes 471072 | tf_op jit(solution)/shard_map/ppermute | solution.py:333
  63.3 0.3 collective-permute-start.18
  63.6 3.4 %filter_whole.6 = (bf16[2,184,640]{2,1,0:T(8,128)(2,1)S(1)}, bf16[2,184,640]{2,1,0:T(8,128)(2,1)S(1)}) custom-call(s32[16]{0:T(128)S(1)} %get-tuple-element.43.rows_ref, s32[2]{0:T(128)S(1)} %pad_add_fusion.1.sign_ref, f32[32,1152]{1,0:T(8,128)S(1)} %pad.4.refs_0_, bf16[2,184,640]{2,1,0:T(8,128)(2,1)S(1)} %get-tuple-element.51.refs_1_, ...), custom_call_target="tpu_custom_call" | custom-call | flops 6039797760 | bytes 3768320 | tf_op jit(solution)/shard_map/filter_whole/pallas_call | solution.py:282
  67.0 2.4 %collective-permute-done.20.refs_2_ = bf16[2,184,640]{2,1,0:T(8,128)(2,1)S(1)} collective-permute-done((bf16[2,184,640]{2,1,0:T(8,128)(2,1)S(1)}, bf16[2,184,640]{2,1,0:T(8,128)(2,1)S(1)}, u32[]{:S(2)}, u32[]{:S(2)}) %collective-permute-start.20) | collective-permute-done | bytes 471072 | tf_op jit(solution)/shard_map/ppermute | solution.py:333
  69.4 1.8 %collective-permute-start.22 = (bf16[2,184,640]{2,1,0:T(8,128)(2,1)S(1)}, bf16[2,184,640]{2,1,0:T(8,128)(2,1)S(1)}, u32[]{:S(2)}, u32[]{:S(2)}) collective-permute-start(bf16[2,184,640]{2,1,0:T(8,128)(2,1)S(1)} %collective-permute-done.20.refs_2_), channel_id=1, source_target_pairs={{0,4},{2,6},{4,0},{6,2},{8,12},{10,14},{12,8},{14,10},{16,20},{18,... | collective-permute-start | bytes 1413128 | tf_op jit(solution)/shard_map/ppermute | solution.py:333
  71.2 0.3 collective-permute-start.7
  71.5 1.2 %collective-permute-done.21.refs_3_ = bf16[2,184,640]{2,1,0:T(8,128)(2,1)S(1)} collective-permute-done((bf16[2,184,640]{2,1,0:T(8,128)(2,1)}, bf16[2,184,640]{2,1,0:T(8,128)(2,1)S(1)}, u32[]{:S(2)}, u32[]{:S(2)}) %collective-permute-start.21) | collective-permute-done | bytes 471072 | tf_op jit(solution)/shard_map/ppermute | solution.py:333
  72.6 0.2 collective-permute-start.23
  72.8 8.7 %collective-permute-done.18.refs_6_ = bf16[2,184,640]{2,1,0:T(8,128)(2,1)S(1)} collective-permute-done((bf16[2,184,640]{2,1,0:T(8,128)(2,1)}, bf16[2,184,640]{2,1,0:T(8,128)(2,1)S(1)}, u32[]{:S(2)}, u32[]{:S(2)}) %collective-permute-start.18) | collective-permute-done | bytes 471072 | tf_op jit(solution)/shard_map/ppermute | solution.py:333
  81.5 1.2 %collective-permute-start.27 = (bf16[2,184,640]{2,1,0:T(8,128)(2,1)S(1)}, bf16[2,184,640]{2,1,0:T(8,128)(2,1)S(1)}, u32[]{:S(2)}, u32[]{:S(2)}) collective-permute-start(bf16[2,184,640]{2,1,0:T(8,128)(2,1)S(1)} %get-tuple-element.76), channel_id=1, source_target_pairs={{0,2},{2,0},{4,6},{6,4},{8,10},{10,8},{12,14},{14,12},{16,18},{18,... | collective-permute-start | bytes 1413128 | tf_op jit(solution)/shard_map/ppermute | solution.py:333
  82.7 0.4 collective-permute-done.22.refs_4_
  83.0 0.7 collective-permute-start.24
  83.8 3.1 %filter_whole.7 = (bf16[2,184,640]{2,1,0:T(8,128)(2,1)S(1)}, bf16[2,184,640]{2,1,0:T(8,128)(2,1)S(1)}) custom-call(s32[16]{0:T(128)S(1)} %get-tuple-element.43.rows_ref, s32[2]{0:T(128)S(1)} %pad_add_fusion.1.sign_ref, f32[32,1152]{1,0:T(8,128)S(1)} %pad.4.refs_0_, bf16[2,184,640]{2,1,0:T(8,128)(2,1)S(1)} %collective-permute-done.13.refs_1_, ...), custom_call_target="tpu_custom_call" | custom-call | flops 6039797760 | bytes 3768320 | tf_op jit(solution)/shard_map/filter_whole/pallas_call | solution.py:282
  86.9 2.5 %filter_early.1 = (f32[2,184,1280]{2,1,0:T(8,128)S(1)}, bf16[2,5,192,184]{3,2,1,0:T(8,128)(2,1)S(1)}) custom-call(s32[16]{0:T(128)S(1)} %get-tuple-element.43.rows_ref, s32[2]{0:T(128)S(1)} %pad_add_fusion.1.sign_ref, f32[32,1152]{1,0:T(8,128)S(1)} %pad.4.refs_0_, bf16[2,184,640]{2,1,0:T(8,128)(2,1)} %collective-permute-done.19.refs_1_, ...), custom_call_target="tpu_custom_call" | custom-call | flops 4227858432 | bytes 3768320 | tf_op jit(solution)/shard_map/filter_early/pallas_call | solution.py:282
  89.5 2.1 %collective-permute-done.23.refs_2_ = bf16[2,184,640]{2,1,0:T(8,128)(2,1)S(1)} collective-permute-done((bf16[2,184,640]{2,1,0:T(8,128)(2,1)S(1)}, bf16[2,184,640]{2,1,0:T(8,128)(2,1)S(1)}, u32[]{:S(2)}, u32[]{:S(2)}) %collective-permute-start.23) | collective-permute-done | bytes 471072 | tf_op jit(solution)/shard_map/ppermute | solution.py:333
  91.6 1.2 %collective-permute-start.28 = (bf16[2,184,640]{2,1,0:T(8,128)(2,1)S(1)}, bf16[2,184,640]{2,1,0:T(8,128)(2,1)S(1)}, u32[]{:S(2)}, u32[]{:S(2)}) collective-permute-start(bf16[2,184,640]{2,1,0:T(8,128)(2,1)S(1)} %get-tuple-element.77), channel_id=1, source_target_pairs={{0,2},{2,0},{4,6},{6,4},{8,10},{10,8},{12,14},{14,12},{16,18},{18,... | collective-permute-start | bytes 1413128 | tf_op jit(solution)/shard_map/ppermute | solution.py:333
  92.8 8.9 %collective-permute-done.24.refs_3_ = bf16[2,184,640]{2,1,0:T(8,128)(2,1)S(1)} collective-permute-done((bf16[2,184,640]{2,1,0:T(8,128)(2,1)S(1)}, bf16[2,184,640]{2,1,0:T(8,128)(2,1)S(1)}, u32[]{:S(2)}, u32[]{:S(2)}) %collective-permute-start.24) | collective-permute-done | bytes 471072 | tf_op jit(solution)/shard_map/ppermute | solution.py:333
  101.7 1.2 %filter_late.1 = (bf16[2,184,640]{2,1,0:T(8,128)(2,1)S(1)}, bf16[2,184,640]{2,1,0:T(8,128)(2,1)S(1)}) custom-call(s32[16]{0:T(128)S(1)} %get-tuple-element.43.rows_ref, s32[2]{0:T(128)S(1)} %pad_add_fusion.1.sign_ref, f32[2,184,1280]{2,1,0:T(8,128)S(1)} %get-tuple-element.70.refs_0_, bf16[2,5,192,184]{3,2,1,0:T(8,128)(2,1)S(1)} %get-tuple-element.71.refs_1_, ...), custom_call_target="tpu_custom_call" | custom-call | flops 1811939328 | bytes 3768320 | tf_op jit(solution)/shard_map/filter_late/pallas_call | solution.py:282
  102.9 0.4 collective-permute-start.29
  103.4 1.7 %filter_whole.4 = (bf16[1,184,640]{2,1,0:T(8,128)(2,1)S(1)}, bf16[1,184,640]{2,1,0:T(8,128)(2,1)S(1)}) custom-call(s32[16]{0:T(128)S(1)} %get-tuple-element.43.rows_ref, s32[2]{0:T(128)S(1)} %pad_add_fusion.1.sign_ref, f32[32,1152]{1,0:T(8,128)S(1)} %pad.4.refs_0_, bf16[1,184,640]{2,1,0:T(8,128)(2,1)S(1)} %get-tuple-element.44.refs_1_.refs_5_, ...), custom_call_target="tpu_custom_call" | custom-call | flops 3019898880 | bytes 1884160 | tf_op jit(solution)/shard_map/filter_whole/pallas_call | solution.py:282
  105.1 0.2 collective-permute-start.25
  105.3 1.3 %collective-permute-done.25.refs_5_ = bf16[1,184,640]{2,1,0:T(8,128)(2,1)S(1)} collective-permute-done((bf16[1,184,640]{2,1,0:T(8,128)(2,1)S(1)}, bf16[1,184,640]{2,1,0:T(8,128)(2,1)S(1)}, u32[]{:S(2)}, u32[]{:S(2)}) %collective-permute-start.25) | collective-permute-done | bytes 235552 | tf_op jit(solution)/shard_map/ppermute | solution.py:333
  106.6 2.8 %put_rows.1 = bf16[180,16,640]{2,1,0:T(8,128)(2,1)} custom-call(s32[16]{0:T(128)S(1)} %get-tuple-element.42.slots_ref, bf16[1,184,640]{2,1,0:T(8,128)(2,1)S(1)} %get-tuple-element.49.refs_0_, bf16[1,184,640]{2,1,0:T(8,128)(2,1)S(1)} %collective-permute-done.7.refs_1_, bf16[2,184,640]{2,1,0:T(8,128)(2,1)S(1)} %get-tuple-element.56.refs_2_, ...), custom_call_target="tpu_custom_call" | custom-call | flops 943718400 | bytes 7372800 | tf_op jit(solution)/shard_map/put_rows/pallas_call | solution.py:186
  (50 shorter events, 0.5 us)
Async XLA Ops:
  0.0 48.2 %copy-start.19 = (s32[32]{0:T(128)S(1)}, s32[32]{0:T(128)}, u32[]{:S(2)}) copy-start(s32[32]{0:T(128)} %param.6) | copy-start | bytes 388
  0.1 2.0 %copy-start = (bf16[16,180,640]{2,0,1:T(8,128)(2,1)S(1)}, bf16[16,180,640]{2,0,1:T(8,128)(2,1)}, u32[]{:S(2)}) copy-start(bf16[16,180,640]{2,0,1:T(8,128)(2,1)} %param.4) | copy-start | bytes 11059204
  2.1 0.7 copy-start.1
  5.9 17.1 %collective-permute-start.8 = (bf16[2,184,640]{2,1,0:T(8,128)(2,1)S(1)}, bf16[2,184,640]{2,1,0:T(8,128)(2,1)S(1)}, u32[]{:S(2)}, u32[]{:S(2)}) collective-permute-start(bf16[2,184,640]{2,1,0:T(8,128)(2,1)S(1)} %get-tuple-element.52), channel_id=1, source_target_pairs={{0,2},{2,0},{4,6},{6,4},{8,10},{10,8},{12,14},{14,12},{16,18},{18,... | collective-permute-start | bytes 1413128 | tf_op jit(solution)/shard_map/ppermute | solution.py:333
  6.4 6.6 %collective-permute-start = (bf16[1,184,640]{2,1,0:T(8,128)(2,1)S(1)}, bf16[1,184,640]{2,1,0:T(8,128)(2,1)S(1)}, u32[]{:S(2)}, u32[]{:S(2)}) collective-permute-start(bf16[1,184,640]{2,1,0:T(8,128)(2,1)S(1)} %get-tuple-element.45), channel_id=1, source_target_pairs={{0,2},{2,0},{4,6},{6,4},{8,10},{10,8},{12,14},{14,12},{16,18},{18,... | collective-permute-start | bytes 706568 | tf_op jit(solution)/shard_map/ppermute | solution.py:333
  6.5 9.0 %collective-permute-start.1 = (bf16[1,184,640]{2,1,0:T(8,128)(2,1)S(1)}, bf16[1,184,640]{2,1,0:T(8,128)(2,1)S(1)}, u32[]{:S(2)}, u32[]{:S(2)}) collective-permute-start(bf16[1,184,640]{2,1,0:T(8,128)(2,1)S(1)} %get-tuple-element.46), channel_id=1, source_target_pairs={{0,4},{2,6},{4,0},{6,2},{8,12},{10,14},{12,8},{14,10},{16,20},{18,... | collective-permute-start | bytes 706568 | tf_op jit(solution)/shard_map/ppermute | solution.py:333
  9.4 9.8 %collective-permute-start.6 = (bf16[1,184,640]{2,1,0:T(8,128)(2,1)S(1)}, bf16[1,184,640]{2,1,0:T(8,128)(2,1)S(1)}, u32[]{:S(2)}, u32[]{:S(2)}) collective-permute-start(bf16[1,184,640]{2,1,0:T(8,128)(2,1)S(1)} %get-tuple-element.44.refs_1_.refs_5_), channel_id=1, source_target_pairs={{0,24},{2,26},{4,12},{6,14},{8,0},{10,2},{12,20},{14,22},{16,8},{1... | collective-permute-start | bytes 706568 | tf_op jit(solution)/shard_map/ppermute | solution.py:333
  13.0 11.5 %collective-permute-start.2 = (bf16[1,184,640]{2,1,0:T(8,128)(2,1)S(1)}, bf16[1,184,640]{2,1,0:T(8,128)(2,1)S(1)}, u32[]{:S(2)}, u32[]{:S(2)}) collective-permute-start(bf16[1,184,640]{2,1,0:T(8,128)(2,1)S(1)} %get-tuple-element.47), channel_id=1, source_target_pairs={{0,6},{2,4},{4,2},{6,0},{8,14},{10,12},{12,10},{14,8},{16,22},{18,... | collective-permute-start | bytes 706568 | tf_op jit(solution)/shard_map/ppermute | solution.py:333
  13.0 11.5 %collective-permute-start.4 = (bf16[1,184,640]{2,1,0:T(8,128)(2,1)S(1)}, bf16[1,184,640]{2,1,0:T(8,128)(2,1)S(1)}, u32[]{:S(2)}, u32[]{:S(2)}) collective-permute-start(bf16[1,184,640]{2,1,0:T(8,128)(2,1)S(1)} %collective-permute-done.refs_2_.refs_6_), channel_id=1, source_target_pairs={{0,24},{2,26},{4,12},{6,14},{8,0},{10,2},{12,20},{14,22},{16,8},{1... | collective-permute-start | bytes 706568 | tf_op jit(solution)/shard_map/ppermute | solution.py:333
  13.5 0.7 copy-start.2
  15.5 13.4 %collective-permute-start.3 = (bf16[1,184,640]{2,1,0:T(8,128)(2,1)S(1)}, bf16[1,184,640]{2,1,0:T(8,128)(2,1)S(1)}, u32[]{:S(2)}, u32[]{:S(2)}) collective-permute-start(bf16[1,184,640]{2,1,0:T(8,128)(2,1)S(1)} %collective-permute-done.1.refs_3_.refs_1_), channel_id=1, source_target_pairs={{0,8},{2,10},{4,28},{6,30},{8,16},{10,18},{12,4},{14,6},{16,24},{1... | collective-permute-start | bytes 706568 | tf_op jit(solution)/shard_map/ppermute | solution.py:333
  18.1 0.7 copy-start.5
  19.2 0.7 copy-start.15
  19.9 14.9 %collective-permute-start.9 = (bf16[2,184,640]{2,1,0:T(8,128)(2,1)S(1)}, bf16[2,184,640]{2,1,0:T(8,128)(2,1)}, u32[]{:S(2)}, u32[]{:S(2)}) collective-permute-start(bf16[2,184,640]{2,1,0:T(8,128)(2,1)S(1)} %get-tuple-element.51.refs_1_), channel_id=1, source_target_pairs={{0,4},{2,6},{4,0},{6,2},{8,12},{10,14},{12,8},{14,10},{16,20},{18,... | collective-permute-start | bytes 1413128 | tf_op jit(solution)/shard_map/ppermute | solution.py:333
  23.0 13.7 %collective-permute-start.13 = (bf16[2,184,640]{2,1,0:T(8,128)(2,1)S(1)}, bf16[2,184,640]{2,1,0:T(8,128)(2,1)S(1)}, u32[]{:S(2)}, u32[]{:S(2)}) collective-permute-start(bf16[2,184,640]{2,1,0:T(8,128)(2,1)S(1)} %get-tuple-element.57), channel_id=1, source_target_pairs={{0,1},{1,0},{2,3},{3,2},{4,5},{5,4},{6,7},{7,6},{8,9},{9,8},{10,11... | collective-permute-start | bytes 1413128 | tf_op jit(solution)/shard_map/ppermute | solution.py:333
  24.5 20.4 %collective-permute-start.10 = (bf16[2,184,640]{2,1,0:T(8,128)(2,1)S(1)}, bf16[2,184,640]{2,1,0:T(8,128)(2,1)}, u32[]{:S(2)}, u32[]{:S(2)}) collective-permute-start(bf16[2,184,640]{2,1,0:T(8,128)(2,1)S(1)} %collective-permute-done.8.refs_2_), channel_id=1, source_target_pairs={{0,4},{2,6},{4,0},{6,2},{8,12},{10,14},{12,8},{14,10},{16,20},{18,... | collective-permute-start | bytes 1413128 | tf_op jit(solution)/shard_map/ppermute | solution.py:333
  24.5 0.7 copy-start.17
  25.2 19.8 %collective-permute-start.14 = (bf16[2,184,640]{2,1,0:T(8,128)(2,1)S(1)}, bf16[2,184,640]{2,1,0:T(8,128)(2,1)S(1)}, u32[]{:S(2)}, u32[]{:S(2)}) collective-permute-start(bf16[2,184,640]{2,1,0:T(8,128)(2,1)S(1)} %get-tuple-element.58), channel_id=1, source_target_pairs={{0,3},{1,2},{2,1},{3,0},{4,7},{5,6},{6,5},{7,4},{8,11},{9,10},{10,... | collective-permute-start | bytes 1413128 | tf_op jit(solution)/shard_map/ppermute | solution.py:333
  29.0 0.7 copy-start.11
  29.7 10.4 %collective-permute-start.5 = (bf16[1,184,640]{2,1,0:T(8,128)(2,1)S(1)}, bf16[1,184,640]{2,1,0:T(8,128)(2,1)S(1)}, u32[]{:S(2)}, u32[]{:S(2)}) collective-permute-start(bf16[1,184,640]{2,1,0:T(8,128)(2,1)S(1)} %collective-permute-done.2.refs_4_.refs_2_), channel_id=1, source_target_pairs={{0,8},{2,10},{4,28},{6,30},{8,16},{10,18},{12,4},{14,6},{16,24},{1... | collective-permute-start | bytes 706568 | tf_op jit(solution)/shard_map/ppermute | solution.py:333
  31.3 0.7 copy-start.8
  34.8 21.6 %collective-permute-start.11 = (bf16[2,184,640]{2,1,0:T(8,128)(2,1)}, bf16[2,184,640]{2,1,0:T(8,128)(2,1)}, u32[]{:S(2)}, u32[]{:S(2)}) collective-permute-start(bf16[2,184,640]{2,1,0:T(8,128)(2,1)} %collective-permute-done.9.refs_3_), channel_id=1, source_target_pairs={{0,8},{2,10},{4,28},{6,30},{8,16},{10,18},{12,4},{14,6},{16,24},{1... | collective-permute-start | bytes 1413128 | tf_op jit(solution)/shard_map/ppermute | solution.py:333
  36.7 19.7 %collective-permute-start.15 = (bf16[2,184,640]{2,1,0:T(8,128)(2,1)S(1)}, bf16[2,184,640]{2,1,0:T(8,128)(2,1)S(1)}, u32[]{:S(2)}, u32[]{:S(2)}) collective-permute-start(bf16[2,184,640]{2,1,0:T(8,128)(2,1)S(1)} %collective-permute-done.13.refs_1_), channel_id=1, source_target_pairs={{0,4},{2,6},{4,0},{6,2},{8,12},{10,14},{12,8},{14,10},{16,20},{18,... | collective-permute-start | bytes 1413128 | tf_op jit(solution)/shard_map/ppermute | solution.py:333
  40.1 0.7 copy-start.13
  40.8 16.5 %collective-permute-start.19 = (bf16[2,184,640]{2,1,0:T(8,128)(2,1)S(1)}, bf16[2,184,640]{2,1,0:T(8,128)(2,1)}, u32[]{:S(2)}, u32[]{:S(2)}) collective-permute-start(bf16[2,184,640]{2,1,0:T(8,128)(2,1)S(1)} %get-tuple-element.65), channel_id=1, source_target_pairs={{0,1},{1,0},{2,3},{3,2},{4,5},{5,4},{6,7},{7,6},{8,9},{9,8},{10,11... | collective-permute-start | bytes 1413128 | tf_op jit(solution)/shard_map/ppermute | solution.py:333
  44.9 14.4 %collective-permute-start.12 = (bf16[2,184,640]{2,1,0:T(8,128)(2,1)}, bf16[2,184,640]{2,1,0:T(8,128)(2,1)}, u32[]{:S(2)}, u32[]{:S(2)}) collective-permute-start(bf16[2,184,640]{2,1,0:T(8,128)(2,1)} %collective-permute-done.10.refs_4_), channel_id=1, source_target_pairs={{0,8},{2,10},{4,28},{6,30},{8,16},{10,18},{12,4},{14,6},{16,24},{1... | collective-permute-start | bytes 1413128 | tf_op jit(solution)/shard_map/ppermute | solution.py:333
  45.0 18.3 %collective-permute-start.16 = (bf16[2,184,640]{2,1,0:T(8,128)(2,1)S(1)}, bf16[2,184,640]{2,1,0:T(8,128)(2,1)}, u32[]{:S(2)}, u32[]{:S(2)}) collective-permute-start(bf16[2,184,640]{2,1,0:T(8,128)(2,1)S(1)} %collective-permute-done.14.refs_2_), channel_id=1, source_target_pairs={{0,4},{2,6},{4,0},{6,2},{8,12},{10,14},{12,8},{14,10},{16,20},{18,... | collective-permute-start | bytes 1413128 | tf_op jit(solution)/shard_map/ppermute | solution.py:333
  50.0 0.9 copy-start.3
  50.9 0.9 copy-start.6
  51.8 0.9 copy-start.9
  52.8 0.9 copy-start.16
  53.7 0.9 copy-start.18
  56.3 13.1 %collective-permute-start.20 = (bf16[2,184,640]{2,1,0:T(8,128)(2,1)S(1)}, bf16[2,184,640]{2,1,0:T(8,128)(2,1)S(1)}, u32[]{:S(2)}, u32[]{:S(2)}) collective-permute-start(bf16[2,184,640]{2,1,0:T(8,128)(2,1)S(1)} %get-tuple-element.67), channel_id=1, source_target_pairs={{0,3},{1,2},{2,1},{3,0},{4,7},{5,6},{6,5},{7,4},{8,11},{9,10},{10,... | collective-permute-start | bytes 1413128 | tf_op jit(solution)/shard_map/ppermute | solution.py:333
  56.4 15.0 %collective-permute-start.17 = (bf16[2,184,640]{2,1,0:T(8,128)(2,1)S(1)}, bf16[2,184,640]{2,1,0:T(8,128)(2,1)S(1)}, u32[]{:S(2)}, u32[]{:S(2)}) collective-permute-start(bf16[2,184,640]{2,1,0:T(8,128)(2,1)S(1)} %collective-permute-done.15.refs_3_), channel_id=1, source_target_pairs={{0,8},{2,10},{4,28},{6,30},{8,16},{10,18},{12,4},{14,6},{16,24},{1... | collective-permute-start | bytes 1413128 | tf_op jit(solution)/shard_map/ppermute | solution.py:333
  57.2 15.4 %collective-permute-start.21 = (bf16[2,184,640]{2,1,0:T(8,128)(2,1)}, bf16[2,184,640]{2,1,0:T(8,128)(2,1)S(1)}, u32[]{:S(2)}, u32[]{:S(2)}) collective-permute-start(bf16[2,184,640]{2,1,0:T(8,128)(2,1)} %collective-permute-done.19.refs_1_), channel_id=1, source_target_pairs={{0,4},{2,6},{4,0},{6,2},{8,12},{10,14},{12,8},{14,10},{16,20},{18,... | collective-permute-start | bytes 1413128 | tf_op jit(solution)/shard_map/ppermute | solution.py:333
  63.3 18.2 %collective-permute-start.18 = (bf16[2,184,640]{2,1,0:T(8,128)(2,1)}, bf16[2,184,640]{2,1,0:T(8,128)(2,1)S(1)}, u32[]{:S(2)}, u32[]{:S(2)}) collective-permute-start(bf16[2,184,640]{2,1,0:T(8,128)(2,1)} %collective-permute-done.16.refs_4_), channel_id=1, source_target_pairs={{0,8},{2,10},{4,28},{6,30},{8,16},{10,18},{12,4},{14,6},{16,24},{1... | collective-permute-start | bytes 1413128 | tf_op jit(solution)/shard_map/ppermute | solution.py:333
  69.4 13.6 %collective-permute-start.22 = (bf16[2,184,640]{2,1,0:T(8,128)(2,1)S(1)}, bf16[2,184,640]{2,1,0:T(8,128)(2,1)S(1)}, u32[]{:S(2)}, u32[]{:S(2)}) collective-permute-start(bf16[2,184,640]{2,1,0:T(8,128)(2,1)S(1)} %collective-permute-done.20.refs_2_), channel_id=1, source_target_pairs={{0,4},{2,6},{4,0},{6,2},{8,12},{10,14},{12,8},{14,10},{16,20},{18,... | collective-permute-start | bytes 1413128 | tf_op jit(solution)/shard_map/ppermute | solution.py:333
  71.2 33.9 %collective-permute-start.7 = (bf16[1,184,640]{2,1,0:T(8,128)(2,1)S(1)}, bf16[1,184,640]{2,1,0:T(8,128)(2,1)S(1)}, u32[]{:S(2)}, u32[]{:S(2)}) collective-permute-start(bf16[1,184,640]{2,1,0:T(8,128)(2,1)S(1)} %get-tuple-element.50), channel_id=1, source_target_pairs={{0,4},{2,6},{4,0},{6,2},{8,12},{10,14},{12,8},{14,10},{16,20},{18,... | collective-permute-start | bytes 706568 | tf_op jit(solution)/shard_map/ppermute | solution.py:333
  71.5 33.8 %collective-permute-start.26 = (bf16[1,184,640]{2,1,0:T(8,128)(2,1)S(1)}, bf16[1,184,640]{2,1,0:T(8,128)(2,1)S(1)}, u32[]{:S(2)}, u32[]{:S(2)}) collective-permute-start(bf16[1,184,640]{2,1,0:T(8,128)(2,1)S(1)} %get-tuple-element.75), channel_id=1, source_target_pairs={{0,6},{2,4},{4,2},{6,0},{8,14},{10,12},{12,10},{14,8},{16,22},{18,... | collective-permute-start | bytes 706568 | tf_op jit(solution)/shard_map/ppermute | solution.py:333
  72.6 19.0 %collective-permute-start.23 = (bf16[2,184,640]{2,1,0:T(8,128)(2,1)S(1)}, bf16[2,184,640]{2,1,0:T(8,128)(2,1)S(1)}, u32[]{:S(2)}, u32[]{:S(2)}) collective-permute-start(bf16[2,184,640]{2,1,0:T(8,128)(2,1)S(1)} %collective-permute-done.21.refs_3_), channel_id=1, source_target_pairs={{0,8},{2,10},{4,28},{6,30},{8,16},{10,18},{12,4},{14,6},{16,24},{1... | collective-permute-start | bytes 1413128 | tf_op jit(solution)/shard_map/ppermute | solution.py:333
  81.5 25.1 %collective-permute-start.27 = (bf16[2,184,640]{2,1,0:T(8,128)(2,1)S(1)}, bf16[2,184,640]{2,1,0:T(8,128)(2,1)S(1)}, u32[]{:S(2)}, u32[]{:S(2)}) collective-permute-start(bf16[2,184,640]{2,1,0:T(8,128)(2,1)S(1)} %get-tuple-element.76), channel_id=1, source_target_pairs={{0,2},{2,0},{4,6},{6,4},{8,10},{10,8},{12,14},{14,12},{16,18},{18,... | collective-permute-start | bytes 1413128 | tf_op jit(solution)/shard_map/ppermute | solution.py:333
  83.0 18.7 %collective-permute-start.24 = (bf16[2,184,640]{2,1,0:T(8,128)(2,1)S(1)}, bf16[2,184,640]{2,1,0:T(8,128)(2,1)S(1)}, u32[]{:S(2)}, u32[]{:S(2)}) collective-permute-start(bf16[2,184,640]{2,1,0:T(8,128)(2,1)S(1)} %collective-permute-done.22.refs_4_), channel_id=1, source_target_pairs={{0,8},{2,10},{4,28},{6,30},{8,16},{10,18},{12,4},{14,6},{16,24},{1... | collective-permute-start | bytes 1413128 | tf_op jit(solution)/shard_map/ppermute | solution.py:333
  89.4 13.9 %copy-start.4 = (bf16[1,184,640]{2,1,0:T(8,128)(2,1)S(1)}, bf16[1,184,640]{2,1,0:T(8,128)(2,1)}, u32[]{:S(2)}) copy-start(bf16[1,184,640]{2,1,0:T(8,128)(2,1)} %copy-done.2) | copy-start | bytes 706564
  89.4 13.9 %copy-start.7 = (bf16[1,184,640]{2,1,0:T(8,128)(2,1)S(1)}, bf16[1,184,640]{2,1,0:T(8,128)(2,1)}, u32[]{:S(2)}) copy-start(bf16[1,184,640]{2,1,0:T(8,128)(2,1)} %copy-done.5) | copy-start | bytes 706564
  89.4 13.9 %copy-start.10 = (bf16[1,184,640]{2,1,0:T(8,128)(2,1)S(1)}, bf16[1,184,640]{2,1,0:T(8,128)(2,1)}, u32[]{:S(2)}) copy-start(bf16[1,184,640]{2,1,0:T(8,128)(2,1)} %copy-done.8) | copy-start | bytes 706564
  89.4 13.9 %copy-start.12 = (bf16[1,184,640]{2,1,0:T(8,128)(2,1)S(1)}, bf16[1,184,640]{2,1,0:T(8,128)(2,1)}, u32[]{:S(2)}) copy-start(bf16[1,184,640]{2,1,0:T(8,128)(2,1)} %copy-done.11) | copy-start | bytes 706564
  89.5 13.9 %copy-start.14 = (bf16[1,184,640]{2,1,0:T(8,128)(2,1)S(1)}, bf16[1,184,640]{2,1,0:T(8,128)(2,1)}, u32[]{:S(2)}) copy-start(bf16[1,184,640]{2,1,0:T(8,128)(2,1)} %copy-done.13) | copy-start | bytes 706564
  91.6 15.0 %collective-permute-start.28 = (bf16[2,184,640]{2,1,0:T(8,128)(2,1)S(1)}, bf16[2,184,640]{2,1,0:T(8,128)(2,1)S(1)}, u32[]{:S(2)}, u32[]{:S(2)}) collective-permute-start(bf16[2,184,640]{2,1,0:T(8,128)(2,1)S(1)} %get-tuple-element.77), channel_id=1, source_target_pairs={{0,2},{2,0},{4,6},{6,4},{8,10},{10,8},{12,14},{14,12},{16,18},{18,... | collective-permute-start | bytes 1413128 | tf_op jit(solution)/shard_map/ppermute | solution.py:333
  102.9 3.7 %collective-permute-start.29 = (bf16[2,184,640]{2,1,0:T(8,128)(2,1)S(1)}, bf16[2,184,640]{2,1,0:T(8,128)(2,1)S(1)}, u32[]{:S(2)}, u32[]{:S(2)}) collective-permute-start(bf16[2,184,640]{2,1,0:T(8,128)(2,1)S(1)} %get-tuple-element.78), channel_id=1, source_target_pairs={{0,2},{2,0},{4,6},{6,4},{8,10},{10,8},{12,14},{14,12},{16,18},{18,... | collective-permute-start | bytes 1413128 | tf_op jit(solution)/shard_map/ppermute | solution.py:333
  105.1 1.6 %collective-permute-start.25 = (bf16[1,184,640]{2,1,0:T(8,128)(2,1)S(1)}, bf16[1,184,640]{2,1,0:T(8,128)(2,1)S(1)}, u32[]{:S(2)}, u32[]{:S(2)}) collective-permute-start(bf16[1,184,640]{2,1,0:T(8,128)(2,1)S(1)} %get-tuple-element.74), channel_id=1, source_target_pairs={{0,2},{2,0},{4,6},{6,4},{8,10},{10,8},{12,14},{14,12},{16,18},{18,... | collective-permute-start | bytes 706568 | tf_op jit(solution)/shard_map/ppermute | solution.py:333

commit v8 on v7

--- a/solution.py
+++ b/solution.py
@@ -7,7 +7,7 @@
 from jax.experimental.pallas import tpu as pltpu
 from jax.sharding import PartitionSpec as P
 
-VMEM_LIMIT = 16 * 1024 * 1024
+VMEM_LIMIT = 12 * 1024 * 1024
 SMEM_SPEC = pl.BlockSpec(memory_space=pltpu.SMEM)
 VMEM_SPEC = pl.BlockSpec(memory_space=pltpu.VMEM)
 HBM_SPEC = pl.BlockSpec(memory_space=pltpu.HBM)
@@ -42,14 +42,34 @@
     return lax.ppermute(x, axis, [(i, (i + by) % count) for i in range(count)])
 
 
-def tap_lines(widths, tap_weights, lon_dev, reach):
-    circle = tap_weights.shape[1]
-    behind = (reach + 1) * lon_dev
-    line = jnp.concatenate([tap_weights[:, circle - behind :], tap_weights[:, :behind]], axis=1)
-    offset = jnp.arange(circle - behind, circle + behind, dtype=jnp.int32) % circle
-    distance = jnp.minimum(offset, circle - offset)
-    line = jnp.where(distance[None, :] <= widths[:, None], line.astype(jnp.float32), jnp.zeros((), jnp.float32))
-    return jnp.pad(line, ((0, 0), (0, up_to(2 * behind, 128) - 2 * behind)))
+def line_kernel(behind, taps_ref, line_ref):
+    circle = taps_ref.shape[1]
+    rows, lanes = line_ref.shape
+    taps = taps_ref[...].astype(jnp.float32)
+    pieces = [taps[:, circle - behind :], taps[:, :behind]]
+    if lanes > 2 * behind:
+        pieces.append(jnp.zeros((rows, lanes - 2 * behind), jnp.float32))
+    line_ref[...] = jnp.concatenate(pieces, axis=1)
+
+
+def tap_lines(tap_weights, behind):
+    rows = tap_weights.shape[0]
+    lanes = up_to(2 * behind, 128)
+    return pl.pallas_call(
+        functools.partial(line_kernel, behind),
+        out_shape=jax.ShapeDtypeStruct((rows, lanes), jnp.float32),
+        in_specs=[VMEM_SPEC],
+        out_specs=VMEM_SPEC,
+        compiler_params=pltpu.CompilerParams(vmem_limit_bytes=VMEM_LIMIT),
+        cost_estimate=pl.CostEstimate(flops=0, bytes_accessed=2 * tap_weights.size, transcendentals=0),
+        name="tap_lines",
+    )(tap_weights)
+
+
+def active_line(line_ref, row, width, behind):
+    line = jnp.broadcast_to(line_ref[pl.ds(row, 1), :], (8, line_ref.shape[1]))
+    distance = jnp.abs(lax.broadcasted_iota(jnp.int32, line.shape, 1) - behind)
+    return jnp.where(distance <= width, line, 0.0)
 
 
 def toeplitz(line, at, lon_dev, width):
@@ -202,9 +222,9 @@
     )(slots, *panels)
 
 
-def pair_kernel(lon_dev, base, plan, phase, rows_ref, sign_ref, *refs):
+def pair_kernel(lon_dev, base, plan, phase, rows_ref, place_ref, widths_ref, *refs):
     count = len(plan)
-    side, along = sign_ref[0], sign_ref[1]
+    side, along = 1 - 2 * place_ref[1], 1 - 2 * place_ref[2]
     if phase == "late":
         (total_in, block_ref), refs = refs[:2], refs[2:]
     else:
@@ -233,7 +253,8 @@
         same = side == along
         if phase != "late":
             own, other, x_own, x_other = panels[:4]
-            line = jnp.broadcast_to(line_ref[pl.ds(rows_ref[base + n], 1), :], (8, line_ref.shape[1]))
+            row = rows_ref[base + n]
+            line = active_line(line_ref, row, widths_ref[row], 3 * lon_dev)
             for s in range(5):
                 block_ref[n, s] = toeplitz(line, (s + 1) * lon_dev, lon_dev, padded)
             here = both(own, other)
@@ -255,7 +276,7 @@
             out_other[n] = total[:, channels:].astype(out_other.dtype)
 
 
-def filter_pair(rows, signs, lines, places, base, lon_dev, phase="whole", early=()):
+def filter_pair(scalars, lines, places, base, lon_dev, phase="whole", early=()):
     arrays = []
     plan = []
     for row in places:
@@ -282,7 +303,7 @@
     return pl.pallas_call(
         functools.partial(pair_kernel, lon_dev, base, tuple(plan), phase),
         out_shape=outs,
-        in_specs=[SMEM_SPEC, SMEM_SPEC] + [VMEM_SPEC] * (len(first) + len(arrays)),
+        in_specs=[SMEM_SPEC] * 3 + [VMEM_SPEC] * (len(first) + len(arrays)),
         out_specs=[VMEM_SPEC] * len(outs),
         scratch_shapes=scratch,
         compiler_params=pltpu.CompilerParams(vmem_limit_bytes=VMEM_LIMIT),
@@ -292,7 +313,7 @@
             transcendentals=0,
         ),
         name="filter_" + phase,
-    )(rows, signs, *first, *arrays)
+    )(*scalars, *first, *arrays)
 
 
 def chip_aware(fields, owner_slot, widths, tap_weights):
@@ -302,7 +323,6 @@
     band = lax.axis_index("lat")
     core, x = at % 2, at // 2 % 2
     place = jnp.stack([band, core, x]).astype(jnp.int32)
-    signs = jnp.stack([1 - 2 * core, 1 - 2 * x]).astype(jnp.int32)
     chunks = STAY + STAY + COME + COME
     taken, rows, slots = take_rows(jnp.transpose(fields, (1, 0, 2)), owner_slot, place, chunks)
     n_stay, n_come = len(STAY), len(COME)
@@ -317,7 +337,8 @@
     across_y = [(i, i ^ 1) for i in range(2 * n_lon)]
     across_both = [(i, i ^ 3) for i in range(2 * n_lon)]
 
-    lines = tap_lines(widths, tap_weights, lon_dev, 2)
+    lines = tap_lines(tap_weights, 3 * lon_dev)
+    scalars = rows, place, widths
     sizes = STAY + COME
     starts = [sum(sizes[:c]) for c in range(len(sizes))]
     done = {}
@@ -356,7 +377,7 @@
                 panels = here + beside + [get("q", 2), get("q", 3)]
             else:
                 panels = beside + [get("q", 0), get("q", 1)] + here
-            result = filter_pair(rows, signs, lines, [[(p, 0) for p in panels]], 0, lon_dev)
+            result = filter_pair(scalars, lines, [[(p, 0) for p in panels]], 0, lon_dev)
         elif kind == "b":
             operand, pairs = ((get("t", 0)[1], across_core), (get("t", 1)[0], across_x), (get("t", 1)[1], across_x_core))[i]
             result = moved(operand, "lon", pairs)
@@ -373,10 +394,10 @@
                 places.append([(p, index) for p in parts])
             base = FILTERS[i][0]
             if i < len(FILTERS) - 1:
-                result = filter_pair(rows, signs, lines, places, base, lon_dev)
+                result = filter_pair(scalars, lines, places, base, lon_dev)
             else:
-                early = filter_pair(rows, signs, lines, [p[:4] for p in places], base, lon_dev, "early")
-                result = filter_pair(rows, signs, lines, [p[4:] for p in places], base, lon_dev, "late", early)
+                early = filter_pair(scalars, lines, [p[:4] for p in places], base, lon_dev, "early")
+                result = filter_pair(scalars, lines, [p[4:] for p in places], base, lon_dev, "late", early)
         else:
             result = moved(get("f", i)[1], "lon", across_core)
         done[kind, i] = result
@@ -388,11 +409,11 @@
     return jnp.transpose(out, (1, 0, 2))
 
 
-def filter_kernel(rows_ref, slots_ref, sector_ref, line_ref, *refs):
+def filter_kernel(reach, rows_ref, slots_ref, sector_ref, widths_ref, line_ref, *refs):
     ins, out_ref = refs[:-1], refs[-1]
     lon_dev, channels = out_ref.shape[1:]
     row = rows_ref[pl.program_id(0)]
-    line = jnp.broadcast_to(line_ref[pl.ds(row, 1), :], (8, line_ref.shape[1]))
+    line = active_line(line_ref, row, widths_ref[row], (reach + 1) * lon_dev)
     total = ins[0][0].astype(jnp.float32)
     for group, ref in enumerate(ins):
         block = toeplitz(line, (sector_ref[group] + 1) * lon_dev, lon_dev, lon_dev)
@@ -400,23 +421,23 @@
     out_ref[0] = total.astype(out_ref.dtype)
 
 
-def filter_rows(rows, slots, sectors, lines, arrays):
+def filter_rows(rows, slots, sectors, widths, lines, arrays, reach):
     lat_dev, lon_dev, channels = arrays[0].shape
-    row_spec = pl.BlockSpec((1, lon_dev, channels), lambda i, rows, slots, sectors: (i, 0, 0))
-    line_spec = pl.BlockSpec(lines.shape, lambda i, rows, slots, sectors: (0, 0))
-    out_spec = pl.BlockSpec((1, lon_dev, channels), lambda i, rows, slots, sectors: (slots[i], 0, 0))
+    row_spec = pl.BlockSpec((1, lon_dev, channels), lambda i, rows, slots, sectors, widths: (i, 0, 0))
+    line_spec = pl.BlockSpec(lines.shape, lambda i, rows, slots, sectors, widths: (0, 0))
+    out_spec = pl.BlockSpec((1, lon_dev, channels), lambda i, rows, slots, sectors, widths: (slots[i], 0, 0))
     return pl.pallas_call(
-        filter_kernel,
+        functools.partial(filter_kernel, reach),
         out_shape=jax.ShapeDtypeStruct(arrays[0].shape, arrays[0].dtype),
         grid_spec=pltpu.PrefetchScalarGridSpec(
-            num_scalar_prefetch=3,
+            num_scalar_prefetch=4,
             grid=(lat_dev,),
             in_specs=[line_spec] + [row_spec] * len(arrays),
             out_specs=out_spec,
         ),
         compiler_params=pltpu.CompilerParams(vmem_limit_bytes=VMEM_LIMIT),
         name="filter_rows",
-    )(rows, slots, sectors, lines, *arrays)
+    )(rows, slots, sectors, widths, lines, *arrays)
 
 
 def any_mesh(fields, owner_slot, widths, tap_weights):
@@ -433,7 +454,7 @@
     outgoing = fields[ordering].reshape(n_lat, lat_dev // n_lat, lon_dev, channels)
     incoming = lax.all_to_all(outgoing, "lat", split_axis=0, concat_axis=0, tiled=True)
     own = incoming.reshape(lat_dev, lon_dev, channels)
-    lines = tap_lines(widths, tap_weights, lon_dev, reach)
+    lines = tap_lines(tap_weights, (reach + 1) * lon_dev)
     arrays, order = [own], [reach]
     ahead = behind = own
     for step in range(1, reach + 1):
@@ -442,7 +463,7 @@
         arrays += [ahead, behind]
         order += [reach + step, reach - step]
     sectors = jnp.array(order, jnp.int32)
-    return filter_rows(rows, slots, sectors, lines, arrays)
+    return filter_rows(rows, slots, sectors, widths, lines, arrays, reach)
 
 
 def solution(mesh):

time: 110 us -> 106 us (0.964)
  starting transfers between devices: 31.6 us -> 48.1 us
  local copies, waits for them, and re-layouts: 14.1 us -> 2.71 us
  waiting for transfers between devices: 43.1 us -> 36.3 us
  Pallas kernels: 19.5 us -> 17.9 us
    ppermute x30, starting transfers between devices: 31.6 us -> 48.1 us  [moved(): return lax.ppermute(operand, axes, pairs)]
    unnamed x40 -> x8, local copies, waits for them, and re-layouts: 12.2 us -> 2.71 us
    ppermute x30, waiting for transfers between devices: 43.1 us -> 36.3 us  [moved(): return lax.ppermute(operand, axes, pairs)]
    pallas_call x6, Pallas kernels: 13.7 us -> 12 us  [filter_pair(): pl.pallas_call(functools.partial(pair_kernel, lon_dev, base, tuple(plan),...]
  transfers between devices with their start and end apart: 30 -> 30, of which waited for: 16 -> 16; matrix products, arithmetic and copies ran while one was open for 2% -> 0% of each run, Pallas kernels for 12% -> 11%
where the time goes in v8:
time: 106 us; the launch traced here: 105 us
  starting transfers between devices  48.1 us (45%)
  waiting for transfers between devices  36.3 us (34%)
  Pallas kernels  17.9 us (17%)
  local copies, waits for them, and re-layouts  2.71 us (3%)
    ppermute x30, starting transfers between devices, moved(): return lax.ppermute(operand, axes, pairs)  48.1 us
    ppermute x30, waiting for transfers between devices, moved(): return lax.ppermute(operand, axes, pairs)  36.3 us
    pallas_call x6, Pallas kernels, filter_pair(): pl.pallas_call(functools.partial(pair_kernel, lon_dev, base, tuple(plan),...  12 us
    pallas_call x1, Pallas kernels, take_rows(): pl.pallas_call(functools.partial(take_kernel, chunks, lat_dev, block), ou...  3.11 us
    pallas_call x1, Pallas kernels, put_rows(): pl.pallas_call(functools.partial(put_kernel, counts, lat_dev, block), out...  2.77 us
    unnamed x8, local copies, waits for them, and re-layouts  2.71 us
  transfers between devices with their start and end apart: 30, of which 16 were waited for; matrix products, arithmetic and copies ran while one was open for 0% of the time, Pallas kernels for 11%

profile of v8, /device:TPU:0, one launch (start us, length us, event | category | flops | bytes accessed | tf_op | source)
XLA Modules:
  0.0 105.4 jit_solution(14149767138071655916)
XLA Ops:
  0.0 0.1 pad_add_fusion.place_ref
  0.1 2.0 %copy-done = bf16[16,180,640]{2,0,1:T(8,128)(2,1)S(1)} copy-done((bf16[16,180,640]{2,0,1:T(8,128)(2,1)S(1)}, bf16[16,180,640]{2,0,1:T(8,128)(2,1)}, u32[]{:S(2)}) %copy-start) | copy-done | bytes 3686424
  2.1 0.7 copy-done.2
  2.8 3.1 %take_rows.1 = (bf16[1,184,640]{2,1,0:T(8,128)(2,1)S(1)}, bf16[1,184,640]{2,1,0:T(8,128)(2,1)S(1)}, bf16[2,184,640]{2,1,0:T(8,128)(2,1)S(1)}, bf16[1,184,640]{2,...) custom-call(s32[32]{0:T(128)S(1)} %copy-done.2, ...), custom_call_target="tpu_custom_call" | custom-call | flops 943718400 | bytes 7372800 | tf_op jit(solution)/shard_map/take_rows/pallas_call | solution.py:154
  5.9 0.5 collective-permute-start.8
  6.4 0.1 collective-permute-start
  6.5 2.9 %collective-permute-start.1 = (bf16[1,184,640]{2,1,0:T(8,128)(2,1)S(1)}, bf16[1,184,640]{2,1,0:T(8,128)(2,1)S(1)}, u32[]{:S(2)}, u32[]{:S(2)}) collective-permute-start(bf16[1,184,640]{2,1,0:T(8,128)(2,1)S(1)} %get-tuple-element.46), channel_id=1, source_target_pairs={{0,4},{2,6},{4,0},{6,2},{8,12},{10,14},{12,8},{14,10},{16,20},{18,... | collective-permute-start | bytes 706568 | tf_op jit(solution)/shard_map/ppermute | solution.py:354
  9.4 3.6 %collective-permute-start.6 = (bf16[1,184,640]{2,1,0:T(8,128)(2,1)S(1)}, bf16[1,184,640]{2,1,0:T(8,128)(2,1)S(1)}, u32[]{:S(2)}, u32[]{:S(2)}) collective-permute-start(bf16[1,184,640]{2,1,0:T(8,128)(2,1)S(1)} %get-tuple-element.44.refs_1_.refs_5_), channel_id=1, source_target_pairs={{0,24},{2,26},{4,12},{6,14},{8,0},{10,2},{12,20},{14,22},{16,8},{1... | collective-permute-start | bytes 706568 | tf_op jit(solution)/shard_map/ppermute | solution.py:354
  13.0 0.0 collective-permute-start.2
  13.0 0.0 collective-permute-done.refs_2_.refs_6_
  13.0 0.5 collective-permute-start.4
  13.5 2.0 %collective-permute-done.1.refs_3_.refs_1_ = bf16[1,184,640]{2,1,0:T(8,128)(2,1)S(1)} collective-permute-done((bf16[1,184,640]{2,1,0:T(8,128)(2,1)S(1)}, bf16[1,184,640]{2,1,0:T(8,128)(2,1)S(1)}, u32[]{:S(2)}, u32[]{:S(2)}) %collective-permute-start.1) | collective-permute-done | bytes 235552 | tf_op jit(solution)/shard_map/ppermute | solution.py:354
  15.5 2.5 %collective-permute-start.9 = (bf16[2,184,640]{2,1,0:T(8,128)(2,1)S(1)}, bf16[2,184,640]{2,1,0:T(8,128)(2,1)S(1)}, u32[]{:S(2)}, u32[]{:S(2)}) collective-permute-start(bf16[2,184,640]{2,1,0:T(8,128)(2,1)S(1)} %get-tuple-element.51.refs_1_), channel_id=1, source_target_pairs={{0,4},{2,6},{4,0},{6,2},{8,12},{10,14},{12,8},{14,10},{16,20},{18,... | collective-permute-start | bytes 1413128 | tf_op jit(solution)/shard_map/ppermute | solution.py:354
  18.0 1.2 %collective-permute-done.6.refs_3_ = bf16[1,184,640]{2,1,0:T(8,128)(2,1)S(1)} collective-permute-done((bf16[1,184,640]{2,1,0:T(8,128)(2,1)S(1)}, bf16[1,184,640]{2,1,0:T(8,128)(2,1)S(1)}, u32[]{:S(2)}, u32[]{:S(2)}) %collective-permute-start.6) | collective-permute-done | bytes 235552 | tf_op jit(solution)/shard_map/ppermute | solution.py:354
  19.2 1.5 %collective-permute-start.13 = (bf16[2,184,640]{2,1,0:T(8,128)(2,1)S(1)}, bf16[2,184,640]{2,1,0:T(8,128)(2,1)S(1)}, u32[]{:S(2)}, u32[]{:S(2)}) collective-permute-start(bf16[2,184,640]{2,1,0:T(8,128)(2,1)S(1)} %get-tuple-element.57), channel_id=1, source_target_pairs={{0,1},{1,0},{2,3},{3,2},{4,5},{5,4},{6,7},{7,6},{8,9},{9,8},{10,11... | collective-permute-start | bytes 1413128 | tf_op jit(solution)/shard_map/ppermute | solution.py:354
  20.7 0.0 collective-permute-done.8.refs_2_
  20.7 0.5 collective-permute-start.3
  21.1 0.0 collective-permute-done.2.refs_4_.refs_2_
  21.1 2.6 %collective-permute-start.10 = (bf16[2,184,640]{2,1,0:T(8,128)(2,1)S(1)}, bf16[2,184,640]{2,1,0:T(8,128)(2,1)S(1)}, u32[]{:S(2)}, u32[]{:S(2)}) collective-permute-start(bf16[2,184,640]{2,1,0:T(8,128)(2,1)S(1)} %collective-permute-done.8.refs_2_), channel_id=1, source_target_pairs={{0,4},{2,6},{4,0},{6,2},{8,12},{10,14},{12,8},{14,10},{16,20},{18,... | collective-permute-start | bytes 1413128 | tf_op jit(solution)/shard_map/ppermute | solution.py:354
  23.7 0.5 collective-permute-done.4.refs_4_
  24.3 0.0 collective-permute-start.14
  24.3 4.9 %collective-permute-done.3.refs_5_ = bf16[1,184,640]{2,1,0:T(8,128)(2,1)S(1)} collective-permute-done((bf16[1,184,640]{2,1,0:T(8,128)(2,1)S(1)}, bf16[1,184,640]{2,1,0:T(8,128)(2,1)S(1)}, u32[]{:S(2)}, u32[]{:S(2)}) %collective-permute-start.3) | collective-permute-done | bytes 235552 | tf_op jit(solution)/shard_map/ppermute | solution.py:354
  29.1 1.5 %collective-permute-start.5 = (bf16[1,184,640]{2,1,0:T(8,128)(2,1)S(1)}, bf16[1,184,640]{2,1,0:T(8,128)(2,1)S(1)}, u32[]{:S(2)}, u32[]{:S(2)}) collective-permute-start(bf16[1,184,640]{2,1,0:T(8,128)(2,1)S(1)} %collective-permute-done.2.refs_4_.refs_2_), channel_id=1, source_target_pairs={{0,8},{2,10},{4,28},{6,30},{8,16},{10,18},{12,4},{14,6},{16,24},{1... | collective-permute-start | bytes 706568 | tf_op jit(solution)/shard_map/ppermute | solution.py:354
  30.6 0.1 collective-permute-done.9.refs_3_
  30.7 2.6 %collective-permute-start.11 = (bf16[2,184,640]{2,1,0:T(8,128)(2,1)S(1)}, bf16[2,184,640]{2,1,0:T(8,128)(2,1)S(1)}, u32[]{:S(2)}, u32[]{:S(2)}) collective-permute-start(bf16[2,184,640]{2,1,0:T(8,128)(2,1)S(1)} %collective-permute-done.9.refs_3_), channel_id=1, source_target_pairs={{0,8},{2,10},{4,28},{6,30},{8,16},{10,18},{12,4},{14,6},{16,24},{1... | collective-permute-start | bytes 1413128 | tf_op jit(solution)/shard_map/ppermute | solution.py:354
  33.2 0.0 collective-permute-done.13.refs_1_
  33.2 3.5 %collective-permute-start.15 = (bf16[2,184,640]{2,1,0:T(8,128)(2,1)S(1)}, bf16[2,184,640]{2,1,0:T(8,128)(2,1)S(1)}, u32[]{:S(2)}, u32[]{:S(2)}) collective-permute-start(bf16[2,184,640]{2,1,0:T(8,128)(2,1)S(1)} %collective-permute-done.13.refs_1_), channel_id=1, source_target_pairs={{0,4},{2,6},{4,0},{6,2},{8,12},{10,14},{12,8},{14,10},{16,20},{18,... | collective-permute-start | bytes 1413128 | tf_op jit(solution)/shard_map/ppermute | solution.py:354
  36.8 1.9 %collective-permute-done.5.refs_6_ = bf16[1,184,640]{2,1,0:T(8,128)(2,1)S(1)} collective-permute-done((bf16[1,184,640]{2,1,0:T(8,128)(2,1)S(1)}, bf16[1,184,640]{2,1,0:T(8,128)(2,1)S(1)}, u32[]{:S(2)}, u32[]{:S(2)}) %collective-permute-start.5) | collective-permute-done | bytes 235552 | tf_op jit(solution)/shard_map/ppermute | solution.py:354
  38.6 2.3 %collective-permute-start.19 = (bf16[2,184,640]{2,1,0:T(8,128)(2,1)S(1)}, bf16[2,184,640]{2,1,0:T(8,128)(2,1)S(1)}, u32[]{:S(2)}, u32[]{:S(2)}) collective-permute-start(bf16[2,184,640]{2,1,0:T(8,128)(2,1)S(1)} %get-tuple-element.65), channel_id=1, source_target_pairs={{0,1},{1,0},{2,3},{3,2},{4,5},{5,4},{6,7},{7,6},{8,9},{9,8},{10,11... | collective-permute-start | bytes 1413128 | tf_op jit(solution)/shard_map/ppermute | solution.py:354
  41.0 0.0 collective-permute-done.10.refs_4_
  41.0 2.4 %collective-permute-start.12 = (bf16[2,184,640]{2,1,0:T(8,128)(2,1)S(1)}, bf16[2,184,640]{2,1,0:T(8,128)(2,1)S(1)}, u32[]{:S(2)}, u32[]{:S(2)}) collective-permute-start(bf16[2,184,640]{2,1,0:T(8,128)(2,1)S(1)} %collective-permute-done.10.refs_4_), channel_id=1, source_target_pairs={{0,8},{2,10},{4,28},{6,30},{8,16},{10,18},{12,4},{14,6},{16,24},{1... | collective-permute-start | bytes 1413128 | tf_op jit(solution)/shard_map/ppermute | solution.py:354
  43.3 0.0 collective-permute-done.14.refs_2_
  43.3 3.5 %collective-permute-start.16 = (bf16[2,184,640]{2,1,0:T(8,128)(2,1)S(1)}, bf16[2,184,640]{2,1,0:T(8,128)(2,1)S(1)}, u32[]{:S(2)}, u32[]{:S(2)}) collective-permute-start(bf16[2,184,640]{2,1,0:T(8,128)(2,1)S(1)} %collective-permute-done.14.refs_2_), channel_id=1, source_target_pairs={{0,4},{2,6},{4,0},{6,2},{8,12},{10,14},{12,8},{14,10},{16,20},{18,... | collective-permute-start | bytes 1413128 | tf_op jit(solution)/shard_map/ppermute | solution.py:354
  46.8 0.1 tap_lines.1.refs_0_
  47.0 1.7 %filter_whole.5 = (bf16[1,184,640]{2,1,0:T(8,128)(2,1)S(1)}, bf16[1,184,640]{2,1,0:T(8,128)(2,1)S(1)}) custom-call(s32[16]{0:T(128)S(1)} %get-tuple-element.43.rows_ref, s32[3]{0:T(128)S(1)} %pad_add_fusion.place_ref, s32[32]{0:T(128)S(1)} %copy-done.3, f32[32,1152]{1,0:T(8,128)S(1)} %tap_lines.1.refs_0_, ...), custom_call_target="tpu_custom_call" | custom-call | flops 3019898880 | bytes 1884160 | tf_op jit(solution)/shard_map/filter_whole/pallas_call | solution.py:303
  48.6 0.1 collective-permute-done.11.refs_5_
  48.7 2.1 %collective-permute-done.15.refs_3_ = bf16[2,184,640]{2,1,0:T(8,128)(2,1)S(1)} collective-permute-done((bf16[2,184,640]{2,1,0:T(8,128)(2,1)S(1)}, bf16[2,184,640]{2,1,0:T(8,128)(2,1)S(1)}, u32[]{:S(2)}, u32[]{:S(2)}) %collective-permute-start.15) | collective-permute-done | bytes 471072 | tf_op jit(solution)/shard_map/ppermute | solution.py:354
  50.9 2.6 %collective-permute-start.17 = (bf16[2,184,640]{2,1,0:T(8,128)(2,1)S(1)}, bf16[2,184,640]{2,1,0:T(8,128)(2,1)S(1)}, u32[]{:S(2)}, u32[]{:S(2)}) collective-permute-start(bf16[2,184,640]{2,1,0:T(8,128)(2,1)S(1)} %collective-permute-done.15.refs_3_), channel_id=1, source_target_pairs={{0,8},{2,10},{4,28},{6,30},{8,16},{10,18},{12,4},{14,6},{16,24},{1... | collective-permute-start | bytes 1413128 | tf_op jit(solution)/shard_map/ppermute | solution.py:354
  53.4 0.0 collective-permute-done.19.refs_1_
  53.4 3.5 %collective-permute-start.21 = (bf16[2,184,640]{2,1,0:T(8,128)(2,1)S(1)}, bf16[2,184,640]{2,1,0:T(8,128)(2,1)S(1)}, u32[]{:S(2)}, u32[]{:S(2)}) collective-permute-start(bf16[2,184,640]{2,1,0:T(8,128)(2,1)S(1)} %collective-permute-done.19.refs_1_), channel_id=1, source_target_pairs={{0,4},{2,6},{4,0},{6,2},{8,12},{10,14},{12,8},{14,10},{16,20},{18,... | collective-permute-start | bytes 1413128 | tf_op jit(solution)/shard_map/ppermute | solution.py:354
  56.9 1.9 %collective-permute-done.12.refs_6_ = bf16[2,184,640]{2,1,0:T(8,128)(2,1)S(1)} collective-permute-done((bf16[2,184,640]{2,1,0:T(8,128)(2,1)S(1)}, bf16[2,184,640]{2,1,0:T(8,128)(2,1)S(1)}, u32[]{:S(2)}, u32[]{:S(2)}) %collective-permute-start.12) | collective-permute-done | bytes 471072 | tf_op jit(solution)/shard_map/ppermute | solution.py:354
  58.8 2.1 %collective-permute-done.16.refs_4_ = bf16[2,184,640]{2,1,0:T(8,128)(2,1)S(1)} collective-permute-done((bf16[2,184,640]{2,1,0:T(8,128)(2,1)S(1)}, bf16[2,184,640]{2,1,0:T(8,128)(2,1)S(1)}, u32[]{:S(2)}, u32[]{:S(2)}) %collective-permute-start.16) | collective-permute-done | bytes 471072 | tf_op jit(solution)/shard_map/ppermute | solution.py:354
  60.9 2.6 %collective-permute-start.18 = (bf16[2,184,640]{2,1,0:T(8,128)(2,1)S(1)}, bf16[2,184,640]{2,1,0:T(8,128)(2,1)S(1)}, u32[]{:S(2)}, u32[]{:S(2)}) collective-permute-start(bf16[2,184,640]{2,1,0:T(8,128)(2,1)S(1)} %collective-permute-done.16.refs_4_), channel_id=1, source_target_pairs={{0,8},{2,10},{4,28},{6,30},{8,16},{10,18},{12,4},{14,6},{16,24},{1... | collective-permute-start | bytes 1413128 | tf_op jit(solution)/shard_map/ppermute | solution.py:354
  63.5 2.6 %filter_whole.6 = (bf16[2,184,640]{2,1,0:T(8,128)(2,1)S(1)}, bf16[2,184,640]{2,1,0:T(8,128)(2,1)S(1)}) custom-call(s32[16]{0:T(128)S(1)} %get-tuple-element.43.rows_ref, s32[3]{0:T(128)S(1)} %pad_add_fusion.place_ref, s32[32]{0:T(128)S(1)} %copy-done.3, f32[32,1152]{1,0:T(8,128)S(1)} %tap_lines.1.refs_0_, ...), custom_call_target="tpu_custom_call" | custom-call | flops 6039797760 | bytes 3768320 | tf_op jit(solution)/shard_map/filter_whole/pallas_call | solution.py:303
  66.2 0.0 collective-permute-done.20.refs_2_
  66.2 3.6 %collective-permute-start.22 = (bf16[2,184,640]{2,1,0:T(8,128)(2,1)S(1)}, bf16[2,184,640]{2,1,0:T(8,128)(2,1)S(1)}, u32[]{:S(2)}, u32[]{:S(2)}) collective-permute-start(bf16[2,184,640]{2,1,0:T(8,128)(2,1)S(1)} %collective-permute-done.20.refs_2_), channel_id=1, source_target_pairs={{0,4},{2,6},{4,0},{6,2},{8,12},{10,14},{12,8},{14,10},{16,20},{18,... | collective-permute-start | bytes 1413128 | tf_op jit(solution)/shard_map/ppermute | solution.py:354
  69.8 0.1 collective-permute-start.7
  69.8 1.2 %collective-permute-done.21.refs_3_ = bf16[2,184,640]{2,1,0:T(8,128)(2,1)S(1)} collective-permute-done((bf16[2,184,640]{2,1,0:T(8,128)(2,1)S(1)}, bf16[2,184,640]{2,1,0:T(8,128)(2,1)S(1)}, u32[]{:S(2)}, u32[]{:S(2)}) %collective-permute-start.21) | collective-permute-done | bytes 471072 | tf_op jit(solution)/shard_map/ppermute | solution.py:354
  71.0 2.6 %collective-permute-start.23 = (bf16[2,184,640]{2,1,0:T(8,128)(2,1)S(1)}, bf16[2,184,640]{2,1,0:T(8,128)(2,1)S(1)}, u32[]{:S(2)}, u32[]{:S(2)}) collective-permute-start(bf16[2,184,640]{2,1,0:T(8,128)(2,1)S(1)} %collective-permute-done.21.refs_3_), channel_id=1, source_target_pairs={{0,8},{2,10},{4,28},{6,30},{8,16},{10,18},{12,4},{14,6},{16,24},{1... | collective-permute-start | bytes 1413128 | tf_op jit(solution)/shard_map/ppermute | solution.py:354
  73.6 5.1 %collective-permute-done.18.refs_6_ = bf16[2,184,640]{2,1,0:T(8,128)(2,1)S(1)} collective-permute-done((bf16[2,184,640]{2,1,0:T(8,128)(2,1)S(1)}, bf16[2,184,640]{2,1,0:T(8,128)(2,1)S(1)}, u32[]{:S(2)}, u32[]{:S(2)}) %collective-permute-start.18) | collective-permute-done | bytes 471072 | tf_op jit(solution)/shard_map/ppermute | solution.py:354
  78.7 2.8 %collective-permute-done.22.refs_4_ = bf16[2,184,640]{2,1,0:T(8,128)(2,1)S(1)} collective-permute-done((bf16[2,184,640]{2,1,0:T(8,128)(2,1)S(1)}, bf16[2,184,640]{2,1,0:T(8,128)(2,1)S(1)}, u32[]{:S(2)}, u32[]{:S(2)}) %collective-permute-start.22) | collective-permute-done | bytes 471072 | tf_op jit(solution)/shard_map/ppermute | solution.py:354
  81.5 2.2 %collective-permute-start.24 = (bf16[2,184,640]{2,1,0:T(8,128)(2,1)S(1)}, bf16[2,184,640]{2,1,0:T(8,128)(2,1)S(1)}, u32[]{:S(2)}, u32[]{:S(2)}) collective-permute-start(bf16[2,184,640]{2,1,0:T(8,128)(2,1)S(1)} %collective-permute-done.22.refs_4_), channel_id=1, source_target_pairs={{0,8},{2,10},{4,28},{6,30},{8,16},{10,18},{12,4},{14,6},{16,24},{1... | collective-permute-start | bytes 1413128 | tf_op jit(solution)/shard_map/ppermute | solution.py:354
  83.7 2.6 %filter_whole.7 = (bf16[2,184,640]{2,1,0:T(8,128)(2,1)S(1)}, bf16[2,184,640]{2,1,0:T(8,128)(2,1)S(1)}) custom-call(s32[16]{0:T(128)S(1)} %get-tuple-element.43.rows_ref, s32[3]{0:T(128)S(1)} %pad_add_fusion.place_ref, s32[32]{0:T(128)S(1)} %copy-done.3, f32[32,1152]{1,0:T(8,128)S(1)} %tap_lines.1.refs_0_, ...), custom_call_target="tpu_custom_call" | custom-call | flops 6039797760 | bytes 3768320 | tf_op jit(solution)/shard_map/filter_whole/pallas_call | solution.py:303
  86.3 2.1 %filter_early.1 = (f32[2,184,1280]{2,1,0:T(8,128)S(1)}, bf16[2,5,192,184]{3,2,1,0:T(8,128)(2,1)S(1)}) custom-call(s32[16]{0:T(128)S(1)} %get-tuple-element.43.rows_ref, s32[3]{0:T(128)S(1)} %pad_add_fusion.place_ref, s32[32]{0:T(128)S(1)} %copy-done.3, f32[32,1152]{1,0:T(8,128)S(1)} %tap_lines.1.refs_0_, ...), custom_call_target="tpu_custom_call" | custom-call | flops 4227858432 | bytes 3768320 | tf_op jit(solution)/shard_map/filter_early/pallas_call | solution.py:303
  88.4 0.4 collective-permute-done.23.refs_2_
  88.8 0.0 collective-permute-start.28
  88.8 8.9 %collective-permute-done.24.refs_3_ = bf16[2,184,640]{2,1,0:T(8,128)(2,1)S(1)} collective-permute-done((bf16[2,184,640]{2,1,0:T(8,128)(2,1)S(1)}, bf16[2,184,640]{2,1,0:T(8,128)(2,1)S(1)}, u32[]{:S(2)}, u32[]{:S(2)}) %collective-permute-start.24) | collective-permute-done | bytes 471072 | tf_op jit(solution)/shard_map/ppermute | solution.py:354
  97.7 1.3 %filter_late.1 = (bf16[2,184,640]{2,1,0:T(8,128)(2,1)S(1)}, bf16[2,184,640]{2,1,0:T(8,128)(2,1)S(1)}) custom-call(s32[16]{0:T(128)S(1)} %get-tuple-element.43.rows_ref, s32[3]{0:T(128)S(1)} %pad_add_fusion.place_ref, s32[32]{0:T(128)S(1)} %copy-done.3, f32[2,184,1280]{2,1,0:T(8,128)S(1)} %get-tuple-element.70.refs_0_, ...), custom_call_target="tpu_custom_call" | custom-call | flops 1811939328 | bytes 3768320 | tf_op jit(solution)/shard_map/filter_late/pallas_call | solution.py:303
  99.0 0.1 collective-permute-start.29
  99.1 1.7 %filter_whole.4 = (bf16[1,184,640]{2,1,0:T(8,128)(2,1)S(1)}, bf16[1,184,640]{2,1,0:T(8,128)(2,1)S(1)}) custom-call(s32[16]{0:T(128)S(1)} %get-tuple-element.43.rows_ref, s32[3]{0:T(128)S(1)} %pad_add_fusion.place_ref, s32[32]{0:T(128)S(1)} %copy-done.3, f32[32,1152]{1,0:T(8,128)S(1)} %tap_lines.1.refs_0_, ...), custom_call_target="tpu_custom_call" | custom-call | flops 3019898880 | bytes 1884160 | tf_op jit(solution)/shard_map/filter_whole/pallas_call | solution.py:303
  100.8 0.6 collective-permute-start.25
  101.3 0.0 collective-permute-done.26.refs_6_
  101.3 1.1 %collective-permute-done.25.refs_5_ = bf16[1,184,640]{2,1,0:T(8,128)(2,1)S(1)} collective-permute-done((bf16[1,184,640]{2,1,0:T(8,128)(2,1)S(1)}, bf16[1,184,640]{2,1,0:T(8,128)(2,1)S(1)}, u32[]{:S(2)}, u32[]{:S(2)}) %collective-permute-start.25) | collective-permute-done | bytes 235552 | tf_op jit(solution)/shard_map/ppermute | solution.py:354
  102.5 2.8 %put_rows.1 = bf16[180,16,640]{2,1,0:T(8,128)(2,1)} custom-call(s32[16]{0:T(128)S(1)} %get-tuple-element.42.slots_ref, bf16[1,184,640]{2,1,0:T(8,128)(2,1)S(1)} %get-tuple-element.49.refs_0_, bf16[1,184,640]{2,1,0:T(8,128)(2,1)S(1)} %collective-permute-done.7.refs_1_, bf16[2,184,640]{2,1,0:T(8,128)(2,1)S(1)} %get-tuple-element.56.refs_2_, ...), custom_call_target="tpu_custom_call" | custom-call | flops 943718400 | bytes 7372800 | tf_op jit(solution)/shard_map/put_rows/pallas_call | solution.py:206
  (14 shorter events, 0.0 us)
Async XLA Ops:
  0.0 46.9 %copy-start.3 = (s32[32]{0:T(128)S(1)}, s32[32]{0:T(128)}, u32[]{:S(2)}) copy-start(s32[32]{0:T(128)} %widths_ref.11) | copy-start | bytes 388
  0.1 2.0 %copy-start = (bf16[16,180,640]{2,0,1:T(8,128)(2,1)S(1)}, bf16[16,180,640]{2,0,1:T(8,128)(2,1)}, u32[]{:S(2)}) copy-start(bf16[16,180,640]{2,0,1:T(8,128)(2,1)} %param.4) | copy-start | bytes 11059204
  2.1 0.7 copy-start.2
  2.8 44.1 %copy-start.1 = (bf16[32,2880]{1,0:T(8,128)(2,1)S(1)}, bf16[32,2880]{1,0:T(8,128)(2,1)}, u32[]{:S(2)}) copy-start(bf16[32,2880]{1,0:T(8,128)(2,1)} %taps_ref.1) | copy-start | bytes 552964
  5.9 14.8 %collective-permute-start.8 = (bf16[2,184,640]{2,1,0:T(8,128)(2,1)S(1)}, bf16[2,184,640]{2,1,0:T(8,128)(2,1)S(1)}, u32[]{:S(2)}, u32[]{:S(2)}) collective-permute-start(bf16[2,184,640]{2,1,0:T(8,128)(2,1)S(1)} %get-tuple-element.52), channel_id=1, source_target_pairs={{0,2},{2,0},{4,6},{6,4},{8,10},{10,8},{12,14},{14,12},{16,18},{18,... | collective-permute-start | bytes 1413128 | tf_op jit(solution)/shard_map/ppermute | solution.py:354
  6.4 6.6 %collective-permute-start = (bf16[1,184,640]{2,1,0:T(8,128)(2,1)S(1)}, bf16[1,184,640]{2,1,0:T(8,128)(2,1)S(1)}, u32[]{:S(2)}, u32[]{:S(2)}) collective-permute-start(bf16[1,184,640]{2,1,0:T(8,128)(2,1)S(1)} %get-tuple-element.45), channel_id=1, source_target_pairs={{0,2},{2,0},{4,6},{6,4},{8,10},{10,8},{12,14},{14,12},{16,18},{18,... | collective-permute-start | bytes 706568 | tf_op jit(solution)/shard_map/ppermute | solution.py:354
  6.5 9.0 %collective-permute-start.1 = (bf16[1,184,640]{2,1,0:T(8,128)(2,1)S(1)}, bf16[1,184,640]{2,1,0:T(8,128)(2,1)S(1)}, u32[]{:S(2)}, u32[]{:S(2)}) collective-permute-start(bf16[1,184,640]{2,1,0:T(8,128)(2,1)S(1)} %get-tuple-element.46), channel_id=1, source_target_pairs={{0,4},{2,6},{4,0},{6,2},{8,12},{10,14},{12,8},{14,10},{16,20},{18,... | collective-permute-start | bytes 706568 | tf_op jit(solution)/shard_map/ppermute | solution.py:354
  9.4 9.8 %collective-permute-start.6 = (bf16[1,184,640]{2,1,0:T(8,128)(2,1)S(1)}, bf16[1,184,640]{2,1,0:T(8,128)(2,1)S(1)}, u32[]{:S(2)}, u32[]{:S(2)}) collective-permute-start(bf16[1,184,640]{2,1,0:T(8,128)(2,1)S(1)} %get-tuple-element.44.refs_1_.refs_5_), channel_id=1, source_target_pairs={{0,24},{2,26},{4,12},{6,14},{8,0},{10,2},{12,20},{14,22},{16,8},{1... | collective-permute-start | bytes 706568 | tf_op jit(solution)/shard_map/ppermute | solution.py:354
  13.0 8.1 %collective-permute-start.2 = (bf16[1,184,640]{2,1,0:T(8,128)(2,1)S(1)}, bf16[1,184,640]{2,1,0:T(8,128)(2,1)S(1)}, u32[]{:S(2)}, u32[]{:S(2)}) collective-permute-start(bf16[1,184,640]{2,1,0:T(8,128)(2,1)S(1)} %get-tuple-element.47), channel_id=1, source_target_pairs={{0,6},{2,4},{4,2},{6,0},{8,14},{10,12},{12,10},{14,8},{16,22},{18,... | collective-permute-start | bytes 706568 | tf_op jit(solution)/shard_map/ppermute | solution.py:354
  13.0 11.2 %collective-permute-start.4 = (bf16[1,184,640]{2,1,0:T(8,128)(2,1)S(1)}, bf16[1,184,640]{2,1,0:T(8,128)(2,1)S(1)}, u32[]{:S(2)}, u32[]{:S(2)}) collective-permute-start(bf16[1,184,640]{2,1,0:T(8,128)(2,1)S(1)} %collective-permute-done.refs_2_.refs_6_), channel_id=1, source_target_pairs={{0,24},{2,26},{4,12},{6,14},{8,0},{10,2},{12,20},{14,22},{16,8},{1... | collective-permute-start | bytes 706568 | tf_op jit(solution)/shard_map/ppermute | solution.py:354
  15.5 15.1 %collective-permute-start.9 = (bf16[2,184,640]{2,1,0:T(8,128)(2,1)S(1)}, bf16[2,184,640]{2,1,0:T(8,128)(2,1)S(1)}, u32[]{:S(2)}, u32[]{:S(2)}) collective-permute-start(bf16[2,184,640]{2,1,0:T(8,128)(2,1)S(1)} %get-tuple-element.51.refs_1_), channel_id=1, source_target_pairs={{0,4},{2,6},{4,0},{6,2},{8,12},{10,14},{12,8},{14,10},{16,20},{18,... | collective-permute-start | bytes 1413128 | tf_op jit(solution)/shard_map/ppermute | solution.py:354
  19.2 14.1 %collective-permute-start.13 = (bf16[2,184,640]{2,1,0:T(8,128)(2,1)S(1)}, bf16[2,184,640]{2,1,0:T(8,128)(2,1)S(1)}, u32[]{:S(2)}, u32[]{:S(2)}) collective-permute-start(bf16[2,184,640]{2,1,0:T(8,128)(2,1)S(1)} %get-tuple-element.57), channel_id=1, source_target_pairs={{0,1},{1,0},{2,3},{3,2},{4,5},{5,4},{6,7},{7,6},{8,9},{9,8},{10,11... | collective-permute-start | bytes 1413128 | tf_op jit(solution)/shard_map/ppermute | solution.py:354
  20.7 8.4 %collective-permute-start.3 = (bf16[1,184,640]{2,1,0:T(8,128)(2,1)S(1)}, bf16[1,184,640]{2,1,0:T(8,128)(2,1)S(1)}, u32[]{:S(2)}, u32[]{:S(2)}) collective-permute-start(bf16[1,184,640]{2,1,0:T(8,128)(2,1)S(1)} %collective-permute-done.1.refs_3_.refs_1_), channel_id=1, source_target_pairs={{0,8},{2,10},{4,28},{6,30},{8,16},{10,18},{12,4},{14,6},{16,24},{1... | collective-permute-start | bytes 706568 | tf_op jit(solution)/shard_map/ppermute | solution.py:354
  21.1 19.8 %collective-permute-start.10 = (bf16[2,184,640]{2,1,0:T(8,128)(2,1)S(1)}, bf16[2,184,640]{2,1,0:T(8,128)(2,1)S(1)}, u32[]{:S(2)}, u32[]{:S(2)}) collective-permute-start(bf16[2,184,640]{2,1,0:T(8,128)(2,1)S(1)} %collective-permute-done.8.refs_2_), channel_id=1, source_target_pairs={{0,4},{2,6},{4,0},{6,2},{8,12},{10,14},{12,8},{14,10},{16,20},{18,... | collective-permute-start | bytes 1413128 | tf_op jit(solution)/shard_map/ppermute | solution.py:354
  24.3 19.1 %collective-permute-start.14 = (bf16[2,184,640]{2,1,0:T(8,128)(2,1)S(1)}, bf16[2,184,640]{2,1,0:T(8,128)(2,1)S(1)}, u32[]{:S(2)}, u32[]{:S(2)}) collective-permute-start(bf16[2,184,640]{2,1,0:T(8,128)(2,1)S(1)} %get-tuple-element.58), channel_id=1, source_target_pairs={{0,3},{1,2},{2,1},{3,0},{4,7},{5,6},{6,5},{7,4},{8,11},{9,10},{10,... | collective-permute-start | bytes 1413128 | tf_op jit(solution)/shard_map/ppermute | solution.py:354
  29.1 9.5 %collective-permute-start.5 = (bf16[1,184,640]{2,1,0:T(8,128)(2,1)S(1)}, bf16[1,184,640]{2,1,0:T(8,128)(2,1)S(1)}, u32[]{:S(2)}, u32[]{:S(2)}) collective-permute-start(bf16[1,184,640]{2,1,0:T(8,128)(2,1)S(1)} %collective-permute-done.2.refs_4_.refs_2_), channel_id=1, source_target_pairs={{0,8},{2,10},{4,28},{6,30},{8,16},{10,18},{12,4},{14,6},{16,24},{1... | collective-permute-start | bytes 706568 | tf_op jit(solution)/shard_map/ppermute | solution.py:354
  30.7 18.1 %collective-permute-start.11 = (bf16[2,184,640]{2,1,0:T(8,128)(2,1)S(1)}, bf16[2,184,640]{2,1,0:T(8,128)(2,1)S(1)}, u32[]{:S(2)}, u32[]{:S(2)}) collective-permute-start(bf16[2,184,640]{2,1,0:T(8,128)(2,1)S(1)} %collective-permute-done.9.refs_3_), channel_id=1, source_target_pairs={{0,8},{2,10},{4,28},{6,30},{8,16},{10,18},{12,4},{14,6},{16,24},{1... | collective-permute-start | bytes 1413128 | tf_op jit(solution)/shard_map/ppermute | solution.py:354
  33.2 17.6 %collective-permute-start.15 = (bf16[2,184,640]{2,1,0:T(8,128)(2,1)S(1)}, bf16[2,184,640]{2,1,0:T(8,128)(2,1)S(1)}, u32[]{:S(2)}, u32[]{:S(2)}) collective-permute-start(bf16[2,184,640]{2,1,0:T(8,128)(2,1)S(1)} %collective-permute-done.13.refs_1_), channel_id=1, source_target_pairs={{0,4},{2,6},{4,0},{6,2},{8,12},{10,14},{12,8},{14,10},{16,20},{18,... | collective-permute-start | bytes 1413128 | tf_op jit(solution)/shard_map/ppermute | solution.py:354
  38.6 14.8 %collective-permute-start.19 = (bf16[2,184,640]{2,1,0:T(8,128)(2,1)S(1)}, bf16[2,184,640]{2,1,0:T(8,128)(2,1)S(1)}, u32[]{:S(2)}, u32[]{:S(2)}) collective-permute-start(bf16[2,184,640]{2,1,0:T(8,128)(2,1)S(1)} %get-tuple-element.65), channel_id=1, source_target_pairs={{0,1},{1,0},{2,3},{3,2},{4,5},{5,4},{6,7},{7,6},{8,9},{9,8},{10,11... | collective-permute-start | bytes 1413128 | tf_op jit(solution)/shard_map/ppermute | solution.py:354
  41.0 17.9 %collective-permute-start.12 = (bf16[2,184,640]{2,1,0:T(8,128)(2,1)S(1)}, bf16[2,184,640]{2,1,0:T(8,128)(2,1)S(1)}, u32[]{:S(2)}, u32[]{:S(2)}) collective-permute-start(bf16[2,184,640]{2,1,0:T(8,128)(2,1)S(1)} %collective-permute-done.10.refs_4_), channel_id=1, source_target_pairs={{0,8},{2,10},{4,28},{6,30},{8,16},{10,18},{12,4},{14,6},{16,24},{1... | collective-permute-start | bytes 1413128 | tf_op jit(solution)/shard_map/ppermute | solution.py:354
  43.3 17.6 %collective-permute-start.16 = (bf16[2,184,640]{2,1,0:T(8,128)(2,1)S(1)}, bf16[2,184,640]{2,1,0:T(8,128)(2,1)S(1)}, u32[]{:S(2)}, u32[]{:S(2)}) collective-permute-start(bf16[2,184,640]{2,1,0:T(8,128)(2,1)S(1)} %collective-permute-done.14.refs_2_), channel_id=1, source_target_pairs={{0,4},{2,6},{4,0},{6,2},{8,12},{10,14},{12,8},{14,10},{16,20},{18,... | collective-permute-start | bytes 1413128 | tf_op jit(solution)/shard_map/ppermute | solution.py:354
  48.7 17.4 %collective-permute-start.20 = (bf16[2,184,640]{2,1,0:T(8,128)(2,1)S(1)}, bf16[2,184,640]{2,1,0:T(8,128)(2,1)S(1)}, u32[]{:S(2)}, u32[]{:S(2)}) collective-permute-start(bf16[2,184,640]{2,1,0:T(8,128)(2,1)S(1)} %get-tuple-element.67), channel_id=1, source_target_pairs={{0,3},{1,2},{2,1},{3,0},{4,7},{5,6},{6,5},{7,4},{8,11},{9,10},{10,... | collective-permute-start | bytes 1413128 | tf_op jit(solution)/shard_map/ppermute | solution.py:354
  50.9 19.0 %collective-permute-start.17 = (bf16[2,184,640]{2,1,0:T(8,128)(2,1)S(1)}, bf16[2,184,640]{2,1,0:T(8,128)(2,1)S(1)}, u32[]{:S(2)}, u32[]{:S(2)}) collective-permute-start(bf16[2,184,640]{2,1,0:T(8,128)(2,1)S(1)} %collective-permute-done.15.refs_3_), channel_id=1, source_target_pairs={{0,8},{2,10},{4,28},{6,30},{8,16},{10,18},{12,4},{14,6},{16,24},{1... | collective-permute-start | bytes 1413128 | tf_op jit(solution)/shard_map/ppermute | solution.py:354
  53.4 17.6 %collective-permute-start.21 = (bf16[2,184,640]{2,1,0:T(8,128)(2,1)S(1)}, bf16[2,184,640]{2,1,0:T(8,128)(2,1)S(1)}, u32[]{:S(2)}, u32[]{:S(2)}) collective-permute-start(bf16[2,184,640]{2,1,0:T(8,128)(2,1)S(1)} %collective-permute-done.19.refs_1_), channel_id=1, source_target_pairs={{0,4},{2,6},{4,0},{6,2},{8,12},{10,14},{12,8},{14,10},{16,20},{18,... | collective-permute-start | bytes 1413128 | tf_op jit(solution)/shard_map/ppermute | solution.py:354
  60.9 17.8 %collective-permute-start.18 = (bf16[2,184,640]{2,1,0:T(8,128)(2,1)S(1)}, bf16[2,184,640]{2,1,0:T(8,128)(2,1)S(1)}, u32[]{:S(2)}, u32[]{:S(2)}) collective-permute-start(bf16[2,184,640]{2,1,0:T(8,128)(2,1)S(1)} %collective-permute-done.16.refs_4_), channel_id=1, source_target_pairs={{0,8},{2,10},{4,28},{6,30},{8,16},{10,18},{12,4},{14,6},{16,24},{1... | collective-permute-start | bytes 1413128 | tf_op jit(solution)/shard_map/ppermute | solution.py:354
  66.2 15.3 %collective-permute-start.22 = (bf16[2,184,640]{2,1,0:T(8,128)(2,1)S(1)}, bf16[2,184,640]{2,1,0:T(8,128)(2,1)S(1)}, u32[]{:S(2)}, u32[]{:S(2)}) collective-permute-start(bf16[2,184,640]{2,1,0:T(8,128)(2,1)S(1)} %collective-permute-done.20.refs_2_), channel_id=1, source_target_pairs={{0,4},{2,6},{4,0},{6,2},{8,12},{10,14},{12,8},{14,10},{16,20},{18,... | collective-permute-start | bytes 1413128 | tf_op jit(solution)/shard_map/ppermute | solution.py:354
  69.8 31.0 %collective-permute-start.7 = (bf16[1,184,640]{2,1,0:T(8,128)(2,1)S(1)}, bf16[1,184,640]{2,1,0:T(8,128)(2,1)S(1)}, u32[]{:S(2)}, u32[]{:S(2)}) collective-permute-start(bf16[1,184,640]{2,1,0:T(8,128)(2,1)S(1)} %get-tuple-element.50), channel_id=1, source_target_pairs={{0,4},{2,6},{4,0},{6,2},{8,12},{10,14},{12,8},{14,10},{16,20},{18,... | collective-permute-start | bytes 706568 | tf_op jit(solution)/shard_map/ppermute | solution.py:354
  69.8 31.5 %collective-permute-start.26 = (bf16[1,184,640]{2,1,0:T(8,128)(2,1)S(1)}, bf16[1,184,640]{2,1,0:T(8,128)(2,1)S(1)}, u32[]{:S(2)}, u32[]{:S(2)}) collective-permute-start(bf16[1,184,640]{2,1,0:T(8,128)(2,1)S(1)} %get-tuple-element.75), channel_id=1, source_target_pairs={{0,6},{2,4},{4,2},{6,0},{8,14},{10,12},{12,10},{14,8},{16,22},{18,... | collective-permute-start | bytes 706568 | tf_op jit(solution)/shard_map/ppermute | solution.py:354
  71.0 17.8 %collective-permute-start.23 = (bf16[2,184,640]{2,1,0:T(8,128)(2,1)S(1)}, bf16[2,184,640]{2,1,0:T(8,128)(2,1)S(1)}, u32[]{:S(2)}, u32[]{:S(2)}) collective-permute-start(bf16[2,184,640]{2,1,0:T(8,128)(2,1)S(1)} %collective-permute-done.21.refs_3_), channel_id=1, source_target_pairs={{0,8},{2,10},{4,28},{6,30},{8,16},{10,18},{12,4},{14,6},{16,24},{1... | collective-permute-start | bytes 1413128 | tf_op jit(solution)/shard_map/ppermute | solution.py:354
  78.7 23.8 %collective-permute-start.27 = (bf16[2,184,640]{2,1,0:T(8,128)(2,1)S(1)}, bf16[2,184,640]{2,1,0:T(8,128)(2,1)S(1)}, u32[]{:S(2)}, u32[]{:S(2)}) collective-permute-start(bf16[2,184,640]{2,1,0:T(8,128)(2,1)S(1)} %get-tuple-element.76), channel_id=1, source_target_pairs={{0,2},{2,0},{4,6},{6,4},{8,10},{10,8},{12,14},{14,12},{16,18},{18,... | collective-permute-start | bytes 1413128 | tf_op jit(solution)/shard_map/ppermute | solution.py:354
  81.5 16.3 %collective-permute-start.24 = (bf16[2,184,640]{2,1,0:T(8,128)(2,1)S(1)}, bf16[2,184,640]{2,1,0:T(8,128)(2,1)S(1)}, u32[]{:S(2)}, u32[]{:S(2)}) collective-permute-start(bf16[2,184,640]{2,1,0:T(8,128)(2,1)S(1)} %collective-permute-done.22.refs_4_), channel_id=1, source_target_pairs={{0,8},{2,10},{4,28},{6,30},{8,16},{10,18},{12,4},{14,6},{16,24},{1... | collective-permute-start | bytes 1413128 | tf_op jit(solution)/shard_map/ppermute | solution.py:354
  88.8 13.7 %collective-permute-start.28 = (bf16[2,184,640]{2,1,0:T(8,128)(2,1)S(1)}, bf16[2,184,640]{2,1,0:T(8,128)(2,1)S(1)}, u32[]{:S(2)}, u32[]{:S(2)}) collective-permute-start(bf16[2,184,640]{2,1,0:T(8,128)(2,1)S(1)} %get-tuple-element.77), channel_id=1, source_target_pairs={{0,2},{2,0},{4,6},{6,4},{8,10},{10,8},{12,14},{14,12},{16,18},{18,... | collective-permute-start | bytes 1413128 | tf_op jit(solution)/shard_map/ppermute | solution.py:354
  99.0 3.5 %collective-permute-start.29 = (bf16[2,184,640]{2,1,0:T(8,128)(2,1)S(1)}, bf16[2,184,640]{2,1,0:T(8,128)(2,1)S(1)}, u32[]{:S(2)}, u32[]{:S(2)}) collective-permute-start(bf16[2,184,640]{2,1,0:T(8,128)(2,1)S(1)} %get-tuple-element.78), channel_id=1, source_target_pairs={{0,2},{2,0},{4,6},{6,4},{8,10},{10,8},{12,14},{14,12},{16,18},{18,... | collective-permute-start | bytes 1413128 | tf_op jit(solution)/shard_map/ppermute | solution.py:354
  100.8 1.7 %collective-permute-start.25 = (bf16[1,184,640]{2,1,0:T(8,128)(2,1)S(1)}, bf16[1,184,640]{2,1,0:T(8,128)(2,1)S(1)}, u32[]{:S(2)}, u32[]{:S(2)}) collective-permute-start(bf16[1,184,640]{2,1,0:T(8,128)(2,1)S(1)} %get-tuple-element.74), channel_id=1, source_target_pairs={{0,2},{2,0},{4,6},{6,4},{8,10},{10,8},{12,14},{14,12},{16,18},{18,... | collective-permute-start | bytes 706568 | tf_op jit(solution)/shard_map/ppermute | solution.py:354

commit v9 on v8

--- a/solution.py
+++ b/solution.py
@@ -11,26 +11,27 @@
 SMEM_SPEC = pl.BlockSpec(memory_space=pltpu.SMEM)
 VMEM_SPEC = pl.BlockSpec(memory_space=pltpu.VMEM)
 HBM_SPEC = pl.BlockSpec(memory_space=pltpu.HBM)
-STAY = (1, 1, 2)
+STAY = (2, 2)
 COME = (2, 2)
-PARTS = [("k", 2), ("c", 2), ("y", 0), ("y", 1), ("y", 2), ("y", 3)]
-FILTERS = ((2, 3), (4, 5), (6, 7))
+PARTS = [("y", 0), ("y", 1), ("y", 2), ("y", 3)]
+FILTERS = ((4, 5), (6, 7))
 WAITS = {
-    ("x", 1): [("q", 0)],
-    ("x", 2): [("x", 0), ("q", 1)],
-    ("x", 3): [("x", 1), ("q", 2)],
-    ("x", 4): [("x", 2), ("q", 3), ("x", 1), ("t", 1)],
-    ("x", 5): [("x", 3), ("z", 0), ("f", 0)],
+    ("x", 0): [("p", 0)],
+    ("x", 1): [("p", 1), ("q", 1)],
+    ("x", 3): [("x", 1)],
+    ("b", 1): [("t", 0)],
+    ("b", 2): [("x", 3)],
+    ("q", 2): [("q", 0)],
     ("q", 3): [("q", 1)],
     ("z", 0): [("q", 2)],
     ("z", 1): [("q", 3)],
     ("z", 2): [("z", 0)],
     ("z", 3): [("z", 1)],
-    ("z", 4): [("z", 2)],
-    ("y", 2): [("y", 0)],
+    ("y", 2): [("y", 0), ("p", 0)],
     ("y", 3): [("y", 1)],
+    ("y", 1): [("q", 0)],
 }
-FLOPS = 6
+FLOPS = 3
 
 
 def up_to(value, multiple):
@@ -98,7 +99,7 @@
 
     def traded(n):
         within = n % quarter
-        return n + jnp.where(within < 2, (within + x) % 2 - within, 0)
+        return n - within + (within + quarter // 2 * x) % quarter
 
     stay, leave, come = jnp.int32(0), jnp.int32(0), jnp.int32(0)
     for j in range(lat_dev):
@@ -377,7 +378,8 @@
                 panels = here + beside + [get("q", 2), get("q", 3)]
             else:
                 panels = beside + [get("q", 0), get("q", 1)] + here
-            result = filter_pair(scalars, lines, [[(p, 0) for p in panels]], 0, lon_dev)
+            places = [[(p, row) for p in panels] for row in range(STAY[0])]
+            result = filter_pair(scalars, lines, places, 0, lon_dev)
         elif kind == "b":
             operand, pairs = ((get("t", 0)[1], across_core), (get("t", 1)[0], across_x), (get("t", 1)[1], across_x_core))[i]
             result = moved(operand, "lon", pairs)

time: 106 us -> 103 us (0.972)
  starting transfers between devices: 48.1 us -> 34.2 us
  waiting for transfers between devices: 36.3 us -> 48.5 us
    ppermute x30 -> x24, starting transfers between devices: 48.1 us -> 34.2 us  [moved(): return lax.ppermute(operand, axes, pairs)]
    ppermute x30 -> x24, waiting for transfers between devices: 36.3 us -> 48.5 us  [moved(): return lax.ppermute(operand, axes, pairs)]
    pallas_call x6 -> x5, Pallas kernels: 12 us -> 11.3 us  [filter_pair(): pl.pallas_call(functools.partial(pair_kernel, lon_dev, base, tuple(plan),...]
  transfers between devices with their start and end apart: 30 -> 24, of which waited for: 16 -> 12; matrix products, arithmetic and copies ran while one was open for 0% -> 0% of each run, Pallas kernels for 11% -> 11%
where the time goes in v9:
time: 103 us
  waiting for transfers between devices  48.5 us (47%)
  starting transfers between devices  34.2 us (33%)
  Pallas kernels  17.2 us (17%)
  local copies, waits for them, and re-layouts  2.71 us (3%)
    ppermute x24, waiting for transfers between devices, moved(): return lax.ppermute(operand, axes, pairs)  48.5 us
    ppermute x24, starting transfers between devices, moved(): return lax.ppermute(operand, axes, pairs)  34.2 us
    pallas_call x5, Pallas kernels, filter_pair(): pl.pallas_call(functools.partial(pair_kernel, lon_dev, base, tuple(plan),...  11.3 us
    pallas_call x1, Pallas kernels, take_rows(): pl.pallas_call(functools.partial(take_kernel, chunks, lat_dev, block), ou...  3.1 us
    pallas_call x1, Pallas kernels, put_rows(): pl.pallas_call(functools.partial(put_kernel, counts, lat_dev, block), out...  2.77 us
    unnamed x8, local copies, waits for them, and re-layouts  2.71 us
  transfers between devices with their start and end apart: 24, of which 12 were waited for; matrix products, arithmetic and copies ran while one was open for 0% of the time, Pallas kernels for 11%

profile of v9, /device:TPU:0, one launch (start us, length us, event | category | flops | bytes accessed | tf_op | source)
XLA Modules:
  0.0 103.0 jit_solution(8770992565607207958)
XLA Ops:
  0.0 0.0 copy-start.3
  0.0 0.1 pad_add_fusion.place_ref
  0.1 0.0 copy-start
  0.1 2.0 %copy-done = bf16[16,180,640]{2,0,1:T(8,128)(2,1)S(1)} copy-done((bf16[16,180,640]{2,0,1:T(8,128)(2,1)S(1)}, bf16[16,180,640]{2,0,1:T(8,128)(2,1)}, u32[]{:S(2)}) %copy-start) | copy-done | bytes 3686424
  2.1 0.0 copy-start.2
  2.1 0.7 copy-done.2
  2.8 3.1 %take_rows.1 = (bf16[2,184,640]{2,1,0:T(8,128)(2,1)S(1)}, bf16[2,184,640]{2,1,0:T(8,128)(2,1)S(1)}, bf16[2,184,640]{2,1,0:T(8,128)(2,1)S(1)}, bf16[2,184,640]{2,...) custom-call(s32[32]{0:T(128)S(1)} %copy-done.2, ...), custom_call_target="tpu_custom_call" | custom-call | flops 943718400 | bytes 7372800 | tf_op jit(solution)/shard_map/take_rows/pallas_call | solution.py:155
  5.9 0.5 collective-permute-start
  6.4 4.7 %collective-permute-start.3 = (bf16[2,184,640]{2,1,0:T(8,128)(2,1)S(1)}, bf16[2,184,640]{2,1,0:T(8,128)(2,1)S(1)}, u32[]{:S(2)}, u32[]{:S(2)}) collective-permute-start(bf16[2,184,640]{2,1,0:T(8,128)(2,1)S(1)} %get-tuple-element.41.refs_1_.refs_5_), channel_id=1, source_target_pairs={{0,24},{2,26},{4,12},{6,14},{8,0},{10,2},{12,20},{14,22},{16,8},{1... | collective-permute-start | bytes 1413128 | tf_op jit(solution)/shard_map/ppermute | solution.py:355
  11.1 0.0 collective-permute-start.1
  11.1 1.5 %collective-permute-start.8 = (bf16[2,184,640]{2,1,0:T(8,128)(2,1)S(1)}, bf16[2,184,640]{2,1,0:T(8,128)(2,1)S(1)}, u32[]{:S(2)}, u32[]{:S(2)}) collective-permute-start(bf16[2,184,640]{2,1,0:T(8,128)(2,1)S(1)} %get-tuple-element.50), channel_id=1, source_target_pairs={{0,1},{1,0},{2,3},{3,2},{4,5},{5,4},{6,7},{7,6},{8,9},{9,8},{10,11... | collective-permute-start | bytes 1413128 | tf_op jit(solution)/shard_map/ppermute | solution.py:355
  12.6 1.2 %collective-permute-start.2 = (bf16[2,184,640]{2,1,0:T(8,128)(2,1)S(1)}, bf16[2,184,640]{2,1,0:T(8,128)(2,1)S(1)}, u32[]{:S(2)}, u32[]{:S(2)}) collective-permute-start(bf16[2,184,640]{2,1,0:T(8,128)(2,1)S(1)} %get-tuple-element.44), channel_id=1, source_target_pairs={{0,6},{2,4},{4,2},{6,0},{8,14},{10,12},{12,10},{14,8},{16,22},{18,... | collective-permute-start | bytes 1413128 | tf_op jit(solution)/shard_map/ppermute | solution.py:355
  13.8 0.0 collective-permute-done.refs_2_.refs_6_
  13.8 0.5 collective-permute-start.5
  14.3 7.9 %collective-permute-done.3.refs_3_ = bf16[2,184,640]{2,1,0:T(8,128)(2,1)S(1)} collective-permute-done((bf16[2,184,640]{2,1,0:T(8,128)(2,1)S(1)}, bf16[2,184,640]{2,1,0:T(8,128)(2,1)S(1)}, u32[]{:S(2)}, u32[]{:S(2)}) %collective-permute-start.3) | collective-permute-done | bytes 471072 | tf_op jit(solution)/shard_map/ppermute | solution.py:355
  22.2 0.3 collective-permute-start.9
  22.5 2.2 %collective-permute-done.1.refs_3_.refs_1_ = bf16[2,184,640]{2,1,0:T(8,128)(2,1)S(1)} collective-permute-done((bf16[2,184,640]{2,1,0:T(8,128)(2,1)S(1)}, bf16[2,184,640]{2,1,0:T(8,128)(2,1)S(1)}, u32[]{:S(2)}, u32[]{:S(2)}) %collective-permute-start.1) | collective-permute-done | bytes 471072 | tf_op jit(solution)/shard_map/ppermute | solution.py:355
  24.7 0.0 collective-permute-start.4
  24.7 0.0 collective-permute-done.8.refs_1_
  24.7 1.8 %collective-permute-start.10 = (bf16[2,184,640]{2,1,0:T(8,128)(2,1)S(1)}, bf16[2,184,640]{2,1,0:T(8,128)(2,1)S(1)}, u32[]{:S(2)}, u32[]{:S(2)}) collective-permute-start(bf16[2,184,640]{2,1,0:T(8,128)(2,1)S(1)} %collective-permute-done.8.refs_1_), channel_id=1, source_target_pairs={{0,4},{2,6},{4,0},{6,2},{8,12},{10,14},{12,8},{14,10},{16,20},{18,... | collective-permute-start | bytes 1413128 | tf_op jit(solution)/shard_map/ppermute | solution.py:355
  26.5 6.8 %collective-permute-done.2.refs_4_.refs_2_ = bf16[2,184,640]{2,1,0:T(8,128)(2,1)S(1)} collective-permute-done((bf16[2,184,640]{2,1,0:T(8,128)(2,1)S(1)}, bf16[2,184,640]{2,1,0:T(8,128)(2,1)S(1)}, u32[]{:S(2)}, u32[]{:S(2)}) %collective-permute-start.2) | collective-permute-done | bytes 471072 | tf_op jit(solution)/shard_map/ppermute | solution.py:355
  33.2 1.5 %collective-permute-start.14 = (bf16[2,184,640]{2,1,0:T(8,128)(2,1)S(1)}, bf16[2,184,640]{2,1,0:T(8,128)(2,1)S(1)}, u32[]{:S(2)}, u32[]{:S(2)}) collective-permute-start(bf16[2,184,640]{2,1,0:T(8,128)(2,1)S(1)} %get-tuple-element.59), channel_id=1, source_target_pairs={{0,1},{1,0},{2,3},{3,2},{4,5},{5,4},{6,7},{7,6},{8,9},{9,8},{10,11... | collective-permute-start | bytes 1413128 | tf_op jit(solution)/shard_map/ppermute | solution.py:355
  34.7 0.0 collective-permute-done.5.refs_4_
  34.7 0.2 collective-permute-start.6
  34.9 0.3 collective-permute-done.9.refs_2_
  35.2 15.8 %collective-permute-start.11 = (bf16[2,184,640]{2,1,0:T(8,128)(2,1)S(1)}, bf16[2,184,640]{2,1,0:T(8,128)(2,1)S(1)}, u32[]{:S(2)}, u32[]{:S(2)}) collective-permute-start(bf16[2,184,640]{2,1,0:T(8,128)(2,1)S(1)} %collective-permute-done.9.refs_2_), channel_id=1, source_target_pairs={{0,4},{2,6},{4,0},{6,2},{8,12},{10,14},{12,8},{14,10},{16,20},{18,... | collective-permute-start | bytes 1413128 | tf_op jit(solution)/shard_map/ppermute | solution.py:355
  50.9 0.0 collective-permute-done.4.refs_5_
  50.9 0.0 collective-permute-start.15
  50.9 0.0 copy-done.1
  50.9 0.1 tap_lines.1.refs_0_
  51.0 0.0 collective-permute-done.10.refs_3_
  51.1 0.1 collective-permute-start.12
  51.1 0.0 collective-permute-done.14.refs_1_
  51.1 0.5 collective-permute-start.16
  51.6 1.3 %collective-permute-done.6.refs_6_ = bf16[2,184,640]{2,1,0:T(8,128)(2,1)S(1)} collective-permute-done((bf16[2,184,640]{2,1,0:T(8,128)(2,1)S(1)}, bf16[2,184,640]{2,1,0:T(8,128)(2,1)S(1)}, u32[]{:S(2)}, u32[]{:S(2)}) %collective-permute-start.6) | collective-permute-done | bytes 471072 | tf_op jit(solution)/shard_map/ppermute | solution.py:355
  52.9 8.0 %collective-permute-done.11.refs_4_ = bf16[2,184,640]{2,1,0:T(8,128)(2,1)S(1)} collective-permute-done((bf16[2,184,640]{2,1,0:T(8,128)(2,1)S(1)}, bf16[2,184,640]{2,1,0:T(8,128)(2,1)S(1)}, u32[]{:S(2)}, u32[]{:S(2)}) %collective-permute-start.11) | collective-permute-done | bytes 471072 | tf_op jit(solution)/shard_map/ppermute | solution.py:355
  60.9 0.0 collective-permute-start.13
  60.9 3.1 %collective-permute-done.15.refs_2_ = bf16[2,184,640]{2,1,0:T(8,128)(2,1)S(1)} collective-permute-done((bf16[2,184,640]{2,1,0:T(8,128)(2,1)S(1)}, bf16[2,184,640]{2,1,0:T(8,128)(2,1)S(1)}, u32[]{:S(2)}, u32[]{:S(2)}) %collective-permute-start.15) | collective-permute-done | bytes 471072 | tf_op jit(solution)/shard_map/ppermute | solution.py:355
  63.9 1.0 %collective-permute-start.17 = (bf16[2,184,640]{2,1,0:T(8,128)(2,1)S(1)}, bf16[2,184,640]{2,1,0:T(8,128)(2,1)S(1)}, u32[]{:S(2)}, u32[]{:S(2)}) collective-permute-start(bf16[2,184,640]{2,1,0:T(8,128)(2,1)S(1)} %collective-permute-done.15.refs_2_), channel_id=1, source_target_pairs={{0,4},{2,6},{4,0},{6,2},{8,12},{10,14},{12,8},{14,10},{16,20},{18,... | collective-permute-start | bytes 1413128 | tf_op jit(solution)/shard_map/ppermute | solution.py:355
  65.0 0.0 copy-done.3
  65.0 2.6 %filter_whole.4 = (bf16[2,184,640]{2,1,0:T(8,128)(2,1)S(1)}, bf16[2,184,640]{2,1,0:T(8,128)(2,1)S(1)}) custom-call(s32[16]{0:T(128)S(1)} %get-tuple-element.40.rows_ref, s32[3]{0:T(128)S(1)} %pad_add_fusion.place_ref, s32[32]{0:T(128)S(1)} %copy-done.3, f32[32,1152]{1,0:T(8,128)S(1)} %tap_lines.1.refs_0_, ...), custom_call_target="tpu_custom_call" | custom-call | flops 3019898880 | bytes 3768320 | tf_op jit(solution)/shard_map/filter_whole/pallas_call | solution.py:304
  67.6 2.6 %filter_whole.3 = (bf16[2,184,640]{2,1,0:T(8,128)(2,1)S(1)}, bf16[2,184,640]{2,1,0:T(8,128)(2,1)S(1)}) custom-call(s32[16]{0:T(128)S(1)} %get-tuple-element.40.rows_ref, s32[3]{0:T(128)S(1)} %pad_add_fusion.place_ref, s32[32]{0:T(128)S(1)} %copy-done.3, f32[32,1152]{1,0:T(8,128)S(1)} %tap_lines.1.refs_0_, ...), custom_call_target="tpu_custom_call" | custom-call | flops 3019898880 | bytes 3768320 | tf_op jit(solution)/shard_map/filter_whole/pallas_call | solution.py:304
  70.2 1.0 %collective-permute-start.7 = (bf16[2,184,640]{2,1,0:T(8,128)(2,1)S(1)}, bf16[2,184,640]{2,1,0:T(8,128)(2,1)S(1)}, u32[]{:S(2)}, u32[]{:S(2)}) collective-permute-start(bf16[2,184,640]{2,1,0:T(8,128)(2,1)S(1)} %get-tuple-element.49), channel_id=1, source_target_pairs={{0,4},{2,6},{4,0},{6,2},{8,12},{10,14},{12,8},{14,10},{16,20},{18,... | collective-permute-start | bytes 1413128 | tf_op jit(solution)/shard_map/ppermute | solution.py:355
  71.2 0.0 collective-permute-done.12.refs_5_
  71.2 0.0 collective-permute-done.16.refs_3_
  71.2 0.0 collective-permute-start.18
  71.3 0.1 collective-permute-start.20
  71.3 5.1 %collective-permute-done.13.refs_6_ = bf16[2,184,640]{2,1,0:T(8,128)(2,1)S(1)} collective-permute-done((bf16[2,184,640]{2,1,0:T(8,128)(2,1)S(1)}, bf16[2,184,640]{2,1,0:T(8,128)(2,1)S(1)}, u32[]{:S(2)}, u32[]{:S(2)}) %collective-permute-start.13) | collective-permute-done | bytes 471072 | tf_op jit(solution)/shard_map/ppermute | solution.py:355
  76.4 3.4 %collective-permute-done.17.refs_4_ = bf16[2,184,640]{2,1,0:T(8,128)(2,1)S(1)} collective-permute-done((bf16[2,184,640]{2,1,0:T(8,128)(2,1)S(1)}, bf16[2,184,640]{2,1,0:T(8,128)(2,1)S(1)}, u32[]{:S(2)}, u32[]{:S(2)}) %collective-permute-start.17) | collective-permute-done | bytes 471072 | tf_op jit(solution)/shard_map/ppermute | solution.py:355
  79.8 0.0 collective-permute-start.19
  79.8 0.0 collective-permute-start.21
  79.8 2.1 %filter_early.1 = (f32[2,184,1280]{2,1,0:T(8,128)S(1)}, bf16[2,5,192,184]{3,2,1,0:T(8,128)(2,1)S(1)}) custom-call(s32[16]{0:T(128)S(1)} %get-tuple-element.40.rows_ref, s32[3]{0:T(128)S(1)} %pad_add_fusion.place_ref, s32[32]{0:T(128)S(1)} %copy-done.3, f32[32,1152]{1,0:T(8,128)S(1)} %tap_lines.1.refs_0_, ...), custom_call_target="tpu_custom_call" | custom-call | flops 2113929216 | bytes 3768320 | tf_op jit(solution)/shard_map/filter_early/pallas_call | solution.py:304
  81.9 2.7 %filter_whole.5 = (bf16[2,184,640]{2,1,0:T(8,128)(2,1)S(1)}, bf16[2,184,640]{2,1,0:T(8,128)(2,1)S(1)}) custom-call(s32[16]{0:T(128)S(1)} %get-tuple-element.40.rows_ref, s32[3]{0:T(128)S(1)} %pad_add_fusion.place_ref, s32[32]{0:T(128)S(1)} %copy-done.3, f32[32,1152]{1,0:T(8,128)S(1)} %tap_lines.1.refs_0_, ...), custom_call_target="tpu_custom_call" | custom-call | flops 3019898880 | bytes 3768320 | tf_op jit(solution)/shard_map/filter_whole/pallas_call | solution.py:304
  84.6 2.2 %collective-permute-done.18.refs_2_ = bf16[2,184,640]{2,1,0:T(8,128)(2,1)S(1)} collective-permute-done((bf16[2,184,640]{2,1,0:T(8,128)(2,1)S(1)}, bf16[2,184,640]{2,1,0:T(8,128)(2,1)S(1)}, u32[]{:S(2)}, u32[]{:S(2)}) %collective-permute-start.18) | collective-permute-done | bytes 471072 | tf_op jit(solution)/shard_map/ppermute | solution.py:355
  86.8 3.4 %collective-permute-start.22 = (bf16[2,184,640]{2,1,0:T(8,128)(2,1)S(1)}, bf16[2,184,640]{2,1,0:T(8,128)(2,1)S(1)}, u32[]{:S(2)}, u32[]{:S(2)}) collective-permute-start(bf16[2,184,640]{2,1,0:T(8,128)(2,1)S(1)} %get-tuple-element.71), channel_id=1, source_target_pairs={{0,2},{2,0},{4,6},{6,4},{8,10},{10,8},{12,14},{14,12},{16,18},{18,... | collective-permute-start | bytes 1413128 | tf_op jit(solution)/shard_map/ppermute | solution.py:355
  90.1 6.7 %collective-permute-done.19.refs_3_ = bf16[2,184,640]{2,1,0:T(8,128)(2,1)S(1)} collective-permute-done((bf16[2,184,640]{2,1,0:T(8,128)(2,1)S(1)}, bf16[2,184,640]{2,1,0:T(8,128)(2,1)S(1)}, u32[]{:S(2)}, u32[]{:S(2)}) %collective-permute-start.19) | collective-permute-done | bytes 471072 | tf_op jit(solution)/shard_map/ppermute | solution.py:355
  96.8 1.3 %filter_late.1 = (bf16[2,184,640]{2,1,0:T(8,128)(2,1)S(1)}, bf16[2,184,640]{2,1,0:T(8,128)(2,1)S(1)}) custom-call(s32[16]{0:T(128)S(1)} %get-tuple-element.40.rows_ref, s32[3]{0:T(128)S(1)} %pad_add_fusion.place_ref, s32[32]{0:T(128)S(1)} %copy-done.3, f32[2,184,1280]{2,1,0:T(8,128)S(1)} %get-tuple-element.63.refs_0_, ...), custom_call_target="tpu_custom_call" | custom-call | flops 905969664 | bytes 3768320 | tf_op jit(solution)/shard_map/filter_late/pallas_call | solution.py:304
  98.2 0.2 collective-permute-start.23
  98.3 0.0 collective-permute-done.7.refs_1_
  98.3 0.0 collective-permute-done.20.refs_4_
  98.3 0.0 collective-permute-done.21.refs_5_
  98.3 0.0 collective-permute-done.22.refs_6_
  98.3 1.7 %collective-permute-done.23.refs_7_ = bf16[2,184,640]{2,1,0:T(8,128)(2,1)S(1)} collective-permute-done((bf16[2,184,640]{2,1,0:T(8,128)(2,1)S(1)}, bf16[2,184,640]{2,1,0:T(8,128)(2,1)S(1)}, u32[]{:S(2)}, u32[]{:S(2)}) %collective-permute-start.23) | collective-permute-done | bytes 471072 | tf_op jit(solution)/shard_map/ppermute | solution.py:355
  100.1 2.8 %put_rows.1 = bf16[180,16,640]{2,1,0:T(8,128)(2,1)} custom-call(s32[16]{0:T(128)S(1)} %get-tuple-element.39.slots_ref, bf16[2,184,640]{2,1,0:T(8,128)(2,1)S(1)} %get-tuple-element.47.refs_0_, bf16[2,184,640]{2,1,0:T(8,128)(2,1)S(1)} %collective-permute-done.7.refs_1_, bf16[2,184,640]{2,1,0:T(8,128)(2,1)S(1)} %get-tuple-element.57.refs_2_, ...), custom_call_target="tpu_custom_call" | custom-call | flops 943718400 | bytes 7372800 | tf_op jit(solution)/shard_map/put_rows/pallas_call | solution.py:207
  (1 shorter events, 0.0 us)
Async XLA Ops:
  0.0 65.0 %copy-start.3 = (s32[32]{0:T(128)S(1)}, s32[32]{0:T(128)}, u32[]{:S(2)}) copy-start(s32[32]{0:T(128)} %widths_ref.9) | copy-start | bytes 388
  0.1 2.0 %copy-start = (bf16[16,180,640]{2,0,1:T(8,128)(2,1)S(1)}, bf16[16,180,640]{2,0,1:T(8,128)(2,1)}, u32[]{:S(2)}) copy-start(bf16[16,180,640]{2,0,1:T(8,128)(2,1)} %param.4) | copy-start | bytes 11059204
  2.1 0.7 copy-start.2
  2.8 48.2 %copy-start.1 = (bf16[32,2880]{1,0:T(8,128)(2,1)S(1)}, bf16[32,2880]{1,0:T(8,128)(2,1)}, u32[]{:S(2)}) copy-start(bf16[32,2880]{1,0:T(8,128)(2,1)} %taps_ref.1) | copy-start | bytes 552964
  5.9 7.9 %collective-permute-start = (bf16[2,184,640]{2,1,0:T(8,128)(2,1)S(1)}, bf16[2,184,640]{2,1,0:T(8,128)(2,1)S(1)}, u32[]{:S(2)}, u32[]{:S(2)}) collective-permute-start(bf16[2,184,640]{2,1,0:T(8,128)(2,1)S(1)} %get-tuple-element.42), channel_id=1, source_target_pairs={{0,2},{2,0},{4,6},{6,4},{8,10},{10,8},{12,14},{14,12},{16,18},{18,... | collective-permute-start | bytes 1413128 | tf_op jit(solution)/shard_map/ppermute | solution.py:355
  6.4 15.8 %collective-permute-start.3 = (bf16[2,184,640]{2,1,0:T(8,128)(2,1)S(1)}, bf16[2,184,640]{2,1,0:T(8,128)(2,1)S(1)}, u32[]{:S(2)}, u32[]{:S(2)}) collective-permute-start(bf16[2,184,640]{2,1,0:T(8,128)(2,1)S(1)} %get-tuple-element.41.refs_1_.refs_5_), channel_id=1, source_target_pairs={{0,24},{2,26},{4,12},{6,14},{8,0},{10,2},{12,20},{14,22},{16,8},{1... | collective-permute-start | bytes 1413128 | tf_op jit(solution)/shard_map/ppermute | solution.py:355
  11.1 13.6 %collective-permute-start.1 = (bf16[2,184,640]{2,1,0:T(8,128)(2,1)S(1)}, bf16[2,184,640]{2,1,0:T(8,128)(2,1)S(1)}, u32[]{:S(2)}, u32[]{:S(2)}) collective-permute-start(bf16[2,184,640]{2,1,0:T(8,128)(2,1)S(1)} %get-tuple-element.43), channel_id=1, source_target_pairs={{0,4},{2,6},{4,0},{6,2},{8,12},{10,14},{12,8},{14,10},{16,20},{18,... | collective-permute-start | bytes 1413128 | tf_op jit(solution)/shard_map/ppermute | solution.py:355
  11.1 13.6 %collective-permute-start.8 = (bf16[2,184,640]{2,1,0:T(8,128)(2,1)S(1)}, bf16[2,184,640]{2,1,0:T(8,128)(2,1)S(1)}, u32[]{:S(2)}, u32[]{:S(2)}) collective-permute-start(bf16[2,184,640]{2,1,0:T(8,128)(2,1)S(1)} %get-tuple-element.50), channel_id=1, source_target_pairs={{0,1},{1,0},{2,3},{3,2},{4,5},{5,4},{6,7},{7,6},{8,9},{9,8},{10,11... | collective-permute-start | bytes 1413128 | tf_op jit(solution)/shard_map/ppermute | solution.py:355
  12.6 20.6 %collective-permute-start.2 = (bf16[2,184,640]{2,1,0:T(8,128)(2,1)S(1)}, bf16[2,184,640]{2,1,0:T(8,128)(2,1)S(1)}, u32[]{:S(2)}, u32[]{:S(2)}) collective-permute-start(bf16[2,184,640]{2,1,0:T(8,128)(2,1)S(1)} %get-tuple-element.44), channel_id=1, source_target_pairs={{0,6},{2,4},{4,2},{6,0},{8,14},{10,12},{12,10},{14,8},{16,22},{18,... | collective-permute-start | bytes 1413128 | tf_op jit(solution)/shard_map/ppermute | solution.py:355
  13.8 20.9 %collective-permute-start.5 = (bf16[2,184,640]{2,1,0:T(8,128)(2,1)S(1)}, bf16[2,184,640]{2,1,0:T(8,128)(2,1)S(1)}, u32[]{:S(2)}, u32[]{:S(2)}) collective-permute-start(bf16[2,184,640]{2,1,0:T(8,128)(2,1)S(1)} %collective-permute-done.refs_2_.refs_6_), channel_id=1, source_target_pairs={{0,24},{2,26},{4,12},{6,14},{8,0},{10,2},{12,20},{14,22},{16,8},{1... | collective-permute-start | bytes 1413128 | tf_op jit(solution)/shard_map/ppermute | solution.py:355
  22.2 13.0 %collective-permute-start.9 = (bf16[2,184,640]{2,1,0:T(8,128)(2,1)S(1)}, bf16[2,184,640]{2,1,0:T(8,128)(2,1)S(1)}, u32[]{:S(2)}, u32[]{:S(2)}) collective-permute-start(bf16[2,184,640]{2,1,0:T(8,128)(2,1)S(1)} %get-tuple-element.52), channel_id=1, source_target_pairs={{0,3},{1,2},{2,1},{3,0},{4,7},{5,6},{6,5},{7,4},{8,11},{9,10},{10,... | collective-permute-start | bytes 1413128 | tf_op jit(solution)/shard_map/ppermute | solution.py:355
  24.7 26.2 %collective-permute-start.4 = (bf16[2,184,640]{2,1,0:T(8,128)(2,1)S(1)}, bf16[2,184,640]{2,1,0:T(8,128)(2,1)S(1)}, u32[]{:S(2)}, u32[]{:S(2)}) collective-permute-start(bf16[2,184,640]{2,1,0:T(8,128)(2,1)S(1)} %collective-permute-done.1.refs_3_.refs_1_), channel_id=1, source_target_pairs={{0,8},{2,10},{4,28},{6,30},{8,16},{10,18},{12,4},{14,6},{16,24},{1... | collective-permute-start | bytes 1413128 | tf_op jit(solution)/shard_map/ppermute | solution.py:355
  24.7 26.3 %collective-permute-start.10 = (bf16[2,184,640]{2,1,0:T(8,128)(2,1)S(1)}, bf16[2,184,640]{2,1,0:T(8,128)(2,1)S(1)}, u32[]{:S(2)}, u32[]{:S(2)}) collective-permute-start(bf16[2,184,640]{2,1,0:T(8,128)(2,1)S(1)} %collective-permute-done.8.refs_1_), channel_id=1, source_target_pairs={{0,4},{2,6},{4,0},{6,2},{8,12},{10,14},{12,8},{14,10},{16,20},{18,... | collective-permute-start | bytes 1413128 | tf_op jit(solution)/shard_map/ppermute | solution.py:355
  33.2 17.9 %collective-permute-start.14 = (bf16[2,184,640]{2,1,0:T(8,128)(2,1)S(1)}, bf16[2,184,640]{2,1,0:T(8,128)(2,1)S(1)}, u32[]{:S(2)}, u32[]{:S(2)}) collective-permute-start(bf16[2,184,640]{2,1,0:T(8,128)(2,1)S(1)} %get-tuple-element.59), channel_id=1, source_target_pairs={{0,1},{1,0},{2,3},{3,2},{4,5},{5,4},{6,7},{7,6},{8,9},{9,8},{10,11... | collective-permute-start | bytes 1413128 | tf_op jit(solution)/shard_map/ppermute | solution.py:355
  34.7 18.2 %collective-permute-start.6 = (bf16[2,184,640]{2,1,0:T(8,128)(2,1)S(1)}, bf16[2,184,640]{2,1,0:T(8,128)(2,1)S(1)}, u32[]{:S(2)}, u32[]{:S(2)}) collective-permute-start(bf16[2,184,640]{2,1,0:T(8,128)(2,1)S(1)} %collective-permute-done.2.refs_4_.refs_2_), channel_id=1, source_target_pairs={{0,8},{2,10},{4,28},{6,30},{8,16},{10,18},{12,4},{14,6},{16,24},{1... | collective-permute-start | bytes 1413128 | tf_op jit(solution)/shard_map/ppermute | solution.py:355
  35.2 25.7 %collective-permute-start.11 = (bf16[2,184,640]{2,1,0:T(8,128)(2,1)S(1)}, bf16[2,184,640]{2,1,0:T(8,128)(2,1)S(1)}, u32[]{:S(2)}, u32[]{:S(2)}) collective-permute-start(bf16[2,184,640]{2,1,0:T(8,128)(2,1)S(1)} %collective-permute-done.9.refs_2_), channel_id=1, source_target_pairs={{0,4},{2,6},{4,0},{6,2},{8,12},{10,14},{12,8},{14,10},{16,20},{18,... | collective-permute-start | bytes 1413128 | tf_op jit(solution)/shard_map/ppermute | solution.py:355
  50.9 13.0 %collective-permute-start.15 = (bf16[2,184,640]{2,1,0:T(8,128)(2,1)S(1)}, bf16[2,184,640]{2,1,0:T(8,128)(2,1)S(1)}, u32[]{:S(2)}, u32[]{:S(2)}) collective-permute-start(bf16[2,184,640]{2,1,0:T(8,128)(2,1)S(1)} %get-tuple-element.61), channel_id=1, source_target_pairs={{0,3},{1,2},{2,1},{3,0},{4,7},{5,6},{6,5},{7,4},{8,11},{9,10},{10,... | collective-permute-start | bytes 1413128 | tf_op jit(solution)/shard_map/ppermute | solution.py:355
  51.1 20.2 %collective-permute-start.12 = (bf16[2,184,640]{2,1,0:T(8,128)(2,1)S(1)}, bf16[2,184,640]{2,1,0:T(8,128)(2,1)S(1)}, u32[]{:S(2)}, u32[]{:S(2)}) collective-permute-start(bf16[2,184,640]{2,1,0:T(8,128)(2,1)S(1)} %collective-permute-done.10.refs_3_), channel_id=1, source_target_pairs={{0,8},{2,10},{4,28},{6,30},{8,16},{10,18},{12,4},{14,6},{16,24},{1... | collective-permute-start | bytes 1413128 | tf_op jit(solution)/shard_map/ppermute | solution.py:355
  51.1 20.1 %collective-permute-start.16 = (bf16[2,184,640]{2,1,0:T(8,128)(2,1)S(1)}, bf16[2,184,640]{2,1,0:T(8,128)(2,1)S(1)}, u32[]{:S(2)}, u32[]{:S(2)}) collective-permute-start(bf16[2,184,640]{2,1,0:T(8,128)(2,1)S(1)} %collective-permute-done.14.refs_1_), channel_id=1, source_target_pairs={{0,4},{2,6},{4,0},{6,2},{8,12},{10,14},{12,8},{14,10},{16,20},{18,... | collective-permute-start | bytes 1413128 | tf_op jit(solution)/shard_map/ppermute | solution.py:355
  60.9 15.5 %collective-permute-start.13 = (bf16[2,184,640]{2,1,0:T(8,128)(2,1)S(1)}, bf16[2,184,640]{2,1,0:T(8,128)(2,1)S(1)}, u32[]{:S(2)}, u32[]{:S(2)}) collective-permute-start(bf16[2,184,640]{2,1,0:T(8,128)(2,1)S(1)} %collective-permute-done.11.refs_4_), channel_id=1, source_target_pairs={{0,8},{2,10},{4,28},{6,30},{8,16},{10,18},{12,4},{14,6},{16,24},{1... | collective-permute-start | bytes 1413128 | tf_op jit(solution)/shard_map/ppermute | solution.py:355
  63.9 15.9 %collective-permute-start.17 = (bf16[2,184,640]{2,1,0:T(8,128)(2,1)S(1)}, bf16[2,184,640]{2,1,0:T(8,128)(2,1)S(1)}, u32[]{:S(2)}, u32[]{:S(2)}) collective-permute-start(bf16[2,184,640]{2,1,0:T(8,128)(2,1)S(1)} %collective-permute-done.15.refs_2_), channel_id=1, source_target_pairs={{0,4},{2,6},{4,0},{6,2},{8,12},{10,14},{12,8},{14,10},{16,20},{18,... | collective-permute-start | bytes 1413128 | tf_op jit(solution)/shard_map/ppermute | solution.py:355
  70.2 28.1 %collective-permute-start.7 = (bf16[2,184,640]{2,1,0:T(8,128)(2,1)S(1)}, bf16[2,184,640]{2,1,0:T(8,128)(2,1)S(1)}, u32[]{:S(2)}, u32[]{:S(2)}) collective-permute-start(bf16[2,184,640]{2,1,0:T(8,128)(2,1)S(1)} %get-tuple-element.49), channel_id=1, source_target_pairs={{0,4},{2,6},{4,0},{6,2},{8,12},{10,14},{12,8},{14,10},{16,20},{18,... | collective-permute-start | bytes 1413128 | tf_op jit(solution)/shard_map/ppermute | solution.py:355
  71.2 15.5 %collective-permute-start.18 = (bf16[2,184,640]{2,1,0:T(8,128)(2,1)S(1)}, bf16[2,184,640]{2,1,0:T(8,128)(2,1)S(1)}, u32[]{:S(2)}, u32[]{:S(2)}) collective-permute-start(bf16[2,184,640]{2,1,0:T(8,128)(2,1)S(1)} %collective-permute-done.16.refs_3_), channel_id=1, source_target_pairs={{0,8},{2,10},{4,28},{6,30},{8,16},{10,18},{12,4},{14,6},{16,24},{1... | collective-permute-start | bytes 1413128 | tf_op jit(solution)/shard_map/ppermute | solution.py:355
  71.3 27.1 %collective-permute-start.20 = (bf16[2,184,640]{2,1,0:T(8,128)(2,1)S(1)}, bf16[2,184,640]{2,1,0:T(8,128)(2,1)S(1)}, u32[]{:S(2)}, u32[]{:S(2)}) collective-permute-start(bf16[2,184,640]{2,1,0:T(8,128)(2,1)S(1)} %get-tuple-element.68), channel_id=1, source_target_pairs={{0,2},{2,0},{4,6},{6,4},{8,10},{10,8},{12,14},{14,12},{16,18},{18,... | collective-permute-start | bytes 1413128 | tf_op jit(solution)/shard_map/ppermute | solution.py:355
  79.8 17.0 %collective-permute-start.19 = (bf16[2,184,640]{2,1,0:T(8,128)(2,1)S(1)}, bf16[2,184,640]{2,1,0:T(8,128)(2,1)S(1)}, u32[]{:S(2)}, u32[]{:S(2)}) collective-permute-start(bf16[2,184,640]{2,1,0:T(8,128)(2,1)S(1)} %collective-permute-done.17.refs_4_), channel_id=1, source_target_pairs={{0,8},{2,10},{4,28},{6,30},{8,16},{10,18},{12,4},{14,6},{16,24},{1... | collective-permute-start | bytes 1413128 | tf_op jit(solution)/shard_map/ppermute | solution.py:355
  79.8 18.5 %collective-permute-start.21 = (bf16[2,184,640]{2,1,0:T(8,128)(2,1)S(1)}, bf16[2,184,640]{2,1,0:T(8,128)(2,1)S(1)}, u32[]{:S(2)}, u32[]{:S(2)}) collective-permute-start(bf16[2,184,640]{2,1,0:T(8,128)(2,1)S(1)} %get-tuple-element.70), channel_id=1, source_target_pairs={{0,6},{2,4},{4,2},{6,0},{8,14},{10,12},{12,10},{14,8},{16,22},{18,... | collective-permute-start | bytes 1413128 | tf_op jit(solution)/shard_map/ppermute | solution.py:355
  86.8 11.6 %collective-permute-start.22 = (bf16[2,184,640]{2,1,0:T(8,128)(2,1)S(1)}, bf16[2,184,640]{2,1,0:T(8,128)(2,1)S(1)}, u32[]{:S(2)}, u32[]{:S(2)}) collective-permute-start(bf16[2,184,640]{2,1,0:T(8,128)(2,1)S(1)} %get-tuple-element.71), channel_id=1, source_target_pairs={{0,2},{2,0},{4,6},{6,4},{8,10},{10,8},{12,14},{14,12},{16,18},{18,... | collective-permute-start | bytes 1413128 | tf_op jit(solution)/shard_map/ppermute | solution.py:355
  98.2 1.9 %collective-permute-start.23 = (bf16[2,184,640]{2,1,0:T(8,128)(2,1)S(1)}, bf16[2,184,640]{2,1,0:T(8,128)(2,1)S(1)}, u32[]{:S(2)}, u32[]{:S(2)}) collective-permute-start(bf16[2,184,640]{2,1,0:T(8,128)(2,1)S(1)} %get-tuple-element.72), channel_id=1, source_target_pairs={{0,2},{2,0},{4,6},{6,4},{8,10},{10,8},{12,14},{14,12},{16,18},{18,... | collective-permute-start | bytes 1413128 | tf_op jit(solution)/shard_map/ppermute | solution.py:355

commit v10 on v9

--- a/solution.py
+++ b/solution.py
@@ -16,19 +16,17 @@
 PARTS = [("y", 0), ("y", 1), ("y", 2), ("y", 3)]
 FILTERS = ((4, 5), (6, 7))
 WAITS = {
-    ("x", 0): [("p", 0)],
-    ("x", 1): [("p", 1), ("q", 1)],
-    ("x", 3): [("x", 1)],
-    ("b", 1): [("t", 0)],
+    ("x", 0): [("p", 0), ("y", 0)],
+    ("x", 1): [("p", 1)],
     ("b", 2): [("x", 3)],
     ("q", 2): [("q", 0)],
     ("q", 3): [("q", 1)],
-    ("z", 0): [("q", 2)],
-    ("z", 1): [("q", 3)],
+    ("z", 0): [("q", 2), ("q", 1)],
+    ("z", 1): [("q", 3), ("t", 1)],
     ("z", 2): [("z", 0)],
     ("z", 3): [("z", 1)],
     ("y", 2): [("y", 0), ("p", 0)],
-    ("y", 3): [("y", 1)],
+    ("y", 3): [("y", 1), ("x", 0)],
     ("y", 1): [("q", 0)],
 }
 FLOPS = 3

time: 103 us -> 103 us (level)
  no operation moved by 1% of the time
where the time goes in v10:
time: 103 us
  waiting for transfers between devices  48.7 us (47%)
  starting transfers between devices  33.7 us (33%)
  Pallas kernels  17.2 us (17%)
  local copies, waits for them, and re-layouts  2.71 us (3%)
    ppermute x24, waiting for transfers between devices, moved(): return lax.ppermute(operand, axes, pairs)  48.7 us
    ppermute x24, starting transfers between devices, moved(): return lax.ppermute(operand, axes, pairs)  33.7 us
    pallas_call x5, Pallas kernels, filter_pair(): pl.pallas_call(functools.partial(pair_kernel, lon_dev, base, tuple(plan),...  11.3 us
    pallas_call x1, Pallas kernels, take_rows(): pl.pallas_call(functools.partial(take_kernel, chunks, lat_dev, block), ou...  3.1 us
    pallas_call x1, Pallas kernels, put_rows(): pl.pallas_call(functools.partial(put_kernel, counts, lat_dev, block), out...  2.77 us
    unnamed x8, local copies, waits for them, and re-layouts  2.71 us
  transfers between devices with their start and end apart: 24, of which 12 were waited for; matrix products, arithmetic and copies ran while one was open for 0% of the time, Pallas kernels for 11%

profile of v10, /device:TPU:0, one launch (start us, length us, event | category | flops | bytes accessed | tf_op | source)
XLA Modules:
  0.0 102.7 jit_solution(4302508219975123258)
XLA Ops:
  0.0 0.1 pad_add_fusion.place_ref
  0.1 0.0 copy-start
  0.1 2.0 %copy-done = bf16[16,180,640]{2,0,1:T(8,128)(2,1)S(1)} copy-done((bf16[16,180,640]{2,0,1:T(8,128)(2,1)S(1)}, bf16[16,180,640]{2,0,1:T(8,128)(2,1)}, u32[]{:S(2)}) %copy-start) | copy-done | bytes 3686424
  2.1 0.0 copy-start.2
  2.1 0.7 copy-done.2
  2.8 0.0 copy-start.1
  2.8 3.1 %take_rows.1 = (bf16[2,184,640]{2,1,0:T(8,128)(2,1)S(1)}, bf16[2,184,640]{2,1,0:T(8,128)(2,1)S(1)}, bf16[2,184,640]{2,1,0:T(8,128)(2,1)S(1)}, bf16[2,184,640]{2,...) custom-call(s32[32]{0:T(128)S(1)} %copy-done.2, ...), custom_call_target="tpu_custom_call" | custom-call | flops 943718400 | bytes 7372800 | tf_op jit(solution)/shard_map/take_rows/pallas_call | solution.py:153
  5.9 0.5 collective-permute-start
  6.4 4.7 %collective-permute-start.3 = (bf16[2,184,640]{2,1,0:T(8,128)(2,1)S(1)}, bf16[2,184,640]{2,1,0:T(8,128)(2,1)S(1)}, u32[]{:S(2)}, u32[]{:S(2)}) collective-permute-start(bf16[2,184,640]{2,1,0:T(8,128)(2,1)S(1)} %get-tuple-element.39.refs_1_.refs_5_), channel_id=1, source_target_pairs={{0,24},{2,26},{4,12},{6,14},{8,0},{10,2},{12,20},{14,22},{16,8},{1... | collective-permute-start | bytes 1413128 | tf_op jit(solution)/shard_map/ppermute | solution.py:353
  11.1 0.0 collective-permute-start.1
  11.1 1.5 %collective-permute-start.8 = (bf16[2,184,640]{2,1,0:T(8,128)(2,1)S(1)}, bf16[2,184,640]{2,1,0:T(8,128)(2,1)S(1)}, u32[]{:S(2)}, u32[]{:S(2)}) collective-permute-start(bf16[2,184,640]{2,1,0:T(8,128)(2,1)S(1)} %get-tuple-element.47), channel_id=1, source_target_pairs={{0,1},{1,0},{2,3},{3,2},{4,5},{5,4},{6,7},{7,6},{8,9},{9,8},{10,11... | collective-permute-start | bytes 1413128 | tf_op jit(solution)/shard_map/ppermute | solution.py:353
  12.6 1.2 %collective-permute-start.2 = (bf16[2,184,640]{2,1,0:T(8,128)(2,1)S(1)}, bf16[2,184,640]{2,1,0:T(8,128)(2,1)S(1)}, u32[]{:S(2)}, u32[]{:S(2)}) collective-permute-start(bf16[2,184,640]{2,1,0:T(8,128)(2,1)S(1)} %get-tuple-element.42), channel_id=1, source_target_pairs={{0,6},{2,4},{4,2},{6,0},{8,14},{10,12},{12,10},{14,8},{16,22},{18,... | collective-permute-start | bytes 1413128 | tf_op jit(solution)/shard_map/ppermute | solution.py:353
  13.8 0.0 collective-permute-done.refs_2_.refs_6_
  13.8 0.5 collective-permute-start.5
  14.3 7.9 %collective-permute-done.3.refs_3_ = bf16[2,184,640]{2,1,0:T(8,128)(2,1)S(1)} collective-permute-done((bf16[2,184,640]{2,1,0:T(8,128)(2,1)S(1)}, bf16[2,184,640]{2,1,0:T(8,128)(2,1)S(1)}, u32[]{:S(2)}, u32[]{:S(2)}) %collective-permute-start.3) | collective-permute-done | bytes 471072 | tf_op jit(solution)/shard_map/ppermute | solution.py:353
  22.2 0.3 collective-permute-start.9
  22.5 2.2 %collective-permute-done.1.refs_3_.refs_1_ = bf16[2,184,640]{2,1,0:T(8,128)(2,1)S(1)} collective-permute-done((bf16[2,184,640]{2,1,0:T(8,128)(2,1)S(1)}, bf16[2,184,640]{2,1,0:T(8,128)(2,1)S(1)}, u32[]{:S(2)}, u32[]{:S(2)}) %collective-permute-start.1) | collective-permute-done | bytes 471072 | tf_op jit(solution)/shard_map/ppermute | solution.py:353
  24.7 0.0 collective-permute-done.8.refs_1_
  24.7 1.0 collective-permute-start.10
  25.7 0.1 collective-permute-start.4
  25.7 7.5 %collective-permute-done.2.refs_4_.refs_2_ = bf16[2,184,640]{2,1,0:T(8,128)(2,1)S(1)} collective-permute-done((bf16[2,184,640]{2,1,0:T(8,128)(2,1)S(1)}, bf16[2,184,640]{2,1,0:T(8,128)(2,1)S(1)}, u32[]{:S(2)}, u32[]{:S(2)}) %collective-permute-start.2) | collective-permute-done | bytes 471072 | tf_op jit(solution)/shard_map/ppermute | solution.py:353
  33.2 1.5 %collective-permute-start.14 = (bf16[2,184,640]{2,1,0:T(8,128)(2,1)S(1)}, bf16[2,184,640]{2,1,0:T(8,128)(2,1)S(1)}, u32[]{:S(2)}, u32[]{:S(2)}) collective-permute-start(bf16[2,184,640]{2,1,0:T(8,128)(2,1)S(1)} %get-tuple-element.56), channel_id=1, source_target_pairs={{0,1},{1,0},{2,3},{3,2},{4,5},{5,4},{6,7},{7,6},{8,9},{9,8},{10,11... | collective-permute-start | bytes 1413128 | tf_op jit(solution)/shard_map/ppermute | solution.py:353
  34.7 0.0 collective-permute-done.5.refs_4_
  34.7 0.2 collective-permute-start.6
  34.9 0.3 collective-permute-done.9.refs_2_
  35.2 15.8 %collective-permute-start.11 = (bf16[2,184,640]{2,1,0:T(8,128)(2,1)S(1)}, bf16[2,184,640]{2,1,0:T(8,128)(2,1)S(1)}, u32[]{:S(2)}, u32[]{:S(2)}) collective-permute-start(bf16[2,184,640]{2,1,0:T(8,128)(2,1)S(1)} %collective-permute-done.9.refs_2_), channel_id=1, source_target_pairs={{0,4},{2,6},{4,0},{6,2},{8,12},{10,14},{12,8},{14,10},{16,20},{18,... | collective-permute-start | bytes 1413128 | tf_op jit(solution)/shard_map/ppermute | solution.py:353
  50.9 0.0 collective-permute-done.10.refs_3_
  50.9 0.0 collective-permute-start.15
  50.9 0.0 copy-done.1
  50.9 0.1 tap_lines.1.refs_0_
  51.0 0.0 collective-permute-done.4.refs_5_
  51.1 0.1 collective-permute-start.12
  51.1 0.0 collective-permute-done.14.refs_1_
  51.1 0.5 collective-permute-start.16
  51.6 0.0 copy-done.3
  51.6 2.6 %filter_whole.4 = (bf16[2,184,640]{2,1,0:T(8,128)(2,1)S(1)}, bf16[2,184,640]{2,1,0:T(8,128)(2,1)S(1)}) custom-call(s32[16]{0:T(128)S(1)} %get-tuple-element.38.rows_ref, s32[3]{0:T(128)S(1)} %pad_add_fusion.place_ref, s32[32]{0:T(128)S(1)} %copy-done.3, f32[32,1152]{1,0:T(8,128)S(1)} %tap_lines.1.refs_0_, ...), custom_call_target="tpu_custom_call" | custom-call | flops 3019898880 | bytes 3768320 | tf_op jit(solution)/shard_map/filter_whole/pallas_call | solution.py:302
  54.3 0.0 collective-permute-done.6.refs_6_
  54.3 6.6 %collective-permute-done.11.refs_4_ = bf16[2,184,640]{2,1,0:T(8,128)(2,1)S(1)} collective-permute-done((bf16[2,184,640]{2,1,0:T(8,128)(2,1)S(1)}, bf16[2,184,640]{2,1,0:T(8,128)(2,1)S(1)}, u32[]{:S(2)}, u32[]{:S(2)}) %collective-permute-start.11) | collective-permute-done | bytes 471072 | tf_op jit(solution)/shard_map/ppermute | solution.py:353
  60.9 0.0 collective-permute-start.13
  60.9 3.1 %collective-permute-done.15.refs_2_ = bf16[2,184,640]{2,1,0:T(8,128)(2,1)S(1)} collective-permute-done((bf16[2,184,640]{2,1,0:T(8,128)(2,1)S(1)}, bf16[2,184,640]{2,1,0:T(8,128)(2,1)S(1)}, u32[]{:S(2)}, u32[]{:S(2)}) %collective-permute-start.15) | collective-permute-done | bytes 471072 | tf_op jit(solution)/shard_map/ppermute | solution.py:353
  63.9 1.0 %collective-permute-start.17 = (bf16[2,184,640]{2,1,0:T(8,128)(2,1)S(1)}, bf16[2,184,640]{2,1,0:T(8,128)(2,1)S(1)}, u32[]{:S(2)}, u32[]{:S(2)}) collective-permute-start(bf16[2,184,640]{2,1,0:T(8,128)(2,1)S(1)} %collective-permute-done.15.refs_2_), channel_id=1, source_target_pairs={{0,4},{2,6},{4,0},{6,2},{8,12},{10,14},{12,8},{14,10},{16,20},{18,... | collective-permute-start | bytes 1413128 | tf_op jit(solution)/shard_map/ppermute | solution.py:353
  65.0 1.0 collective-permute-start.7
  66.0 0.0 collective-permute-done.12.refs_5_
  66.0 3.7 %collective-permute-done.16.refs_3_ = bf16[2,184,640]{2,1,0:T(8,128)(2,1)S(1)} collective-permute-done((bf16[2,184,640]{2,1,0:T(8,128)(2,1)S(1)}, bf16[2,184,640]{2,1,0:T(8,128)(2,1)S(1)}, u32[]{:S(2)}, u32[]{:S(2)}) %collective-permute-start.16) | collective-permute-done | bytes 471072 | tf_op jit(solution)/shard_map/ppermute | solution.py:353
  69.7 0.0 collective-permute-start.18
  69.7 2.6 %filter_whole.3 = (bf16[2,184,640]{2,1,0:T(8,128)(2,1)S(1)}, bf16[2,184,640]{2,1,0:T(8,128)(2,1)S(1)}) custom-call(s32[16]{0:T(128)S(1)} %get-tuple-element.38.rows_ref, s32[3]{0:T(128)S(1)} %pad_add_fusion.place_ref, s32[32]{0:T(128)S(1)} %copy-done.3, f32[32,1152]{1,0:T(8,128)S(1)} %tap_lines.1.refs_0_, ...), custom_call_target="tpu_custom_call" | custom-call | flops 3019898880 | bytes 3768320 | tf_op jit(solution)/shard_map/filter_whole/pallas_call | solution.py:302
  72.3 0.1 collective-permute-start.20
  72.4 4.0 %collective-permute-done.13.refs_6_ = bf16[2,184,640]{2,1,0:T(8,128)(2,1)S(1)} collective-permute-done((bf16[2,184,640]{2,1,0:T(8,128)(2,1)S(1)}, bf16[2,184,640]{2,1,0:T(8,128)(2,1)S(1)}, u32[]{:S(2)}, u32[]{:S(2)}) %collective-permute-start.13) | collective-permute-done | bytes 471072 | tf_op jit(solution)/shard_map/ppermute | solution.py:353
  76.4 3.4 %collective-permute-done.17.refs_4_ = bf16[2,184,640]{2,1,0:T(8,128)(2,1)S(1)} collective-permute-done((bf16[2,184,640]{2,1,0:T(8,128)(2,1)S(1)}, bf16[2,184,640]{2,1,0:T(8,128)(2,1)S(1)}, u32[]{:S(2)}, u32[]{:S(2)}) %collective-permute-start.17) | collective-permute-done | bytes 471072 | tf_op jit(solution)/shard_map/ppermute | solution.py:353
  79.8 0.0 collective-permute-start.19
  79.8 0.0 collective-permute-start.21
  79.8 2.1 %filter_early.1 = (f32[2,184,1280]{2,1,0:T(8,128)S(1)}, bf16[2,5,192,184]{3,2,1,0:T(8,128)(2,1)S(1)}) custom-call(s32[16]{0:T(128)S(1)} %get-tuple-element.38.rows_ref, s32[3]{0:T(128)S(1)} %pad_add_fusion.place_ref, s32[32]{0:T(128)S(1)} %copy-done.3, f32[32,1152]{1,0:T(8,128)S(1)} %tap_lines.1.refs_0_, ...), custom_call_target="tpu_custom_call" | custom-call | flops 2113929216 | bytes 3768320 | tf_op jit(solution)/shard_map/filter_early/pallas_call | solution.py:302
  81.9 2.6 %filter_whole.5 = (bf16[2,184,640]{2,1,0:T(8,128)(2,1)S(1)}, bf16[2,184,640]{2,1,0:T(8,128)(2,1)S(1)}) custom-call(s32[16]{0:T(128)S(1)} %get-tuple-element.38.rows_ref, s32[3]{0:T(128)S(1)} %pad_add_fusion.place_ref, s32[32]{0:T(128)S(1)} %copy-done.3, f32[32,1152]{1,0:T(8,128)S(1)} %tap_lines.1.refs_0_, ...), custom_call_target="tpu_custom_call" | custom-call | flops 3019898880 | bytes 3768320 | tf_op jit(solution)/shard_map/filter_whole/pallas_call | solution.py:302
  84.6 1.9 %collective-permute-done.18.refs_2_ = bf16[2,184,640]{2,1,0:T(8,128)(2,1)S(1)} collective-permute-done((bf16[2,184,640]{2,1,0:T(8,128)(2,1)S(1)}, bf16[2,184,640]{2,1,0:T(8,128)(2,1)S(1)}, u32[]{:S(2)}, u32[]{:S(2)}) %collective-permute-start.18) | collective-permute-done | bytes 471072 | tf_op jit(solution)/shard_map/ppermute | solution.py:353
  86.5 3.6 %collective-permute-start.22 = (bf16[2,184,640]{2,1,0:T(8,128)(2,1)S(1)}, bf16[2,184,640]{2,1,0:T(8,128)(2,1)S(1)}, u32[]{:S(2)}, u32[]{:S(2)}) collective-permute-start(bf16[2,184,640]{2,1,0:T(8,128)(2,1)S(1)} %get-tuple-element.67), channel_id=1, source_target_pairs={{0,2},{2,0},{4,6},{6,4},{8,10},{10,8},{12,14},{14,12},{16,18},{18,... | collective-permute-start | bytes 1413128 | tf_op jit(solution)/shard_map/ppermute | solution.py:353
  90.1 6.5 %collective-permute-done.19.refs_3_ = bf16[2,184,640]{2,1,0:T(8,128)(2,1)S(1)} collective-permute-done((bf16[2,184,640]{2,1,0:T(8,128)(2,1)S(1)}, bf16[2,184,640]{2,1,0:T(8,128)(2,1)S(1)}, u32[]{:S(2)}, u32[]{:S(2)}) %collective-permute-start.19) | collective-permute-done | bytes 471072 | tf_op jit(solution)/shard_map/ppermute | solution.py:353
  96.6 1.3 %filter_late.1 = (bf16[2,184,640]{2,1,0:T(8,128)(2,1)S(1)}, bf16[2,184,640]{2,1,0:T(8,128)(2,1)S(1)}) custom-call(s32[16]{0:T(128)S(1)} %get-tuple-element.38.rows_ref, s32[3]{0:T(128)S(1)} %pad_add_fusion.place_ref, s32[32]{0:T(128)S(1)} %copy-done.3, f32[2,184,1280]{2,1,0:T(8,128)S(1)} %get-tuple-element.59.refs_0_, ...), custom_call_target="tpu_custom_call" | custom-call | flops 905969664 | bytes 3768320 | tf_op jit(solution)/shard_map/filter_late/pallas_call | solution.py:302
  97.9 0.2 collective-permute-start.23
  98.1 0.0 collective-permute-done.7.refs_1_
  98.1 0.0 collective-permute-done.20.refs_4_
  98.1 0.0 collective-permute-done.21.refs_5_
  98.1 0.0 collective-permute-done.22.refs_6_
  98.1 1.7 %collective-permute-done.23.refs_7_ = bf16[2,184,640]{2,1,0:T(8,128)(2,1)S(1)} collective-permute-done((bf16[2,184,640]{2,1,0:T(8,128)(2,1)S(1)}, bf16[2,184,640]{2,1,0:T(8,128)(2,1)S(1)}, u32[]{:S(2)}, u32[]{:S(2)}) %collective-permute-start.23) | collective-permute-done | bytes 471072 | tf_op jit(solution)/shard_map/ppermute | solution.py:353
  99.8 2.8 %put_rows.1 = bf16[180,16,640]{2,1,0:T(8,128)(2,1)} custom-call(s32[16]{0:T(128)S(1)} %get-tuple-element.37.slots_ref, bf16[2,184,640]{2,1,0:T(8,128)(2,1)S(1)} %get-tuple-element.45.refs_0_, bf16[2,184,640]{2,1,0:T(8,128)(2,1)S(1)} %collective-permute-done.7.refs_1_, bf16[2,184,640]{2,1,0:T(8,128)(2,1)S(1)} %get-tuple-element.54.refs_2_, ...), custom_call_target="tpu_custom_call" | custom-call | flops 943718400 | bytes 7372800 | tf_op jit(solution)/shard_map/put_rows/pallas_call | solution.py:205
  (1 shorter events, 0.0 us)
Async XLA Ops:
  0.0 51.6 %copy-start.3 = (s32[32]{0:T(128)S(1)}, s32[32]{0:T(128)}, u32[]{:S(2)}) copy-start(s32[32]{0:T(128)} %widths_ref.9) | copy-start | bytes 388
  0.1 2.0 %copy-start = (bf16[16,180,640]{2,0,1:T(8,128)(2,1)S(1)}, bf16[16,180,640]{2,0,1:T(8,128)(2,1)}, u32[]{:S(2)}) copy-start(bf16[16,180,640]{2,0,1:T(8,128)(2,1)} %param.4) | copy-start | bytes 11059204
  2.1 0.7 copy-start.2
  2.8 48.2 %copy-start.1 = (bf16[32,2880]{1,0:T(8,128)(2,1)S(1)}, bf16[32,2880]{1,0:T(8,128)(2,1)}, u32[]{:S(2)}) copy-start(bf16[32,2880]{1,0:T(8,128)(2,1)} %taps_ref.1) | copy-start | bytes 552964
  5.9 7.9 %collective-permute-start = (bf16[2,184,640]{2,1,0:T(8,128)(2,1)S(1)}, bf16[2,184,640]{2,1,0:T(8,128)(2,1)S(1)}, u32[]{:S(2)}, u32[]{:S(2)}) collective-permute-start(bf16[2,184,640]{2,1,0:T(8,128)(2,1)S(1)} %get-tuple-element.40), channel_id=1, source_target_pairs={{0,2},{2,0},{4,6},{6,4},{8,10},{10,8},{12,14},{14,12},{16,18},{18,... | collective-permute-start | bytes 1413128 | tf_op jit(solution)/shard_map/ppermute | solution.py:353
  6.4 15.8 %collective-permute-start.3 = (bf16[2,184,640]{2,1,0:T(8,128)(2,1)S(1)}, bf16[2,184,640]{2,1,0:T(8,128)(2,1)S(1)}, u32[]{:S(2)}, u32[]{:S(2)}) collective-permute-start(bf16[2,184,640]{2,1,0:T(8,128)(2,1)S(1)} %get-tuple-element.39.refs_1_.refs_5_), channel_id=1, source_target_pairs={{0,24},{2,26},{4,12},{6,14},{8,0},{10,2},{12,20},{14,22},{16,8},{1... | collective-permute-start | bytes 1413128 | tf_op jit(solution)/shard_map/ppermute | solution.py:353
  11.1 13.6 %collective-permute-start.1 = (bf16[2,184,640]{2,1,0:T(8,128)(2,1)S(1)}, bf16[2,184,640]{2,1,0:T(8,128)(2,1)S(1)}, u32[]{:S(2)}, u32[]{:S(2)}) collective-permute-start(bf16[2,184,640]{2,1,0:T(8,128)(2,1)S(1)} %get-tuple-element.41), channel_id=1, source_target_pairs={{0,4},{2,6},{4,0},{6,2},{8,12},{10,14},{12,8},{14,10},{16,20},{18,... | collective-permute-start | bytes 1413128 | tf_op jit(solution)/shard_map/ppermute | solution.py:353
  11.1 13.6 %collective-permute-start.8 = (bf16[2,184,640]{2,1,0:T(8,128)(2,1)S(1)}, bf16[2,184,640]{2,1,0:T(8,128)(2,1)S(1)}, u32[]{:S(2)}, u32[]{:S(2)}) collective-permute-start(bf16[2,184,640]{2,1,0:T(8,128)(2,1)S(1)} %get-tuple-element.47), channel_id=1, source_target_pairs={{0,1},{1,0},{2,3},{3,2},{4,5},{5,4},{6,7},{7,6},{8,9},{9,8},{10,11... | collective-permute-start | bytes 1413128 | tf_op jit(solution)/shard_map/ppermute | solution.py:353
  12.6 20.6 %collective-permute-start.2 = (bf16[2,184,640]{2,1,0:T(8,128)(2,1)S(1)}, bf16[2,184,640]{2,1,0:T(8,128)(2,1)S(1)}, u32[]{:S(2)}, u32[]{:S(2)}) collective-permute-start(bf16[2,184,640]{2,1,0:T(8,128)(2,1)S(1)} %get-tuple-element.42), channel_id=1, source_target_pairs={{0,6},{2,4},{4,2},{6,0},{8,14},{10,12},{12,10},{14,8},{16,22},{18,... | collective-permute-start | bytes 1413128 | tf_op jit(solution)/shard_map/ppermute | solution.py:353
  13.8 20.9 %collective-permute-start.5 = (bf16[2,184,640]{2,1,0:T(8,128)(2,1)S(1)}, bf16[2,184,640]{2,1,0:T(8,128)(2,1)S(1)}, u32[]{:S(2)}, u32[]{:S(2)}) collective-permute-start(bf16[2,184,640]{2,1,0:T(8,128)(2,1)S(1)} %collective-permute-done.refs_2_.refs_6_), channel_id=1, source_target_pairs={{0,24},{2,26},{4,12},{6,14},{8,0},{10,2},{12,20},{14,22},{16,8},{1... | collective-permute-start | bytes 1413128 | tf_op jit(solution)/shard_map/ppermute | solution.py:353
  22.2 13.0 %collective-permute-start.9 = (bf16[2,184,640]{2,1,0:T(8,128)(2,1)S(1)}, bf16[2,184,640]{2,1,0:T(8,128)(2,1)S(1)}, u32[]{:S(2)}, u32[]{:S(2)}) collective-permute-start(bf16[2,184,640]{2,1,0:T(8,128)(2,1)S(1)} %get-tuple-element.49), channel_id=1, source_target_pairs={{0,3},{1,2},{2,1},{3,0},{4,7},{5,6},{6,5},{7,4},{8,11},{9,10},{10,... | collective-permute-start | bytes 1413128 | tf_op jit(solution)/shard_map/ppermute | solution.py:353
  24.7 26.2 %collective-permute-start.10 = (bf16[2,184,640]{2,1,0:T(8,128)(2,1)S(1)}, bf16[2,184,640]{2,1,0:T(8,128)(2,1)S(1)}, u32[]{:S(2)}, u32[]{:S(2)}) collective-permute-start(bf16[2,184,640]{2,1,0:T(8,128)(2,1)S(1)} %collective-permute-done.8.refs_1_), channel_id=1, source_target_pairs={{0,4},{2,6},{4,0},{6,2},{8,12},{10,14},{12,8},{14,10},{16,20},{18,... | collective-permute-start | bytes 1413128 | tf_op jit(solution)/shard_map/ppermute | solution.py:353
  25.7 25.4 %collective-permute-start.4 = (bf16[2,184,640]{2,1,0:T(8,128)(2,1)S(1)}, bf16[2,184,640]{2,1,0:T(8,128)(2,1)S(1)}, u32[]{:S(2)}, u32[]{:S(2)}) collective-permute-start(bf16[2,184,640]{2,1,0:T(8,128)(2,1)S(1)} %collective-permute-done.1.refs_3_.refs_1_), channel_id=1, source_target_pairs={{0,8},{2,10},{4,28},{6,30},{8,16},{10,18},{12,4},{14,6},{16,24},{1... | collective-permute-start | bytes 1413128 | tf_op jit(solution)/shard_map/ppermute | solution.py:353
  33.2 17.9 %collective-permute-start.14 = (bf16[2,184,640]{2,1,0:T(8,128)(2,1)S(1)}, bf16[2,184,640]{2,1,0:T(8,128)(2,1)S(1)}, u32[]{:S(2)}, u32[]{:S(2)}) collective-permute-start(bf16[2,184,640]{2,1,0:T(8,128)(2,1)S(1)} %get-tuple-element.56), channel_id=1, source_target_pairs={{0,1},{1,0},{2,3},{3,2},{4,5},{5,4},{6,7},{7,6},{8,9},{9,8},{10,11... | collective-permute-start | bytes 1413128 | tf_op jit(solution)/shard_map/ppermute | solution.py:353
  34.7 19.6 %collective-permute-start.6 = (bf16[2,184,640]{2,1,0:T(8,128)(2,1)S(1)}, bf16[2,184,640]{2,1,0:T(8,128)(2,1)S(1)}, u32[]{:S(2)}, u32[]{:S(2)}) collective-permute-start(bf16[2,184,640]{2,1,0:T(8,128)(2,1)S(1)} %collective-permute-done.2.refs_4_.refs_2_), channel_id=1, source_target_pairs={{0,8},{2,10},{4,28},{6,30},{8,16},{10,18},{12,4},{14,6},{16,24},{1... | collective-permute-start | bytes 1413128 | tf_op jit(solution)/shard_map/ppermute | solution.py:353
  35.2 25.7 %collective-permute-start.11 = (bf16[2,184,640]{2,1,0:T(8,128)(2,1)S(1)}, bf16[2,184,640]{2,1,0:T(8,128)(2,1)S(1)}, u32[]{:S(2)}, u32[]{:S(2)}) collective-permute-start(bf16[2,184,640]{2,1,0:T(8,128)(2,1)S(1)} %collective-permute-done.9.refs_2_), channel_id=1, source_target_pairs={{0,4},{2,6},{4,0},{6,2},{8,12},{10,14},{12,8},{14,10},{16,20},{18,... | collective-permute-start | bytes 1413128 | tf_op jit(solution)/shard_map/ppermute | solution.py:353
  50.9 13.0 %collective-permute-start.15 = (bf16[2,184,640]{2,1,0:T(8,128)(2,1)S(1)}, bf16[2,184,640]{2,1,0:T(8,128)(2,1)S(1)}, u32[]{:S(2)}, u32[]{:S(2)}) collective-permute-start(bf16[2,184,640]{2,1,0:T(8,128)(2,1)S(1)} %get-tuple-element.58), channel_id=1, source_target_pairs={{0,3},{1,2},{2,1},{3,0},{4,7},{5,6},{6,5},{7,4},{8,11},{9,10},{10,... | collective-permute-start | bytes 1413128 | tf_op jit(solution)/shard_map/ppermute | solution.py:353
  51.1 14.9 %collective-permute-start.12 = (bf16[2,184,640]{2,1,0:T(8,128)(2,1)S(1)}, bf16[2,184,640]{2,1,0:T(8,128)(2,1)S(1)}, u32[]{:S(2)}, u32[]{:S(2)}) collective-permute-start(bf16[2,184,640]{2,1,0:T(8,128)(2,1)S(1)} %collective-permute-done.10.refs_3_), channel_id=1, source_target_pairs={{0,8},{2,10},{4,28},{6,30},{8,16},{10,18},{12,4},{14,6},{16,24},{1... | collective-permute-start | bytes 1413128 | tf_op jit(solution)/shard_map/ppermute | solution.py:353
  51.1 18.6 %collective-permute-start.16 = (bf16[2,184,640]{2,1,0:T(8,128)(2,1)S(1)}, bf16[2,184,640]{2,1,0:T(8,128)(2,1)S(1)}, u32[]{:S(2)}, u32[]{:S(2)}) collective-permute-start(bf16[2,184,640]{2,1,0:T(8,128)(2,1)S(1)} %collective-permute-done.14.refs_1_), channel_id=1, source_target_pairs={{0,4},{2,6},{4,0},{6,2},{8,12},{10,14},{12,8},{14,10},{16,20},{18,... | collective-permute-start | bytes 1413128 | tf_op jit(solution)/shard_map/ppermute | solution.py:353
  60.9 15.5 %collective-permute-start.13 = (bf16[2,184,640]{2,1,0:T(8,128)(2,1)S(1)}, bf16[2,184,640]{2,1,0:T(8,128)(2,1)S(1)}, u32[]{:S(2)}, u32[]{:S(2)}) collective-permute-start(bf16[2,184,640]{2,1,0:T(8,128)(2,1)S(1)} %collective-permute-done.11.refs_4_), channel_id=1, source_target_pairs={{0,8},{2,10},{4,28},{6,30},{8,16},{10,18},{12,4},{14,6},{16,24},{1... | collective-permute-start | bytes 1413128 | tf_op jit(solution)/shard_map/ppermute | solution.py:353
  63.9 15.9 %collective-permute-start.17 = (bf16[2,184,640]{2,1,0:T(8,128)(2,1)S(1)}, bf16[2,184,640]{2,1,0:T(8,128)(2,1)S(1)}, u32[]{:S(2)}, u32[]{:S(2)}) collective-permute-start(bf16[2,184,640]{2,1,0:T(8,128)(2,1)S(1)} %collective-permute-done.15.refs_2_), channel_id=1, source_target_pairs={{0,4},{2,6},{4,0},{6,2},{8,12},{10,14},{12,8},{14,10},{16,20},{18,... | collective-permute-start | bytes 1413128 | tf_op jit(solution)/shard_map/ppermute | solution.py:353
  65.0 33.1 %collective-permute-start.7 = (bf16[2,184,640]{2,1,0:T(8,128)(2,1)S(1)}, bf16[2,184,640]{2,1,0:T(8,128)(2,1)S(1)}, u32[]{:S(2)}, u32[]{:S(2)}) collective-permute-start(bf16[2,184,640]{2,1,0:T(8,128)(2,1)S(1)} %get-tuple-element.46), channel_id=1, source_target_pairs={{0,4},{2,6},{4,0},{6,2},{8,12},{10,14},{12,8},{14,10},{16,20},{18,... | collective-permute-start | bytes 1413128 | tf_op jit(solution)/shard_map/ppermute | solution.py:353
  69.7 16.8 %collective-permute-start.18 = (bf16[2,184,640]{2,1,0:T(8,128)(2,1)S(1)}, bf16[2,184,640]{2,1,0:T(8,128)(2,1)S(1)}, u32[]{:S(2)}, u32[]{:S(2)}) collective-permute-start(bf16[2,184,640]{2,1,0:T(8,128)(2,1)S(1)} %collective-permute-done.16.refs_3_), channel_id=1, source_target_pairs={{0,8},{2,10},{4,28},{6,30},{8,16},{10,18},{12,4},{14,6},{16,24},{1... | collective-permute-start | bytes 1413128 | tf_op jit(solution)/shard_map/ppermute | solution.py:353
  72.3 25.8 %collective-permute-start.20 = (bf16[2,184,640]{2,1,0:T(8,128)(2,1)S(1)}, bf16[2,184,640]{2,1,0:T(8,128)(2,1)S(1)}, u32[]{:S(2)}, u32[]{:S(2)}) collective-permute-start(bf16[2,184,640]{2,1,0:T(8,128)(2,1)S(1)} %get-tuple-element.64), channel_id=1, source_target_pairs={{0,2},{2,0},{4,6},{6,4},{8,10},{10,8},{12,14},{14,12},{16,18},{18,... | collective-permute-start | bytes 1413128 | tf_op jit(solution)/shard_map/ppermute | solution.py:353
  79.8 16.8 %collective-permute-start.19 = (bf16[2,184,640]{2,1,0:T(8,128)(2,1)S(1)}, bf16[2,184,640]{2,1,0:T(8,128)(2,1)S(1)}, u32[]{:S(2)}, u32[]{:S(2)}) collective-permute-start(bf16[2,184,640]{2,1,0:T(8,128)(2,1)S(1)} %collective-permute-done.17.refs_4_), channel_id=1, source_target_pairs={{0,8},{2,10},{4,28},{6,30},{8,16},{10,18},{12,4},{14,6},{16,24},{1... | collective-permute-start | bytes 1413128 | tf_op jit(solution)/shard_map/ppermute | solution.py:353
  79.8 18.3 %collective-permute-start.21 = (bf16[2,184,640]{2,1,0:T(8,128)(2,1)S(1)}, bf16[2,184,640]{2,1,0:T(8,128)(2,1)S(1)}, u32[]{:S(2)}, u32[]{:S(2)}) collective-permute-start(bf16[2,184,640]{2,1,0:T(8,128)(2,1)S(1)} %get-tuple-element.66), channel_id=1, source_target_pairs={{0,6},{2,4},{4,2},{6,0},{8,14},{10,12},{12,10},{14,8},{16,22},{18,... | collective-permute-start | bytes 1413128 | tf_op jit(solution)/shard_map/ppermute | solution.py:353
  86.5 11.6 %collective-permute-start.22 = (bf16[2,184,640]{2,1,0:T(8,128)(2,1)S(1)}, bf16[2,184,640]{2,1,0:T(8,128)(2,1)S(1)}, u32[]{:S(2)}, u32[]{:S(2)}) collective-permute-start(bf16[2,184,640]{2,1,0:T(8,128)(2,1)S(1)} %get-tuple-element.67), channel_id=1, source_target_pairs={{0,2},{2,0},{4,6},{6,4},{8,10},{10,8},{12,14},{14,12},{16,18},{18,... | collective-permute-start | bytes 1413128 | tf_op jit(solution)/shard_map/ppermute | solution.py:353
  97.9 1.9 %collective-permute-start.23 = (bf16[2,184,640]{2,1,0:T(8,128)(2,1)S(1)}, bf16[2,184,640]{2,1,0:T(8,128)(2,1)S(1)}, u32[]{:S(2)}, u32[]{:S(2)}) collective-permute-start(bf16[2,184,640]{2,1,0:T(8,128)(2,1)S(1)} %get-tuple-element.68), channel_id=1, source_target_pairs={{0,2},{2,0},{4,6},{6,4},{8,10},{10,8},{12,14},{14,12},{16,18},{18,... | collective-permute-start | bytes 1413128 | tf_op jit(solution)/shard_map/ppermute | solution.py:353

commit v11 on v10

--- a/solution.py
+++ b/solution.py
@@ -83,7 +83,7 @@
     return jnp.concatenate(bands, axis=0)
 
 
-def take_kernel(chunks, lat_dev, block, slot_ref, place_ref, fields_ref, *refs):
+def take_kernel(chunks, lat_dev, block, place_ref, fields_ref, *refs):
     outs = refs[: len(chunks)]
     rows_ref, slots_ref, home_ref, take_ref = refs[len(chunks) :]
     lon_dev, _, channels = fields_ref.shape
@@ -103,8 +103,8 @@
     for j in range(lat_dev):
         here = band * lat_dev + j
         there = (1 - band) * lat_dev + j
-        stays = slot_ref[here] // lat_dev == band
-        comes = slot_ref[there] // lat_dev == band
+        stays = place_ref[3 + here] // lat_dev == band
+        comes = place_ref[3 + there] // lat_dev == band
         home_ref[jnp.where(stays, traded(at(stay)), half + at(leave))] = jnp.int32(j)
 
         @pl.when(stays)
@@ -112,48 +112,49 @@
             spot = traded(at(stay))
             spot = spot + jnp.where(spot >= quarter, quarter, 0)
             rows_ref[spot] = here
-            slots_ref[spot] = slot_ref[here] % lat_dev
+            slots_ref[spot] = place_ref[3 + here] % lat_dev
 
         @pl.when(comes)
         def _():
             spot = at(come)
             spot = spot + jnp.where(spot >= quarter, half, quarter)
             rows_ref[spot] = there
-            slots_ref[spot] = slot_ref[there] % lat_dev
+            slots_ref[spot] = place_ref[3 + there] % lat_dev
 
         stay = stay + stays.astype(jnp.int32)
         leave = leave + 1 - stays.astype(jnp.int32)
         come = come + comes.astype(jnp.int32)
 
-    def selector(lon_in, lon_out):
-        lon = lax.broadcasted_iota(jnp.int32, (lon_out, lon_in * lat_dev), 0)
-        column = lax.broadcasted_iota(jnp.int32, (lon_out, lon_in * lat_dev), 1)
-        strips = [jnp.where(column == lon * lat_dev + home_ref[p], 1.0, 0.0) for p in range(lat_dev)]
-        return jnp.concatenate(strips, axis=0).astype(jnp.bfloat16)
-
-    take_ref[...] = selector(block, block)
+    def selector(lon):
+        row = lax.broadcasted_iota(jnp.int32, (lat_dev * lon, 128), 0)
+        wanted = row % lon * lat_dev
+        for p in range(lat_dev):
+            wanted += jnp.where(row // lon == p, home_ref[p], 0)
+        column = lax.broadcasted_iota(jnp.int32, (lat_dev * lon, lon * lat_dev), 1)
+        return jnp.where(column == wanted[:, :1], 1.0, 0.0).astype(jnp.bfloat16)
+
+    take_ref[...] = selector(block)
     for start in starts:
-        lon_in = min(block, lon_dev - start)
-        lon_out = min(block, outs[0].shape[1] - start)
-        panel = fields_ref[start : start + lon_in].reshape(lon_in * lat_dev, channels)
-        take = take_ref[...] if (lon_in, lon_out) == (block, block) else selector(lon_in, lon_out)
-        taken = jnp.dot(take, panel, preferred_element_type=jnp.float32).astype(jnp.bfloat16)
+        lon = min(block, lon_dev - start)
+        panel = fields_ref[start : start + lon].reshape(lon * lat_dev, channels)
+        take = take_ref[...] if lon == block else selector(lon)
+        taken = jnp.dot(take, panel, preferred_element_type=jnp.float32)
         place = 0
         for out, count in zip(outs, chunks):
             for i in range(count):
-                out[i, start : start + lon_out, :] = taken[place * lon_out : (place + 1) * lon_out]
+                piece = taken[place * lon : (place + 1) * lon].astype(out.dtype)
+                out[i * lon_dev + start : i * lon_dev + start + lon, :] = piece
                 place += 1
 
 
-def take_rows(fields, owner_slot, place, chunks):
+def take_rows(fields, place, chunks):
     lon_dev, lat_dev, channels = fields.shape
     block = 16
-    padded = up_to(lon_dev, 8)
     ints = jax.ShapeDtypeStruct((lat_dev,), jnp.int32)
     result = pl.pallas_call(
         functools.partial(take_kernel, chunks, lat_dev, block),
-        out_shape=[jax.ShapeDtypeStruct((n, padded, channels), fields.dtype) for n in chunks] + [ints, ints],
-        in_specs=[SMEM_SPEC, SMEM_SPEC, VMEM_SPEC],
+        out_shape=[jax.ShapeDtypeStruct((n * lon_dev, channels), fields.dtype) for n in chunks] + [ints, ints],
+        in_specs=[SMEM_SPEC, VMEM_SPEC],
         out_specs=[VMEM_SPEC] * len(chunks) + [SMEM_SPEC, SMEM_SPEC],
         scratch_shapes=[
             pltpu.SMEM((lat_dev,), jnp.int32),
@@ -164,7 +165,7 @@
             flops=2 * fields.size * block * lat_dev, bytes_accessed=4 * fields.size, transcendentals=0
         ),
         name="take_rows",
-    )(owner_slot, place, fields)
+    )(place, fields)
     return result[:-2], result[-2], result[-1]
 
 
@@ -172,25 +173,25 @@
     ins, (out_ref, panel_ref, sems) = refs[:-3], refs[-3:]
     lon_dev, _, channels = out_ref.shape
 
-    def selector(lon_in, lon_out):
-        shape = (lon_out * lat_dev, lat_dev * lon_in)
-        row = lax.broadcasted_iota(jnp.int32, shape, 0)
-        column = lax.broadcasted_iota(jnp.int32, (8, lat_dev * lon_in), 1)
-        wanted = column % lon_in * lat_dev
+    def selector(lon):
+        row = lax.broadcasted_iota(jnp.int32, (lon * lat_dev, lat_dev * lon), 0)
+        column = lax.broadcasted_iota(jnp.int32, (8, lat_dev * lon), 1)
+        wanted = column % lon * lat_dev
         for p in range(lat_dev):
-            wanted += jnp.where(column // lon_in == p, slots_ref[p], 0)
+            wanted += jnp.where(column // lon == p, slots_ref[p], 0)
         return jnp.where(row == wanted[:1], 1.0, 0.0).astype(jnp.bfloat16)
 
-    whole = selector(block, block)
+    whole = selector(block)
     copies = []
     for n, start in enumerate(range(0, lon_dev, block)):
-        lon_out = min(block, lon_dev - start)
-        lon_in = min(block, ins[0].shape[1] - start)
-        pieces = [r[i, start : start + lon_in, :] for r, count in zip(ins, counts) for i in range(count)]
-        put = whole if (lon_in, lon_out) == (block, block) else selector(lon_in, lon_out)
-        spread = jnp.dot(put, jnp.concatenate(pieces, axis=0), preferred_element_type=jnp.float32)
-        window = pl.ds(start, lon_out)
-        panel_ref[window] = spread.astype(jnp.bfloat16).reshape(lon_out, lat_dev, channels)
+        lon = min(block, lon_dev - start)
+        pieces = [r[i * lon_dev + start : i * lon_dev + start + lon, :] for r, count in zip(ins, counts) for i in range(count)]
+        if lon < block:
+            pieces = [p.astype(jnp.float32) for p in pieces]
+        panel = jnp.concatenate(pieces, axis=0).astype(jnp.bfloat16)
+        spread = jnp.dot(whole if lon == block else selector(lon), panel, preferred_element_type=jnp.float32)
+        window = pl.ds(start, lon)
+        panel_ref[window] = spread.astype(jnp.bfloat16).reshape(lon, lat_dev, channels)
         copies.append(pltpu.make_async_copy(panel_ref.at[window], out_ref.at[window], sems.at[n]))
         copies[-1].start()
     for copy in copies:
@@ -198,9 +199,9 @@
 
 
 def put_rows(panels, slots, lon_dev, lat_dev):
-    padded, channels = panels[0].shape[1:]
+    channels = panels[0].shape[1]
     block = 16
-    counts = tuple(p.shape[0] for p in panels)
+    counts = tuple(p.shape[0] // lon_dev for p in panels)
     shape = (lon_dev, lat_dev, channels)
     return pl.pallas_call(
         functools.partial(put_kernel, counts, lat_dev, block),
@@ -234,28 +235,28 @@
         ins, (out_own, out_other) = refs[:-2], refs[-2:]
     else:
         ins, (out_own, out_other, block_ref) = refs[:-3], refs[-3:]
-    padded, channels = ins[0].shape[1:]
+    channels = ins[0].shape[1]
 
     def both(first, second):
         return jnp.concatenate([first[...], second[...]], axis=1)
 
     for n, places in enumerate(plan):
-        panels = [ins[array].at[i] for array, i in places]
+        panels = [ins[array].at[pl.ds(i * lon_dev, lon_dev), :] for array, i in places]
 
         def times(offset, panel):
-            return jnp.dot(block_ref[n, 2 + offset], panel, preferred_element_type=jnp.float32)[:padded]
+            return jnp.dot(block_ref[n, 2 + offset], panel, preferred_element_type=jnp.float32)[:lon_dev]
 
         def halves(first, second):
             return jnp.concatenate([first, second], axis=1)
 
-        nothing = jnp.zeros((padded, channels), jnp.float32)
+        nothing = jnp.zeros((lon_dev, channels), jnp.float32)
         same = side == along
         if phase != "late":
             own, other, x_own, x_other = panels[:4]
             row = rows_ref[base + n]
             line = active_line(line_ref, row, widths_ref[row], 3 * lon_dev)
             for s in range(5):
-                block_ref[n, s] = toeplitz(line, (s + 1) * lon_dev, lon_dev, padded)
+                block_ref[n, s] = toeplitz(line, (s + 1) * lon_dev, lon_dev, lon_dev)
             here = both(own, other)
             total = here.astype(jnp.float32) + times(0, here)
             total += times(2 * along, both(x_own, x_other))
@@ -271,8 +272,9 @@
             total += times(-2 * along, both(z_own, z_other))
             more = times(-along, jnp.where(same, z_other[...], z_own[...]))
             total += halves(jnp.where(same, more, nothing), jnp.where(same, nothing, more))
-            out_own[n] = total[:, :channels].astype(out_own.dtype)
-            out_other[n] = total[:, channels:].astype(out_other.dtype)
+            here = pl.ds(n * lon_dev, lon_dev)
+            out_own[here, :] = total[:, :channels].astype(out_own.dtype)
+            out_other[here, :] = total[:, channels:].astype(out_other.dtype)
 
 
 def filter_pair(scalars, lines, places, base, lon_dev, phase="whole", early=()):
@@ -287,10 +289,10 @@
             found.append((at, i))
         plan.append(tuple(found))
     count = len(plan)
-    padded, channels = arrays[0].shape[1:]
-    total = (count, padded, 2 * channels), jnp.float32
-    block = (count, 5, up_to(lon_dev, 96), padded), jnp.bfloat16
-    out = jax.ShapeDtypeStruct((count, padded, channels), arrays[0].dtype)
+    channels = arrays[0].shape[1]
+    total = (count, lon_dev, 2 * channels), jnp.float32
+    block = (count, 5, up_to(lon_dev, 96), lon_dev), jnp.bfloat16
+    out = jax.ShapeDtypeStruct((count * lon_dev, channels), arrays[0].dtype)
     first = [lines] if phase != "late" else list(early)
     if phase == "early":
         outs, scratch = [jax.ShapeDtypeStruct(*total), jax.ShapeDtypeStruct(*block)], []
@@ -308,7 +310,7 @@
         compiler_params=pltpu.CompilerParams(vmem_limit_bytes=VMEM_LIMIT),
         cost_estimate=pl.CostEstimate(
             flops=FLOPS * count * weight * 256 * 256 * 768,
-            bytes_accessed=16 * count * padded * channels,
+            bytes_accessed=16 * count * lon_dev * channels,
             transcendentals=0,
         ),
         name="filter_" + phase,
@@ -321,9 +323,9 @@
     at = lax.axis_index("lon")
     band = lax.axis_index("lat")
     core, x = at % 2, at // 2 % 2
-    place = jnp.stack([band, core, x]).astype(jnp.int32)
+    place = jnp.concatenate([jnp.stack([band, core, x]).astype(jnp.int32), owner_slot])
     chunks = STAY + STAY + COME + COME
-    taken, rows, slots = take_rows(jnp.transpose(fields, (1, 0, 2)), owner_slot, place, chunks)
+    taken, rows, slots = take_rows(jnp.transpose(fields, (1, 0, 2)), place, chunks)
     n_stay, n_come = len(STAY), len(COME)
     keep, give = taken[:n_stay], taken[n_stay : 2 * n_stay]
     straight, cross = taken[2 * n_stay : 2 * n_stay + n_come], taken[2 * n_stay + n_come :]

time: 103 us -> 101 us (0.981)
  waiting for transfers between devices: 48.7 us -> 45.7 us
  Pallas kernels: 17.2 us -> 18.5 us
    ppermute x24, waiting for transfers between devices: 48.7 us -> 45.7 us  [moved(): return lax.ppermute(operand, axes, pairs)]
    pallas_call x5, Pallas kernels: 11.3 us -> 12.5 us  [filter_pair(): pl.pallas_call(functools.partial(pair_kernel, lon_dev, base, tuple(plan),...]
    unnamed x8 -> x6, local copies, waits for them, and re-layouts: 2.71 us -> 2.05 us
  transfers between devices with their start and end apart: 24 -> 24, of which waited for: 12 -> 12; matrix products, arithmetic and copies ran while one was open for 0% -> 0% of each run, Pallas kernels for 11% -> 12%
where the time goes in v11:
time: 101 us
  waiting for transfers between devices  45.7 us (45%)
  starting transfers between devices  34 us (34%)
  Pallas kernels  18.5 us (18%)
  local copies, waits for them, and re-layouts  2.05 us (2%)
    ppermute x24, waiting for transfers between devices, moved(): return lax.ppermute(operand, axes, pairs)  45.7 us
    ppermute x24, starting transfers between devices, moved(): return lax.ppermute(operand, axes, pairs)  34 us
    pallas_call x5, Pallas kernels, filter_pair(): pl.pallas_call(functools.partial(pair_kernel, lon_dev, base, tuple(plan),...  12.5 us
    pallas_call x1, Pallas kernels, take_rows(): pl.pallas_call(functools.partial(take_kernel, chunks, lat_dev, block), ou...  3.1 us
    pallas_call x1, Pallas kernels, put_rows(): pl.pallas_call(functools.partial(put_kernel, counts, lat_dev, block), out...  2.8 us
    unnamed x6, local copies, waits for them, and re-layouts  2.05 us
  transfers between devices with their start and end apart: 24, of which 12 were waited for; matrix products, arithmetic and copies ran while one was open for 0% of the time, Pallas kernels for 12%

profile of v11, /device:TPU:0, one launch (start us, length us, event | category | flops | bytes accessed | tf_op | source)
XLA Modules:
  0.0 101.2 jit_solution(2850430497699128080)
XLA Ops:
  0.0 0.0 copy-start.2
  0.0 0.7 pad_add_fusion.place_ref
  0.7 0.0 copy-start
  0.7 2.0 %copy-done = bf16[16,180,640]{2,0,1:T(8,128)(2,1)S(1)} copy-done((bf16[16,180,640]{2,0,1:T(8,128)(2,1)S(1)}, bf16[16,180,640]{2,0,1:T(8,128)(2,1)}, u32[]{:S(2)}) %copy-start) | copy-done | bytes 3686424
  2.8 0.0 copy-start.1
  2.8 3.1 %take_rows.1 = (bf16[360,640]{1,0:T(8,128)(2,1)S(1)}, bf16[360,640]{1,0:T(8,128)(2,1)S(1)}, bf16[360,640]{1,0:T(8,128)(2,1)S(1)}, bf16[360,640]{1,0:T(8,128)(2,1...) custom-call(s32[35]{0:T(128)S(1)} %pad_add_fusion.place_ref, ...), custom_call_target="tpu_custom_call" | custom-call | flops 943718400 | bytes 7372800 | tf_op jit(solution)/shard_map/take_rows/pallas_call | solution.py:154
  5.9 0.5 collective-permute-start
  6.4 4.7 %collective-permute-start.3 = (bf16[360,640]{1,0:T(8,128)(2,1)S(1)}, bf16[360,640]{1,0:T(8,128)(2,1)S(1)}, u32[]{:S(2)}, u32[]{:S(2)}) collective-permute-start(bf16[360,640]{1,0:T(8,128)(2,1)S(1)} %get-tuple-element.39.refs_1_.refs_5_), channel_id=1, source_target_pairs={{0,24},{2,26},{4,12},{6,14},{8,0},{10,2},{12,20},{14,22},{16,8},{1... | collective-permute-start | bytes 1382408 | tf_op jit(solution)/shard_map/ppermute | solution.py:355
  11.1 0.0 collective-permute-start.1
  11.1 1.5 %collective-permute-start.8 = (bf16[360,640]{1,0:T(8,128)(2,1)S(1)}, bf16[360,640]{1,0:T(8,128)(2,1)S(1)}, u32[]{:S(2)}, u32[]{:S(2)}) collective-permute-start(bf16[360,640]{1,0:T(8,128)(2,1)S(1)} %get-tuple-element.47), channel_id=1, source_target_pairs={{0,1},{1,0},{2,3},{3,2},{4,5},{5,4},{6,7},{7,6},{8,9},{9,8},{10,11... | collective-permute-start | bytes 1382408 | tf_op jit(solution)/shard_map/ppermute | solution.py:355
  12.6 1.2 %collective-permute-start.2 = (bf16[360,640]{1,0:T(8,128)(2,1)S(1)}, bf16[360,640]{1,0:T(8,128)(2,1)S(1)}, u32[]{:S(2)}, u32[]{:S(2)}) collective-permute-start(bf16[360,640]{1,0:T(8,128)(2,1)S(1)} %get-tuple-element.42), channel_id=1, source_target_pairs={{0,6},{2,4},{4,2},{6,0},{8,14},{10,12},{12,10},{14,8},{16,22},{18,... | collective-permute-start | bytes 1382408 | tf_op jit(solution)/shard_map/ppermute | solution.py:355
  13.8 0.0 collective-permute-done.refs_2_.refs_6_
  13.8 0.5 collective-permute-start.5
  14.3 7.6 %collective-permute-done.3.refs_3_ = bf16[360,640]{1,0:T(8,128)(2,1)S(1)} collective-permute-done((bf16[360,640]{1,0:T(8,128)(2,1)S(1)}, bf16[360,640]{1,0:T(8,128)(2,1)S(1)}, u32[]{:S(2)}, u32[]{:S(2)}) %collective-permute-start.3) | collective-permute-done | bytes 460832 | tf_op jit(solution)/shard_map/ppermute | solution.py:355
  22.0 0.3 collective-permute-start.9
  22.3 2.2 %collective-permute-done.1.refs_3_.refs_1_ = bf16[360,640]{1,0:T(8,128)(2,1)S(1)} collective-permute-done((bf16[360,640]{1,0:T(8,128)(2,1)S(1)}, bf16[360,640]{1,0:T(8,128)(2,1)S(1)}, u32[]{:S(2)}, u32[]{:S(2)}) %collective-permute-start.1) | collective-permute-done | bytes 460832 | tf_op jit(solution)/shard_map/ppermute | solution.py:355
  24.5 0.0 collective-permute-done.8.refs_1_
  24.5 1.0 collective-permute-start.10
  25.5 0.1 collective-permute-start.4
  25.5 7.3 %collective-permute-done.2.refs_4_.refs_2_ = bf16[360,640]{1,0:T(8,128)(2,1)S(1)} collective-permute-done((bf16[360,640]{1,0:T(8,128)(2,1)S(1)}, bf16[360,640]{1,0:T(8,128)(2,1)S(1)}, u32[]{:S(2)}, u32[]{:S(2)}) %collective-permute-start.2) | collective-permute-done | bytes 460832 | tf_op jit(solution)/shard_map/ppermute | solution.py:355
  32.8 1.5 %collective-permute-start.14 = (bf16[360,640]{1,0:T(8,128)(2,1)S(1)}, bf16[360,640]{1,0:T(8,128)(2,1)S(1)}, u32[]{:S(2)}, u32[]{:S(2)}) collective-permute-start(bf16[360,640]{1,0:T(8,128)(2,1)S(1)} %get-tuple-element.56), channel_id=1, source_target_pairs={{0,1},{1,0},{2,3},{3,2},{4,5},{5,4},{6,7},{7,6},{8,9},{9,8},{10,11... | collective-permute-start | bytes 1382408 | tf_op jit(solution)/shard_map/ppermute | solution.py:355
  34.3 0.0 collective-permute-done.5.refs_4_
  34.3 0.2 collective-permute-start.6
  34.5 0.3 collective-permute-done.9.refs_2_
  34.8 15.4 %collective-permute-start.11 = (bf16[360,640]{1,0:T(8,128)(2,1)S(1)}, bf16[360,640]{1,0:T(8,128)(2,1)S(1)}, u32[]{:S(2)}, u32[]{:S(2)}) collective-permute-start(bf16[360,640]{1,0:T(8,128)(2,1)S(1)} %collective-permute-done.9.refs_2_), channel_id=1, source_target_pairs={{0,4},{2,6},{4,0},{6,2},{8,12},{10,14},{12,8},{14,10},{16,20},{18,... | collective-permute-start | bytes 1382408 | tf_op jit(solution)/shard_map/ppermute | solution.py:355
  50.2 0.0 collective-permute-done.10.refs_3_
  50.2 0.0 collective-permute-start.15
  50.2 0.0 copy-done.1
  50.2 0.1 tap_lines.1.refs_0_
  50.3 0.0 collective-permute-done.4.refs_5_
  50.3 0.1 collective-permute-start.12
  50.4 0.0 collective-permute-done.14.refs_1_
  50.4 0.5 collective-permute-start.16
  50.9 0.0 copy-done.2
  50.9 2.9 %filter_whole.4 = (bf16[360,640]{1,0:T(8,128)(2,1)S(1)}, bf16[360,640]{1,0:T(8,128)(2,1)S(1)}) custom-call(s32[16]{0:T(128)S(1)} %get-tuple-element.38.rows_ref, s32[35]{0:T(128)S(1)} %pad_add_fusion.place_ref, s32[32]{0:T(128)S(1)} %copy-done.2, f32[32,1152]{1,0:T(8,128)S(1)} %tap_lines.1.refs_0_, ...), custom_call_target="tpu_custom_call" | custom-call | flops 3019898880 | bytes 3686400 | tf_op jit(solution)/shard_map/filter_whole/pallas_call | solution.py:304
  53.8 0.0 collective-permute-done.6.refs_6_
  53.8 6.1 %collective-permute-done.11.refs_4_ = bf16[360,640]{1,0:T(8,128)(2,1)S(1)} collective-permute-done((bf16[360,640]{1,0:T(8,128)(2,1)S(1)}, bf16[360,640]{1,0:T(8,128)(2,1)S(1)}, u32[]{:S(2)}, u32[]{:S(2)}) %collective-permute-start.11) | collective-permute-done | bytes 460832 | tf_op jit(solution)/shard_map/ppermute | solution.py:355
  59.9 0.0 collective-permute-start.13
  59.9 3.1 %collective-permute-done.15.refs_2_ = bf16[360,640]{1,0:T(8,128)(2,1)S(1)} collective-permute-done((bf16[360,640]{1,0:T(8,128)(2,1)S(1)}, bf16[360,640]{1,0:T(8,128)(2,1)S(1)}, u32[]{:S(2)}, u32[]{:S(2)}) %collective-permute-start.15) | collective-permute-done | bytes 460832 | tf_op jit(solution)/shard_map/ppermute | solution.py:355
  63.0 1.0 %collective-permute-start.17 = (bf16[360,640]{1,0:T(8,128)(2,1)S(1)}, bf16[360,640]{1,0:T(8,128)(2,1)S(1)}, u32[]{:S(2)}, u32[]{:S(2)}) collective-permute-start(bf16[360,640]{1,0:T(8,128)(2,1)S(1)} %collective-permute-done.15.refs_2_), channel_id=1, source_target_pairs={{0,4},{2,6},{4,0},{6,2},{8,12},{10,14},{12,8},{14,10},{16,20},{18,... | collective-permute-start | bytes 1382408 | tf_op jit(solution)/shard_map/ppermute | solution.py:355
  64.0 1.0 collective-permute-start.7
  65.0 0.0 collective-permute-done.12.refs_5_
  65.0 3.5 %collective-permute-done.16.refs_3_ = bf16[360,640]{1,0:T(8,128)(2,1)S(1)} collective-permute-done((bf16[360,640]{1,0:T(8,128)(2,1)S(1)}, bf16[360,640]{1,0:T(8,128)(2,1)S(1)}, u32[]{:S(2)}, u32[]{:S(2)}) %collective-permute-start.16) | collective-permute-done | bytes 460832 | tf_op jit(solution)/shard_map/ppermute | solution.py:355
  68.5 0.0 collective-permute-start.18
  68.5 2.9 %filter_whole.3 = (bf16[360,640]{1,0:T(8,128)(2,1)S(1)}, bf16[360,640]{1,0:T(8,128)(2,1)S(1)}) custom-call(s32[16]{0:T(128)S(1)} %get-tuple-element.38.rows_ref, s32[35]{0:T(128)S(1)} %pad_add_fusion.place_ref, s32[32]{0:T(128)S(1)} %copy-done.2, f32[32,1152]{1,0:T(8,128)S(1)} %tap_lines.1.refs_0_, bf16[360,640]{1,0:T(8,128)(2,1)S(1)} %get-tuple-element.39.refs_1_.refs_5_, ...), custom_call_target="tpu_custom_call" | custom-call | flops 3019898880 | bytes 3686400 | tf_op jit(solution)/shard_map/filter_whole/pallas_call | solution.py:304
  71.4 0.1 collective-permute-start.20
  71.5 3.7 %collective-permute-done.13.refs_6_ = bf16[360,640]{1,0:T(8,128)(2,1)S(1)} collective-permute-done((bf16[360,640]{1,0:T(8,128)(2,1)S(1)}, bf16[360,640]{1,0:T(8,128)(2,1)S(1)}, u32[]{:S(2)}, u32[]{:S(2)}) %collective-permute-start.13) | collective-permute-done | bytes 460832 | tf_op jit(solution)/shard_map/ppermute | solution.py:355
  75.2 3.2 %collective-permute-done.17.refs_4_ = bf16[360,640]{1,0:T(8,128)(2,1)S(1)} collective-permute-done((bf16[360,640]{1,0:T(8,128)(2,1)S(1)}, bf16[360,640]{1,0:T(8,128)(2,1)S(1)}, u32[]{:S(2)}, u32[]{:S(2)}) %collective-permute-start.17) | collective-permute-done | bytes 460832 | tf_op jit(solution)/shard_map/ppermute | solution.py:355
  78.4 0.0 collective-permute-start.19
  78.4 0.0 collective-permute-start.21
  78.4 2.5 %filter_early.1 = (f32[2,180,1280]{2,1,0:T(8,128)S(1)}, bf16[2,5,192,180]{3,2,1,0:T(8,128)(2,1)S(1)}) custom-call(s32[16]{0:T(128)S(1)} %get-tuple-element.38.rows_ref, s32[35]{0:T(128)S(1)} %pad_add_fusion.place_ref, s32[32]{0:T(128)S(1)} %copy-done.2, f32[32,1152]{1,0:T(8,128)S(1)} %tap_lines.1.refs_0_, ...), custom_call_target="tpu_custom_call" | custom-call | flops 2113929216 | bytes 3686400 | tf_op jit(solution)/shard_map/filter_early/pallas_call | solution.py:304
  80.9 2.8 %filter_whole.5 = (bf16[360,640]{1,0:T(8,128)(2,1)S(1)}, bf16[360,640]{1,0:T(8,128)(2,1)S(1)}) custom-call(s32[16]{0:T(128)S(1)} %get-tuple-element.38.rows_ref, s32[35]{0:T(128)S(1)} %pad_add_fusion.place_ref, s32[32]{0:T(128)S(1)} %copy-done.2, f32[32,1152]{1,0:T(8,128)S(1)} %tap_lines.1.refs_0_, bf16[360,640]{1,0:T(8,128)(2,1)S(1)} %collective-permute-done.8.refs_1_, ...), custom_call_target="tpu_custom_call" | custom-call | flops 3019898880 | bytes 3686400 | tf_op jit(solution)/shard_map/filter_whole/pallas_call | solution.py:304
  83.7 1.3 %collective-permute-done.18.refs_2_ = bf16[360,640]{1,0:T(8,128)(2,1)S(1)} collective-permute-done((bf16[360,640]{1,0:T(8,128)(2,1)S(1)}, bf16[360,640]{1,0:T(8,128)(2,1)S(1)}, u32[]{:S(2)}, u32[]{:S(2)}) %collective-permute-start.18) | collective-permute-done | bytes 460832 | tf_op jit(solution)/shard_map/ppermute | solution.py:355
  85.1 4.2 %collective-permute-start.22 = (bf16[360,640]{1,0:T(8,128)(2,1)S(1)}, bf16[360,640]{1,0:T(8,128)(2,1)S(1)}, u32[]{:S(2)}, u32[]{:S(2)}) collective-permute-start(bf16[360,640]{1,0:T(8,128)(2,1)S(1)} %get-tuple-element.67), channel_id=1, source_target_pairs={{0,2},{2,0},{4,6},{6,4},{8,10},{10,8},{12,14},{14,12},{16,18},{18,... | collective-permute-start | bytes 1382408 | tf_op jit(solution)/shard_map/ppermute | solution.py:355
  89.3 5.7 %collective-permute-done.19.refs_3_ = bf16[360,640]{1,0:T(8,128)(2,1)S(1)} collective-permute-done((bf16[360,640]{1,0:T(8,128)(2,1)S(1)}, bf16[360,640]{1,0:T(8,128)(2,1)S(1)}, u32[]{:S(2)}, u32[]{:S(2)}) %collective-permute-start.19) | collective-permute-done | bytes 460832 | tf_op jit(solution)/shard_map/ppermute | solution.py:355
  94.9 1.3 %filter_late.1 = (bf16[360,640]{1,0:T(8,128)(2,1)S(1)}, bf16[360,640]{1,0:T(8,128)(2,1)S(1)}) custom-call(s32[16]{0:T(128)S(1)} %get-tuple-element.38.rows_ref, s32[35]{0:T(128)S(1)} %pad_add_fusion.place_ref, s32[32]{0:T(128)S(1)} %copy-done.2, f32[2,180,1280]{2,1,0:T(8,128)S(1)} %get-tuple-element.59.refs_0_, ...), custom_call_target="tpu_custom_call" | custom-call | flops 905969664 | bytes 3686400 | tf_op jit(solution)/shard_map/filter_late/pallas_call | solution.py:304
  96.3 0.2 collective-permute-start.23
  96.5 0.0 collective-permute-done.7.refs_1_
  96.5 0.0 collective-permute-done.20.refs_4_
  96.5 0.0 collective-permute-done.21.refs_5_
  96.5 0.0 collective-permute-done.22.refs_6_
  96.5 1.7 %collective-permute-done.23.refs_7_ = bf16[360,640]{1,0:T(8,128)(2,1)S(1)} collective-permute-done((bf16[360,640]{1,0:T(8,128)(2,1)S(1)}, bf16[360,640]{1,0:T(8,128)(2,1)S(1)}, u32[]{:S(2)}, u32[]{:S(2)}) %collective-permute-start.23) | collective-permute-done | bytes 460832 | tf_op jit(solution)/shard_map/ppermute | solution.py:355
  98.2 2.8 %put_rows.1 = bf16[180,16,640]{2,1,0:T(8,128)(2,1)} custom-call(s32[16]{0:T(128)S(1)} %get-tuple-element.37.slots_ref, bf16[360,640]{1,0:T(8,128)(2,1)S(1)} %get-tuple-element.45.refs_0_, bf16[360,640]{1,0:T(8,128)(2,1)S(1)} %collective-permute-done.7.refs_1_, bf16[360,640]{1,0:T(8,128)(2,1)S(1)} %get-tuple-element.54.refs_2_, ...), custom_call_target="tpu_custom_call" | custom-call | flops 943718400 | bytes 7372800 | tf_op jit(solution)/shard_map/put_rows/pallas_call | solution.py:206
Async XLA Ops:
  0.0 50.9 %copy-start.2 = (s32[32]{0:T(128)S(1)}, s32[32]{0:T(128)}, u32[]{:S(2)}) copy-start(s32[32]{0:T(128)} %widths_ref.9) | copy-start | bytes 388
  0.7 2.0 %copy-start = (bf16[16,180,640]{2,0,1:T(8,128)(2,1)S(1)}, bf16[16,180,640]{2,0,1:T(8,128)(2,1)}, u32[]{:S(2)}) copy-start(bf16[16,180,640]{2,0,1:T(8,128)(2,1)} %param.4) | copy-start | bytes 11059204
  2.8 47.4 %copy-start.1 = (bf16[32,2880]{1,0:T(8,128)(2,1)S(1)}, bf16[32,2880]{1,0:T(8,128)(2,1)}, u32[]{:S(2)}) copy-start(bf16[32,2880]{1,0:T(8,128)(2,1)} %taps_ref.1) | copy-start | bytes 552964
  5.9 7.9 %collective-permute-start = (bf16[360,640]{1,0:T(8,128)(2,1)S(1)}, bf16[360,640]{1,0:T(8,128)(2,1)S(1)}, u32[]{:S(2)}, u32[]{:S(2)}) collective-permute-start(bf16[360,640]{1,0:T(8,128)(2,1)S(1)} %get-tuple-element.40), channel_id=1, source_target_pairs={{0,2},{2,0},{4,6},{6,4},{8,10},{10,8},{12,14},{14,12},{16,18},{18,... | collective-permute-start | bytes 1382408 | tf_op jit(solution)/shard_map/ppermute | solution.py:355
  6.4 15.5 %collective-permute-start.3 = (bf16[360,640]{1,0:T(8,128)(2,1)S(1)}, bf16[360,640]{1,0:T(8,128)(2,1)S(1)}, u32[]{:S(2)}, u32[]{:S(2)}) collective-permute-start(bf16[360,640]{1,0:T(8,128)(2,1)S(1)} %get-tuple-element.39.refs_1_.refs_5_), channel_id=1, source_target_pairs={{0,24},{2,26},{4,12},{6,14},{8,0},{10,2},{12,20},{14,22},{16,8},{1... | collective-permute-start | bytes 1382408 | tf_op jit(solution)/shard_map/ppermute | solution.py:355
  11.1 13.4 %collective-permute-start.1 = (bf16[360,640]{1,0:T(8,128)(2,1)S(1)}, bf16[360,640]{1,0:T(8,128)(2,1)S(1)}, u32[]{:S(2)}, u32[]{:S(2)}) collective-permute-start(bf16[360,640]{1,0:T(8,128)(2,1)S(1)} %get-tuple-element.41), channel_id=1, source_target_pairs={{0,4},{2,6},{4,0},{6,2},{8,12},{10,14},{12,8},{14,10},{16,20},{18,... | collective-permute-start | bytes 1382408 | tf_op jit(solution)/shard_map/ppermute | solution.py:355
  11.1 13.4 %collective-permute-start.8 = (bf16[360,640]{1,0:T(8,128)(2,1)S(1)}, bf16[360,640]{1,0:T(8,128)(2,1)S(1)}, u32[]{:S(2)}, u32[]{:S(2)}) collective-permute-start(bf16[360,640]{1,0:T(8,128)(2,1)S(1)} %get-tuple-element.47), channel_id=1, source_target_pairs={{0,1},{1,0},{2,3},{3,2},{4,5},{5,4},{6,7},{7,6},{8,9},{9,8},{10,11... | collective-permute-start | bytes 1382408 | tf_op jit(solution)/shard_map/ppermute | solution.py:355
  12.6 20.2 %collective-permute-start.2 = (bf16[360,640]{1,0:T(8,128)(2,1)S(1)}, bf16[360,640]{1,0:T(8,128)(2,1)S(1)}, u32[]{:S(2)}, u32[]{:S(2)}) collective-permute-start(bf16[360,640]{1,0:T(8,128)(2,1)S(1)} %get-tuple-element.42), channel_id=1, source_target_pairs={{0,6},{2,4},{4,2},{6,0},{8,14},{10,12},{12,10},{14,8},{16,22},{18,... | collective-permute-start | bytes 1382408 | tf_op jit(solution)/shard_map/ppermute | solution.py:355
  13.8 20.5 %collective-permute-start.5 = (bf16[360,640]{1,0:T(8,128)(2,1)S(1)}, bf16[360,640]{1,0:T(8,128)(2,1)S(1)}, u32[]{:S(2)}, u32[]{:S(2)}) collective-permute-start(bf16[360,640]{1,0:T(8,128)(2,1)S(1)} %collective-permute-done.refs_2_.refs_6_), channel_id=1, source_target_pairs={{0,24},{2,26},{4,12},{6,14},{8,0},{10,2},{12,20},{14,22},{16,8},{1... | collective-permute-start | bytes 1382408 | tf_op jit(solution)/shard_map/ppermute | solution.py:355
  22.0 12.8 %collective-permute-start.9 = (bf16[360,640]{1,0:T(8,128)(2,1)S(1)}, bf16[360,640]{1,0:T(8,128)(2,1)S(1)}, u32[]{:S(2)}, u32[]{:S(2)}) collective-permute-start(bf16[360,640]{1,0:T(8,128)(2,1)S(1)} %get-tuple-element.49), channel_id=1, source_target_pairs={{0,3},{1,2},{2,1},{3,0},{4,7},{5,6},{6,5},{7,4},{8,11},{9,10},{10,... | collective-permute-start | bytes 1382408 | tf_op jit(solution)/shard_map/ppermute | solution.py:355
  24.5 25.7 %collective-permute-start.10 = (bf16[360,640]{1,0:T(8,128)(2,1)S(1)}, bf16[360,640]{1,0:T(8,128)(2,1)S(1)}, u32[]{:S(2)}, u32[]{:S(2)}) collective-permute-start(bf16[360,640]{1,0:T(8,128)(2,1)S(1)} %collective-permute-done.8.refs_1_), channel_id=1, source_target_pairs={{0,4},{2,6},{4,0},{6,2},{8,12},{10,14},{12,8},{14,10},{16,20},{18,... | collective-permute-start | bytes 1382408 | tf_op jit(solution)/shard_map/ppermute | solution.py:355
  25.5 24.8 %collective-permute-start.4 = (bf16[360,640]{1,0:T(8,128)(2,1)S(1)}, bf16[360,640]{1,0:T(8,128)(2,1)S(1)}, u32[]{:S(2)}, u32[]{:S(2)}) collective-permute-start(bf16[360,640]{1,0:T(8,128)(2,1)S(1)} %collective-permute-done.1.refs_3_.refs_1_), channel_id=1, source_target_pairs={{0,8},{2,10},{4,28},{6,30},{8,16},{10,18},{12,4},{14,6},{16,24},{1... | collective-permute-start | bytes 1382408 | tf_op jit(solution)/shard_map/ppermute | solution.py:355
  32.8 17.6 %collective-permute-start.14 = (bf16[360,640]{1,0:T(8,128)(2,1)S(1)}, bf16[360,640]{1,0:T(8,128)(2,1)S(1)}, u32[]{:S(2)}, u32[]{:S(2)}) collective-permute-start(bf16[360,640]{1,0:T(8,128)(2,1)S(1)} %get-tuple-element.56), channel_id=1, source_target_pairs={{0,1},{1,0},{2,3},{3,2},{4,5},{5,4},{6,7},{7,6},{8,9},{9,8},{10,11... | collective-permute-start | bytes 1382408 | tf_op jit(solution)/shard_map/ppermute | solution.py:355
  34.3 19.5 %collective-permute-start.6 = (bf16[360,640]{1,0:T(8,128)(2,1)S(1)}, bf16[360,640]{1,0:T(8,128)(2,1)S(1)}, u32[]{:S(2)}, u32[]{:S(2)}) collective-permute-start(bf16[360,640]{1,0:T(8,128)(2,1)S(1)} %collective-permute-done.2.refs_4_.refs_2_), channel_id=1, source_target_pairs={{0,8},{2,10},{4,28},{6,30},{8,16},{10,18},{12,4},{14,6},{16,24},{1... | collective-permute-start | bytes 1382408 | tf_op jit(solution)/shard_map/ppermute | solution.py:355
  34.8 25.1 %collective-permute-start.11 = (bf16[360,640]{1,0:T(8,128)(2,1)S(1)}, bf16[360,640]{1,0:T(8,128)(2,1)S(1)}, u32[]{:S(2)}, u32[]{:S(2)}) collective-permute-start(bf16[360,640]{1,0:T(8,128)(2,1)S(1)} %collective-permute-done.9.refs_2_), channel_id=1, source_target_pairs={{0,4},{2,6},{4,0},{6,2},{8,12},{10,14},{12,8},{14,10},{16,20},{18,... | collective-permute-start | bytes 1382408 | tf_op jit(solution)/shard_map/ppermute | solution.py:355
  50.2 12.8 %collective-permute-start.15 = (bf16[360,640]{1,0:T(8,128)(2,1)S(1)}, bf16[360,640]{1,0:T(8,128)(2,1)S(1)}, u32[]{:S(2)}, u32[]{:S(2)}) collective-permute-start(bf16[360,640]{1,0:T(8,128)(2,1)S(1)} %get-tuple-element.58), channel_id=1, source_target_pairs={{0,3},{1,2},{2,1},{3,0},{4,7},{5,6},{6,5},{7,4},{8,11},{9,10},{10,... | collective-permute-start | bytes 1382408 | tf_op jit(solution)/shard_map/ppermute | solution.py:355
  50.3 14.7 %collective-permute-start.12 = (bf16[360,640]{1,0:T(8,128)(2,1)S(1)}, bf16[360,640]{1,0:T(8,128)(2,1)S(1)}, u32[]{:S(2)}, u32[]{:S(2)}) collective-permute-start(bf16[360,640]{1,0:T(8,128)(2,1)S(1)} %collective-permute-done.10.refs_3_), channel_id=1, source_target_pairs={{0,8},{2,10},{4,28},{6,30},{8,16},{10,18},{12,4},{14,6},{16,24},{1... | collective-permute-start | bytes 1382408 | tf_op jit(solution)/shard_map/ppermute | solution.py:355
  50.4 18.1 %collective-permute-start.16 = (bf16[360,640]{1,0:T(8,128)(2,1)S(1)}, bf16[360,640]{1,0:T(8,128)(2,1)S(1)}, u32[]{:S(2)}, u32[]{:S(2)}) collective-permute-start(bf16[360,640]{1,0:T(8,128)(2,1)S(1)} %collective-permute-done.14.refs_1_), channel_id=1, source_target_pairs={{0,4},{2,6},{4,0},{6,2},{8,12},{10,14},{12,8},{14,10},{16,20},{18,... | collective-permute-start | bytes 1382408 | tf_op jit(solution)/shard_map/ppermute | solution.py:355
  59.9 15.3 %collective-permute-start.13 = (bf16[360,640]{1,0:T(8,128)(2,1)S(1)}, bf16[360,640]{1,0:T(8,128)(2,1)S(1)}, u32[]{:S(2)}, u32[]{:S(2)}) collective-permute-start(bf16[360,640]{1,0:T(8,128)(2,1)S(1)} %collective-permute-done.11.refs_4_), channel_id=1, source_target_pairs={{0,8},{2,10},{4,28},{6,30},{8,16},{10,18},{12,4},{14,6},{16,24},{1... | collective-permute-start | bytes 1382408 | tf_op jit(solution)/shard_map/ppermute | solution.py:355
  63.0 15.4 %collective-permute-start.17 = (bf16[360,640]{1,0:T(8,128)(2,1)S(1)}, bf16[360,640]{1,0:T(8,128)(2,1)S(1)}, u32[]{:S(2)}, u32[]{:S(2)}) collective-permute-start(bf16[360,640]{1,0:T(8,128)(2,1)S(1)} %collective-permute-done.15.refs_2_), channel_id=1, source_target_pairs={{0,4},{2,6},{4,0},{6,2},{8,12},{10,14},{12,8},{14,10},{16,20},{18,... | collective-permute-start | bytes 1382408 | tf_op jit(solution)/shard_map/ppermute | solution.py:355
  64.0 32.5 %collective-permute-start.7 = (bf16[360,640]{1,0:T(8,128)(2,1)S(1)}, bf16[360,640]{1,0:T(8,128)(2,1)S(1)}, u32[]{:S(2)}, u32[]{:S(2)}) collective-permute-start(bf16[360,640]{1,0:T(8,128)(2,1)S(1)} %get-tuple-element.46), channel_id=1, source_target_pairs={{0,4},{2,6},{4,0},{6,2},{8,12},{10,14},{12,8},{14,10},{16,20},{18,... | collective-permute-start | bytes 1382408 | tf_op jit(solution)/shard_map/ppermute | solution.py:355
  68.5 16.6 %collective-permute-start.18 = (bf16[360,640]{1,0:T(8,128)(2,1)S(1)}, bf16[360,640]{1,0:T(8,128)(2,1)S(1)}, u32[]{:S(2)}, u32[]{:S(2)}) collective-permute-start(bf16[360,640]{1,0:T(8,128)(2,1)S(1)} %collective-permute-done.16.refs_3_), channel_id=1, source_target_pairs={{0,8},{2,10},{4,28},{6,30},{8,16},{10,18},{12,4},{14,6},{16,24},{1... | collective-permute-start | bytes 1382408 | tf_op jit(solution)/shard_map/ppermute | solution.py:355
  71.4 25.0 %collective-permute-start.20 = (bf16[360,640]{1,0:T(8,128)(2,1)S(1)}, bf16[360,640]{1,0:T(8,128)(2,1)S(1)}, u32[]{:S(2)}, u32[]{:S(2)}) collective-permute-start(bf16[360,640]{1,0:T(8,128)(2,1)S(1)} %get-tuple-element.64), channel_id=1, source_target_pairs={{0,2},{2,0},{4,6},{6,4},{8,10},{10,8},{12,14},{14,12},{16,18},{18,... | collective-permute-start | bytes 1382408 | tf_op jit(solution)/shard_map/ppermute | solution.py:355
  78.4 16.6 %collective-permute-start.19 = (bf16[360,640]{1,0:T(8,128)(2,1)S(1)}, bf16[360,640]{1,0:T(8,128)(2,1)S(1)}, u32[]{:S(2)}, u32[]{:S(2)}) collective-permute-start(bf16[360,640]{1,0:T(8,128)(2,1)S(1)} %collective-permute-done.17.refs_4_), channel_id=1, source_target_pairs={{0,8},{2,10},{4,28},{6,30},{8,16},{10,18},{12,4},{14,6},{16,24},{1... | collective-permute-start | bytes 1382408 | tf_op jit(solution)/shard_map/ppermute | solution.py:355
  78.4 18.1 %collective-permute-start.21 = (bf16[360,640]{1,0:T(8,128)(2,1)S(1)}, bf16[360,640]{1,0:T(8,128)(2,1)S(1)}, u32[]{:S(2)}, u32[]{:S(2)}) collective-permute-start(bf16[360,640]{1,0:T(8,128)(2,1)S(1)} %get-tuple-element.66), channel_id=1, source_target_pairs={{0,6},{2,4},{4,2},{6,0},{8,14},{10,12},{12,10},{14,8},{16,22},{18,... | collective-permute-start | bytes 1382408 | tf_op jit(solution)/shard_map/ppermute | solution.py:355
  85.1 11.4 %collective-permute-start.22 = (bf16[360,640]{1,0:T(8,128)(2,1)S(1)}, bf16[360,640]{1,0:T(8,128)(2,1)S(1)}, u32[]{:S(2)}, u32[]{:S(2)}) collective-permute-start(bf16[360,640]{1,0:T(8,128)(2,1)S(1)} %get-tuple-element.67), channel_id=1, source_target_pairs={{0,2},{2,0},{4,6},{6,4},{8,10},{10,8},{12,14},{14,12},{16,18},{18,... | collective-permute-start | bytes 1382408 | tf_op jit(solution)/shard_map/ppermute | solution.py:355
  96.3 1.9 %collective-permute-start.23 = (bf16[360,640]{1,0:T(8,128)(2,1)S(1)}, bf16[360,640]{1,0:T(8,128)(2,1)S(1)}, u32[]{:S(2)}, u32[]{:S(2)}) collective-permute-start(bf16[360,640]{1,0:T(8,128)(2,1)S(1)} %get-tuple-element.68), channel_id=1, source_target_pairs={{0,2},{2,0},{4,6},{6,4},{8,10},{10,8},{12,14},{14,12},{16,18},{18,... | collective-permute-start | bytes 1382408 | tf_op jit(solution)/shard_map/ppermute | solution.py:355

commit v12 on v11

--- a/solution.py
+++ b/solution.py
@@ -8,6 +8,9 @@
 from jax.sharding import PartitionSpec as P
 
 VMEM_LIMIT = 12 * 1024 * 1024
+TAKE_VMEM_LIMIT = 50 * 1024 * 1024
+PIECE = 3
+AHEAD = 2
 SMEM_SPEC = pl.BlockSpec(memory_space=pltpu.SMEM)
 VMEM_SPEC = pl.BlockSpec(memory_space=pltpu.VMEM)
 HBM_SPEC = pl.BlockSpec(memory_space=pltpu.HBM)
@@ -83,61 +86,99 @@
     return jnp.concatenate(bands, axis=0)
 
 
-def take_kernel(chunks, lat_dev, block, place_ref, fields_ref, *refs):
-    outs = refs[: len(chunks)]
-    rows_ref, slots_ref, home_ref, take_ref = refs[len(chunks) :]
-    lon_dev, _, channels = fields_ref.shape
+def listed(n, quarter, core):
+    within = n % quarter
+    return within + jnp.where(n // quarter == core, 0, quarter)
+
+
+def traded(n, quarter, x):
+    within = n % quarter
+    return n - within + (within + quarter // 2 * x) % quarter
+
+
+def list_kernel(lat_dev, place_ref, rows_ref, slots_ref):
     half, quarter = lat_dev // 2, lat_dev // 4
-    starts = list(range(0, lon_dev, block))
     band, core, x = place_ref[0], place_ref[1], place_ref[2]
-
-    def at(n):
-        within = n % quarter
-        return within + jnp.where(n // quarter == core, 0, quarter)
-
-    def traded(n):
-        within = n % quarter
-        return n - within + (within + quarter // 2 * x) % quarter
-
-    stay, leave, come = jnp.int32(0), jnp.int32(0), jnp.int32(0)
+    stay, come = jnp.int32(0), jnp.int32(0)
     for j in range(lat_dev):
         here = band * lat_dev + j
         there = (1 - band) * lat_dev + j
         stays = place_ref[3 + here] // lat_dev == band
         comes = place_ref[3 + there] // lat_dev == band
-        home_ref[jnp.where(stays, traded(at(stay)), half + at(leave))] = jnp.int32(j)
 
         @pl.when(stays)
         def _():
-            spot = traded(at(stay))
+            spot = traded(listed(stay, quarter, core), quarter, x)
             spot = spot + jnp.where(spot >= quarter, quarter, 0)
             rows_ref[spot] = here
             slots_ref[spot] = place_ref[3 + here] % lat_dev
 
         @pl.when(comes)
         def _():
-            spot = at(come)
+            spot = listed(come, quarter, core)
             spot = spot + jnp.where(spot >= quarter, half, quarter)
             rows_ref[spot] = there
             slots_ref[spot] = place_ref[3 + there] % lat_dev
 
         stay = stay + stays.astype(jnp.int32)
+        come = come + comes.astype(jnp.int32)
+
+
+def list_rows(place, lat_dev):
+    ints = jax.ShapeDtypeStruct((lat_dev,), jnp.int32)
+    return pl.pallas_call(
+        functools.partial(list_kernel, lat_dev),
+        out_shape=[ints, ints],
+        in_specs=[SMEM_SPEC],
+        out_specs=[SMEM_SPEC, SMEM_SPEC],
+        compiler_params=pltpu.CompilerParams(vmem_limit_bytes=VMEM_LIMIT),
+        cost_estimate=pl.CostEstimate(flops=0, bytes_accessed=256, transcendentals=0),
+        name="list_rows",
+    )(place)
+
+
+def take_kernel(chunks, lat_dev, block, place_ref, fields_ref, *refs):
+    outs = refs[: len(chunks)]
+    home_ref, take_ref, panel_ref, sems = refs[len(chunks) :]
+    lon_dev, _, channels = fields_ref.shape
+    half, quarter = lat_dev // 2, lat_dev // 4
+    copies = []
+    for n, start in enumerate(range(0, lon_dev, PIECE * block)):
+        window = pl.ds(start, min(PIECE * block, lon_dev - start))
+        copies.append(pltpu.make_async_copy(fields_ref.at[window], panel_ref.at[window], sems.at[n]))
+    for copy in copies[:AHEAD]:
+        copy.start()
+
+    band, core, x = place_ref[0], place_ref[1], place_ref[2]
+    stay, leave = jnp.int32(0), jnp.int32(0)
+    for j in range(lat_dev):
+        stays = place_ref[3 + band * lat_dev + j] // lat_dev == band
+        spot = traded(listed(stay, quarter, core), quarter, x)
+        home_ref[jnp.where(stays, spot, half + listed(leave, quarter, core))] = jnp.int32(j)
+        stay = stay + stays.astype(jnp.int32)
         leave = leave + 1 - stays.astype(jnp.int32)
-        come = come + comes.astype(jnp.int32)
 
     def selector(lon):
         row = lax.broadcasted_iota(jnp.int32, (lat_dev * lon, 128), 0)
-        wanted = row % lon * lat_dev
-        for p in range(lat_dev):
-            wanted += jnp.where(row // lon == p, home_ref[p], 0)
+        if lon % 8 == 0:
+            home = jnp.concatenate([jnp.full((lon, 128), home_ref[p], jnp.int32) for p in range(lat_dev)], axis=0)
+        else:
+            home = sum(jnp.where(row // lon == p, home_ref[p], 0) for p in range(lat_dev))
+        wanted = row % lon * lat_dev + home
         column = lax.broadcasted_iota(jnp.int32, (lat_dev * lon, lon * lat_dev), 1)
         return jnp.where(column == wanted[:, :1], 1.0, 0.0).astype(jnp.bfloat16)
 
     take_ref[...] = selector(block)
-    for start in starts:
+    rest = lon_dev % block
+    small = selector(rest) if rest else None
+    for n, start in enumerate(range(0, lon_dev, block)):
+        if n % PIECE == 0:
+            copies[n // PIECE].wait()
+            if n // PIECE + AHEAD < len(copies):
+                copies[n // PIECE + AHEAD].start()
         lon = min(block, lon_dev - start)
-        panel = fields_ref[start : start + lon].reshape(lon * lat_dev, channels)
-        take = take_ref[...] if lon == block else selector(lon)
+        panel = panel_ref[start : start + lon].reshape(lon * lat_dev, channels)
+        take = take_ref[...] if lon == block else small
         taken = jnp.dot(take, panel, preferred_element_type=jnp.float32)
         place = 0
         for out, count in zip(outs, chunks):
@@ -150,23 +191,23 @@
 def take_rows(fields, place, chunks):
     lon_dev, lat_dev, channels = fields.shape
     block = 16
-    ints = jax.ShapeDtypeStruct((lat_dev,), jnp.int32)
-    result = pl.pallas_call(
+    return pl.pallas_call(
         functools.partial(take_kernel, chunks, lat_dev, block),
-        out_shape=[jax.ShapeDtypeStruct((n * lon_dev, channels), fields.dtype) for n in chunks] + [ints, ints],
-        in_specs=[SMEM_SPEC, VMEM_SPEC],
-        out_specs=[VMEM_SPEC] * len(chunks) + [SMEM_SPEC, SMEM_SPEC],
+        out_shape=[jax.ShapeDtypeStruct((n * lon_dev, channels), fields.dtype) for n in chunks],
+        in_specs=[SMEM_SPEC, HBM_SPEC],
+        out_specs=[VMEM_SPEC] * len(chunks),
         scratch_shapes=[
             pltpu.SMEM((lat_dev,), jnp.int32),
             pltpu.VMEM((block * lat_dev, block * lat_dev), jnp.bfloat16),
+            pltpu.VMEM(fields.shape, fields.dtype),
+            pltpu.SemaphoreType.DMA((pl.cdiv(lon_dev, PIECE * block),)),
         ],
-        compiler_params=pltpu.CompilerParams(vmem_limit_bytes=VMEM_LIMIT),
+        compiler_params=pltpu.CompilerParams(vmem_limit_bytes=TAKE_VMEM_LIMIT),
         cost_estimate=pl.CostEstimate(
             flops=2 * fields.size * block * lat_dev, bytes_accessed=4 * fields.size, transcendentals=0
         ),
         name="take_rows",
     )(place, fields)
-    return result[:-2], result[-2], result[-1]
 
 
 def put_kernel(counts, lat_dev, block, slots_ref, *refs):
@@ -182,6 +223,8 @@
         return jnp.where(row == wanted[:1], 1.0, 0.0).astype(jnp.bfloat16)
 
     whole = selector(block)
+    rest = lon_dev % block
+    small = selector(rest) if rest else None
     copies = []
     for n, start in enumerate(range(0, lon_dev, block)):
         lon = min(block, lon_dev - start)
@@ -189,7 +232,7 @@
         if lon < block:
             pieces = [p.astype(jnp.float32) for p in pieces]
         panel = jnp.concatenate(pieces, axis=0).astype(jnp.bfloat16)
-        spread = jnp.dot(whole if lon == block else selector(lon), panel, preferred_element_type=jnp.float32)
+        spread = jnp.dot(whole if lon == block else small, panel, preferred_element_type=jnp.float32)
         window = pl.ds(start, lon)
         panel_ref[window] = spread.astype(jnp.bfloat16).reshape(lon, lat_dev, channels)
         copies.append(pltpu.make_async_copy(panel_ref.at[window], out_ref.at[window], sems.at[n]))
@@ -325,7 +368,7 @@
     core, x = at % 2, at // 2 % 2
     place = jnp.concatenate([jnp.stack([band, core, x]).astype(jnp.int32), owner_slot])
     chunks = STAY + STAY + COME + COME
-    taken, rows, slots = take_rows(jnp.transpose(fields, (1, 0, 2)), place, chunks)
+    taken = take_rows(jnp.transpose(fields, (1, 0, 2)), place, chunks)
     n_stay, n_come = len(STAY), len(COME)
     keep, give = taken[:n_stay], taken[n_stay : 2 * n_stay]
     straight, cross = taken[2 * n_stay : 2 * n_stay + n_come], taken[2 * n_stay + n_come :]
@@ -339,6 +382,7 @@
     across_both = [(i, i ^ 3) for i in range(2 * n_lon)]
 
     lines = tap_lines(tap_weights, 3 * lon_dev)
+    rows, slots = list_rows(place, lat_dev)
     scalars = rows, place, widths
     sizes = STAY + COME
     starts = [sum(sizes[:c]) for c in range(len(sizes))]

time: 101 us -> 102 us (level)
  Pallas kernels: 18.5 us -> 21.6 us
  local copies, waits for them, and re-layouts: 2.05 us -> 0.01 us
    unnamed x6 -> x4, local copies, waits for them, and re-layouts: 2.05 us -> 0.01 us
    pallas_call x0 -> x1, Pallas kernels: none -> 1.81 us  [list_rows(): pl.pallas_call(functools.partial(list_kernel, lat_dev), out_shape=[ints,...]
    pallas_call x1, Pallas kernels: 3.1 us -> 4.35 us  [take_rows(): pl.pallas_call(functools.partial(take_kernel, chunks, lat_dev, block), ou...]
  transfers between devices with their start and end apart: 24 -> 24, of which waited for: 12 -> 13; matrix products, arithmetic and copies ran while one was open for 0% -> 0% of each run, Pallas kernels for 12% -> 14%
where the time goes in v12:
time: 102 us
  waiting for transfers between devices  46 us (45%)
  starting transfers between devices  33.2 us (33%)
  Pallas kernels  21.6 us (21%)
    ppermute x24, waiting for transfers between devices, moved(): return lax.ppermute(operand, axes, pairs)  46 us
    ppermute x24, starting transfers between devices, moved(): return lax.ppermute(operand, axes, pairs)  33.2 us
    pallas_call x5, Pallas kernels, filter_pair(): pl.pallas_call(functools.partial(pair_kernel, lon_dev, base, tuple(plan),...  12.6 us
    pallas_call x1, Pallas kernels, take_rows(): pl.pallas_call(functools.partial(take_kernel, chunks, lat_dev, block), ou...  4.35 us
    pallas_call x1, Pallas kernels, put_rows(): pl.pallas_call(functools.partial(put_kernel, counts, lat_dev, block), out...  2.8 us
  transfers between devices with their start and end apart: 24, of which 13 were waited for; matrix products, arithmetic and copies ran while one was open for 0% of the time, Pallas kernels for 14%

profile of v12, /device:TPU:0, one launch (start us, length us, event | category | flops | bytes accessed | tf_op | source)
XLA Modules:
  0.0 101.9 jit_solution(1428135767202995836)
XLA Ops:
  0.0 0.0 copy-start
  0.0 0.0 copy-start.1
  0.0 0.8 pad_add_fusion.place_ref
  0.8 4.3 %take_rows.1 = (bf16[360,640]{1,0:T(8,128)(2,1)S(1)}, bf16[360,640]{1,0:T(8,128)(2,1)S(1)}, bf16[360,640]{1,0:T(8,128)(2,1)S(1)}, bf16[360,640]{1,0:T(8,128)(2,1...) custom-call(s32[35]{0:T(128)S(1)} %pad_add_fusion.place_ref, ...), custom_call_target="tpu_custom_call" | custom-call | flops 943718400 | bytes 7372800 | tf_op jit(solution)/shard_map/take_rows/pallas_call | solution.py:194
  5.1 0.5 collective-permute-start
  5.6 4.7 %collective-permute-start.3 = (bf16[360,640]{1,0:T(8,128)(2,1)S(1)}, bf16[360,640]{1,0:T(8,128)(2,1)S(1)}, u32[]{:S(2)}, u32[]{:S(2)}) collective-permute-start(bf16[360,640]{1,0:T(8,128)(2,1)S(1)} %get-tuple-element.39.refs_1_.refs_5_), channel_id=1, source_target_pairs={{0,24},{2,26},{4,12},{6,14},{8,0},{10,2},{12,20},{14,22},{16,8},{1... | collective-permute-start | bytes 1382408 | tf_op jit(solution)/shard_map/ppermute | solution.py:399
  10.3 0.0 collective-permute-start.1
  10.3 1.5 %collective-permute-start.8 = (bf16[360,640]{1,0:T(8,128)(2,1)S(1)}, bf16[360,640]{1,0:T(8,128)(2,1)S(1)}, u32[]{:S(2)}, u32[]{:S(2)}) collective-permute-start(bf16[360,640]{1,0:T(8,128)(2,1)S(1)} %get-tuple-element.47), channel_id=1, source_target_pairs={{0,1},{1,0},{2,3},{3,2},{4,5},{5,4},{6,7},{7,6},{8,9},{9,8},{10,11... | collective-permute-start | bytes 1382408 | tf_op jit(solution)/shard_map/ppermute | solution.py:399
  11.8 1.2 %collective-permute-start.2 = (bf16[360,640]{1,0:T(8,128)(2,1)S(1)}, bf16[360,640]{1,0:T(8,128)(2,1)S(1)}, u32[]{:S(2)}, u32[]{:S(2)}) collective-permute-start(bf16[360,640]{1,0:T(8,128)(2,1)S(1)} %get-tuple-element.42), channel_id=1, source_target_pairs={{0,6},{2,4},{4,2},{6,0},{8,14},{10,12},{12,10},{14,8},{16,22},{18,... | collective-permute-start | bytes 1382408 | tf_op jit(solution)/shard_map/ppermute | solution.py:399
  13.1 0.0 collective-permute-done.refs_2_.refs_6_
  13.1 0.5 collective-permute-start.5
  13.6 7.6 %collective-permute-done.3.refs_3_ = bf16[360,640]{1,0:T(8,128)(2,1)S(1)} collective-permute-done((bf16[360,640]{1,0:T(8,128)(2,1)S(1)}, bf16[360,640]{1,0:T(8,128)(2,1)S(1)}, u32[]{:S(2)}, u32[]{:S(2)}) %collective-permute-start.3) | collective-permute-done | bytes 460832 | tf_op jit(solution)/shard_map/ppermute | solution.py:399
  21.2 0.3 collective-permute-start.9
  21.5 2.2 %collective-permute-done.1.refs_3_.refs_1_ = bf16[360,640]{1,0:T(8,128)(2,1)S(1)} collective-permute-done((bf16[360,640]{1,0:T(8,128)(2,1)S(1)}, bf16[360,640]{1,0:T(8,128)(2,1)S(1)}, u32[]{:S(2)}, u32[]{:S(2)}) %collective-permute-start.1) | collective-permute-done | bytes 460832 | tf_op jit(solution)/shard_map/ppermute | solution.py:399
  23.7 0.0 collective-permute-done.8.refs_1_
  23.7 1.0 collective-permute-start.10
  24.7 0.1 collective-permute-start.4
  24.8 7.3 %collective-permute-done.2.refs_4_.refs_2_ = bf16[360,640]{1,0:T(8,128)(2,1)S(1)} collective-permute-done((bf16[360,640]{1,0:T(8,128)(2,1)S(1)}, bf16[360,640]{1,0:T(8,128)(2,1)S(1)}, u32[]{:S(2)}, u32[]{:S(2)}) %collective-permute-start.2) | collective-permute-done | bytes 460832 | tf_op jit(solution)/shard_map/ppermute | solution.py:399
  32.0 1.5 %collective-permute-start.14 = (bf16[360,640]{1,0:T(8,128)(2,1)S(1)}, bf16[360,640]{1,0:T(8,128)(2,1)S(1)}, u32[]{:S(2)}, u32[]{:S(2)}) collective-permute-start(bf16[360,640]{1,0:T(8,128)(2,1)S(1)} %get-tuple-element.56), channel_id=1, source_target_pairs={{0,1},{1,0},{2,3},{3,2},{4,5},{5,4},{6,7},{7,6},{8,9},{9,8},{10,11... | collective-permute-start | bytes 1382408 | tf_op jit(solution)/shard_map/ppermute | solution.py:399
  33.6 0.0 collective-permute-done.5.refs_4_
  33.6 0.1 collective-permute-start.6
  33.7 0.3 collective-permute-done.9.refs_2_
  34.0 15.4 %collective-permute-start.11 = (bf16[360,640]{1,0:T(8,128)(2,1)S(1)}, bf16[360,640]{1,0:T(8,128)(2,1)S(1)}, u32[]{:S(2)}, u32[]{:S(2)}) collective-permute-start(bf16[360,640]{1,0:T(8,128)(2,1)S(1)} %collective-permute-done.9.refs_2_), channel_id=1, source_target_pairs={{0,4},{2,6},{4,0},{6,2},{8,12},{10,14},{12,8},{14,10},{16,20},{18,... | collective-permute-start | bytes 1382408 | tf_op jit(solution)/shard_map/ppermute | solution.py:399
  49.4 0.0 collective-permute-done.10.refs_3_
  49.4 0.0 collective-permute-start.15
  49.4 1.8 %list_rows.1 = (s32[16]{0:T(128)S(1)}, s32[16]{0:T(128)S(1)}) custom-call(s32[35]{0:T(128)S(1)} %pad_add_fusion.place_ref), custom_call_target="tpu_custom_call" | custom-call | bytes 256 | tf_op jit(solution)/shard_map/list_rows/pallas_call | solution.py:129
  51.2 0.0 copy-done
  51.2 0.1 tap_lines.1.refs_0_
  51.3 0.0 collective-permute-done.4.refs_5_
  51.3 0.1 collective-permute-start.12
  51.4 0.0 collective-permute-done.14.refs_1_
  51.4 0.5 collective-permute-start.16
  51.9 0.0 copy-done.1
  51.9 2.9 %filter_whole.4 = (bf16[360,640]{1,0:T(8,128)(2,1)S(1)}, bf16[360,640]{1,0:T(8,128)(2,1)S(1)}) custom-call(s32[16]{0:T(128)S(1)} %get-tuple-element.38.rows_ref, s32[35]{0:T(128)S(1)} %pad_add_fusion.place_ref, s32[32]{0:T(128)S(1)} %copy-done.1, f32[32,1152]{1,0:T(8,128)S(1)} %tap_lines.1.refs_0_, ...), custom_call_target="tpu_custom_call" | custom-call | flops 3019898880 | bytes 3686400 | tf_op jit(solution)/shard_map/filter_whole/pallas_call | solution.py:347
  54.8 0.0 collective-permute-done.6.refs_6_
  54.9 2.4 %collective-permute-done.11.refs_4_ = bf16[360,640]{1,0:T(8,128)(2,1)S(1)} collective-permute-done((bf16[360,640]{1,0:T(8,128)(2,1)S(1)}, bf16[360,640]{1,0:T(8,128)(2,1)S(1)}, u32[]{:S(2)}, u32[]{:S(2)}) %collective-permute-start.11) | collective-permute-done | bytes 460832 | tf_op jit(solution)/shard_map/ppermute | solution.py:399
  57.3 0.0 collective-permute-start.13
  57.3 4.9 %collective-permute-done.15.refs_2_ = bf16[360,640]{1,0:T(8,128)(2,1)S(1)} collective-permute-done((bf16[360,640]{1,0:T(8,128)(2,1)S(1)}, bf16[360,640]{1,0:T(8,128)(2,1)S(1)}, u32[]{:S(2)}, u32[]{:S(2)}) %collective-permute-start.15) | collective-permute-done | bytes 460832 | tf_op jit(solution)/shard_map/ppermute | solution.py:399
  62.2 0.1 collective-permute-start.17
  62.3 2.0 %collective-permute-start.7 = (bf16[360,640]{1,0:T(8,128)(2,1)S(1)}, bf16[360,640]{1,0:T(8,128)(2,1)S(1)}, u32[]{:S(2)}, u32[]{:S(2)}) collective-permute-start(bf16[360,640]{1,0:T(8,128)(2,1)S(1)} %get-tuple-element.46), channel_id=1, source_target_pairs={{0,4},{2,6},{4,0},{6,2},{8,12},{10,14},{12,8},{14,10},{16,20},{18,... | collective-permute-start | bytes 1382408 | tf_op jit(solution)/shard_map/ppermute | solution.py:399
  64.2 1.8 %collective-permute-done.12.refs_5_ = bf16[360,640]{1,0:T(8,128)(2,1)S(1)} collective-permute-done((bf16[360,640]{1,0:T(8,128)(2,1)S(1)}, bf16[360,640]{1,0:T(8,128)(2,1)S(1)}, u32[]{:S(2)}, u32[]{:S(2)}) %collective-permute-start.12) | collective-permute-done | bytes 460832 | tf_op jit(solution)/shard_map/ppermute | solution.py:399
  66.0 1.1 %collective-permute-done.16.refs_3_ = bf16[360,640]{1,0:T(8,128)(2,1)S(1)} collective-permute-done((bf16[360,640]{1,0:T(8,128)(2,1)S(1)}, bf16[360,640]{1,0:T(8,128)(2,1)S(1)}, u32[]{:S(2)}, u32[]{:S(2)}) %collective-permute-start.16) | collective-permute-done | bytes 460832 | tf_op jit(solution)/shard_map/ppermute | solution.py:399
  67.1 0.0 collective-permute-start.18
  67.1 2.9 %filter_whole.3 = (bf16[360,640]{1,0:T(8,128)(2,1)S(1)}, bf16[360,640]{1,0:T(8,128)(2,1)S(1)}) custom-call(s32[16]{0:T(128)S(1)} %get-tuple-element.38.rows_ref, s32[35]{0:T(128)S(1)} %pad_add_fusion.place_ref, s32[32]{0:T(128)S(1)} %copy-done.1, f32[32,1152]{1,0:T(8,128)S(1)} %tap_lines.1.refs_0_, bf16[360,640]{1,0:T(8,128)(2,1)S(1)} %get-tuple-element.39.refs_1_.refs_5_, ...), custom_call_target="tpu_custom_call" | custom-call | flops 3019898880 | bytes 3686400 | tf_op jit(solution)/shard_map/filter_whole/pallas_call | solution.py:347
  70.1 0.3 collective-permute-start.20
  70.4 5.5 %collective-permute-done.13.refs_6_ = bf16[360,640]{1,0:T(8,128)(2,1)S(1)} collective-permute-done((bf16[360,640]{1,0:T(8,128)(2,1)S(1)}, bf16[360,640]{1,0:T(8,128)(2,1)S(1)}, u32[]{:S(2)}, u32[]{:S(2)}) %collective-permute-start.13) | collective-permute-done | bytes 460832 | tf_op jit(solution)/shard_map/ppermute | solution.py:399
  75.9 1.1 %collective-permute-done.17.refs_4_ = bf16[360,640]{1,0:T(8,128)(2,1)S(1)} collective-permute-done((bf16[360,640]{1,0:T(8,128)(2,1)S(1)}, bf16[360,640]{1,0:T(8,128)(2,1)S(1)}, u32[]{:S(2)}, u32[]{:S(2)}) %collective-permute-start.17) | collective-permute-done | bytes 460832 | tf_op jit(solution)/shard_map/ppermute | solution.py:399
  77.0 0.0 collective-permute-start.19
  77.0 1.6 %collective-permute-start.21 = (bf16[360,640]{1,0:T(8,128)(2,1)S(1)}, bf16[360,640]{1,0:T(8,128)(2,1)S(1)}, u32[]{:S(2)}, u32[]{:S(2)}) collective-permute-start(bf16[360,640]{1,0:T(8,128)(2,1)S(1)} %get-tuple-element.66), channel_id=1, source_target_pairs={{0,6},{2,4},{4,2},{6,0},{8,14},{10,12},{12,10},{14,8},{16,22},{18,... | collective-permute-start | bytes 1382408 | tf_op jit(solution)/shard_map/ppermute | solution.py:399
  78.6 2.5 %filter_early.1 = (f32[2,180,1280]{2,1,0:T(8,128)S(1)}, bf16[2,5,192,180]{3,2,1,0:T(8,128)(2,1)S(1)}) custom-call(s32[16]{0:T(128)S(1)} %get-tuple-element.38.rows_ref, s32[35]{0:T(128)S(1)} %pad_add_fusion.place_ref, s32[32]{0:T(128)S(1)} %copy-done.1, f32[32,1152]{1,0:T(8,128)S(1)} %tap_lines.1.refs_0_, ...), custom_call_target="tpu_custom_call" | custom-call | flops 2113929216 | bytes 3686400 | tf_op jit(solution)/shard_map/filter_early/pallas_call | solution.py:347
  81.1 2.9 %filter_whole.5 = (bf16[360,640]{1,0:T(8,128)(2,1)S(1)}, bf16[360,640]{1,0:T(8,128)(2,1)S(1)}) custom-call(s32[16]{0:T(128)S(1)} %get-tuple-element.38.rows_ref, s32[35]{0:T(128)S(1)} %pad_add_fusion.place_ref, s32[32]{0:T(128)S(1)} %copy-done.1, f32[32,1152]{1,0:T(8,128)S(1)} %tap_lines.1.refs_0_, bf16[360,640]{1,0:T(8,128)(2,1)S(1)} %collective-permute-done.8.refs_1_, ...), custom_call_target="tpu_custom_call" | custom-call | flops 3019898880 | bytes 3686400 | tf_op jit(solution)/shard_map/filter_whole/pallas_call | solution.py:347
  84.0 1.7 %collective-permute-done.18.refs_2_ = bf16[360,640]{1,0:T(8,128)(2,1)S(1)} collective-permute-done((bf16[360,640]{1,0:T(8,128)(2,1)S(1)}, bf16[360,640]{1,0:T(8,128)(2,1)S(1)}, u32[]{:S(2)}, u32[]{:S(2)}) %collective-permute-start.18) | collective-permute-done | bytes 460832 | tf_op jit(solution)/shard_map/ppermute | solution.py:399
  85.8 1.4 %collective-permute-start.22 = (bf16[360,640]{1,0:T(8,128)(2,1)S(1)}, bf16[360,640]{1,0:T(8,128)(2,1)S(1)}, u32[]{:S(2)}, u32[]{:S(2)}) collective-permute-start(bf16[360,640]{1,0:T(8,128)(2,1)S(1)} %get-tuple-element.67), channel_id=1, source_target_pairs={{0,2},{2,0},{4,6},{6,4},{8,10},{10,8},{12,14},{14,12},{16,18},{18,... | collective-permute-start | bytes 1382408 | tf_op jit(solution)/shard_map/ppermute | solution.py:399
  87.1 8.5 %collective-permute-done.19.refs_3_ = bf16[360,640]{1,0:T(8,128)(2,1)S(1)} collective-permute-done((bf16[360,640]{1,0:T(8,128)(2,1)S(1)}, bf16[360,640]{1,0:T(8,128)(2,1)S(1)}, u32[]{:S(2)}, u32[]{:S(2)}) %collective-permute-start.19) | collective-permute-done | bytes 460832 | tf_op jit(solution)/shard_map/ppermute | solution.py:399
  95.6 1.3 %filter_late.1 = (bf16[360,640]{1,0:T(8,128)(2,1)S(1)}, bf16[360,640]{1,0:T(8,128)(2,1)S(1)}) custom-call(s32[16]{0:T(128)S(1)} %get-tuple-element.38.rows_ref, s32[35]{0:T(128)S(1)} %pad_add_fusion.place_ref, s32[32]{0:T(128)S(1)} %copy-done.1, f32[2,180,1280]{2,1,0:T(8,128)S(1)} %get-tuple-element.59.refs_0_, ...), custom_call_target="tpu_custom_call" | custom-call | flops 905969664 | bytes 3686400 | tf_op jit(solution)/shard_map/filter_late/pallas_call | solution.py:347
  97.0 0.5 collective-permute-start.23
  97.5 0.0 collective-permute-done.7.refs_1_
  97.5 0.0 collective-permute-done.20.refs_4_
  97.5 0.0 collective-permute-done.21.refs_5_
  97.5 0.0 collective-permute-done.22.refs_6_
  97.5 1.4 %collective-permute-done.23.refs_7_ = bf16[360,640]{1,0:T(8,128)(2,1)S(1)} collective-permute-done((bf16[360,640]{1,0:T(8,128)(2,1)S(1)}, bf16[360,640]{1,0:T(8,128)(2,1)S(1)}, u32[]{:S(2)}, u32[]{:S(2)}) %collective-permute-start.23) | collective-permute-done | bytes 460832 | tf_op jit(solution)/shard_map/ppermute | solution.py:399
  98.9 2.8 %put_rows.1 = bf16[180,16,640]{2,1,0:T(8,128)(2,1)} custom-call(s32[16]{0:T(128)S(1)} %get-tuple-element.37.slots_ref, bf16[360,640]{1,0:T(8,128)(2,1)S(1)} %get-tuple-element.45.refs_0_, bf16[360,640]{1,0:T(8,128)(2,1)S(1)} %collective-permute-done.7.refs_1_, bf16[360,640]{1,0:T(8,128)(2,1)S(1)} %get-tuple-element.54.refs_2_, ...), custom_call_target="tpu_custom_call" | custom-call | flops 943718400 | bytes 7372800 | tf_op jit(solution)/shard_map/put_rows/pallas_call | solution.py:249
Async XLA Ops:
  0.0 51.2 %copy-start = (bf16[32,2880]{1,0:T(8,128)(2,1)S(1)}, bf16[32,2880]{1,0:T(8,128)(2,1)}, u32[]{:S(2)}) copy-start(bf16[32,2880]{1,0:T(8,128)(2,1)} %taps_ref.1) | copy-start | bytes 552964
  0.0 51.9 %copy-start.1 = (s32[32]{0:T(128)S(1)}, s32[32]{0:T(128)}, u32[]{:S(2)}) copy-start(s32[32]{0:T(128)} %widths_ref.9) | copy-start | bytes 388
  5.1 7.9 %collective-permute-start = (bf16[360,640]{1,0:T(8,128)(2,1)S(1)}, bf16[360,640]{1,0:T(8,128)(2,1)S(1)}, u32[]{:S(2)}, u32[]{:S(2)}) collective-permute-start(bf16[360,640]{1,0:T(8,128)(2,1)S(1)} %get-tuple-element.40), channel_id=1, source_target_pairs={{0,2},{2,0},{4,6},{6,4},{8,10},{10,8},{12,14},{14,12},{16,18},{18,... | collective-permute-start | bytes 1382408 | tf_op jit(solution)/shard_map/ppermute | solution.py:399
  5.6 15.6 %collective-permute-start.3 = (bf16[360,640]{1,0:T(8,128)(2,1)S(1)}, bf16[360,640]{1,0:T(8,128)(2,1)S(1)}, u32[]{:S(2)}, u32[]{:S(2)}) collective-permute-start(bf16[360,640]{1,0:T(8,128)(2,1)S(1)} %get-tuple-element.39.refs_1_.refs_5_), channel_id=1, source_target_pairs={{0,24},{2,26},{4,12},{6,14},{8,0},{10,2},{12,20},{14,22},{16,8},{1... | collective-permute-start | bytes 1382408 | tf_op jit(solution)/shard_map/ppermute | solution.py:399
  10.3 13.4 %collective-permute-start.1 = (bf16[360,640]{1,0:T(8,128)(2,1)S(1)}, bf16[360,640]{1,0:T(8,128)(2,1)S(1)}, u32[]{:S(2)}, u32[]{:S(2)}) collective-permute-start(bf16[360,640]{1,0:T(8,128)(2,1)S(1)} %get-tuple-element.41), channel_id=1, source_target_pairs={{0,4},{2,6},{4,0},{6,2},{8,12},{10,14},{12,8},{14,10},{16,20},{18,... | collective-permute-start | bytes 1382408 | tf_op jit(solution)/shard_map/ppermute | solution.py:399
  10.3 13.4 %collective-permute-start.8 = (bf16[360,640]{1,0:T(8,128)(2,1)S(1)}, bf16[360,640]{1,0:T(8,128)(2,1)S(1)}, u32[]{:S(2)}, u32[]{:S(2)}) collective-permute-start(bf16[360,640]{1,0:T(8,128)(2,1)S(1)} %get-tuple-element.47), channel_id=1, source_target_pairs={{0,1},{1,0},{2,3},{3,2},{4,5},{5,4},{6,7},{7,6},{8,9},{9,8},{10,11... | collective-permute-start | bytes 1382408 | tf_op jit(solution)/shard_map/ppermute | solution.py:399
  11.8 20.2 %collective-permute-start.2 = (bf16[360,640]{1,0:T(8,128)(2,1)S(1)}, bf16[360,640]{1,0:T(8,128)(2,1)S(1)}, u32[]{:S(2)}, u32[]{:S(2)}) collective-permute-start(bf16[360,640]{1,0:T(8,128)(2,1)S(1)} %get-tuple-element.42), channel_id=1, source_target_pairs={{0,6},{2,4},{4,2},{6,0},{8,14},{10,12},{12,10},{14,8},{16,22},{18,... | collective-permute-start | bytes 1382408 | tf_op jit(solution)/shard_map/ppermute | solution.py:399
  13.1 20.5 %collective-permute-start.5 = (bf16[360,640]{1,0:T(8,128)(2,1)S(1)}, bf16[360,640]{1,0:T(8,128)(2,1)S(1)}, u32[]{:S(2)}, u32[]{:S(2)}) collective-permute-start(bf16[360,640]{1,0:T(8,128)(2,1)S(1)} %collective-permute-done.refs_2_.refs_6_), channel_id=1, source_target_pairs={{0,24},{2,26},{4,12},{6,14},{8,0},{10,2},{12,20},{14,22},{16,8},{1... | collective-permute-start | bytes 1382408 | tf_op jit(solution)/shard_map/ppermute | solution.py:399
  21.2 12.8 %collective-permute-start.9 = (bf16[360,640]{1,0:T(8,128)(2,1)S(1)}, bf16[360,640]{1,0:T(8,128)(2,1)S(1)}, u32[]{:S(2)}, u32[]{:S(2)}) collective-permute-start(bf16[360,640]{1,0:T(8,128)(2,1)S(1)} %get-tuple-element.49), channel_id=1, source_target_pairs={{0,3},{1,2},{2,1},{3,0},{4,7},{5,6},{6,5},{7,4},{8,11},{9,10},{10,... | collective-permute-start | bytes 1382408 | tf_op jit(solution)/shard_map/ppermute | solution.py:399
  23.7 25.7 %collective-permute-start.10 = (bf16[360,640]{1,0:T(8,128)(2,1)S(1)}, bf16[360,640]{1,0:T(8,128)(2,1)S(1)}, u32[]{:S(2)}, u32[]{:S(2)}) collective-permute-start(bf16[360,640]{1,0:T(8,128)(2,1)S(1)} %collective-permute-done.8.refs_1_), channel_id=1, source_target_pairs={{0,4},{2,6},{4,0},{6,2},{8,12},{10,14},{12,8},{14,10},{16,20},{18,... | collective-permute-start | bytes 1382408 | tf_op jit(solution)/shard_map/ppermute | solution.py:399
  24.7 26.6 %collective-permute-start.4 = (bf16[360,640]{1,0:T(8,128)(2,1)S(1)}, bf16[360,640]{1,0:T(8,128)(2,1)S(1)}, u32[]{:S(2)}, u32[]{:S(2)}) collective-permute-start(bf16[360,640]{1,0:T(8,128)(2,1)S(1)} %collective-permute-done.1.refs_3_.refs_1_), channel_id=1, source_target_pairs={{0,8},{2,10},{4,28},{6,30},{8,16},{10,18},{12,4},{14,6},{16,24},{1... | collective-permute-start | bytes 1382408 | tf_op jit(solution)/shard_map/ppermute | solution.py:399
  32.0 19.4 %collective-permute-start.14 = (bf16[360,640]{1,0:T(8,128)(2,1)S(1)}, bf16[360,640]{1,0:T(8,128)(2,1)S(1)}, u32[]{:S(2)}, u32[]{:S(2)}) collective-permute-start(bf16[360,640]{1,0:T(8,128)(2,1)S(1)} %get-tuple-element.56), channel_id=1, source_target_pairs={{0,1},{1,0},{2,3},{3,2},{4,5},{5,4},{6,7},{7,6},{8,9},{9,8},{10,11... | collective-permute-start | bytes 1382408 | tf_op jit(solution)/shard_map/ppermute | solution.py:399
  33.6 21.3 %collective-permute-start.6 = (bf16[360,640]{1,0:T(8,128)(2,1)S(1)}, bf16[360,640]{1,0:T(8,128)(2,1)S(1)}, u32[]{:S(2)}, u32[]{:S(2)}) collective-permute-start(bf16[360,640]{1,0:T(8,128)(2,1)S(1)} %collective-permute-done.2.refs_4_.refs_2_), channel_id=1, source_target_pairs={{0,8},{2,10},{4,28},{6,30},{8,16},{10,18},{12,4},{14,6},{16,24},{1... | collective-permute-start | bytes 1382408 | tf_op jit(solution)/shard_map/ppermute | solution.py:399
  34.0 23.3 %collective-permute-start.11 = (bf16[360,640]{1,0:T(8,128)(2,1)S(1)}, bf16[360,640]{1,0:T(8,128)(2,1)S(1)}, u32[]{:S(2)}, u32[]{:S(2)}) collective-permute-start(bf16[360,640]{1,0:T(8,128)(2,1)S(1)} %collective-permute-done.9.refs_2_), channel_id=1, source_target_pairs={{0,4},{2,6},{4,0},{6,2},{8,12},{10,14},{12,8},{14,10},{16,20},{18,... | collective-permute-start | bytes 1382408 | tf_op jit(solution)/shard_map/ppermute | solution.py:399
  49.4 12.8 %collective-permute-start.15 = (bf16[360,640]{1,0:T(8,128)(2,1)S(1)}, bf16[360,640]{1,0:T(8,128)(2,1)S(1)}, u32[]{:S(2)}, u32[]{:S(2)}) collective-permute-start(bf16[360,640]{1,0:T(8,128)(2,1)S(1)} %get-tuple-element.58), channel_id=1, source_target_pairs={{0,3},{1,2},{2,1},{3,0},{4,7},{5,6},{6,5},{7,4},{8,11},{9,10},{10,... | collective-permute-start | bytes 1382408 | tf_op jit(solution)/shard_map/ppermute | solution.py:399
  51.3 14.7 %collective-permute-start.12 = (bf16[360,640]{1,0:T(8,128)(2,1)S(1)}, bf16[360,640]{1,0:T(8,128)(2,1)S(1)}, u32[]{:S(2)}, u32[]{:S(2)}) collective-permute-start(bf16[360,640]{1,0:T(8,128)(2,1)S(1)} %collective-permute-done.10.refs_3_), channel_id=1, source_target_pairs={{0,8},{2,10},{4,28},{6,30},{8,16},{10,18},{12,4},{14,6},{16,24},{1... | collective-permute-start | bytes 1382408 | tf_op jit(solution)/shard_map/ppermute | solution.py:399
  51.4 15.7 %collective-permute-start.16 = (bf16[360,640]{1,0:T(8,128)(2,1)S(1)}, bf16[360,640]{1,0:T(8,128)(2,1)S(1)}, u32[]{:S(2)}, u32[]{:S(2)}) collective-permute-start(bf16[360,640]{1,0:T(8,128)(2,1)S(1)} %collective-permute-done.14.refs_1_), channel_id=1, source_target_pairs={{0,4},{2,6},{4,0},{6,2},{8,12},{10,14},{12,8},{14,10},{16,20},{18,... | collective-permute-start | bytes 1382408 | tf_op jit(solution)/shard_map/ppermute | solution.py:399
  57.3 18.6 %collective-permute-start.13 = (bf16[360,640]{1,0:T(8,128)(2,1)S(1)}, bf16[360,640]{1,0:T(8,128)(2,1)S(1)}, u32[]{:S(2)}, u32[]{:S(2)}) collective-permute-start(bf16[360,640]{1,0:T(8,128)(2,1)S(1)} %collective-permute-done.11.refs_4_), channel_id=1, source_target_pairs={{0,8},{2,10},{4,28},{6,30},{8,16},{10,18},{12,4},{14,6},{16,24},{1... | collective-permute-start | bytes 1382408 | tf_op jit(solution)/shard_map/ppermute | solution.py:399
  62.2 14.8 %collective-permute-start.17 = (bf16[360,640]{1,0:T(8,128)(2,1)S(1)}, bf16[360,640]{1,0:T(8,128)(2,1)S(1)}, u32[]{:S(2)}, u32[]{:S(2)}) collective-permute-start(bf16[360,640]{1,0:T(8,128)(2,1)S(1)} %collective-permute-done.15.refs_2_), channel_id=1, source_target_pairs={{0,4},{2,6},{4,0},{6,2},{8,12},{10,14},{12,8},{14,10},{16,20},{18,... | collective-permute-start | bytes 1382408 | tf_op jit(solution)/shard_map/ppermute | solution.py:399
  62.3 35.2 %collective-permute-start.7 = (bf16[360,640]{1,0:T(8,128)(2,1)S(1)}, bf16[360,640]{1,0:T(8,128)(2,1)S(1)}, u32[]{:S(2)}, u32[]{:S(2)}) collective-permute-start(bf16[360,640]{1,0:T(8,128)(2,1)S(1)} %get-tuple-element.46), channel_id=1, source_target_pairs={{0,4},{2,6},{4,0},{6,2},{8,12},{10,14},{12,8},{14,10},{16,20},{18,... | collective-permute-start | bytes 1382408 | tf_op jit(solution)/shard_map/ppermute | solution.py:399
  67.1 18.6 %collective-permute-start.18 = (bf16[360,640]{1,0:T(8,128)(2,1)S(1)}, bf16[360,640]{1,0:T(8,128)(2,1)S(1)}, u32[]{:S(2)}, u32[]{:S(2)}) collective-permute-start(bf16[360,640]{1,0:T(8,128)(2,1)S(1)} %collective-permute-done.16.refs_3_), channel_id=1, source_target_pairs={{0,8},{2,10},{4,28},{6,30},{8,16},{10,18},{12,4},{14,6},{16,24},{1... | collective-permute-start | bytes 1382408 | tf_op jit(solution)/shard_map/ppermute | solution.py:399
  70.1 27.4 %collective-permute-start.20 = (bf16[360,640]{1,0:T(8,128)(2,1)S(1)}, bf16[360,640]{1,0:T(8,128)(2,1)S(1)}, u32[]{:S(2)}, u32[]{:S(2)}) collective-permute-start(bf16[360,640]{1,0:T(8,128)(2,1)S(1)} %get-tuple-element.64), channel_id=1, source_target_pairs={{0,2},{2,0},{4,6},{6,4},{8,10},{10,8},{12,14},{14,12},{16,18},{18,... | collective-permute-start | bytes 1382408 | tf_op jit(solution)/shard_map/ppermute | solution.py:399
  77.0 18.6 %collective-permute-start.19 = (bf16[360,640]{1,0:T(8,128)(2,1)S(1)}, bf16[360,640]{1,0:T(8,128)(2,1)S(1)}, u32[]{:S(2)}, u32[]{:S(2)}) collective-permute-start(bf16[360,640]{1,0:T(8,128)(2,1)S(1)} %collective-permute-done.17.refs_4_), channel_id=1, source_target_pairs={{0,8},{2,10},{4,28},{6,30},{8,16},{10,18},{12,4},{14,6},{16,24},{1... | collective-permute-start | bytes 1382408 | tf_op jit(solution)/shard_map/ppermute | solution.py:399
  77.0 20.5 %collective-permute-start.21 = (bf16[360,640]{1,0:T(8,128)(2,1)S(1)}, bf16[360,640]{1,0:T(8,128)(2,1)S(1)}, u32[]{:S(2)}, u32[]{:S(2)}) collective-permute-start(bf16[360,640]{1,0:T(8,128)(2,1)S(1)} %get-tuple-element.66), channel_id=1, source_target_pairs={{0,6},{2,4},{4,2},{6,0},{8,14},{10,12},{12,10},{14,8},{16,22},{18,... | collective-permute-start | bytes 1382408 | tf_op jit(solution)/shard_map/ppermute | solution.py:399
  85.8 11.8 %collective-permute-start.22 = (bf16[360,640]{1,0:T(8,128)(2,1)S(1)}, bf16[360,640]{1,0:T(8,128)(2,1)S(1)}, u32[]{:S(2)}, u32[]{:S(2)}) collective-permute-start(bf16[360,640]{1,0:T(8,128)(2,1)S(1)} %get-tuple-element.67), channel_id=1, source_target_pairs={{0,2},{2,0},{4,6},{6,4},{8,10},{10,8},{12,14},{14,12},{16,18},{18,... | collective-permute-start | bytes 1382408 | tf_op jit(solution)/shard_map/ppermute | solution.py:399
  97.0 1.9 %collective-permute-start.23 = (bf16[360,640]{1,0:T(8,128)(2,1)S(1)}, bf16[360,640]{1,0:T(8,128)(2,1)S(1)}, u32[]{:S(2)}, u32[]{:S(2)}) collective-permute-start(bf16[360,640]{1,0:T(8,128)(2,1)S(1)} %get-tuple-element.68), channel_id=1, source_target_pairs={{0,2},{2,0},{4,6},{6,4},{8,10},{10,8},{12,14},{14,12},{16,18},{18,... | collective-permute-start | bytes 1382408 | tf_op jit(solution)/shard_map/ppermute | solution.py:399

commit v13 on v12

--- a/solution.py
+++ b/solution.py
@@ -30,7 +30,7 @@
     ("z", 3): [("z", 1)],
     ("y", 2): [("y", 0), ("p", 0)],
     ("y", 3): [("y", 1), ("x", 0)],
-    ("y", 1): [("q", 0)],
+    ("y", 1): [("q", 0), ("l", 0), ("l", 1)],
 }
 FLOPS = 3
 
@@ -106,26 +106,20 @@
         stays = place_ref[3 + here] // lat_dev == band
         comes = place_ref[3 + there] // lat_dev == band
 
-        @pl.when(stays)
-        def _():
-            spot = traded(listed(stay, quarter, core), quarter, x)
-            spot = spot + jnp.where(spot >= quarter, quarter, 0)
-            rows_ref[spot] = here
-            slots_ref[spot] = place_ref[3 + here] % lat_dev
-
-        @pl.when(comes)
-        def _():
-            spot = listed(come, quarter, core)
-            spot = spot + jnp.where(spot >= quarter, half, quarter)
-            rows_ref[spot] = there
-            slots_ref[spot] = place_ref[3 + there] % lat_dev
-
+        spot = traded(listed(stay, quarter, core), quarter, x)
+        spot = jnp.where(stays, spot + jnp.where(spot >= quarter, quarter, 0), lat_dev)
+        rows_ref[spot] = here
+        slots_ref[spot] = place_ref[3 + here] % lat_dev
+        spot = listed(come, quarter, core)
+        spot = jnp.where(comes, spot + jnp.where(spot >= quarter, half, quarter), lat_dev)
+        rows_ref[spot] = there
+        slots_ref[spot] = place_ref[3 + there] % lat_dev
         stay = stay + stays.astype(jnp.int32)
         come = come + comes.astype(jnp.int32)
 
 
 def list_rows(place, lat_dev):
-    ints = jax.ShapeDtypeStruct((lat_dev,), jnp.int32)
+    ints = jax.ShapeDtypeStruct((lat_dev + 1,), jnp.int32)
     return pl.pallas_call(
         functools.partial(list_kernel, lat_dev),
         out_shape=[ints, ints],
@@ -400,6 +394,8 @@
 
         if kind == "k":
             result = keep[i]
+        elif kind == "l":
+            result = (rows, lines)[i]
         elif kind == "c":
             result = moved(give[i], "lon", across_core)
         elif kind == "y":

time: 102 us -> 101 us (level)
  waiting for transfers between devices: 46 us -> 43.9 us
    ppermute x24, waiting for transfers between devices: 46 us -> 43.9 us  [moved(): return lax.ppermute(operand, axes, pairs)]
  transfers between devices with their start and end apart: 24 -> 24, of which waited for: 13 -> 12; matrix products, arithmetic and copies ran while one was open for 0% -> 0% of each run, Pallas kernels for 14% -> 14%
where the time goes in v13:
time: 101 us
  waiting for transfers between devices  43.9 us (43%)
  starting transfers between devices  34 us (34%)
  Pallas kernels  21.5 us (21%)
    ppermute x24, waiting for transfers between devices, moved(): return lax.ppermute(operand, axes, pairs)  43.9 us
    ppermute x24, starting transfers between devices, moved(): return lax.ppermute(operand, axes, pairs)  34 us
    pallas_call x5, Pallas kernels, filter_pair(): pl.pallas_call(functools.partial(pair_kernel, lon_dev, base, tuple(plan),...  12.6 us
    pallas_call x1, Pallas kernels, take_rows(): pl.pallas_call(functools.partial(take_kernel, chunks, lat_dev, block), ou...  4.35 us
    pallas_call x1, Pallas kernels, put_rows(): pl.pallas_call(functools.partial(put_kernel, counts, lat_dev, block), out...  2.8 us
  transfers between devices with their start and end apart: 24, of which 12 were waited for; matrix products, arithmetic and copies ran while one was open for 0% of the time, Pallas kernels for 14%

profile of v13, /device:TPU:0, one launch (start us, length us, event | category | flops | bytes accessed | tf_op | source)
XLA Modules:
  0.0 100.5 jit_solution(11957328327825491022)
XLA Ops:
  0.0 0.0 copy-start
  0.0 0.0 copy-start.1
  0.0 0.8 pad_add_fusion.place_ref
  0.8 4.3 %take_rows.1 = (bf16[360,640]{1,0:T(8,128)(2,1)S(1)}, bf16[360,640]{1,0:T(8,128)(2,1)S(1)}, bf16[360,640]{1,0:T(8,128)(2,1)S(1)}, bf16[360,640]{1,0:T(8,128)(2,1...) custom-call(s32[35]{0:T(128)S(1)} %pad_add_fusion.place_ref, ...), custom_call_target="tpu_custom_call" | custom-call | flops 943718400 | bytes 7372800 | tf_op jit(solution)/shard_map/take_rows/pallas_call | solution.py:188
  5.1 0.5 collective-permute-start
  5.6 4.7 %collective-permute-start.3 = (bf16[360,640]{1,0:T(8,128)(2,1)S(1)}, bf16[360,640]{1,0:T(8,128)(2,1)S(1)}, u32[]{:S(2)}, u32[]{:S(2)}) collective-permute-start(bf16[360,640]{1,0:T(8,128)(2,1)S(1)} %get-tuple-element.39.refs_1_.refs_5_), channel_id=1, source_target_pairs={{0,24},{2,26},{4,12},{6,14},{8,0},{10,2},{12,20},{14,22},{16,8},{1... | collective-permute-start | bytes 1382408 | tf_op jit(solution)/shard_map/ppermute | solution.py:393
  10.3 0.0 collective-permute-start.1
  10.3 1.5 %collective-permute-start.8 = (bf16[360,640]{1,0:T(8,128)(2,1)S(1)}, bf16[360,640]{1,0:T(8,128)(2,1)S(1)}, u32[]{:S(2)}, u32[]{:S(2)}) collective-permute-start(bf16[360,640]{1,0:T(8,128)(2,1)S(1)} %get-tuple-element.47), channel_id=1, source_target_pairs={{0,1},{1,0},{2,3},{3,2},{4,5},{5,4},{6,7},{7,6},{8,9},{9,8},{10,11... | collective-permute-start | bytes 1382408 | tf_op jit(solution)/shard_map/ppermute | solution.py:393
  11.8 1.2 %collective-permute-start.2 = (bf16[360,640]{1,0:T(8,128)(2,1)S(1)}, bf16[360,640]{1,0:T(8,128)(2,1)S(1)}, u32[]{:S(2)}, u32[]{:S(2)}) collective-permute-start(bf16[360,640]{1,0:T(8,128)(2,1)S(1)} %get-tuple-element.42), channel_id=1, source_target_pairs={{0,6},{2,4},{4,2},{6,0},{8,14},{10,12},{12,10},{14,8},{16,22},{18,... | collective-permute-start | bytes 1382408 | tf_op jit(solution)/shard_map/ppermute | solution.py:393
  13.1 1.7 %list_rows.1 = (s32[17]{0:T(128)S(1)}, s32[17]{0:T(128)S(1)}) custom-call(s32[35]{0:T(128)S(1)} %pad_add_fusion.place_ref), custom_call_target="tpu_custom_call" | custom-call | bytes 256 | tf_op jit(solution)/shard_map/list_rows/pallas_call | solution.py:123
  14.8 0.0 copy-done
  14.8 0.1 tap_lines.1.refs_0_
  14.9 0.0 collective-permute-done.refs_2_.refs_6_
  14.9 0.5 collective-permute-start.5
  15.5 5.7 %collective-permute-done.3.refs_3_ = bf16[360,640]{1,0:T(8,128)(2,1)S(1)} collective-permute-done((bf16[360,640]{1,0:T(8,128)(2,1)S(1)}, bf16[360,640]{1,0:T(8,128)(2,1)S(1)}, u32[]{:S(2)}, u32[]{:S(2)}) %collective-permute-start.3) | collective-permute-done | bytes 460832 | tf_op jit(solution)/shard_map/ppermute | solution.py:393
  21.2 0.3 collective-permute-start.9
  21.5 2.2 %collective-permute-done.1.refs_3_.refs_1_ = bf16[360,640]{1,0:T(8,128)(2,1)S(1)} collective-permute-done((bf16[360,640]{1,0:T(8,128)(2,1)S(1)}, bf16[360,640]{1,0:T(8,128)(2,1)S(1)}, u32[]{:S(2)}, u32[]{:S(2)}) %collective-permute-start.1) | collective-permute-done | bytes 460832 | tf_op jit(solution)/shard_map/ppermute | solution.py:393
  23.7 0.0 collective-permute-done.8.refs_1_
  23.7 1.0 collective-permute-start.10
  24.7 0.1 collective-permute-start.4
  24.8 7.3 %collective-permute-done.2.refs_4_.refs_2_ = bf16[360,640]{1,0:T(8,128)(2,1)S(1)} collective-permute-done((bf16[360,640]{1,0:T(8,128)(2,1)S(1)}, bf16[360,640]{1,0:T(8,128)(2,1)S(1)}, u32[]{:S(2)}, u32[]{:S(2)}) %collective-permute-start.2) | collective-permute-done | bytes 460832 | tf_op jit(solution)/shard_map/ppermute | solution.py:393
  32.0 1.5 %collective-permute-start.14 = (bf16[360,640]{1,0:T(8,128)(2,1)S(1)}, bf16[360,640]{1,0:T(8,128)(2,1)S(1)}, u32[]{:S(2)}, u32[]{:S(2)}) collective-permute-start(bf16[360,640]{1,0:T(8,128)(2,1)S(1)} %get-tuple-element.56), channel_id=1, source_target_pairs={{0,1},{1,0},{2,3},{3,2},{4,5},{5,4},{6,7},{7,6},{8,9},{9,8},{10,11... | collective-permute-start | bytes 1382408 | tf_op jit(solution)/shard_map/ppermute | solution.py:393
  33.6 0.0 collective-permute-done.5.refs_4_
  33.6 0.1 collective-permute-start.6
  33.7 0.3 collective-permute-done.9.refs_2_
  34.0 15.4 %collective-permute-start.11 = (bf16[360,640]{1,0:T(8,128)(2,1)S(1)}, bf16[360,640]{1,0:T(8,128)(2,1)S(1)}, u32[]{:S(2)}, u32[]{:S(2)}) collective-permute-start(bf16[360,640]{1,0:T(8,128)(2,1)S(1)} %collective-permute-done.9.refs_2_), channel_id=1, source_target_pairs={{0,4},{2,6},{4,0},{6,2},{8,12},{10,14},{12,8},{14,10},{16,20},{18,... | collective-permute-start | bytes 1382408 | tf_op jit(solution)/shard_map/ppermute | solution.py:393
  49.4 0.0 collective-permute-done.10.refs_3_
  49.4 0.0 collective-permute-start.15
  49.4 0.0 collective-permute-done.4.refs_5_
  49.4 0.1 collective-permute-start.12
  49.5 0.0 collective-permute-done.14.refs_1_
  49.5 0.5 collective-permute-start.16
  50.0 0.0 copy-done.1
  50.0 2.9 %filter_whole.4 = (bf16[360,640]{1,0:T(8,128)(2,1)S(1)}, bf16[360,640]{1,0:T(8,128)(2,1)S(1)}) custom-call(s32[17]{0:T(128)S(1)} %get-tuple-element.38.rows_ref, s32[35]{0:T(128)S(1)} %pad_add_fusion.place_ref, s32[32]{0:T(128)S(1)} %copy-done.1, f32[32,1152]{1,0:T(8,128)S(1)} %tap_lines.1.refs_0_, ...), custom_call_target="tpu_custom_call" | custom-call | flops 3019898880 | bytes 3686400 | tf_op jit(solution)/shard_map/filter_whole/pallas_call | solution.py:341
  52.9 0.0 collective-permute-done.6.refs_6_
  52.9 6.4 %collective-permute-done.11.refs_4_ = bf16[360,640]{1,0:T(8,128)(2,1)S(1)} collective-permute-done((bf16[360,640]{1,0:T(8,128)(2,1)S(1)}, bf16[360,640]{1,0:T(8,128)(2,1)S(1)}, u32[]{:S(2)}, u32[]{:S(2)}) %collective-permute-start.11) | collective-permute-done | bytes 460832 | tf_op jit(solution)/shard_map/ppermute | solution.py:393
  59.3 0.0 collective-permute-start.13
  59.3 2.9 %collective-permute-done.15.refs_2_ = bf16[360,640]{1,0:T(8,128)(2,1)S(1)} collective-permute-done((bf16[360,640]{1,0:T(8,128)(2,1)S(1)}, bf16[360,640]{1,0:T(8,128)(2,1)S(1)}, u32[]{:S(2)}, u32[]{:S(2)}) %collective-permute-start.15) | collective-permute-done | bytes 460832 | tf_op jit(solution)/shard_map/ppermute | solution.py:393
  62.2 1.2 %collective-permute-start.17 = (bf16[360,640]{1,0:T(8,128)(2,1)S(1)}, bf16[360,640]{1,0:T(8,128)(2,1)S(1)}, u32[]{:S(2)}, u32[]{:S(2)}) collective-permute-start(bf16[360,640]{1,0:T(8,128)(2,1)S(1)} %collective-permute-done.15.refs_2_), channel_id=1, source_target_pairs={{0,4},{2,6},{4,0},{6,2},{8,12},{10,14},{12,8},{14,10},{16,20},{18,... | collective-permute-start | bytes 1382408 | tf_op jit(solution)/shard_map/ppermute | solution.py:393
  63.4 0.8 collective-permute-start.7
  64.2 0.0 collective-permute-done.12.refs_5_
  64.2 3.5 %collective-permute-done.16.refs_3_ = bf16[360,640]{1,0:T(8,128)(2,1)S(1)} collective-permute-done((bf16[360,640]{1,0:T(8,128)(2,1)S(1)}, bf16[360,640]{1,0:T(8,128)(2,1)S(1)}, u32[]{:S(2)}, u32[]{:S(2)}) %collective-permute-start.16) | collective-permute-done | bytes 460832 | tf_op jit(solution)/shard_map/ppermute | solution.py:393
  67.7 0.0 collective-permute-start.18
  67.7 2.9 %filter_whole.3 = (bf16[360,640]{1,0:T(8,128)(2,1)S(1)}, bf16[360,640]{1,0:T(8,128)(2,1)S(1)}) custom-call(s32[17]{0:T(128)S(1)} %get-tuple-element.38.rows_ref, s32[35]{0:T(128)S(1)} %pad_add_fusion.place_ref, s32[32]{0:T(128)S(1)} %copy-done.1, f32[32,1152]{1,0:T(8,128)S(1)} %tap_lines.1.refs_0_, bf16[360,640]{1,0:T(8,128)(2,1)S(1)} %get-tuple-element.39.refs_1_.refs_5_, ...), custom_call_target="tpu_custom_call" | custom-call | flops 3019898880 | bytes 3686400 | tf_op jit(solution)/shard_map/filter_whole/pallas_call | solution.py:341
  70.7 0.1 collective-permute-start.20
  70.7 3.9 %collective-permute-done.13.refs_6_ = bf16[360,640]{1,0:T(8,128)(2,1)S(1)} collective-permute-done((bf16[360,640]{1,0:T(8,128)(2,1)S(1)}, bf16[360,640]{1,0:T(8,128)(2,1)S(1)}, u32[]{:S(2)}, u32[]{:S(2)}) %collective-permute-start.13) | collective-permute-done | bytes 460832 | tf_op jit(solution)/shard_map/ppermute | solution.py:393
  74.6 3.0 %collective-permute-done.17.refs_4_ = bf16[360,640]{1,0:T(8,128)(2,1)S(1)} collective-permute-done((bf16[360,640]{1,0:T(8,128)(2,1)S(1)}, bf16[360,640]{1,0:T(8,128)(2,1)S(1)}, u32[]{:S(2)}, u32[]{:S(2)}) %collective-permute-start.17) | collective-permute-done | bytes 460832 | tf_op jit(solution)/shard_map/ppermute | solution.py:393
  77.6 0.0 collective-permute-start.19
  77.6 0.0 collective-permute-start.21
  77.6 2.5 %filter_early.1 = (f32[2,180,1280]{2,1,0:T(8,128)S(1)}, bf16[2,5,192,180]{3,2,1,0:T(8,128)(2,1)S(1)}) custom-call(s32[17]{0:T(128)S(1)} %get-tuple-element.38.rows_ref, s32[35]{0:T(128)S(1)} %pad_add_fusion.place_ref, s32[32]{0:T(128)S(1)} %copy-done.1, f32[32,1152]{1,0:T(8,128)S(1)} %tap_lines.1.refs_0_, ...), custom_call_target="tpu_custom_call" | custom-call | flops 2113929216 | bytes 3686400 | tf_op jit(solution)/shard_map/filter_early/pallas_call | solution.py:341
  80.1 2.9 %filter_whole.5 = (bf16[360,640]{1,0:T(8,128)(2,1)S(1)}, bf16[360,640]{1,0:T(8,128)(2,1)S(1)}) custom-call(s32[17]{0:T(128)S(1)} %get-tuple-element.38.rows_ref, s32[35]{0:T(128)S(1)} %pad_add_fusion.place_ref, s32[32]{0:T(128)S(1)} %copy-done.1, f32[32,1152]{1,0:T(8,128)S(1)} %tap_lines.1.refs_0_, bf16[360,640]{1,0:T(8,128)(2,1)S(1)} %collective-permute-done.8.refs_1_, ...), custom_call_target="tpu_custom_call" | custom-call | flops 3019898880 | bytes 3686400 | tf_op jit(solution)/shard_map/filter_whole/pallas_call | solution.py:341
  83.0 1.4 %collective-permute-done.18.refs_2_ = bf16[360,640]{1,0:T(8,128)(2,1)S(1)} collective-permute-done((bf16[360,640]{1,0:T(8,128)(2,1)S(1)}, bf16[360,640]{1,0:T(8,128)(2,1)S(1)}, u32[]{:S(2)}, u32[]{:S(2)}) %collective-permute-start.18) | collective-permute-done | bytes 460832 | tf_op jit(solution)/shard_map/ppermute | solution.py:393
  84.5 4.3 %collective-permute-start.22 = (bf16[360,640]{1,0:T(8,128)(2,1)S(1)}, bf16[360,640]{1,0:T(8,128)(2,1)S(1)}, u32[]{:S(2)}, u32[]{:S(2)}) collective-permute-start(bf16[360,640]{1,0:T(8,128)(2,1)S(1)} %get-tuple-element.67), channel_id=1, source_target_pairs={{0,2},{2,0},{4,6},{6,4},{8,10},{10,8},{12,14},{14,12},{16,18},{18,... | collective-permute-start | bytes 1382408 | tf_op jit(solution)/shard_map/ppermute | solution.py:393
  88.8 5.5 %collective-permute-done.19.refs_3_ = bf16[360,640]{1,0:T(8,128)(2,1)S(1)} collective-permute-done((bf16[360,640]{1,0:T(8,128)(2,1)S(1)}, bf16[360,640]{1,0:T(8,128)(2,1)S(1)}, u32[]{:S(2)}, u32[]{:S(2)}) %collective-permute-start.19) | collective-permute-done | bytes 460832 | tf_op jit(solution)/shard_map/ppermute | solution.py:393
  94.3 1.3 %filter_late.1 = (bf16[360,640]{1,0:T(8,128)(2,1)S(1)}, bf16[360,640]{1,0:T(8,128)(2,1)S(1)}) custom-call(s32[17]{0:T(128)S(1)} %get-tuple-element.38.rows_ref, s32[35]{0:T(128)S(1)} %pad_add_fusion.place_ref, s32[32]{0:T(128)S(1)} %copy-done.1, f32[2,180,1280]{2,1,0:T(8,128)S(1)} %get-tuple-element.59.refs_0_, ...), custom_call_target="tpu_custom_call" | custom-call | flops 905969664 | bytes 3686400 | tf_op jit(solution)/shard_map/filter_late/pallas_call | solution.py:341
  95.7 0.1 collective-permute-start.23
  95.8 0.0 collective-permute-done.7.refs_1_
  95.8 0.0 collective-permute-done.20.refs_4_
  95.8 0.0 collective-permute-done.21.refs_5_
  95.8 0.0 collective-permute-done.22.refs_6_
  95.8 1.7 %collective-permute-done.23.refs_7_ = bf16[360,640]{1,0:T(8,128)(2,1)S(1)} collective-permute-done((bf16[360,640]{1,0:T(8,128)(2,1)S(1)}, bf16[360,640]{1,0:T(8,128)(2,1)S(1)}, u32[]{:S(2)}, u32[]{:S(2)}) %collective-permute-start.23) | collective-permute-done | bytes 460832 | tf_op jit(solution)/shard_map/ppermute | solution.py:393
  97.6 2.8 %put_rows.1 = bf16[180,16,640]{2,1,0:T(8,128)(2,1)} custom-call(s32[17]{0:T(128)S(1)} %get-tuple-element.37.slots_ref, bf16[360,640]{1,0:T(8,128)(2,1)S(1)} %get-tuple-element.45.refs_0_, bf16[360,640]{1,0:T(8,128)(2,1)S(1)} %collective-permute-done.7.refs_1_, bf16[360,640]{1,0:T(8,128)(2,1)S(1)} %get-tuple-element.54.refs_2_, ...), custom_call_target="tpu_custom_call" | custom-call | flops 943718400 | bytes 7372800 | tf_op jit(solution)/shard_map/put_rows/pallas_call | solution.py:243
Async XLA Ops:
  0.0 14.8 %copy-start = (bf16[32,2880]{1,0:T(8,128)(2,1)S(1)}, bf16[32,2880]{1,0:T(8,128)(2,1)}, u32[]{:S(2)}) copy-start(bf16[32,2880]{1,0:T(8,128)(2,1)} %taps_ref.1) | copy-start | bytes 552964
  0.0 50.0 %copy-start.1 = (s32[32]{0:T(128)S(1)}, s32[32]{0:T(128)}, u32[]{:S(2)}) copy-start(s32[32]{0:T(128)} %widths_ref.9) | copy-start | bytes 388
  5.1 9.8 %collective-permute-start = (bf16[360,640]{1,0:T(8,128)(2,1)S(1)}, bf16[360,640]{1,0:T(8,128)(2,1)S(1)}, u32[]{:S(2)}, u32[]{:S(2)}) collective-permute-start(bf16[360,640]{1,0:T(8,128)(2,1)S(1)} %get-tuple-element.40), channel_id=1, source_target_pairs={{0,2},{2,0},{4,6},{6,4},{8,10},{10,8},{12,14},{14,12},{16,18},{18,... | collective-permute-start | bytes 1382408 | tf_op jit(solution)/shard_map/ppermute | solution.py:393
  5.6 15.6 %collective-permute-start.3 = (bf16[360,640]{1,0:T(8,128)(2,1)S(1)}, bf16[360,640]{1,0:T(8,128)(2,1)S(1)}, u32[]{:S(2)}, u32[]{:S(2)}) collective-permute-start(bf16[360,640]{1,0:T(8,128)(2,1)S(1)} %get-tuple-element.39.refs_1_.refs_5_), channel_id=1, source_target_pairs={{0,24},{2,26},{4,12},{6,14},{8,0},{10,2},{12,20},{14,22},{16,8},{1... | collective-permute-start | bytes 1382408 | tf_op jit(solution)/shard_map/ppermute | solution.py:393
  10.3 13.4 %collective-permute-start.1 = (bf16[360,640]{1,0:T(8,128)(2,1)S(1)}, bf16[360,640]{1,0:T(8,128)(2,1)S(1)}, u32[]{:S(2)}, u32[]{:S(2)}) collective-permute-start(bf16[360,640]{1,0:T(8,128)(2,1)S(1)} %get-tuple-element.41), channel_id=1, source_target_pairs={{0,4},{2,6},{4,0},{6,2},{8,12},{10,14},{12,8},{14,10},{16,20},{18,... | collective-permute-start | bytes 1382408 | tf_op jit(solution)/shard_map/ppermute | solution.py:393
  10.3 13.4 %collective-permute-start.8 = (bf16[360,640]{1,0:T(8,128)(2,1)S(1)}, bf16[360,640]{1,0:T(8,128)(2,1)S(1)}, u32[]{:S(2)}, u32[]{:S(2)}) collective-permute-start(bf16[360,640]{1,0:T(8,128)(2,1)S(1)} %get-tuple-element.47), channel_id=1, source_target_pairs={{0,1},{1,0},{2,3},{3,2},{4,5},{5,4},{6,7},{7,6},{8,9},{9,8},{10,11... | collective-permute-start | bytes 1382408 | tf_op jit(solution)/shard_map/ppermute | solution.py:393
  11.8 20.2 %collective-permute-start.2 = (bf16[360,640]{1,0:T(8,128)(2,1)S(1)}, bf16[360,640]{1,0:T(8,128)(2,1)S(1)}, u32[]{:S(2)}, u32[]{:S(2)}) collective-permute-start(bf16[360,640]{1,0:T(8,128)(2,1)S(1)} %get-tuple-element.42), channel_id=1, source_target_pairs={{0,6},{2,4},{4,2},{6,0},{8,14},{10,12},{12,10},{14,8},{16,22},{18,... | collective-permute-start | bytes 1382408 | tf_op jit(solution)/shard_map/ppermute | solution.py:393
  14.9 18.6 %collective-permute-start.5 = (bf16[360,640]{1,0:T(8,128)(2,1)S(1)}, bf16[360,640]{1,0:T(8,128)(2,1)S(1)}, u32[]{:S(2)}, u32[]{:S(2)}) collective-permute-start(bf16[360,640]{1,0:T(8,128)(2,1)S(1)} %collective-permute-done.refs_2_.refs_6_), channel_id=1, source_target_pairs={{0,24},{2,26},{4,12},{6,14},{8,0},{10,2},{12,20},{14,22},{16,8},{1... | collective-permute-start | bytes 1382408 | tf_op jit(solution)/shard_map/ppermute | solution.py:393
  21.2 12.8 %collective-permute-start.9 = (bf16[360,640]{1,0:T(8,128)(2,1)S(1)}, bf16[360,640]{1,0:T(8,128)(2,1)S(1)}, u32[]{:S(2)}, u32[]{:S(2)}) collective-permute-start(bf16[360,640]{1,0:T(8,128)(2,1)S(1)} %get-tuple-element.49), channel_id=1, source_target_pairs={{0,3},{1,2},{2,1},{3,0},{4,7},{5,6},{6,5},{7,4},{8,11},{9,10},{10,... | collective-permute-start | bytes 1382408 | tf_op jit(solution)/shard_map/ppermute | solution.py:393
  23.7 25.7 %collective-permute-start.10 = (bf16[360,640]{1,0:T(8,128)(2,1)S(1)}, bf16[360,640]{1,0:T(8,128)(2,1)S(1)}, u32[]{:S(2)}, u32[]{:S(2)}) collective-permute-start(bf16[360,640]{1,0:T(8,128)(2,1)S(1)} %collective-permute-done.8.refs_1_), channel_id=1, source_target_pairs={{0,4},{2,6},{4,0},{6,2},{8,12},{10,14},{12,8},{14,10},{16,20},{18,... | collective-permute-start | bytes 1382408 | tf_op jit(solution)/shard_map/ppermute | solution.py:393
  24.7 24.7 %collective-permute-start.4 = (bf16[360,640]{1,0:T(8,128)(2,1)S(1)}, bf16[360,640]{1,0:T(8,128)(2,1)S(1)}, u32[]{:S(2)}, u32[]{:S(2)}) collective-permute-start(bf16[360,640]{1,0:T(8,128)(2,1)S(1)} %collective-permute-done.1.refs_3_.refs_1_), channel_id=1, source_target_pairs={{0,8},{2,10},{4,28},{6,30},{8,16},{10,18},{12,4},{14,6},{16,24},{1... | collective-permute-start | bytes 1382408 | tf_op jit(solution)/shard_map/ppermute | solution.py:393
  32.0 17.4 %collective-permute-start.14 = (bf16[360,640]{1,0:T(8,128)(2,1)S(1)}, bf16[360,640]{1,0:T(8,128)(2,1)S(1)}, u32[]{:S(2)}, u32[]{:S(2)}) collective-permute-start(bf16[360,640]{1,0:T(8,128)(2,1)S(1)} %get-tuple-element.56), channel_id=1, source_target_pairs={{0,1},{1,0},{2,3},{3,2},{4,5},{5,4},{6,7},{7,6},{8,9},{9,8},{10,11... | collective-permute-start | bytes 1382408 | tf_op jit(solution)/shard_map/ppermute | solution.py:393
  33.6 19.3 %collective-permute-start.6 = (bf16[360,640]{1,0:T(8,128)(2,1)S(1)}, bf16[360,640]{1,0:T(8,128)(2,1)S(1)}, u32[]{:S(2)}, u32[]{:S(2)}) collective-permute-start(bf16[360,640]{1,0:T(8,128)(2,1)S(1)} %collective-permute-done.2.refs_4_.refs_2_), channel_id=1, source_target_pairs={{0,8},{2,10},{4,28},{6,30},{8,16},{10,18},{12,4},{14,6},{16,24},{1... | collective-permute-start | bytes 1382408 | tf_op jit(solution)/shard_map/ppermute | solution.py:393
  34.0 25.3 %collective-permute-start.11 = (bf16[360,640]{1,0:T(8,128)(2,1)S(1)}, bf16[360,640]{1,0:T(8,128)(2,1)S(1)}, u32[]{:S(2)}, u32[]{:S(2)}) collective-permute-start(bf16[360,640]{1,0:T(8,128)(2,1)S(1)} %collective-permute-done.9.refs_2_), channel_id=1, source_target_pairs={{0,4},{2,6},{4,0},{6,2},{8,12},{10,14},{12,8},{14,10},{16,20},{18,... | collective-permute-start | bytes 1382408 | tf_op jit(solution)/shard_map/ppermute | solution.py:393
  49.4 12.8 %collective-permute-start.15 = (bf16[360,640]{1,0:T(8,128)(2,1)S(1)}, bf16[360,640]{1,0:T(8,128)(2,1)S(1)}, u32[]{:S(2)}, u32[]{:S(2)}) collective-permute-start(bf16[360,640]{1,0:T(8,128)(2,1)S(1)} %get-tuple-element.58), channel_id=1, source_target_pairs={{0,3},{1,2},{2,1},{3,0},{4,7},{5,6},{6,5},{7,4},{8,11},{9,10},{10,... | collective-permute-start | bytes 1382408 | tf_op jit(solution)/shard_map/ppermute | solution.py:393
  49.4 14.8 %collective-permute-start.12 = (bf16[360,640]{1,0:T(8,128)(2,1)S(1)}, bf16[360,640]{1,0:T(8,128)(2,1)S(1)}, u32[]{:S(2)}, u32[]{:S(2)}) collective-permute-start(bf16[360,640]{1,0:T(8,128)(2,1)S(1)} %collective-permute-done.10.refs_3_), channel_id=1, source_target_pairs={{0,8},{2,10},{4,28},{6,30},{8,16},{10,18},{12,4},{14,6},{16,24},{1... | collective-permute-start | bytes 1382408 | tf_op jit(solution)/shard_map/ppermute | solution.py:393
  49.5 18.3 %collective-permute-start.16 = (bf16[360,640]{1,0:T(8,128)(2,1)S(1)}, bf16[360,640]{1,0:T(8,128)(2,1)S(1)}, u32[]{:S(2)}, u32[]{:S(2)}) collective-permute-start(bf16[360,640]{1,0:T(8,128)(2,1)S(1)} %collective-permute-done.14.refs_1_), channel_id=1, source_target_pairs={{0,4},{2,6},{4,0},{6,2},{8,12},{10,14},{12,8},{14,10},{16,20},{18,... | collective-permute-start | bytes 1382408 | tf_op jit(solution)/shard_map/ppermute | solution.py:393
  59.3 15.3 %collective-permute-start.13 = (bf16[360,640]{1,0:T(8,128)(2,1)S(1)}, bf16[360,640]{1,0:T(8,128)(2,1)S(1)}, u32[]{:S(2)}, u32[]{:S(2)}) collective-permute-start(bf16[360,640]{1,0:T(8,128)(2,1)S(1)} %collective-permute-done.11.refs_4_), channel_id=1, source_target_pairs={{0,8},{2,10},{4,28},{6,30},{8,16},{10,18},{12,4},{14,6},{16,24},{1... | collective-permute-start | bytes 1382408 | tf_op jit(solution)/shard_map/ppermute | solution.py:393
  62.2 15.4 %collective-permute-start.17 = (bf16[360,640]{1,0:T(8,128)(2,1)S(1)}, bf16[360,640]{1,0:T(8,128)(2,1)S(1)}, u32[]{:S(2)}, u32[]{:S(2)}) collective-permute-start(bf16[360,640]{1,0:T(8,128)(2,1)S(1)} %collective-permute-done.15.refs_2_), channel_id=1, source_target_pairs={{0,4},{2,6},{4,0},{6,2},{8,12},{10,14},{12,8},{14,10},{16,20},{18,... | collective-permute-start | bytes 1382408 | tf_op jit(solution)/shard_map/ppermute | solution.py:393
  63.4 32.4 %collective-permute-start.7 = (bf16[360,640]{1,0:T(8,128)(2,1)S(1)}, bf16[360,640]{1,0:T(8,128)(2,1)S(1)}, u32[]{:S(2)}, u32[]{:S(2)}) collective-permute-start(bf16[360,640]{1,0:T(8,128)(2,1)S(1)} %get-tuple-element.46), channel_id=1, source_target_pairs={{0,4},{2,6},{4,0},{6,2},{8,12},{10,14},{12,8},{14,10},{16,20},{18,... | collective-permute-start | bytes 1382408 | tf_op jit(solution)/shard_map/ppermute | solution.py:393
  67.7 16.7 %collective-permute-start.18 = (bf16[360,640]{1,0:T(8,128)(2,1)S(1)}, bf16[360,640]{1,0:T(8,128)(2,1)S(1)}, u32[]{:S(2)}, u32[]{:S(2)}) collective-permute-start(bf16[360,640]{1,0:T(8,128)(2,1)S(1)} %collective-permute-done.16.refs_3_), channel_id=1, source_target_pairs={{0,8},{2,10},{4,28},{6,30},{8,16},{10,18},{12,4},{14,6},{16,24},{1... | collective-permute-start | bytes 1382408 | tf_op jit(solution)/shard_map/ppermute | solution.py:393
  70.7 25.2 %collective-permute-start.20 = (bf16[360,640]{1,0:T(8,128)(2,1)S(1)}, bf16[360,640]{1,0:T(8,128)(2,1)S(1)}, u32[]{:S(2)}, u32[]{:S(2)}) collective-permute-start(bf16[360,640]{1,0:T(8,128)(2,1)S(1)} %get-tuple-element.64), channel_id=1, source_target_pairs={{0,2},{2,0},{4,6},{6,4},{8,10},{10,8},{12,14},{14,12},{16,18},{18,... | collective-permute-start | bytes 1382408 | tf_op jit(solution)/shard_map/ppermute | solution.py:393
  77.6 16.7 %collective-permute-start.19 = (bf16[360,640]{1,0:T(8,128)(2,1)S(1)}, bf16[360,640]{1,0:T(8,128)(2,1)S(1)}, u32[]{:S(2)}, u32[]{:S(2)}) collective-permute-start(bf16[360,640]{1,0:T(8,128)(2,1)S(1)} %collective-permute-done.17.refs_4_), channel_id=1, source_target_pairs={{0,8},{2,10},{4,28},{6,30},{8,16},{10,18},{12,4},{14,6},{16,24},{1... | collective-permute-start | bytes 1382408 | tf_op jit(solution)/shard_map/ppermute | solution.py:393
  77.6 18.2 %collective-permute-start.21 = (bf16[360,640]{1,0:T(8,128)(2,1)S(1)}, bf16[360,640]{1,0:T(8,128)(2,1)S(1)}, u32[]{:S(2)}, u32[]{:S(2)}) collective-permute-start(bf16[360,640]{1,0:T(8,128)(2,1)S(1)} %get-tuple-element.66), channel_id=1, source_target_pairs={{0,6},{2,4},{4,2},{6,0},{8,14},{10,12},{12,10},{14,8},{16,22},{18,... | collective-permute-start | bytes 1382408 | tf_op jit(solution)/shard_map/ppermute | solution.py:393
  84.5 11.4 %collective-permute-start.22 = (bf16[360,640]{1,0:T(8,128)(2,1)S(1)}, bf16[360,640]{1,0:T(8,128)(2,1)S(1)}, u32[]{:S(2)}, u32[]{:S(2)}) collective-permute-start(bf16[360,640]{1,0:T(8,128)(2,1)S(1)} %get-tuple-element.67), channel_id=1, source_target_pairs={{0,2},{2,0},{4,6},{6,4},{8,10},{10,8},{12,14},{14,12},{16,18},{18,... | collective-permute-start | bytes 1382408 | tf_op jit(solution)/shard_map/ppermute | solution.py:393
  95.7 1.9 %collective-permute-start.23 = (bf16[360,640]{1,0:T(8,128)(2,1)S(1)}, bf16[360,640]{1,0:T(8,128)(2,1)S(1)}, u32[]{:S(2)}, u32[]{:S(2)}) collective-permute-start(bf16[360,640]{1,0:T(8,128)(2,1)S(1)} %get-tuple-element.68), channel_id=1, source_target_pairs={{0,2},{2,0},{4,6},{6,4},{8,10},{10,8},{12,14},{14,12},{16,18},{18,... | collective-permute-start | bytes 1382408 | tf_op jit(solution)/shard_map/ppermute | solution.py:393

commit v14 on v13

--- a/solution.py
+++ b/solution.py
@@ -9,8 +9,8 @@
 
 VMEM_LIMIT = 12 * 1024 * 1024
 TAKE_VMEM_LIMIT = 50 * 1024 * 1024
-PIECE = 3
-AHEAD = 2
+PIECE = 2
+AHEAD = 3
 SMEM_SPEC = pl.BlockSpec(memory_space=pltpu.SMEM)
 VMEM_SPEC = pl.BlockSpec(memory_space=pltpu.VMEM)
 HBM_SPEC = pl.BlockSpec(memory_space=pltpu.HBM)

time: 101 us -> 101 us (level)
  no operation moved by 1% of the time
where the time goes in v14:
time: 101 us; the launch traced here: 100 us
  waiting for transfers between devices  43.9 us (43%)
  starting transfers between devices  34 us (34%)
  Pallas kernels  21.4 us (21%)
    ppermute x24, waiting for transfers between devices, moved(): return lax.ppermute(operand, axes, pairs)  43.9 us
    ppermute x24, starting transfers between devices, moved(): return lax.ppermute(operand, axes, pairs)  34 us
    pallas_call x5, Pallas kernels, filter_pair(): pl.pallas_call(functools.partial(pair_kernel, lon_dev, base, tuple(plan),...  12.6 us
    pallas_call x1, Pallas kernels, take_rows(): pl.pallas_call(functools.partial(take_kernel, chunks, lat_dev, block), ou...  4.25 us
    pallas_call x1, Pallas kernels, put_rows(): pl.pallas_call(functools.partial(put_kernel, counts, lat_dev, block), out...  2.8 us
  transfers between devices with their start and end apart: 24, of which 12 were waited for; matrix products, arithmetic and copies ran while one was open for 0% of the time, Pallas kernels for 14%

profile of v14, /device:TPU:0, one launch (start us, length us, event | category | flops | bytes accessed | tf_op | source)
XLA Modules:
  0.0 100.4 jit_solution(7756263151911248310)
XLA Ops:
  0.0 0.0 copy-start
  0.0 0.0 copy-start.1
  0.0 0.8 pad_add_fusion.place_ref
  0.8 4.2 %take_rows.1 = (bf16[360,640]{1,0:T(8,128)(2,1)S(1)}, bf16[360,640]{1,0:T(8,128)(2,1)S(1)}, bf16[360,640]{1,0:T(8,128)(2,1)S(1)}, bf16[360,640]{1,0:T(8,128)(2,1...) custom-call(s32[35]{0:T(128)S(1)} %pad_add_fusion.place_ref, ...), custom_call_target="tpu_custom_call" | custom-call | flops 943718400 | bytes 7372800 | tf_op jit(solution)/shard_map/take_rows/pallas_call | solution.py:188
  5.0 0.5 collective-permute-start
  5.5 4.7 %collective-permute-start.3 = (bf16[360,640]{1,0:T(8,128)(2,1)S(1)}, bf16[360,640]{1,0:T(8,128)(2,1)S(1)}, u32[]{:S(2)}, u32[]{:S(2)}) collective-permute-start(bf16[360,640]{1,0:T(8,128)(2,1)S(1)} %get-tuple-element.39.refs_1_.refs_5_), channel_id=1, source_target_pairs={{0,24},{2,26},{4,12},{6,14},{8,0},{10,2},{12,20},{14,22},{16,8},{1... | collective-permute-start | bytes 1382408 | tf_op jit(solution)/shard_map/ppermute | solution.py:393
  10.2 0.0 collective-permute-start.1
  10.2 1.5 %collective-permute-start.8 = (bf16[360,640]{1,0:T(8,128)(2,1)S(1)}, bf16[360,640]{1,0:T(8,128)(2,1)S(1)}, u32[]{:S(2)}, u32[]{:S(2)}) collective-permute-start(bf16[360,640]{1,0:T(8,128)(2,1)S(1)} %get-tuple-element.47), channel_id=1, source_target_pairs={{0,1},{1,0},{2,3},{3,2},{4,5},{5,4},{6,7},{7,6},{8,9},{9,8},{10,11... | collective-permute-start | bytes 1382408 | tf_op jit(solution)/shard_map/ppermute | solution.py:393
  11.7 1.2 %collective-permute-start.2 = (bf16[360,640]{1,0:T(8,128)(2,1)S(1)}, bf16[360,640]{1,0:T(8,128)(2,1)S(1)}, u32[]{:S(2)}, u32[]{:S(2)}) collective-permute-start(bf16[360,640]{1,0:T(8,128)(2,1)S(1)} %get-tuple-element.42), channel_id=1, source_target_pairs={{0,6},{2,4},{4,2},{6,0},{8,14},{10,12},{12,10},{14,8},{16,22},{18,... | collective-permute-start | bytes 1382408 | tf_op jit(solution)/shard_map/ppermute | solution.py:393
  13.0 1.7 %list_rows.1 = (s32[17]{0:T(128)S(1)}, s32[17]{0:T(128)S(1)}) custom-call(s32[35]{0:T(128)S(1)} %pad_add_fusion.place_ref), custom_call_target="tpu_custom_call" | custom-call | bytes 256 | tf_op jit(solution)/shard_map/list_rows/pallas_call | solution.py:123
  14.7 0.0 copy-done
  14.7 0.1 tap_lines.1.refs_0_
  14.8 0.0 collective-permute-done.refs_2_.refs_6_
  14.8 0.5 collective-permute-start.5
  15.4 5.7 %collective-permute-done.3.refs_3_ = bf16[360,640]{1,0:T(8,128)(2,1)S(1)} collective-permute-done((bf16[360,640]{1,0:T(8,128)(2,1)S(1)}, bf16[360,640]{1,0:T(8,128)(2,1)S(1)}, u32[]{:S(2)}, u32[]{:S(2)}) %collective-permute-start.3) | collective-permute-done | bytes 460832 | tf_op jit(solution)/shard_map/ppermute | solution.py:393
  21.1 0.3 collective-permute-start.9
  21.4 2.2 %collective-permute-done.1.refs_3_.refs_1_ = bf16[360,640]{1,0:T(8,128)(2,1)S(1)} collective-permute-done((bf16[360,640]{1,0:T(8,128)(2,1)S(1)}, bf16[360,640]{1,0:T(8,128)(2,1)S(1)}, u32[]{:S(2)}, u32[]{:S(2)}) %collective-permute-start.1) | collective-permute-done | bytes 460832 | tf_op jit(solution)/shard_map/ppermute | solution.py:393
  23.6 0.0 collective-permute-done.8.refs_1_
  23.6 1.0 collective-permute-start.10
  24.6 0.1 collective-permute-start.4
  24.7 7.3 %collective-permute-done.2.refs_4_.refs_2_ = bf16[360,640]{1,0:T(8,128)(2,1)S(1)} collective-permute-done((bf16[360,640]{1,0:T(8,128)(2,1)S(1)}, bf16[360,640]{1,0:T(8,128)(2,1)S(1)}, u32[]{:S(2)}, u32[]{:S(2)}) %collective-permute-start.2) | collective-permute-done | bytes 460832 | tf_op jit(solution)/shard_map/ppermute | solution.py:393
  31.9 1.5 %collective-permute-start.14 = (bf16[360,640]{1,0:T(8,128)(2,1)S(1)}, bf16[360,640]{1,0:T(8,128)(2,1)S(1)}, u32[]{:S(2)}, u32[]{:S(2)}) collective-permute-start(bf16[360,640]{1,0:T(8,128)(2,1)S(1)} %get-tuple-element.56), channel_id=1, source_target_pairs={{0,1},{1,0},{2,3},{3,2},{4,5},{5,4},{6,7},{7,6},{8,9},{9,8},{10,11... | collective-permute-start | bytes 1382408 | tf_op jit(solution)/shard_map/ppermute | solution.py:393
  33.5 0.0 collective-permute-done.5.refs_4_
  33.5 0.1 collective-permute-start.6
  33.6 0.3 collective-permute-done.9.refs_2_
  33.9 15.4 %collective-permute-start.11 = (bf16[360,640]{1,0:T(8,128)(2,1)S(1)}, bf16[360,640]{1,0:T(8,128)(2,1)S(1)}, u32[]{:S(2)}, u32[]{:S(2)}) collective-permute-start(bf16[360,640]{1,0:T(8,128)(2,1)S(1)} %collective-permute-done.9.refs_2_), channel_id=1, source_target_pairs={{0,4},{2,6},{4,0},{6,2},{8,12},{10,14},{12,8},{14,10},{16,20},{18,... | collective-permute-start | bytes 1382408 | tf_op jit(solution)/shard_map/ppermute | solution.py:393
  49.3 0.0 collective-permute-done.10.refs_3_
  49.3 0.0 collective-permute-start.15
  49.3 0.0 collective-permute-done.4.refs_5_
  49.3 0.1 collective-permute-start.12
  49.4 0.0 collective-permute-done.14.refs_1_
  49.4 0.5 collective-permute-start.16
  49.9 0.0 copy-done.1
  49.9 2.9 %filter_whole.4 = (bf16[360,640]{1,0:T(8,128)(2,1)S(1)}, bf16[360,640]{1,0:T(8,128)(2,1)S(1)}) custom-call(s32[17]{0:T(128)S(1)} %get-tuple-element.38.rows_ref, s32[35]{0:T(128)S(1)} %pad_add_fusion.place_ref, s32[32]{0:T(128)S(1)} %copy-done.1, f32[32,1152]{1,0:T(8,128)S(1)} %tap_lines.1.refs_0_, ...), custom_call_target="tpu_custom_call" | custom-call | flops 3019898880 | bytes 3686400 | tf_op jit(solution)/shard_map/filter_whole/pallas_call | solution.py:341
  52.8 0.0 collective-permute-done.6.refs_6_
  52.8 6.4 %collective-permute-done.11.refs_4_ = bf16[360,640]{1,0:T(8,128)(2,1)S(1)} collective-permute-done((bf16[360,640]{1,0:T(8,128)(2,1)S(1)}, bf16[360,640]{1,0:T(8,128)(2,1)S(1)}, u32[]{:S(2)}, u32[]{:S(2)}) %collective-permute-start.11) | collective-permute-done | bytes 460832 | tf_op jit(solution)/shard_map/ppermute | solution.py:393
  59.2 0.0 collective-permute-start.13
  59.2 2.9 %collective-permute-done.15.refs_2_ = bf16[360,640]{1,0:T(8,128)(2,1)S(1)} collective-permute-done((bf16[360,640]{1,0:T(8,128)(2,1)S(1)}, bf16[360,640]{1,0:T(8,128)(2,1)S(1)}, u32[]{:S(2)}, u32[]{:S(2)}) %collective-permute-start.15) | collective-permute-done | bytes 460832 | tf_op jit(solution)/shard_map/ppermute | solution.py:393
  62.1 1.2 %collective-permute-start.17 = (bf16[360,640]{1,0:T(8,128)(2,1)S(1)}, bf16[360,640]{1,0:T(8,128)(2,1)S(1)}, u32[]{:S(2)}, u32[]{:S(2)}) collective-permute-start(bf16[360,640]{1,0:T(8,128)(2,1)S(1)} %collective-permute-done.15.refs_2_), channel_id=1, source_target_pairs={{0,4},{2,6},{4,0},{6,2},{8,12},{10,14},{12,8},{14,10},{16,20},{18,... | collective-permute-start | bytes 1382408 | tf_op jit(solution)/shard_map/ppermute | solution.py:393
  63.3 0.8 collective-permute-start.7
  64.1 0.0 collective-permute-done.12.refs_5_
  64.1 3.5 %collective-permute-done.16.refs_3_ = bf16[360,640]{1,0:T(8,128)(2,1)S(1)} collective-permute-done((bf16[360,640]{1,0:T(8,128)(2,1)S(1)}, bf16[360,640]{1,0:T(8,128)(2,1)S(1)}, u32[]{:S(2)}, u32[]{:S(2)}) %collective-permute-start.16) | collective-permute-done | bytes 460832 | tf_op jit(solution)/shard_map/ppermute | solution.py:393
  67.6 0.0 collective-permute-start.18
  67.7 2.9 %filter_whole.3 = (bf16[360,640]{1,0:T(8,128)(2,1)S(1)}, bf16[360,640]{1,0:T(8,128)(2,1)S(1)}) custom-call(s32[17]{0:T(128)S(1)} %get-tuple-element.38.rows_ref, s32[35]{0:T(128)S(1)} %pad_add_fusion.place_ref, s32[32]{0:T(128)S(1)} %copy-done.1, f32[32,1152]{1,0:T(8,128)S(1)} %tap_lines.1.refs_0_, bf16[360,640]{1,0:T(8,128)(2,1)S(1)} %get-tuple-element.39.refs_1_.refs_5_, ...), custom_call_target="tpu_custom_call" | custom-call | flops 3019898880 | bytes 3686400 | tf_op jit(solution)/shard_map/filter_whole/pallas_call | solution.py:341
  70.6 0.1 collective-permute-start.20
  70.7 3.9 %collective-permute-done.13.refs_6_ = bf16[360,640]{1,0:T(8,128)(2,1)S(1)} collective-permute-done((bf16[360,640]{1,0:T(8,128)(2,1)S(1)}, bf16[360,640]{1,0:T(8,128)(2,1)S(1)}, u32[]{:S(2)}, u32[]{:S(2)}) %collective-permute-start.13) | collective-permute-done | bytes 460832 | tf_op jit(solution)/shard_map/ppermute | solution.py:393
  74.5 3.0 %collective-permute-done.17.refs_4_ = bf16[360,640]{1,0:T(8,128)(2,1)S(1)} collective-permute-done((bf16[360,640]{1,0:T(8,128)(2,1)S(1)}, bf16[360,640]{1,0:T(8,128)(2,1)S(1)}, u32[]{:S(2)}, u32[]{:S(2)}) %collective-permute-start.17) | collective-permute-done | bytes 460832 | tf_op jit(solution)/shard_map/ppermute | solution.py:393
  77.5 0.0 collective-permute-start.19
  77.5 0.0 collective-permute-start.21
  77.5 2.5 %filter_early.1 = (f32[2,180,1280]{2,1,0:T(8,128)S(1)}, bf16[2,5,192,180]{3,2,1,0:T(8,128)(2,1)S(1)}) custom-call(s32[17]{0:T(128)S(1)} %get-tuple-element.38.rows_ref, s32[35]{0:T(128)S(1)} %pad_add_fusion.place_ref, s32[32]{0:T(128)S(1)} %copy-done.1, f32[32,1152]{1,0:T(8,128)S(1)} %tap_lines.1.refs_0_, ...), custom_call_target="tpu_custom_call" | custom-call | flops 2113929216 | bytes 3686400 | tf_op jit(solution)/shard_map/filter_early/pallas_call | solution.py:341
  80.0 2.9 %filter_whole.5 = (bf16[360,640]{1,0:T(8,128)(2,1)S(1)}, bf16[360,640]{1,0:T(8,128)(2,1)S(1)}) custom-call(s32[17]{0:T(128)S(1)} %get-tuple-element.38.rows_ref, s32[35]{0:T(128)S(1)} %pad_add_fusion.place_ref, s32[32]{0:T(128)S(1)} %copy-done.1, f32[32,1152]{1,0:T(8,128)S(1)} %tap_lines.1.refs_0_, bf16[360,640]{1,0:T(8,128)(2,1)S(1)} %collective-permute-done.8.refs_1_, ...), custom_call_target="tpu_custom_call" | custom-call | flops 3019898880 | bytes 3686400 | tf_op jit(solution)/shard_map/filter_whole/pallas_call | solution.py:341
  82.9 1.5 %collective-permute-done.18.refs_2_ = bf16[360,640]{1,0:T(8,128)(2,1)S(1)} collective-permute-done((bf16[360,640]{1,0:T(8,128)(2,1)S(1)}, bf16[360,640]{1,0:T(8,128)(2,1)S(1)}, u32[]{:S(2)}, u32[]{:S(2)}) %collective-permute-start.18) | collective-permute-done | bytes 460832 | tf_op jit(solution)/shard_map/ppermute | solution.py:393
  84.4 4.3 %collective-permute-start.22 = (bf16[360,640]{1,0:T(8,128)(2,1)S(1)}, bf16[360,640]{1,0:T(8,128)(2,1)S(1)}, u32[]{:S(2)}, u32[]{:S(2)}) collective-permute-start(bf16[360,640]{1,0:T(8,128)(2,1)S(1)} %get-tuple-element.67), channel_id=1, source_target_pairs={{0,2},{2,0},{4,6},{6,4},{8,10},{10,8},{12,14},{14,12},{16,18},{18,... | collective-permute-start | bytes 1382408 | tf_op jit(solution)/shard_map/ppermute | solution.py:393
  88.7 5.6 %collective-permute-done.19.refs_3_ = bf16[360,640]{1,0:T(8,128)(2,1)S(1)} collective-permute-done((bf16[360,640]{1,0:T(8,128)(2,1)S(1)}, bf16[360,640]{1,0:T(8,128)(2,1)S(1)}, u32[]{:S(2)}, u32[]{:S(2)}) %collective-permute-start.19) | collective-permute-done | bytes 460832 | tf_op jit(solution)/shard_map/ppermute | solution.py:393
  94.2 1.3 %filter_late.1 = (bf16[360,640]{1,0:T(8,128)(2,1)S(1)}, bf16[360,640]{1,0:T(8,128)(2,1)S(1)}) custom-call(s32[17]{0:T(128)S(1)} %get-tuple-element.38.rows_ref, s32[35]{0:T(128)S(1)} %pad_add_fusion.place_ref, s32[32]{0:T(128)S(1)} %copy-done.1, f32[2,180,1280]{2,1,0:T(8,128)S(1)} %get-tuple-element.59.refs_0_, ...), custom_call_target="tpu_custom_call" | custom-call | flops 905969664 | bytes 3686400 | tf_op jit(solution)/shard_map/filter_late/pallas_call | solution.py:341
  95.6 0.1 collective-permute-start.23
  95.7 0.0 collective-permute-done.7.refs_1_
  95.7 0.0 collective-permute-done.20.refs_4_
  95.7 0.0 collective-permute-done.21.refs_5_
  95.7 0.0 collective-permute-done.22.refs_6_
  95.7 1.7 %collective-permute-done.23.refs_7_ = bf16[360,640]{1,0:T(8,128)(2,1)S(1)} collective-permute-done((bf16[360,640]{1,0:T(8,128)(2,1)S(1)}, bf16[360,640]{1,0:T(8,128)(2,1)S(1)}, u32[]{:S(2)}, u32[]{:S(2)}) %collective-permute-start.23) | collective-permute-done | bytes 460832 | tf_op jit(solution)/shard_map/ppermute | solution.py:393
  97.5 2.8 %put_rows.1 = bf16[180,16,640]{2,1,0:T(8,128)(2,1)} custom-call(s32[17]{0:T(128)S(1)} %get-tuple-element.37.slots_ref, bf16[360,640]{1,0:T(8,128)(2,1)S(1)} %get-tuple-element.45.refs_0_, bf16[360,640]{1,0:T(8,128)(2,1)S(1)} %collective-permute-done.7.refs_1_, bf16[360,640]{1,0:T(8,128)(2,1)S(1)} %get-tuple-element.54.refs_2_, ...), custom_call_target="tpu_custom_call" | custom-call | flops 943718400 | bytes 7372800 | tf_op jit(solution)/shard_map/put_rows/pallas_call | solution.py:243
Async XLA Ops:
  0.0 14.7 %copy-start = (bf16[32,2880]{1,0:T(8,128)(2,1)S(1)}, bf16[32,2880]{1,0:T(8,128)(2,1)}, u32[]{:S(2)}) copy-start(bf16[32,2880]{1,0:T(8,128)(2,1)} %taps_ref.1) | copy-start | bytes 552964
  0.0 49.9 %copy-start.1 = (s32[32]{0:T(128)S(1)}, s32[32]{0:T(128)}, u32[]{:S(2)}) copy-start(s32[32]{0:T(128)} %widths_ref.9) | copy-start | bytes 388
  5.0 9.8 %collective-permute-start = (bf16[360,640]{1,0:T(8,128)(2,1)S(1)}, bf16[360,640]{1,0:T(8,128)(2,1)S(1)}, u32[]{:S(2)}, u32[]{:S(2)}) collective-permute-start(bf16[360,640]{1,0:T(8,128)(2,1)S(1)} %get-tuple-element.40), channel_id=1, source_target_pairs={{0,2},{2,0},{4,6},{6,4},{8,10},{10,8},{12,14},{14,12},{16,18},{18,... | collective-permute-start | bytes 1382408 | tf_op jit(solution)/shard_map/ppermute | solution.py:393
  5.5 15.5 %collective-permute-start.3 = (bf16[360,640]{1,0:T(8,128)(2,1)S(1)}, bf16[360,640]{1,0:T(8,128)(2,1)S(1)}, u32[]{:S(2)}, u32[]{:S(2)}) collective-permute-start(bf16[360,640]{1,0:T(8,128)(2,1)S(1)} %get-tuple-element.39.refs_1_.refs_5_), channel_id=1, source_target_pairs={{0,24},{2,26},{4,12},{6,14},{8,0},{10,2},{12,20},{14,22},{16,8},{1... | collective-permute-start | bytes 1382408 | tf_op jit(solution)/shard_map/ppermute | solution.py:393
  10.2 13.4 %collective-permute-start.1 = (bf16[360,640]{1,0:T(8,128)(2,1)S(1)}, bf16[360,640]{1,0:T(8,128)(2,1)S(1)}, u32[]{:S(2)}, u32[]{:S(2)}) collective-permute-start(bf16[360,640]{1,0:T(8,128)(2,1)S(1)} %get-tuple-element.41), channel_id=1, source_target_pairs={{0,4},{2,6},{4,0},{6,2},{8,12},{10,14},{12,8},{14,10},{16,20},{18,... | collective-permute-start | bytes 1382408 | tf_op jit(solution)/shard_map/ppermute | solution.py:393
  10.2 13.4 %collective-permute-start.8 = (bf16[360,640]{1,0:T(8,128)(2,1)S(1)}, bf16[360,640]{1,0:T(8,128)(2,1)S(1)}, u32[]{:S(2)}, u32[]{:S(2)}) collective-permute-start(bf16[360,640]{1,0:T(8,128)(2,1)S(1)} %get-tuple-element.47), channel_id=1, source_target_pairs={{0,1},{1,0},{2,3},{3,2},{4,5},{5,4},{6,7},{7,6},{8,9},{9,8},{10,11... | collective-permute-start | bytes 1382408 | tf_op jit(solution)/shard_map/ppermute | solution.py:393
  11.7 20.2 %collective-permute-start.2 = (bf16[360,640]{1,0:T(8,128)(2,1)S(1)}, bf16[360,640]{1,0:T(8,128)(2,1)S(1)}, u32[]{:S(2)}, u32[]{:S(2)}) collective-permute-start(bf16[360,640]{1,0:T(8,128)(2,1)S(1)} %get-tuple-element.42), channel_id=1, source_target_pairs={{0,6},{2,4},{4,2},{6,0},{8,14},{10,12},{12,10},{14,8},{16,22},{18,... | collective-permute-start | bytes 1382408 | tf_op jit(solution)/shard_map/ppermute | solution.py:393
  14.8 18.6 %collective-permute-start.5 = (bf16[360,640]{1,0:T(8,128)(2,1)S(1)}, bf16[360,640]{1,0:T(8,128)(2,1)S(1)}, u32[]{:S(2)}, u32[]{:S(2)}) collective-permute-start(bf16[360,640]{1,0:T(8,128)(2,1)S(1)} %collective-permute-done.refs_2_.refs_6_), channel_id=1, source_target_pairs={{0,24},{2,26},{4,12},{6,14},{8,0},{10,2},{12,20},{14,22},{16,8},{1... | collective-permute-start | bytes 1382408 | tf_op jit(solution)/shard_map/ppermute | solution.py:393
  21.1 12.8 %collective-permute-start.9 = (bf16[360,640]{1,0:T(8,128)(2,1)S(1)}, bf16[360,640]{1,0:T(8,128)(2,1)S(1)}, u32[]{:S(2)}, u32[]{:S(2)}) collective-permute-start(bf16[360,640]{1,0:T(8,128)(2,1)S(1)} %get-tuple-element.49), channel_id=1, source_target_pairs={{0,3},{1,2},{2,1},{3,0},{4,7},{5,6},{6,5},{7,4},{8,11},{9,10},{10,... | collective-permute-start | bytes 1382408 | tf_op jit(solution)/shard_map/ppermute | solution.py:393
  23.6 25.7 %collective-permute-start.10 = (bf16[360,640]{1,0:T(8,128)(2,1)S(1)}, bf16[360,640]{1,0:T(8,128)(2,1)S(1)}, u32[]{:S(2)}, u32[]{:S(2)}) collective-permute-start(bf16[360,640]{1,0:T(8,128)(2,1)S(1)} %collective-permute-done.8.refs_1_), channel_id=1, source_target_pairs={{0,4},{2,6},{4,0},{6,2},{8,12},{10,14},{12,8},{14,10},{16,20},{18,... | collective-permute-start | bytes 1382408 | tf_op jit(solution)/shard_map/ppermute | solution.py:393
  24.6 24.7 %collective-permute-start.4 = (bf16[360,640]{1,0:T(8,128)(2,1)S(1)}, bf16[360,640]{1,0:T(8,128)(2,1)S(1)}, u32[]{:S(2)}, u32[]{:S(2)}) collective-permute-start(bf16[360,640]{1,0:T(8,128)(2,1)S(1)} %collective-permute-done.1.refs_3_.refs_1_), channel_id=1, source_target_pairs={{0,8},{2,10},{4,28},{6,30},{8,16},{10,18},{12,4},{14,6},{16,24},{1... | collective-permute-start | bytes 1382408 | tf_op jit(solution)/shard_map/ppermute | solution.py:393
  31.9 17.4 %collective-permute-start.14 = (bf16[360,640]{1,0:T(8,128)(2,1)S(1)}, bf16[360,640]{1,0:T(8,128)(2,1)S(1)}, u32[]{:S(2)}, u32[]{:S(2)}) collective-permute-start(bf16[360,640]{1,0:T(8,128)(2,1)S(1)} %get-tuple-element.56), channel_id=1, source_target_pairs={{0,1},{1,0},{2,3},{3,2},{4,5},{5,4},{6,7},{7,6},{8,9},{9,8},{10,11... | collective-permute-start | bytes 1382408 | tf_op jit(solution)/shard_map/ppermute | solution.py:393
  33.5 19.4 %collective-permute-start.6 = (bf16[360,640]{1,0:T(8,128)(2,1)S(1)}, bf16[360,640]{1,0:T(8,128)(2,1)S(1)}, u32[]{:S(2)}, u32[]{:S(2)}) collective-permute-start(bf16[360,640]{1,0:T(8,128)(2,1)S(1)} %collective-permute-done.2.refs_4_.refs_2_), channel_id=1, source_target_pairs={{0,8},{2,10},{4,28},{6,30},{8,16},{10,18},{12,4},{14,6},{16,24},{1... | collective-permute-start | bytes 1382408 | tf_op jit(solution)/shard_map/ppermute | solution.py:393
  33.9 25.3 %collective-permute-start.11 = (bf16[360,640]{1,0:T(8,128)(2,1)S(1)}, bf16[360,640]{1,0:T(8,128)(2,1)S(1)}, u32[]{:S(2)}, u32[]{:S(2)}) collective-permute-start(bf16[360,640]{1,0:T(8,128)(2,1)S(1)} %collective-permute-done.9.refs_2_), channel_id=1, source_target_pairs={{0,4},{2,6},{4,0},{6,2},{8,12},{10,14},{12,8},{14,10},{16,20},{18,... | collective-permute-start | bytes 1382408 | tf_op jit(solution)/shard_map/ppermute | solution.py:393
  49.3 12.8 %collective-permute-start.15 = (bf16[360,640]{1,0:T(8,128)(2,1)S(1)}, bf16[360,640]{1,0:T(8,128)(2,1)S(1)}, u32[]{:S(2)}, u32[]{:S(2)}) collective-permute-start(bf16[360,640]{1,0:T(8,128)(2,1)S(1)} %get-tuple-element.58), channel_id=1, source_target_pairs={{0,3},{1,2},{2,1},{3,0},{4,7},{5,6},{6,5},{7,4},{8,11},{9,10},{10,... | collective-permute-start | bytes 1382408 | tf_op jit(solution)/shard_map/ppermute | solution.py:393
  49.3 14.8 %collective-permute-start.12 = (bf16[360,640]{1,0:T(8,128)(2,1)S(1)}, bf16[360,640]{1,0:T(8,128)(2,1)S(1)}, u32[]{:S(2)}, u32[]{:S(2)}) collective-permute-start(bf16[360,640]{1,0:T(8,128)(2,1)S(1)} %collective-permute-done.10.refs_3_), channel_id=1, source_target_pairs={{0,8},{2,10},{4,28},{6,30},{8,16},{10,18},{12,4},{14,6},{16,24},{1... | collective-permute-start | bytes 1382408 | tf_op jit(solution)/shard_map/ppermute | solution.py:393
  49.4 18.3 %collective-permute-start.16 = (bf16[360,640]{1,0:T(8,128)(2,1)S(1)}, bf16[360,640]{1,0:T(8,128)(2,1)S(1)}, u32[]{:S(2)}, u32[]{:S(2)}) collective-permute-start(bf16[360,640]{1,0:T(8,128)(2,1)S(1)} %collective-permute-done.14.refs_1_), channel_id=1, source_target_pairs={{0,4},{2,6},{4,0},{6,2},{8,12},{10,14},{12,8},{14,10},{16,20},{18,... | collective-permute-start | bytes 1382408 | tf_op jit(solution)/shard_map/ppermute | solution.py:393
  59.2 15.3 %collective-permute-start.13 = (bf16[360,640]{1,0:T(8,128)(2,1)S(1)}, bf16[360,640]{1,0:T(8,128)(2,1)S(1)}, u32[]{:S(2)}, u32[]{:S(2)}) collective-permute-start(bf16[360,640]{1,0:T(8,128)(2,1)S(1)} %collective-permute-done.11.refs_4_), channel_id=1, source_target_pairs={{0,8},{2,10},{4,28},{6,30},{8,16},{10,18},{12,4},{14,6},{16,24},{1... | collective-permute-start | bytes 1382408 | tf_op jit(solution)/shard_map/ppermute | solution.py:393
  62.1 15.4 %collective-permute-start.17 = (bf16[360,640]{1,0:T(8,128)(2,1)S(1)}, bf16[360,640]{1,0:T(8,128)(2,1)S(1)}, u32[]{:S(2)}, u32[]{:S(2)}) collective-permute-start(bf16[360,640]{1,0:T(8,128)(2,1)S(1)} %collective-permute-done.15.refs_2_), channel_id=1, source_target_pairs={{0,4},{2,6},{4,0},{6,2},{8,12},{10,14},{12,8},{14,10},{16,20},{18,... | collective-permute-start | bytes 1382408 | tf_op jit(solution)/shard_map/ppermute | solution.py:393
  63.3 32.4 %collective-permute-start.7 = (bf16[360,640]{1,0:T(8,128)(2,1)S(1)}, bf16[360,640]{1,0:T(8,128)(2,1)S(1)}, u32[]{:S(2)}, u32[]{:S(2)}) collective-permute-start(bf16[360,640]{1,0:T(8,128)(2,1)S(1)} %get-tuple-element.46), channel_id=1, source_target_pairs={{0,4},{2,6},{4,0},{6,2},{8,12},{10,14},{12,8},{14,10},{16,20},{18,... | collective-permute-start | bytes 1382408 | tf_op jit(solution)/shard_map/ppermute | solution.py:393
  67.6 16.8 %collective-permute-start.18 = (bf16[360,640]{1,0:T(8,128)(2,1)S(1)}, bf16[360,640]{1,0:T(8,128)(2,1)S(1)}, u32[]{:S(2)}, u32[]{:S(2)}) collective-permute-start(bf16[360,640]{1,0:T(8,128)(2,1)S(1)} %collective-permute-done.16.refs_3_), channel_id=1, source_target_pairs={{0,8},{2,10},{4,28},{6,30},{8,16},{10,18},{12,4},{14,6},{16,24},{1... | collective-permute-start | bytes 1382408 | tf_op jit(solution)/shard_map/ppermute | solution.py:393
  70.6 25.1 %collective-permute-start.20 = (bf16[360,640]{1,0:T(8,128)(2,1)S(1)}, bf16[360,640]{1,0:T(8,128)(2,1)S(1)}, u32[]{:S(2)}, u32[]{:S(2)}) collective-permute-start(bf16[360,640]{1,0:T(8,128)(2,1)S(1)} %get-tuple-element.64), channel_id=1, source_target_pairs={{0,2},{2,0},{4,6},{6,4},{8,10},{10,8},{12,14},{14,12},{16,18},{18,... | collective-permute-start | bytes 1382408 | tf_op jit(solution)/shard_map/ppermute | solution.py:393
  77.5 16.7 %collective-permute-start.19 = (bf16[360,640]{1,0:T(8,128)(2,1)S(1)}, bf16[360,640]{1,0:T(8,128)(2,1)S(1)}, u32[]{:S(2)}, u32[]{:S(2)}) collective-permute-start(bf16[360,640]{1,0:T(8,128)(2,1)S(1)} %collective-permute-done.17.refs_4_), channel_id=1, source_target_pairs={{0,8},{2,10},{4,28},{6,30},{8,16},{10,18},{12,4},{14,6},{16,24},{1... | collective-permute-start | bytes 1382408 | tf_op jit(solution)/shard_map/ppermute | solution.py:393
  77.5 18.2 %collective-permute-start.21 = (bf16[360,640]{1,0:T(8,128)(2,1)S(1)}, bf16[360,640]{1,0:T(8,128)(2,1)S(1)}, u32[]{:S(2)}, u32[]{:S(2)}) collective-permute-start(bf16[360,640]{1,0:T(8,128)(2,1)S(1)} %get-tuple-element.66), channel_id=1, source_target_pairs={{0,6},{2,4},{4,2},{6,0},{8,14},{10,12},{12,10},{14,8},{16,22},{18,... | collective-permute-start | bytes 1382408 | tf_op jit(solution)/shard_map/ppermute | solution.py:393
  84.4 11.3 %collective-permute-start.22 = (bf16[360,640]{1,0:T(8,128)(2,1)S(1)}, bf16[360,640]{1,0:T(8,128)(2,1)S(1)}, u32[]{:S(2)}, u32[]{:S(2)}) collective-permute-start(bf16[360,640]{1,0:T(8,128)(2,1)S(1)} %get-tuple-element.67), channel_id=1, source_target_pairs={{0,2},{2,0},{4,6},{6,4},{8,10},{10,8},{12,14},{14,12},{16,18},{18,... | collective-permute-start | bytes 1382408 | tf_op jit(solution)/shard_map/ppermute | solution.py:393
  95.6 1.9 %collective-permute-start.23 = (bf16[360,640]{1,0:T(8,128)(2,1)S(1)}, bf16[360,640]{1,0:T(8,128)(2,1)S(1)}, u32[]{:S(2)}, u32[]{:S(2)}) collective-permute-start(bf16[360,640]{1,0:T(8,128)(2,1)S(1)} %get-tuple-element.68), channel_id=1, source_target_pairs={{0,2},{2,0},{4,6},{6,4},{8,10},{10,8},{12,14},{14,12},{16,18},{18,... | collective-permute-start | bytes 1382408 | tf_op jit(solution)/shard_map/ppermute | solution.py:393

commit v15 on v13

--- a/solution.py
+++ b/solution.py
@@ -22,7 +22,7 @@
     ("x", 0): [("p", 0), ("y", 0)],
     ("x", 1): [("p", 1)],
     ("b", 2): [("x", 3)],
-    ("q", 2): [("q", 0)],
+    ("q", 2): [("q", 0), ("l", 0), ("l", 1)],
     ("q", 3): [("q", 1)],
     ("z", 0): [("q", 2), ("q", 1)],
     ("z", 1): [("q", 3), ("t", 1)],
@@ -30,7 +30,7 @@
     ("z", 3): [("z", 1)],
     ("y", 2): [("y", 0), ("p", 0)],
     ("y", 3): [("y", 1), ("x", 0)],
-    ("y", 1): [("q", 0), ("l", 0), ("l", 1)],
+    ("y", 1): [("q", 0)],
 }
 FLOPS = 3
 

time: 101 us -> 96.6 us (0.956)
  starting transfers between devices: 34 us -> 30 us
    ppermute x24, starting transfers between devices: 34 us -> 30 us  [moved(): return lax.ppermute(operand, axes, pairs)]
  transfers between devices with their start and end apart: 24 -> 24, of which waited for: 12 -> 15; matrix products, arithmetic and copies ran while one was open for 0% -> 0% of each run, Pallas kernels for 14% -> 15%
where the time goes in v15:
time: 96.6 us; the launch traced here: 96.4 us
  waiting for transfers between devices  43.8 us (45%)
  starting transfers between devices  30 us (31%)
  Pallas kernels  21.6 us (22%)
    ppermute x24, waiting for transfers between devices, moved(): return lax.ppermute(operand, axes, pairs)  43.8 us
    ppermute x24, starting transfers between devices, moved(): return lax.ppermute(operand, axes, pairs)  30 us
    pallas_call x5, Pallas kernels, filter_pair(): pl.pallas_call(functools.partial(pair_kernel, lon_dev, base, tuple(plan),...  12.6 us
    pallas_call x1, Pallas kernels, take_rows(): pl.pallas_call(functools.partial(take_kernel, chunks, lat_dev, block), ou...  4.35 us
    pallas_call x1, Pallas kernels, put_rows(): pl.pallas_call(functools.partial(put_kernel, counts, lat_dev, block), out...  2.8 us
  transfers between devices with their start and end apart: 24, of which 15 were waited for; matrix products, arithmetic and copies ran while one was open for 0% of the time, Pallas kernels for 15%

profile of v15, /device:TPU:0, one launch (start us, length us, event | category | flops | bytes accessed | tf_op | source)
XLA Modules:
  0.0 96.4 jit_solution(9239460099554909117)
XLA Ops:
  0.0 0.0 copy-start
  0.0 0.0 copy-start.1
  0.0 0.8 pad_add_fusion.place_ref
  0.8 4.3 %take_rows.1 = (bf16[360,640]{1,0:T(8,128)(2,1)S(1)}, bf16[360,640]{1,0:T(8,128)(2,1)S(1)}, bf16[360,640]{1,0:T(8,128)(2,1)S(1)}, bf16[360,640]{1,0:T(8,128)(2,1...) custom-call(s32[35]{0:T(128)S(1)} %pad_add_fusion.place_ref, ...), custom_call_target="tpu_custom_call" | custom-call | flops 943718400 | bytes 7372800 | tf_op jit(solution)/shard_map/take_rows/pallas_call | solution.py:188
  5.1 0.5 collective-permute-start
  5.6 4.7 %collective-permute-start.3 = (bf16[360,640]{1,0:T(8,128)(2,1)S(1)}, bf16[360,640]{1,0:T(8,128)(2,1)S(1)}, u32[]{:S(2)}, u32[]{:S(2)}) collective-permute-start(bf16[360,640]{1,0:T(8,128)(2,1)S(1)} %get-tuple-element.39.refs_1_.refs_5_), channel_id=1, source_target_pairs={{0,24},{2,26},{4,12},{6,14},{8,0},{10,2},{12,20},{14,22},{16,8},{1... | collective-permute-start | bytes 1382408 | tf_op jit(solution)/shard_map/ppermute | solution.py:393
  10.3 0.0 collective-permute-start.1
  10.3 1.5 %collective-permute-start.8 = (bf16[360,640]{1,0:T(8,128)(2,1)S(1)}, bf16[360,640]{1,0:T(8,128)(2,1)S(1)}, u32[]{:S(2)}, u32[]{:S(2)}) collective-permute-start(bf16[360,640]{1,0:T(8,128)(2,1)S(1)} %get-tuple-element.47), channel_id=1, source_target_pairs={{0,1},{1,0},{2,3},{3,2},{4,5},{5,4},{6,7},{7,6},{8,9},{9,8},{10,11... | collective-permute-start | bytes 1382408 | tf_op jit(solution)/shard_map/ppermute | solution.py:393
  11.8 1.2 %collective-permute-start.2 = (bf16[360,640]{1,0:T(8,128)(2,1)S(1)}, bf16[360,640]{1,0:T(8,128)(2,1)S(1)}, u32[]{:S(2)}, u32[]{:S(2)}) collective-permute-start(bf16[360,640]{1,0:T(8,128)(2,1)S(1)} %get-tuple-element.42), channel_id=1, source_target_pairs={{0,6},{2,4},{4,2},{6,0},{8,14},{10,12},{12,10},{14,8},{16,22},{18,... | collective-permute-start | bytes 1382408 | tf_op jit(solution)/shard_map/ppermute | solution.py:393
  13.1 0.0 collective-permute-done.refs_2_.refs_6_
  13.1 0.5 collective-permute-start.5
  13.6 7.6 %collective-permute-done.3.refs_3_ = bf16[360,640]{1,0:T(8,128)(2,1)S(1)} collective-permute-done((bf16[360,640]{1,0:T(8,128)(2,1)S(1)}, bf16[360,640]{1,0:T(8,128)(2,1)S(1)}, u32[]{:S(2)}, u32[]{:S(2)}) %collective-permute-start.3) | collective-permute-done | bytes 460832 | tf_op jit(solution)/shard_map/ppermute | solution.py:393
  21.2 0.3 collective-permute-start.9
  21.5 2.2 %collective-permute-done.1.refs_3_.refs_1_ = bf16[360,640]{1,0:T(8,128)(2,1)S(1)} collective-permute-done((bf16[360,640]{1,0:T(8,128)(2,1)S(1)}, bf16[360,640]{1,0:T(8,128)(2,1)S(1)}, u32[]{:S(2)}, u32[]{:S(2)}) %collective-permute-start.1) | collective-permute-done | bytes 460832 | tf_op jit(solution)/shard_map/ppermute | solution.py:393
  23.7 0.0 collective-permute-done.8.refs_1_
  23.7 1.0 %collective-permute-start.10 = (bf16[360,640]{1,0:T(8,128)(2,1)S(1)}, bf16[360,640]{1,0:T(8,128)(2,1)S(1)}, u32[]{:S(2)}, u32[]{:S(2)}) collective-permute-start(bf16[360,640]{1,0:T(8,128)(2,1)S(1)} %collective-permute-done.8.refs_1_), channel_id=1, source_target_pairs={{0,4},{2,6},{4,0},{6,2},{8,12},{10,14},{12,8},{14,10},{16,20},{18,... | collective-permute-start | bytes 1382408 | tf_op jit(solution)/shard_map/ppermute | solution.py:393
  24.7 1.7 %list_rows.1 = (s32[17]{0:T(128)S(1)}, s32[17]{0:T(128)S(1)}) custom-call(s32[35]{0:T(128)S(1)} %pad_add_fusion.place_ref), custom_call_target="tpu_custom_call" | custom-call | bytes 256 | tf_op jit(solution)/shard_map/list_rows/pallas_call | solution.py:123
  26.5 0.0 copy-done
  26.5 0.1 tap_lines.1.refs_0_
  26.6 0.1 collective-permute-start.4
  26.7 5.4 %collective-permute-done.2.refs_4_.refs_2_ = bf16[360,640]{1,0:T(8,128)(2,1)S(1)} collective-permute-done((bf16[360,640]{1,0:T(8,128)(2,1)S(1)}, bf16[360,640]{1,0:T(8,128)(2,1)S(1)}, u32[]{:S(2)}, u32[]{:S(2)}) %collective-permute-start.2) | collective-permute-done | bytes 460832 | tf_op jit(solution)/shard_map/ppermute | solution.py:393
  32.0 1.5 %collective-permute-start.14 = (bf16[360,640]{1,0:T(8,128)(2,1)S(1)}, bf16[360,640]{1,0:T(8,128)(2,1)S(1)}, u32[]{:S(2)}, u32[]{:S(2)}) collective-permute-start(bf16[360,640]{1,0:T(8,128)(2,1)S(1)} %get-tuple-element.56), channel_id=1, source_target_pairs={{0,1},{1,0},{2,3},{3,2},{4,5},{5,4},{6,7},{7,6},{8,9},{9,8},{10,11... | collective-permute-start | bytes 1382408 | tf_op jit(solution)/shard_map/ppermute | solution.py:393
  33.6 0.0 collective-permute-done.5.refs_4_
  33.6 0.1 collective-permute-start.6
  33.7 0.3 collective-permute-done.9.refs_2_
  34.0 2.1 %collective-permute-start.11 = (bf16[360,640]{1,0:T(8,128)(2,1)S(1)}, bf16[360,640]{1,0:T(8,128)(2,1)S(1)}, u32[]{:S(2)}, u32[]{:S(2)}) collective-permute-start(bf16[360,640]{1,0:T(8,128)(2,1)S(1)} %collective-permute-done.9.refs_2_), channel_id=1, source_target_pairs={{0,4},{2,6},{4,0},{6,2},{8,12},{10,14},{12,8},{14,10},{16,20},{18,... | collective-permute-start | bytes 1382408 | tf_op jit(solution)/shard_map/ppermute | solution.py:393
  36.1 7.3 %collective-permute-done.10.refs_3_ = bf16[360,640]{1,0:T(8,128)(2,1)S(1)} collective-permute-done((bf16[360,640]{1,0:T(8,128)(2,1)S(1)}, bf16[360,640]{1,0:T(8,128)(2,1)S(1)}, u32[]{:S(2)}, u32[]{:S(2)}) %collective-permute-start.10) | collective-permute-done | bytes 460832 | tf_op jit(solution)/shard_map/ppermute | solution.py:393
  43.5 0.0 collective-permute-start.15
  43.5 0.0 collective-permute-done.4.refs_5_
  43.5 0.0 collective-permute-start.12
  43.5 1.3 %collective-permute-done.14.refs_1_ = bf16[360,640]{1,0:T(8,128)(2,1)S(1)} collective-permute-done((bf16[360,640]{1,0:T(8,128)(2,1)S(1)}, bf16[360,640]{1,0:T(8,128)(2,1)S(1)}, u32[]{:S(2)}, u32[]{:S(2)}) %collective-permute-start.14) | collective-permute-done | bytes 460832 | tf_op jit(solution)/shard_map/ppermute | solution.py:393
  44.8 1.3 %collective-permute-start.16 = (bf16[360,640]{1,0:T(8,128)(2,1)S(1)}, bf16[360,640]{1,0:T(8,128)(2,1)S(1)}, u32[]{:S(2)}, u32[]{:S(2)}) collective-permute-start(bf16[360,640]{1,0:T(8,128)(2,1)S(1)} %collective-permute-done.14.refs_1_), channel_id=1, source_target_pairs={{0,4},{2,6},{4,0},{6,2},{8,12},{10,14},{12,8},{14,10},{16,20},{18,... | collective-permute-start | bytes 1382408 | tf_op jit(solution)/shard_map/ppermute | solution.py:393
  46.1 0.0 copy-done.1
  46.1 2.9 %filter_whole.4 = (bf16[360,640]{1,0:T(8,128)(2,1)S(1)}, bf16[360,640]{1,0:T(8,128)(2,1)S(1)}) custom-call(s32[17]{0:T(128)S(1)} %get-tuple-element.38.rows_ref, s32[35]{0:T(128)S(1)} %pad_add_fusion.place_ref, s32[32]{0:T(128)S(1)} %copy-done.1, f32[32,1152]{1,0:T(8,128)S(1)} %tap_lines.1.refs_0_, ...), custom_call_target="tpu_custom_call" | custom-call | flops 3019898880 | bytes 3686400 | tf_op jit(solution)/shard_map/filter_whole/pallas_call | solution.py:341
  49.1 2.2 %collective-permute-done.6.refs_6_ = bf16[360,640]{1,0:T(8,128)(2,1)S(1)} collective-permute-done((bf16[360,640]{1,0:T(8,128)(2,1)S(1)}, bf16[360,640]{1,0:T(8,128)(2,1)S(1)}, u32[]{:S(2)}, u32[]{:S(2)}) %collective-permute-start.6) | collective-permute-done | bytes 460832 | tf_op jit(solution)/shard_map/ppermute | solution.py:393
  51.3 1.3 %collective-permute-done.11.refs_4_ = bf16[360,640]{1,0:T(8,128)(2,1)S(1)} collective-permute-done((bf16[360,640]{1,0:T(8,128)(2,1)S(1)}, bf16[360,640]{1,0:T(8,128)(2,1)S(1)}, u32[]{:S(2)}, u32[]{:S(2)}) %collective-permute-start.11) | collective-permute-done | bytes 460832 | tf_op jit(solution)/shard_map/ppermute | solution.py:393
  52.6 0.3 collective-permute-start.13
  52.9 0.0 collective-permute-done.15.refs_2_
  52.9 1.9 %collective-permute-start.17 = (bf16[360,640]{1,0:T(8,128)(2,1)S(1)}, bf16[360,640]{1,0:T(8,128)(2,1)S(1)}, u32[]{:S(2)}, u32[]{:S(2)}) collective-permute-start(bf16[360,640]{1,0:T(8,128)(2,1)S(1)} %collective-permute-done.15.refs_2_), channel_id=1, source_target_pairs={{0,4},{2,6},{4,0},{6,2},{8,12},{10,14},{12,8},{14,10},{16,20},{18,... | collective-permute-start | bytes 1382408 | tf_op jit(solution)/shard_map/ppermute | solution.py:393
  54.8 0.1 collective-permute-start.7
  54.9 4.3 %collective-permute-done.12.refs_5_ = bf16[360,640]{1,0:T(8,128)(2,1)S(1)} collective-permute-done((bf16[360,640]{1,0:T(8,128)(2,1)S(1)}, bf16[360,640]{1,0:T(8,128)(2,1)S(1)}, u32[]{:S(2)}, u32[]{:S(2)}) %collective-permute-start.12) | collective-permute-done | bytes 460832 | tf_op jit(solution)/shard_map/ppermute | solution.py:393
  59.2 2.0 %collective-permute-done.16.refs_3_ = bf16[360,640]{1,0:T(8,128)(2,1)S(1)} collective-permute-done((bf16[360,640]{1,0:T(8,128)(2,1)S(1)}, bf16[360,640]{1,0:T(8,128)(2,1)S(1)}, u32[]{:S(2)}, u32[]{:S(2)}) %collective-permute-start.16) | collective-permute-done | bytes 460832 | tf_op jit(solution)/shard_map/ppermute | solution.py:393
  61.2 0.6 collective-permute-start.18
  61.8 2.9 %filter_whole.3 = (bf16[360,640]{1,0:T(8,128)(2,1)S(1)}, bf16[360,640]{1,0:T(8,128)(2,1)S(1)}) custom-call(s32[17]{0:T(128)S(1)} %get-tuple-element.38.rows_ref, s32[35]{0:T(128)S(1)} %pad_add_fusion.place_ref, s32[32]{0:T(128)S(1)} %copy-done.1, f32[32,1152]{1,0:T(8,128)S(1)} %tap_lines.1.refs_0_, bf16[360,640]{1,0:T(8,128)(2,1)S(1)} %get-tuple-element.39.refs_1_.refs_5_, ...), custom_call_target="tpu_custom_call" | custom-call | flops 3019898880 | bytes 3686400 | tf_op jit(solution)/shard_map/filter_whole/pallas_call | solution.py:341
  64.7 2.7 %collective-permute-start.20 = (bf16[360,640]{1,0:T(8,128)(2,1)S(1)}, bf16[360,640]{1,0:T(8,128)(2,1)S(1)}, u32[]{:S(2)}, u32[]{:S(2)}) collective-permute-start(bf16[360,640]{1,0:T(8,128)(2,1)S(1)} %get-tuple-element.64), channel_id=1, source_target_pairs={{0,2},{2,0},{4,6},{6,4},{8,10},{10,8},{12,14},{14,12},{16,18},{18,... | collective-permute-start | bytes 1382408 | tf_op jit(solution)/shard_map/ppermute | solution.py:393
  67.4 1.7 %collective-permute-done.13.refs_6_ = bf16[360,640]{1,0:T(8,128)(2,1)S(1)} collective-permute-done((bf16[360,640]{1,0:T(8,128)(2,1)S(1)}, bf16[360,640]{1,0:T(8,128)(2,1)S(1)}, u32[]{:S(2)}, u32[]{:S(2)}) %collective-permute-start.13) | collective-permute-done | bytes 460832 | tf_op jit(solution)/shard_map/ppermute | solution.py:393
  69.1 2.0 %collective-permute-done.17.refs_4_ = bf16[360,640]{1,0:T(8,128)(2,1)S(1)} collective-permute-done((bf16[360,640]{1,0:T(8,128)(2,1)S(1)}, bf16[360,640]{1,0:T(8,128)(2,1)S(1)}, u32[]{:S(2)}, u32[]{:S(2)}) %collective-permute-start.17) | collective-permute-done | bytes 460832 | tf_op jit(solution)/shard_map/ppermute | solution.py:393
  71.1 0.6 collective-permute-start.19
  71.7 5.0 %collective-permute-start.21 = (bf16[360,640]{1,0:T(8,128)(2,1)S(1)}, bf16[360,640]{1,0:T(8,128)(2,1)S(1)}, u32[]{:S(2)}, u32[]{:S(2)}) collective-permute-start(bf16[360,640]{1,0:T(8,128)(2,1)S(1)} %get-tuple-element.66), channel_id=1, source_target_pairs={{0,6},{2,4},{4,2},{6,0},{8,14},{10,12},{12,10},{14,8},{16,22},{18,... | collective-permute-start | bytes 1382408 | tf_op jit(solution)/shard_map/ppermute | solution.py:393
  76.7 2.5 %filter_early.1 = (f32[2,180,1280]{2,1,0:T(8,128)S(1)}, bf16[2,5,192,180]{3,2,1,0:T(8,128)(2,1)S(1)}) custom-call(s32[17]{0:T(128)S(1)} %get-tuple-element.38.rows_ref, s32[35]{0:T(128)S(1)} %pad_add_fusion.place_ref, s32[32]{0:T(128)S(1)} %copy-done.1, f32[32,1152]{1,0:T(8,128)S(1)} %tap_lines.1.refs_0_, ...), custom_call_target="tpu_custom_call" | custom-call | flops 2113929216 | bytes 3686400 | tf_op jit(solution)/shard_map/filter_early/pallas_call | solution.py:341
  79.2 2.9 %filter_whole.5 = (bf16[360,640]{1,0:T(8,128)(2,1)S(1)}, bf16[360,640]{1,0:T(8,128)(2,1)S(1)}) custom-call(s32[17]{0:T(128)S(1)} %get-tuple-element.38.rows_ref, s32[35]{0:T(128)S(1)} %pad_add_fusion.place_ref, s32[32]{0:T(128)S(1)} %copy-done.1, f32[32,1152]{1,0:T(8,128)S(1)} %tap_lines.1.refs_0_, bf16[360,640]{1,0:T(8,128)(2,1)S(1)} %collective-permute-done.8.refs_1_, ...), custom_call_target="tpu_custom_call" | custom-call | flops 3019898880 | bytes 3686400 | tf_op jit(solution)/shard_map/filter_whole/pallas_call | solution.py:341
  82.2 0.0 collective-permute-done.18.refs_2_
  82.2 2.0 %collective-permute-start.22 = (bf16[360,640]{1,0:T(8,128)(2,1)S(1)}, bf16[360,640]{1,0:T(8,128)(2,1)S(1)}, u32[]{:S(2)}, u32[]{:S(2)}) collective-permute-start(bf16[360,640]{1,0:T(8,128)(2,1)S(1)} %get-tuple-element.67), channel_id=1, source_target_pairs={{0,2},{2,0},{4,6},{6,4},{8,10},{10,8},{12,14},{14,12},{16,18},{18,... | collective-permute-start | bytes 1382408 | tf_op jit(solution)/shard_map/ppermute | solution.py:393
  84.1 4.7 %collective-permute-done.19.refs_3_ = bf16[360,640]{1,0:T(8,128)(2,1)S(1)} collective-permute-done((bf16[360,640]{1,0:T(8,128)(2,1)S(1)}, bf16[360,640]{1,0:T(8,128)(2,1)S(1)}, u32[]{:S(2)}, u32[]{:S(2)}) %collective-permute-start.19) | collective-permute-done | bytes 460832 | tf_op jit(solution)/shard_map/ppermute | solution.py:393
  88.8 1.3 %filter_late.1 = (bf16[360,640]{1,0:T(8,128)(2,1)S(1)}, bf16[360,640]{1,0:T(8,128)(2,1)S(1)}) custom-call(s32[17]{0:T(128)S(1)} %get-tuple-element.38.rows_ref, s32[35]{0:T(128)S(1)} %pad_add_fusion.place_ref, s32[32]{0:T(128)S(1)} %copy-done.1, f32[2,180,1280]{2,1,0:T(8,128)S(1)} %get-tuple-element.59.refs_0_, ...), custom_call_target="tpu_custom_call" | custom-call | flops 905969664 | bytes 3686400 | tf_op jit(solution)/shard_map/filter_late/pallas_call | solution.py:341
  90.2 1.8 %collective-permute-start.23 = (bf16[360,640]{1,0:T(8,128)(2,1)S(1)}, bf16[360,640]{1,0:T(8,128)(2,1)S(1)}, u32[]{:S(2)}, u32[]{:S(2)}) collective-permute-start(bf16[360,640]{1,0:T(8,128)(2,1)S(1)} %get-tuple-element.68), channel_id=1, source_target_pairs={{0,2},{2,0},{4,6},{6,4},{8,10},{10,8},{12,14},{14,12},{16,18},{18,... | collective-permute-start | bytes 1382408 | tf_op jit(solution)/shard_map/ppermute | solution.py:393
  92.0 0.0 collective-permute-done.7.refs_1_
  92.0 0.0 collective-permute-done.20.refs_4_
  92.0 0.1 collective-permute-done.21.refs_5_
  92.1 0.0 collective-permute-done.22.refs_6_
  92.1 1.4 %collective-permute-done.23.refs_7_ = bf16[360,640]{1,0:T(8,128)(2,1)S(1)} collective-permute-done((bf16[360,640]{1,0:T(8,128)(2,1)S(1)}, bf16[360,640]{1,0:T(8,128)(2,1)S(1)}, u32[]{:S(2)}, u32[]{:S(2)}) %collective-permute-start.23) | collective-permute-done | bytes 460832 | tf_op jit(solution)/shard_map/ppermute | solution.py:393
  93.5 2.8 %put_rows.1 = bf16[180,16,640]{2,1,0:T(8,128)(2,1)} custom-call(s32[17]{0:T(128)S(1)} %get-tuple-element.37.slots_ref, bf16[360,640]{1,0:T(8,128)(2,1)S(1)} %get-tuple-element.45.refs_0_, bf16[360,640]{1,0:T(8,128)(2,1)S(1)} %collective-permute-done.7.refs_1_, bf16[360,640]{1,0:T(8,128)(2,1)S(1)} %get-tuple-element.54.refs_2_, ...), custom_call_target="tpu_custom_call" | custom-call | flops 943718400 | bytes 7372800 | tf_op jit(solution)/shard_map/put_rows/pallas_call | solution.py:243
Async XLA Ops:
  0.0 26.5 %copy-start = (bf16[32,2880]{1,0:T(8,128)(2,1)S(1)}, bf16[32,2880]{1,0:T(8,128)(2,1)}, u32[]{:S(2)}) copy-start(bf16[32,2880]{1,0:T(8,128)(2,1)} %taps_ref.1) | copy-start | bytes 552964
  0.0 46.1 %copy-start.1 = (s32[32]{0:T(128)S(1)}, s32[32]{0:T(128)}, u32[]{:S(2)}) copy-start(s32[32]{0:T(128)} %widths_ref.9) | copy-start | bytes 388
  5.1 7.9 %collective-permute-start = (bf16[360,640]{1,0:T(8,128)(2,1)S(1)}, bf16[360,640]{1,0:T(8,128)(2,1)S(1)}, u32[]{:S(2)}, u32[]{:S(2)}) collective-permute-start(bf16[360,640]{1,0:T(8,128)(2,1)S(1)} %get-tuple-element.40), channel_id=1, source_target_pairs={{0,2},{2,0},{4,6},{6,4},{8,10},{10,8},{12,14},{14,12},{16,18},{18,... | collective-permute-start | bytes 1382408 | tf_op jit(solution)/shard_map/ppermute | solution.py:393
  5.6 15.6 %collective-permute-start.3 = (bf16[360,640]{1,0:T(8,128)(2,1)S(1)}, bf16[360,640]{1,0:T(8,128)(2,1)S(1)}, u32[]{:S(2)}, u32[]{:S(2)}) collective-permute-start(bf16[360,640]{1,0:T(8,128)(2,1)S(1)} %get-tuple-element.39.refs_1_.refs_5_), channel_id=1, source_target_pairs={{0,24},{2,26},{4,12},{6,14},{8,0},{10,2},{12,20},{14,22},{16,8},{1... | collective-permute-start | bytes 1382408 | tf_op jit(solution)/shard_map/ppermute | solution.py:393
  10.3 13.4 %collective-permute-start.1 = (bf16[360,640]{1,0:T(8,128)(2,1)S(1)}, bf16[360,640]{1,0:T(8,128)(2,1)S(1)}, u32[]{:S(2)}, u32[]{:S(2)}) collective-permute-start(bf16[360,640]{1,0:T(8,128)(2,1)S(1)} %get-tuple-element.41), channel_id=1, source_target_pairs={{0,4},{2,6},{4,0},{6,2},{8,12},{10,14},{12,8},{14,10},{16,20},{18,... | collective-permute-start | bytes 1382408 | tf_op jit(solution)/shard_map/ppermute | solution.py:393
  10.3 13.4 %collective-permute-start.8 = (bf16[360,640]{1,0:T(8,128)(2,1)S(1)}, bf16[360,640]{1,0:T(8,128)(2,1)S(1)}, u32[]{:S(2)}, u32[]{:S(2)}) collective-permute-start(bf16[360,640]{1,0:T(8,128)(2,1)S(1)} %get-tuple-element.47), channel_id=1, source_target_pairs={{0,1},{1,0},{2,3},{3,2},{4,5},{5,4},{6,7},{7,6},{8,9},{9,8},{10,11... | collective-permute-start | bytes 1382408 | tf_op jit(solution)/shard_map/ppermute | solution.py:393
  11.8 20.2 %collective-permute-start.2 = (bf16[360,640]{1,0:T(8,128)(2,1)S(1)}, bf16[360,640]{1,0:T(8,128)(2,1)S(1)}, u32[]{:S(2)}, u32[]{:S(2)}) collective-permute-start(bf16[360,640]{1,0:T(8,128)(2,1)S(1)} %get-tuple-element.42), channel_id=1, source_target_pairs={{0,6},{2,4},{4,2},{6,0},{8,14},{10,12},{12,10},{14,8},{16,22},{18,... | collective-permute-start | bytes 1382408 | tf_op jit(solution)/shard_map/ppermute | solution.py:393
  13.1 20.5 %collective-permute-start.5 = (bf16[360,640]{1,0:T(8,128)(2,1)S(1)}, bf16[360,640]{1,0:T(8,128)(2,1)S(1)}, u32[]{:S(2)}, u32[]{:S(2)}) collective-permute-start(bf16[360,640]{1,0:T(8,128)(2,1)S(1)} %collective-permute-done.refs_2_.refs_6_), channel_id=1, source_target_pairs={{0,24},{2,26},{4,12},{6,14},{8,0},{10,2},{12,20},{14,22},{16,8},{1... | collective-permute-start | bytes 1382408 | tf_op jit(solution)/shard_map/ppermute | solution.py:393
  21.2 12.8 %collective-permute-start.9 = (bf16[360,640]{1,0:T(8,128)(2,1)S(1)}, bf16[360,640]{1,0:T(8,128)(2,1)S(1)}, u32[]{:S(2)}, u32[]{:S(2)}) collective-permute-start(bf16[360,640]{1,0:T(8,128)(2,1)S(1)} %get-tuple-element.49), channel_id=1, source_target_pairs={{0,3},{1,2},{2,1},{3,0},{4,7},{5,6},{6,5},{7,4},{8,11},{9,10},{10,... | collective-permute-start | bytes 1382408 | tf_op jit(solution)/shard_map/ppermute | solution.py:393
  23.7 19.7 %collective-permute-start.10 = (bf16[360,640]{1,0:T(8,128)(2,1)S(1)}, bf16[360,640]{1,0:T(8,128)(2,1)S(1)}, u32[]{:S(2)}, u32[]{:S(2)}) collective-permute-start(bf16[360,640]{1,0:T(8,128)(2,1)S(1)} %collective-permute-done.8.refs_1_), channel_id=1, source_target_pairs={{0,4},{2,6},{4,0},{6,2},{8,12},{10,14},{12,8},{14,10},{16,20},{18,... | collective-permute-start | bytes 1382408 | tf_op jit(solution)/shard_map/ppermute | solution.py:393
  26.6 16.9 %collective-permute-start.4 = (bf16[360,640]{1,0:T(8,128)(2,1)S(1)}, bf16[360,640]{1,0:T(8,128)(2,1)S(1)}, u32[]{:S(2)}, u32[]{:S(2)}) collective-permute-start(bf16[360,640]{1,0:T(8,128)(2,1)S(1)} %collective-permute-done.1.refs_3_.refs_1_), channel_id=1, source_target_pairs={{0,8},{2,10},{4,28},{6,30},{8,16},{10,18},{12,4},{14,6},{16,24},{1... | collective-permute-start | bytes 1382408 | tf_op jit(solution)/shard_map/ppermute | solution.py:393
  32.0 12.8 %collective-permute-start.14 = (bf16[360,640]{1,0:T(8,128)(2,1)S(1)}, bf16[360,640]{1,0:T(8,128)(2,1)S(1)}, u32[]{:S(2)}, u32[]{:S(2)}) collective-permute-start(bf16[360,640]{1,0:T(8,128)(2,1)S(1)} %get-tuple-element.56), channel_id=1, source_target_pairs={{0,1},{1,0},{2,3},{3,2},{4,5},{5,4},{6,7},{7,6},{8,9},{9,8},{10,11... | collective-permute-start | bytes 1382408 | tf_op jit(solution)/shard_map/ppermute | solution.py:393
  33.6 17.7 %collective-permute-start.6 = (bf16[360,640]{1,0:T(8,128)(2,1)S(1)}, bf16[360,640]{1,0:T(8,128)(2,1)S(1)}, u32[]{:S(2)}, u32[]{:S(2)}) collective-permute-start(bf16[360,640]{1,0:T(8,128)(2,1)S(1)} %collective-permute-done.2.refs_4_.refs_2_), channel_id=1, source_target_pairs={{0,8},{2,10},{4,28},{6,30},{8,16},{10,18},{12,4},{14,6},{16,24},{1... | collective-permute-start | bytes 1382408 | tf_op jit(solution)/shard_map/ppermute | solution.py:393
  34.0 18.6 %collective-permute-start.11 = (bf16[360,640]{1,0:T(8,128)(2,1)S(1)}, bf16[360,640]{1,0:T(8,128)(2,1)S(1)}, u32[]{:S(2)}, u32[]{:S(2)}) collective-permute-start(bf16[360,640]{1,0:T(8,128)(2,1)S(1)} %collective-permute-done.9.refs_2_), channel_id=1, source_target_pairs={{0,4},{2,6},{4,0},{6,2},{8,12},{10,14},{12,8},{14,10},{16,20},{18,... | collective-permute-start | bytes 1382408 | tf_op jit(solution)/shard_map/ppermute | solution.py:393
  43.5 9.4 %collective-permute-start.15 = (bf16[360,640]{1,0:T(8,128)(2,1)S(1)}, bf16[360,640]{1,0:T(8,128)(2,1)S(1)}, u32[]{:S(2)}, u32[]{:S(2)}) collective-permute-start(bf16[360,640]{1,0:T(8,128)(2,1)S(1)} %get-tuple-element.58), channel_id=1, source_target_pairs={{0,3},{1,2},{2,1},{3,0},{4,7},{5,6},{6,5},{7,4},{8,11},{9,10},{10,... | collective-permute-start | bytes 1382408 | tf_op jit(solution)/shard_map/ppermute | solution.py:393
  43.5 15.7 %collective-permute-start.12 = (bf16[360,640]{1,0:T(8,128)(2,1)S(1)}, bf16[360,640]{1,0:T(8,128)(2,1)S(1)}, u32[]{:S(2)}, u32[]{:S(2)}) collective-permute-start(bf16[360,640]{1,0:T(8,128)(2,1)S(1)} %collective-permute-done.10.refs_3_), channel_id=1, source_target_pairs={{0,8},{2,10},{4,28},{6,30},{8,16},{10,18},{12,4},{14,6},{16,24},{1... | collective-permute-start | bytes 1382408 | tf_op jit(solution)/shard_map/ppermute | solution.py:393
  44.8 16.4 %collective-permute-start.16 = (bf16[360,640]{1,0:T(8,128)(2,1)S(1)}, bf16[360,640]{1,0:T(8,128)(2,1)S(1)}, u32[]{:S(2)}, u32[]{:S(2)}) collective-permute-start(bf16[360,640]{1,0:T(8,128)(2,1)S(1)} %collective-permute-done.14.refs_1_), channel_id=1, source_target_pairs={{0,4},{2,6},{4,0},{6,2},{8,12},{10,14},{12,8},{14,10},{16,20},{18,... | collective-permute-start | bytes 1382408 | tf_op jit(solution)/shard_map/ppermute | solution.py:393
  52.6 16.5 %collective-permute-start.13 = (bf16[360,640]{1,0:T(8,128)(2,1)S(1)}, bf16[360,640]{1,0:T(8,128)(2,1)S(1)}, u32[]{:S(2)}, u32[]{:S(2)}) collective-permute-start(bf16[360,640]{1,0:T(8,128)(2,1)S(1)} %collective-permute-done.11.refs_4_), channel_id=1, source_target_pairs={{0,8},{2,10},{4,28},{6,30},{8,16},{10,18},{12,4},{14,6},{16,24},{1... | collective-permute-start | bytes 1382408 | tf_op jit(solution)/shard_map/ppermute | solution.py:393
  52.9 18.2 %collective-permute-start.17 = (bf16[360,640]{1,0:T(8,128)(2,1)S(1)}, bf16[360,640]{1,0:T(8,128)(2,1)S(1)}, u32[]{:S(2)}, u32[]{:S(2)}) collective-permute-start(bf16[360,640]{1,0:T(8,128)(2,1)S(1)} %collective-permute-done.15.refs_2_), channel_id=1, source_target_pairs={{0,4},{2,6},{4,0},{6,2},{8,12},{10,14},{12,8},{14,10},{16,20},{18,... | collective-permute-start | bytes 1382408 | tf_op jit(solution)/shard_map/ppermute | solution.py:393
  54.8 37.2 %collective-permute-start.7 = (bf16[360,640]{1,0:T(8,128)(2,1)S(1)}, bf16[360,640]{1,0:T(8,128)(2,1)S(1)}, u32[]{:S(2)}, u32[]{:S(2)}) collective-permute-start(bf16[360,640]{1,0:T(8,128)(2,1)S(1)} %get-tuple-element.46), channel_id=1, source_target_pairs={{0,4},{2,6},{4,0},{6,2},{8,12},{10,14},{12,8},{14,10},{16,20},{18,... | collective-permute-start | bytes 1382408 | tf_op jit(solution)/shard_map/ppermute | solution.py:393
  61.2 20.9 %collective-permute-start.18 = (bf16[360,640]{1,0:T(8,128)(2,1)S(1)}, bf16[360,640]{1,0:T(8,128)(2,1)S(1)}, u32[]{:S(2)}, u32[]{:S(2)}) collective-permute-start(bf16[360,640]{1,0:T(8,128)(2,1)S(1)} %collective-permute-done.16.refs_3_), channel_id=1, source_target_pairs={{0,8},{2,10},{4,28},{6,30},{8,16},{10,18},{12,4},{14,6},{16,24},{1... | collective-permute-start | bytes 1382408 | tf_op jit(solution)/shard_map/ppermute | solution.py:393
  64.7 27.3 %collective-permute-start.20 = (bf16[360,640]{1,0:T(8,128)(2,1)S(1)}, bf16[360,640]{1,0:T(8,128)(2,1)S(1)}, u32[]{:S(2)}, u32[]{:S(2)}) collective-permute-start(bf16[360,640]{1,0:T(8,128)(2,1)S(1)} %get-tuple-element.64), channel_id=1, source_target_pairs={{0,2},{2,0},{4,6},{6,4},{8,10},{10,8},{12,14},{14,12},{16,18},{18,... | collective-permute-start | bytes 1382408 | tf_op jit(solution)/shard_map/ppermute | solution.py:393
  71.1 17.7 %collective-permute-start.19 = (bf16[360,640]{1,0:T(8,128)(2,1)S(1)}, bf16[360,640]{1,0:T(8,128)(2,1)S(1)}, u32[]{:S(2)}, u32[]{:S(2)}) collective-permute-start(bf16[360,640]{1,0:T(8,128)(2,1)S(1)} %collective-permute-done.17.refs_4_), channel_id=1, source_target_pairs={{0,8},{2,10},{4,28},{6,30},{8,16},{10,18},{12,4},{14,6},{16,24},{1... | collective-permute-start | bytes 1382408 | tf_op jit(solution)/shard_map/ppermute | solution.py:393
  71.7 20.4 %collective-permute-start.21 = (bf16[360,640]{1,0:T(8,128)(2,1)S(1)}, bf16[360,640]{1,0:T(8,128)(2,1)S(1)}, u32[]{:S(2)}, u32[]{:S(2)}) collective-permute-start(bf16[360,640]{1,0:T(8,128)(2,1)S(1)} %get-tuple-element.66), channel_id=1, source_target_pairs={{0,6},{2,4},{4,2},{6,0},{8,14},{10,12},{12,10},{14,8},{16,22},{18,... | collective-permute-start | bytes 1382408 | tf_op jit(solution)/shard_map/ppermute | solution.py:393
  82.2 9.9 %collective-permute-start.22 = (bf16[360,640]{1,0:T(8,128)(2,1)S(1)}, bf16[360,640]{1,0:T(8,128)(2,1)S(1)}, u32[]{:S(2)}, u32[]{:S(2)}) collective-permute-start(bf16[360,640]{1,0:T(8,128)(2,1)S(1)} %get-tuple-element.67), channel_id=1, source_target_pairs={{0,2},{2,0},{4,6},{6,4},{8,10},{10,8},{12,14},{14,12},{16,18},{18,... | collective-permute-start | bytes 1382408 | tf_op jit(solution)/shard_map/ppermute | solution.py:393
  90.2 3.3 %collective-permute-start.23 = (bf16[360,640]{1,0:T(8,128)(2,1)S(1)}, bf16[360,640]{1,0:T(8,128)(2,1)S(1)}, u32[]{:S(2)}, u32[]{:S(2)}) collective-permute-start(bf16[360,640]{1,0:T(8,128)(2,1)S(1)} %get-tuple-element.68), channel_id=1, source_target_pairs={{0,2},{2,0},{4,6},{6,4},{8,10},{10,8},{12,14},{14,12},{16,18},{18,... | collective-permute-start | bytes 1382408 | tf_op jit(solution)/shard_map/ppermute | solution.py:393

commit v16 on v15

--- a/solution.py
+++ b/solution.py
@@ -10,7 +10,7 @@
 VMEM_LIMIT = 12 * 1024 * 1024
 TAKE_VMEM_LIMIT = 50 * 1024 * 1024
 PIECE = 3
-AHEAD = 2
+AHEAD = 4
 SMEM_SPEC = pl.BlockSpec(memory_space=pltpu.SMEM)
 VMEM_SPEC = pl.BlockSpec(memory_space=pltpu.VMEM)
 HBM_SPEC = pl.BlockSpec(memory_space=pltpu.HBM)

time: 96.6 us -> 96.3 us (level)
  no operation moved by 1% of the time
where the time goes in v16:
time: 96.3 us; the launch traced here: 96.2 us
  waiting for transfers between devices  43.7 us (45%)
  starting transfers between devices  30.1 us (31%)
  Pallas kernels  21.3 us (22%)
    ppermute x24, waiting for transfers between devices, moved(): return lax.ppermute(operand, axes, pairs)  43.7 us
    ppermute x24, starting transfers between devices, moved(): return lax.ppermute(operand, axes, pairs)  30.1 us
    pallas_call x5, Pallas kernels, filter_pair(): pl.pallas_call(functools.partial(pair_kernel, lon_dev, base, tuple(plan),...  12.6 us
    pallas_call x1, Pallas kernels, take_rows(): pl.pallas_call(functools.partial(take_kernel, chunks, lat_dev, block), ou...  4.1 us
    pallas_call x1, Pallas kernels, put_rows(): pl.pallas_call(functools.partial(put_kernel, counts, lat_dev, block), out...  2.8 us
  transfers between devices with their start and end apart: 24, of which 15 were waited for; matrix products, arithmetic and copies ran while one was open for 0% of the time, Pallas kernels for 15%

profile of v16, /device:TPU:0, one launch (start us, length us, event | category | flops | bytes accessed | tf_op | source)
XLA Modules:
  0.0 96.2 jit_solution(15466591766203167584)
XLA Ops:
  0.0 0.0 copy-start
  0.0 0.0 copy-start.1
  0.0 0.8 pad_add_fusion.place_ref
  0.8 4.1 %take_rows.1 = (bf16[360,640]{1,0:T(8,128)(2,1)S(1)}, bf16[360,640]{1,0:T(8,128)(2,1)S(1)}, bf16[360,640]{1,0:T(8,128)(2,1)S(1)}, bf16[360,640]{1,0:T(8,128)(2,1...) custom-call(s32[35]{0:T(128)S(1)} %pad_add_fusion.place_ref, ...), custom_call_target="tpu_custom_call" | custom-call | flops 943718400 | bytes 7372800 | tf_op jit(solution)/shard_map/take_rows/pallas_call | solution.py:188
  4.9 0.5 collective-permute-start
  5.4 4.7 %collective-permute-start.3 = (bf16[360,640]{1,0:T(8,128)(2,1)S(1)}, bf16[360,640]{1,0:T(8,128)(2,1)S(1)}, u32[]{:S(2)}, u32[]{:S(2)}) collective-permute-start(bf16[360,640]{1,0:T(8,128)(2,1)S(1)} %get-tuple-element.39.refs_1_.refs_5_), channel_id=1, source_target_pairs={{0,24},{2,26},{4,12},{6,14},{8,0},{10,2},{12,20},{14,22},{16,8},{1... | collective-permute-start | bytes 1382408 | tf_op jit(solution)/shard_map/ppermute | solution.py:393
  10.1 0.0 collective-permute-start.1
  10.1 1.5 %collective-permute-start.8 = (bf16[360,640]{1,0:T(8,128)(2,1)S(1)}, bf16[360,640]{1,0:T(8,128)(2,1)S(1)}, u32[]{:S(2)}, u32[]{:S(2)}) collective-permute-start(bf16[360,640]{1,0:T(8,128)(2,1)S(1)} %get-tuple-element.47), channel_id=1, source_target_pairs={{0,1},{1,0},{2,3},{3,2},{4,5},{5,4},{6,7},{7,6},{8,9},{9,8},{10,11... | collective-permute-start | bytes 1382408 | tf_op jit(solution)/shard_map/ppermute | solution.py:393
  11.6 1.2 %collective-permute-start.2 = (bf16[360,640]{1,0:T(8,128)(2,1)S(1)}, bf16[360,640]{1,0:T(8,128)(2,1)S(1)}, u32[]{:S(2)}, u32[]{:S(2)}) collective-permute-start(bf16[360,640]{1,0:T(8,128)(2,1)S(1)} %get-tuple-element.42), channel_id=1, source_target_pairs={{0,6},{2,4},{4,2},{6,0},{8,14},{10,12},{12,10},{14,8},{16,22},{18,... | collective-permute-start | bytes 1382408 | tf_op jit(solution)/shard_map/ppermute | solution.py:393
  12.8 0.0 collective-permute-done.refs_2_.refs_6_
  12.8 0.5 collective-permute-start.5
  13.3 7.6 %collective-permute-done.3.refs_3_ = bf16[360,640]{1,0:T(8,128)(2,1)S(1)} collective-permute-done((bf16[360,640]{1,0:T(8,128)(2,1)S(1)}, bf16[360,640]{1,0:T(8,128)(2,1)S(1)}, u32[]{:S(2)}, u32[]{:S(2)}) %collective-permute-start.3) | collective-permute-done | bytes 460832 | tf_op jit(solution)/shard_map/ppermute | solution.py:393
  20.9 0.3 collective-permute-start.9
  21.3 2.2 %collective-permute-done.1.refs_3_.refs_1_ = bf16[360,640]{1,0:T(8,128)(2,1)S(1)} collective-permute-done((bf16[360,640]{1,0:T(8,128)(2,1)S(1)}, bf16[360,640]{1,0:T(8,128)(2,1)S(1)}, u32[]{:S(2)}, u32[]{:S(2)}) %collective-permute-start.1) | collective-permute-done | bytes 460832 | tf_op jit(solution)/shard_map/ppermute | solution.py:393
  23.5 0.0 collective-permute-done.8.refs_1_
  23.5 1.0 %collective-permute-start.10 = (bf16[360,640]{1,0:T(8,128)(2,1)S(1)}, bf16[360,640]{1,0:T(8,128)(2,1)S(1)}, u32[]{:S(2)}, u32[]{:S(2)}) collective-permute-start(bf16[360,640]{1,0:T(8,128)(2,1)S(1)} %collective-permute-done.8.refs_1_), channel_id=1, source_target_pairs={{0,4},{2,6},{4,0},{6,2},{8,12},{10,14},{12,8},{14,10},{16,20},{18,... | collective-permute-start | bytes 1382408 | tf_op jit(solution)/shard_map/ppermute | solution.py:393
  24.4 1.7 %list_rows.1 = (s32[17]{0:T(128)S(1)}, s32[17]{0:T(128)S(1)}) custom-call(s32[35]{0:T(128)S(1)} %pad_add_fusion.place_ref), custom_call_target="tpu_custom_call" | custom-call | bytes 256 | tf_op jit(solution)/shard_map/list_rows/pallas_call | solution.py:123
  26.2 0.0 copy-done
  26.2 0.1 tap_lines.1.refs_0_
  26.3 0.1 collective-permute-start.4
  26.4 5.4 %collective-permute-done.2.refs_4_.refs_2_ = bf16[360,640]{1,0:T(8,128)(2,1)S(1)} collective-permute-done((bf16[360,640]{1,0:T(8,128)(2,1)S(1)}, bf16[360,640]{1,0:T(8,128)(2,1)S(1)}, u32[]{:S(2)}, u32[]{:S(2)}) %collective-permute-start.2) | collective-permute-done | bytes 460832 | tf_op jit(solution)/shard_map/ppermute | solution.py:393
  31.8 1.5 %collective-permute-start.14 = (bf16[360,640]{1,0:T(8,128)(2,1)S(1)}, bf16[360,640]{1,0:T(8,128)(2,1)S(1)}, u32[]{:S(2)}, u32[]{:S(2)}) collective-permute-start(bf16[360,640]{1,0:T(8,128)(2,1)S(1)} %get-tuple-element.56), channel_id=1, source_target_pairs={{0,1},{1,0},{2,3},{3,2},{4,5},{5,4},{6,7},{7,6},{8,9},{9,8},{10,11... | collective-permute-start | bytes 1382408 | tf_op jit(solution)/shard_map/ppermute | solution.py:393
  33.3 0.0 collective-permute-done.5.refs_4_
  33.3 0.1 collective-permute-start.6
  33.5 0.3 collective-permute-done.9.refs_2_
  33.7 2.2 %collective-permute-start.11 = (bf16[360,640]{1,0:T(8,128)(2,1)S(1)}, bf16[360,640]{1,0:T(8,128)(2,1)S(1)}, u32[]{:S(2)}, u32[]{:S(2)}) collective-permute-start(bf16[360,640]{1,0:T(8,128)(2,1)S(1)} %collective-permute-done.9.refs_2_), channel_id=1, source_target_pairs={{0,4},{2,6},{4,0},{6,2},{8,12},{10,14},{12,8},{14,10},{16,20},{18,... | collective-permute-start | bytes 1382408 | tf_op jit(solution)/shard_map/ppermute | solution.py:393
  35.9 7.3 %collective-permute-done.10.refs_3_ = bf16[360,640]{1,0:T(8,128)(2,1)S(1)} collective-permute-done((bf16[360,640]{1,0:T(8,128)(2,1)S(1)}, bf16[360,640]{1,0:T(8,128)(2,1)S(1)}, u32[]{:S(2)}, u32[]{:S(2)}) %collective-permute-start.10) | collective-permute-done | bytes 460832 | tf_op jit(solution)/shard_map/ppermute | solution.py:393
  43.2 0.0 collective-permute-start.15
  43.2 0.0 collective-permute-done.4.refs_5_
  43.2 0.0 collective-permute-start.12
  43.2 1.3 %collective-permute-done.14.refs_1_ = bf16[360,640]{1,0:T(8,128)(2,1)S(1)} collective-permute-done((bf16[360,640]{1,0:T(8,128)(2,1)S(1)}, bf16[360,640]{1,0:T(8,128)(2,1)S(1)}, u32[]{:S(2)}, u32[]{:S(2)}) %collective-permute-start.14) | collective-permute-done | bytes 460832 | tf_op jit(solution)/shard_map/ppermute | solution.py:393
  44.6 1.3 %collective-permute-start.16 = (bf16[360,640]{1,0:T(8,128)(2,1)S(1)}, bf16[360,640]{1,0:T(8,128)(2,1)S(1)}, u32[]{:S(2)}, u32[]{:S(2)}) collective-permute-start(bf16[360,640]{1,0:T(8,128)(2,1)S(1)} %collective-permute-done.14.refs_1_), channel_id=1, source_target_pairs={{0,4},{2,6},{4,0},{6,2},{8,12},{10,14},{12,8},{14,10},{16,20},{18,... | collective-permute-start | bytes 1382408 | tf_op jit(solution)/shard_map/ppermute | solution.py:393
  45.9 0.0 copy-done.1
  45.9 2.9 %filter_whole.4 = (bf16[360,640]{1,0:T(8,128)(2,1)S(1)}, bf16[360,640]{1,0:T(8,128)(2,1)S(1)}) custom-call(s32[17]{0:T(128)S(1)} %get-tuple-element.38.rows_ref, s32[35]{0:T(128)S(1)} %pad_add_fusion.place_ref, s32[32]{0:T(128)S(1)} %copy-done.1, f32[32,1152]{1,0:T(8,128)S(1)} %tap_lines.1.refs_0_, ...), custom_call_target="tpu_custom_call" | custom-call | flops 3019898880 | bytes 3686400 | tf_op jit(solution)/shard_map/filter_whole/pallas_call | solution.py:341
  48.8 2.2 %collective-permute-done.6.refs_6_ = bf16[360,640]{1,0:T(8,128)(2,1)S(1)} collective-permute-done((bf16[360,640]{1,0:T(8,128)(2,1)S(1)}, bf16[360,640]{1,0:T(8,128)(2,1)S(1)}, u32[]{:S(2)}, u32[]{:S(2)}) %collective-permute-start.6) | collective-permute-done | bytes 460832 | tf_op jit(solution)/shard_map/ppermute | solution.py:393
  51.0 1.3 %collective-permute-done.11.refs_4_ = bf16[360,640]{1,0:T(8,128)(2,1)S(1)} collective-permute-done((bf16[360,640]{1,0:T(8,128)(2,1)S(1)}, bf16[360,640]{1,0:T(8,128)(2,1)S(1)}, u32[]{:S(2)}, u32[]{:S(2)}) %collective-permute-start.11) | collective-permute-done | bytes 460832 | tf_op jit(solution)/shard_map/ppermute | solution.py:393
  52.3 0.3 collective-permute-start.13
  52.6 0.0 collective-permute-done.15.refs_2_
  52.6 1.9 %collective-permute-start.17 = (bf16[360,640]{1,0:T(8,128)(2,1)S(1)}, bf16[360,640]{1,0:T(8,128)(2,1)S(1)}, u32[]{:S(2)}, u32[]{:S(2)}) collective-permute-start(bf16[360,640]{1,0:T(8,128)(2,1)S(1)} %collective-permute-done.15.refs_2_), channel_id=1, source_target_pairs={{0,4},{2,6},{4,0},{6,2},{8,12},{10,14},{12,8},{14,10},{16,20},{18,... | collective-permute-start | bytes 1382408 | tf_op jit(solution)/shard_map/ppermute | solution.py:393
  54.6 0.1 collective-permute-start.7
  54.7 4.3 %collective-permute-done.12.refs_5_ = bf16[360,640]{1,0:T(8,128)(2,1)S(1)} collective-permute-done((bf16[360,640]{1,0:T(8,128)(2,1)S(1)}, bf16[360,640]{1,0:T(8,128)(2,1)S(1)}, u32[]{:S(2)}, u32[]{:S(2)}) %collective-permute-start.12) | collective-permute-done | bytes 460832 | tf_op jit(solution)/shard_map/ppermute | solution.py:393
  58.9 2.0 %collective-permute-done.16.refs_3_ = bf16[360,640]{1,0:T(8,128)(2,1)S(1)} collective-permute-done((bf16[360,640]{1,0:T(8,128)(2,1)S(1)}, bf16[360,640]{1,0:T(8,128)(2,1)S(1)}, u32[]{:S(2)}, u32[]{:S(2)}) %collective-permute-start.16) | collective-permute-done | bytes 460832 | tf_op jit(solution)/shard_map/ppermute | solution.py:393
  61.0 0.6 collective-permute-start.18
  61.6 2.9 %filter_whole.3 = (bf16[360,640]{1,0:T(8,128)(2,1)S(1)}, bf16[360,640]{1,0:T(8,128)(2,1)S(1)}) custom-call(s32[17]{0:T(128)S(1)} %get-tuple-element.38.rows_ref, s32[35]{0:T(128)S(1)} %pad_add_fusion.place_ref, s32[32]{0:T(128)S(1)} %copy-done.1, f32[32,1152]{1,0:T(8,128)S(1)} %tap_lines.1.refs_0_, bf16[360,640]{1,0:T(8,128)(2,1)S(1)} %get-tuple-element.39.refs_1_.refs_5_, ...), custom_call_target="tpu_custom_call" | custom-call | flops 3019898880 | bytes 3686400 | tf_op jit(solution)/shard_map/filter_whole/pallas_call | solution.py:341
  64.5 2.7 %collective-permute-start.20 = (bf16[360,640]{1,0:T(8,128)(2,1)S(1)}, bf16[360,640]{1,0:T(8,128)(2,1)S(1)}, u32[]{:S(2)}, u32[]{:S(2)}) collective-permute-start(bf16[360,640]{1,0:T(8,128)(2,1)S(1)} %get-tuple-element.64), channel_id=1, source_target_pairs={{0,2},{2,0},{4,6},{6,4},{8,10},{10,8},{12,14},{14,12},{16,18},{18,... | collective-permute-start | bytes 1382408 | tf_op jit(solution)/shard_map/ppermute | solution.py:393
  67.2 1.6 %collective-permute-done.13.refs_6_ = bf16[360,640]{1,0:T(8,128)(2,1)S(1)} collective-permute-done((bf16[360,640]{1,0:T(8,128)(2,1)S(1)}, bf16[360,640]{1,0:T(8,128)(2,1)S(1)}, u32[]{:S(2)}, u32[]{:S(2)}) %collective-permute-start.13) | collective-permute-done | bytes 460832 | tf_op jit(solution)/shard_map/ppermute | solution.py:393
  68.8 2.0 %collective-permute-done.17.refs_4_ = bf16[360,640]{1,0:T(8,128)(2,1)S(1)} collective-permute-done((bf16[360,640]{1,0:T(8,128)(2,1)S(1)}, bf16[360,640]{1,0:T(8,128)(2,1)S(1)}, u32[]{:S(2)}, u32[]{:S(2)}) %collective-permute-start.17) | collective-permute-done | bytes 460832 | tf_op jit(solution)/shard_map/ppermute | solution.py:393
  70.9 0.6 collective-permute-start.19
  71.4 5.0 %collective-permute-start.21 = (bf16[360,640]{1,0:T(8,128)(2,1)S(1)}, bf16[360,640]{1,0:T(8,128)(2,1)S(1)}, u32[]{:S(2)}, u32[]{:S(2)}) collective-permute-start(bf16[360,640]{1,0:T(8,128)(2,1)S(1)} %get-tuple-element.66), channel_id=1, source_target_pairs={{0,6},{2,4},{4,2},{6,0},{8,14},{10,12},{12,10},{14,8},{16,22},{18,... | collective-permute-start | bytes 1382408 | tf_op jit(solution)/shard_map/ppermute | solution.py:393
  76.5 2.5 %filter_early.1 = (f32[2,180,1280]{2,1,0:T(8,128)S(1)}, bf16[2,5,192,180]{3,2,1,0:T(8,128)(2,1)S(1)}) custom-call(s32[17]{0:T(128)S(1)} %get-tuple-element.38.rows_ref, s32[35]{0:T(128)S(1)} %pad_add_fusion.place_ref, s32[32]{0:T(128)S(1)} %copy-done.1, f32[32,1152]{1,0:T(8,128)S(1)} %tap_lines.1.refs_0_, ...), custom_call_target="tpu_custom_call" | custom-call | flops 2113929216 | bytes 3686400 | tf_op jit(solution)/shard_map/filter_early/pallas_call | solution.py:341
  79.0 2.9 %filter_whole.5 = (bf16[360,640]{1,0:T(8,128)(2,1)S(1)}, bf16[360,640]{1,0:T(8,128)(2,1)S(1)}) custom-call(s32[17]{0:T(128)S(1)} %get-tuple-element.38.rows_ref, s32[35]{0:T(128)S(1)} %pad_add_fusion.place_ref, s32[32]{0:T(128)S(1)} %copy-done.1, f32[32,1152]{1,0:T(8,128)S(1)} %tap_lines.1.refs_0_, bf16[360,640]{1,0:T(8,128)(2,1)S(1)} %collective-permute-done.8.refs_1_, ...), custom_call_target="tpu_custom_call" | custom-call | flops 3019898880 | bytes 3686400 | tf_op jit(solution)/shard_map/filter_whole/pallas_call | solution.py:341
  81.9 0.0 collective-permute-done.18.refs_2_
  81.9 2.0 %collective-permute-start.22 = (bf16[360,640]{1,0:T(8,128)(2,1)S(1)}, bf16[360,640]{1,0:T(8,128)(2,1)S(1)}, u32[]{:S(2)}, u32[]{:S(2)}) collective-permute-start(bf16[360,640]{1,0:T(8,128)(2,1)S(1)} %get-tuple-element.67), channel_id=1, source_target_pairs={{0,2},{2,0},{4,6},{6,4},{8,10},{10,8},{12,14},{14,12},{16,18},{18,... | collective-permute-start | bytes 1382408 | tf_op jit(solution)/shard_map/ppermute | solution.py:393
  83.9 4.7 %collective-permute-done.19.refs_3_ = bf16[360,640]{1,0:T(8,128)(2,1)S(1)} collective-permute-done((bf16[360,640]{1,0:T(8,128)(2,1)S(1)}, bf16[360,640]{1,0:T(8,128)(2,1)S(1)}, u32[]{:S(2)}, u32[]{:S(2)}) %collective-permute-start.19) | collective-permute-done | bytes 460832 | tf_op jit(solution)/shard_map/ppermute | solution.py:393
  88.6 1.4 %filter_late.1 = (bf16[360,640]{1,0:T(8,128)(2,1)S(1)}, bf16[360,640]{1,0:T(8,128)(2,1)S(1)}) custom-call(s32[17]{0:T(128)S(1)} %get-tuple-element.38.rows_ref, s32[35]{0:T(128)S(1)} %pad_add_fusion.place_ref, s32[32]{0:T(128)S(1)} %copy-done.1, f32[2,180,1280]{2,1,0:T(8,128)S(1)} %get-tuple-element.59.refs_0_, ...), custom_call_target="tpu_custom_call" | custom-call | flops 905969664 | bytes 3686400 | tf_op jit(solution)/shard_map/filter_late/pallas_call | solution.py:341
  89.9 1.8 %collective-permute-start.23 = (bf16[360,640]{1,0:T(8,128)(2,1)S(1)}, bf16[360,640]{1,0:T(8,128)(2,1)S(1)}, u32[]{:S(2)}, u32[]{:S(2)}) collective-permute-start(bf16[360,640]{1,0:T(8,128)(2,1)S(1)} %get-tuple-element.68), channel_id=1, source_target_pairs={{0,2},{2,0},{4,6},{6,4},{8,10},{10,8},{12,14},{14,12},{16,18},{18,... | collective-permute-start | bytes 1382408 | tf_op jit(solution)/shard_map/ppermute | solution.py:393
  91.8 0.0 collective-permute-done.7.refs_1_
  91.8 0.0 collective-permute-done.20.refs_4_
  91.8 0.1 collective-permute-done.21.refs_5_
  91.8 0.0 collective-permute-done.22.refs_6_
  91.8 1.4 %collective-permute-done.23.refs_7_ = bf16[360,640]{1,0:T(8,128)(2,1)S(1)} collective-permute-done((bf16[360,640]{1,0:T(8,128)(2,1)S(1)}, bf16[360,640]{1,0:T(8,128)(2,1)S(1)}, u32[]{:S(2)}, u32[]{:S(2)}) %collective-permute-start.23) | collective-permute-done | bytes 460832 | tf_op jit(solution)/shard_map/ppermute | solution.py:393
  93.2 2.8 %put_rows.1 = bf16[180,16,640]{2,1,0:T(8,128)(2,1)} custom-call(s32[17]{0:T(128)S(1)} %get-tuple-element.37.slots_ref, bf16[360,640]{1,0:T(8,128)(2,1)S(1)} %get-tuple-element.45.refs_0_, bf16[360,640]{1,0:T(8,128)(2,1)S(1)} %collective-permute-done.7.refs_1_, bf16[360,640]{1,0:T(8,128)(2,1)S(1)} %get-tuple-element.54.refs_2_, ...), custom_call_target="tpu_custom_call" | custom-call | flops 943718400 | bytes 7372800 | tf_op jit(solution)/shard_map/put_rows/pallas_call | solution.py:243
Async XLA Ops:
  0.0 26.2 %copy-start = (bf16[32,2880]{1,0:T(8,128)(2,1)S(1)}, bf16[32,2880]{1,0:T(8,128)(2,1)}, u32[]{:S(2)}) copy-start(bf16[32,2880]{1,0:T(8,128)(2,1)} %taps_ref.1) | copy-start | bytes 552964
  0.0 45.9 %copy-start.1 = (s32[32]{0:T(128)S(1)}, s32[32]{0:T(128)}, u32[]{:S(2)}) copy-start(s32[32]{0:T(128)} %widths_ref.9) | copy-start | bytes 388
  4.9 7.9 %collective-permute-start = (bf16[360,640]{1,0:T(8,128)(2,1)S(1)}, bf16[360,640]{1,0:T(8,128)(2,1)S(1)}, u32[]{:S(2)}, u32[]{:S(2)}) collective-permute-start(bf16[360,640]{1,0:T(8,128)(2,1)S(1)} %get-tuple-element.40), channel_id=1, source_target_pairs={{0,2},{2,0},{4,6},{6,4},{8,10},{10,8},{12,14},{14,12},{16,18},{18,... | collective-permute-start | bytes 1382408 | tf_op jit(solution)/shard_map/ppermute | solution.py:393
  5.4 15.5 %collective-permute-start.3 = (bf16[360,640]{1,0:T(8,128)(2,1)S(1)}, bf16[360,640]{1,0:T(8,128)(2,1)S(1)}, u32[]{:S(2)}, u32[]{:S(2)}) collective-permute-start(bf16[360,640]{1,0:T(8,128)(2,1)S(1)} %get-tuple-element.39.refs_1_.refs_5_), channel_id=1, source_target_pairs={{0,24},{2,26},{4,12},{6,14},{8,0},{10,2},{12,20},{14,22},{16,8},{1... | collective-permute-start | bytes 1382408 | tf_op jit(solution)/shard_map/ppermute | solution.py:393
  10.1 13.4 %collective-permute-start.1 = (bf16[360,640]{1,0:T(8,128)(2,1)S(1)}, bf16[360,640]{1,0:T(8,128)(2,1)S(1)}, u32[]{:S(2)}, u32[]{:S(2)}) collective-permute-start(bf16[360,640]{1,0:T(8,128)(2,1)S(1)} %get-tuple-element.41), channel_id=1, source_target_pairs={{0,4},{2,6},{4,0},{6,2},{8,12},{10,14},{12,8},{14,10},{16,20},{18,... | collective-permute-start | bytes 1382408 | tf_op jit(solution)/shard_map/ppermute | solution.py:393
  10.1 13.4 %collective-permute-start.8 = (bf16[360,640]{1,0:T(8,128)(2,1)S(1)}, bf16[360,640]{1,0:T(8,128)(2,1)S(1)}, u32[]{:S(2)}, u32[]{:S(2)}) collective-permute-start(bf16[360,640]{1,0:T(8,128)(2,1)S(1)} %get-tuple-element.47), channel_id=1, source_target_pairs={{0,1},{1,0},{2,3},{3,2},{4,5},{5,4},{6,7},{7,6},{8,9},{9,8},{10,11... | collective-permute-start | bytes 1382408 | tf_op jit(solution)/shard_map/ppermute | solution.py:393
  11.6 20.2 %collective-permute-start.2 = (bf16[360,640]{1,0:T(8,128)(2,1)S(1)}, bf16[360,640]{1,0:T(8,128)(2,1)S(1)}, u32[]{:S(2)}, u32[]{:S(2)}) collective-permute-start(bf16[360,640]{1,0:T(8,128)(2,1)S(1)} %get-tuple-element.42), channel_id=1, source_target_pairs={{0,6},{2,4},{4,2},{6,0},{8,14},{10,12},{12,10},{14,8},{16,22},{18,... | collective-permute-start | bytes 1382408 | tf_op jit(solution)/shard_map/ppermute | solution.py:393
  12.8 20.5 %collective-permute-start.5 = (bf16[360,640]{1,0:T(8,128)(2,1)S(1)}, bf16[360,640]{1,0:T(8,128)(2,1)S(1)}, u32[]{:S(2)}, u32[]{:S(2)}) collective-permute-start(bf16[360,640]{1,0:T(8,128)(2,1)S(1)} %collective-permute-done.refs_2_.refs_6_), channel_id=1, source_target_pairs={{0,24},{2,26},{4,12},{6,14},{8,0},{10,2},{12,20},{14,22},{16,8},{1... | collective-permute-start | bytes 1382408 | tf_op jit(solution)/shard_map/ppermute | solution.py:393
  20.9 12.8 %collective-permute-start.9 = (bf16[360,640]{1,0:T(8,128)(2,1)S(1)}, bf16[360,640]{1,0:T(8,128)(2,1)S(1)}, u32[]{:S(2)}, u32[]{:S(2)}) collective-permute-start(bf16[360,640]{1,0:T(8,128)(2,1)S(1)} %get-tuple-element.49), channel_id=1, source_target_pairs={{0,3},{1,2},{2,1},{3,0},{4,7},{5,6},{6,5},{7,4},{8,11},{9,10},{10,... | collective-permute-start | bytes 1382408 | tf_op jit(solution)/shard_map/ppermute | solution.py:393
  23.5 19.7 %collective-permute-start.10 = (bf16[360,640]{1,0:T(8,128)(2,1)S(1)}, bf16[360,640]{1,0:T(8,128)(2,1)S(1)}, u32[]{:S(2)}, u32[]{:S(2)}) collective-permute-start(bf16[360,640]{1,0:T(8,128)(2,1)S(1)} %collective-permute-done.8.refs_1_), channel_id=1, source_target_pairs={{0,4},{2,6},{4,0},{6,2},{8,12},{10,14},{12,8},{14,10},{16,20},{18,... | collective-permute-start | bytes 1382408 | tf_op jit(solution)/shard_map/ppermute | solution.py:393
  26.3 16.9 %collective-permute-start.4 = (bf16[360,640]{1,0:T(8,128)(2,1)S(1)}, bf16[360,640]{1,0:T(8,128)(2,1)S(1)}, u32[]{:S(2)}, u32[]{:S(2)}) collective-permute-start(bf16[360,640]{1,0:T(8,128)(2,1)S(1)} %collective-permute-done.1.refs_3_.refs_1_), channel_id=1, source_target_pairs={{0,8},{2,10},{4,28},{6,30},{8,16},{10,18},{12,4},{14,6},{16,24},{1... | collective-permute-start | bytes 1382408 | tf_op jit(solution)/shard_map/ppermute | solution.py:393
  31.8 12.8 %collective-permute-start.14 = (bf16[360,640]{1,0:T(8,128)(2,1)S(1)}, bf16[360,640]{1,0:T(8,128)(2,1)S(1)}, u32[]{:S(2)}, u32[]{:S(2)}) collective-permute-start(bf16[360,640]{1,0:T(8,128)(2,1)S(1)} %get-tuple-element.56), channel_id=1, source_target_pairs={{0,1},{1,0},{2,3},{3,2},{4,5},{5,4},{6,7},{7,6},{8,9},{9,8},{10,11... | collective-permute-start | bytes 1382408 | tf_op jit(solution)/shard_map/ppermute | solution.py:393
  33.3 17.7 %collective-permute-start.6 = (bf16[360,640]{1,0:T(8,128)(2,1)S(1)}, bf16[360,640]{1,0:T(8,128)(2,1)S(1)}, u32[]{:S(2)}, u32[]{:S(2)}) collective-permute-start(bf16[360,640]{1,0:T(8,128)(2,1)S(1)} %collective-permute-done.2.refs_4_.refs_2_), channel_id=1, source_target_pairs={{0,8},{2,10},{4,28},{6,30},{8,16},{10,18},{12,4},{14,6},{16,24},{1... | collective-permute-start | bytes 1382408 | tf_op jit(solution)/shard_map/ppermute | solution.py:393
  33.7 18.6 %collective-permute-start.11 = (bf16[360,640]{1,0:T(8,128)(2,1)S(1)}, bf16[360,640]{1,0:T(8,128)(2,1)S(1)}, u32[]{:S(2)}, u32[]{:S(2)}) collective-permute-start(bf16[360,640]{1,0:T(8,128)(2,1)S(1)} %collective-permute-done.9.refs_2_), channel_id=1, source_target_pairs={{0,4},{2,6},{4,0},{6,2},{8,12},{10,14},{12,8},{14,10},{16,20},{18,... | collective-permute-start | bytes 1382408 | tf_op jit(solution)/shard_map/ppermute | solution.py:393
  43.2 9.4 %collective-permute-start.15 = (bf16[360,640]{1,0:T(8,128)(2,1)S(1)}, bf16[360,640]{1,0:T(8,128)(2,1)S(1)}, u32[]{:S(2)}, u32[]{:S(2)}) collective-permute-start(bf16[360,640]{1,0:T(8,128)(2,1)S(1)} %get-tuple-element.58), channel_id=1, source_target_pairs={{0,3},{1,2},{2,1},{3,0},{4,7},{5,6},{6,5},{7,4},{8,11},{9,10},{10,... | collective-permute-start | bytes 1382408 | tf_op jit(solution)/shard_map/ppermute | solution.py:393
  43.2 15.7 %collective-permute-start.12 = (bf16[360,640]{1,0:T(8,128)(2,1)S(1)}, bf16[360,640]{1,0:T(8,128)(2,1)S(1)}, u32[]{:S(2)}, u32[]{:S(2)}) collective-permute-start(bf16[360,640]{1,0:T(8,128)(2,1)S(1)} %collective-permute-done.10.refs_3_), channel_id=1, source_target_pairs={{0,8},{2,10},{4,28},{6,30},{8,16},{10,18},{12,4},{14,6},{16,24},{1... | collective-permute-start | bytes 1382408 | tf_op jit(solution)/shard_map/ppermute | solution.py:393
  44.6 16.4 %collective-permute-start.16 = (bf16[360,640]{1,0:T(8,128)(2,1)S(1)}, bf16[360,640]{1,0:T(8,128)(2,1)S(1)}, u32[]{:S(2)}, u32[]{:S(2)}) collective-permute-start(bf16[360,640]{1,0:T(8,128)(2,1)S(1)} %collective-permute-done.14.refs_1_), channel_id=1, source_target_pairs={{0,4},{2,6},{4,0},{6,2},{8,12},{10,14},{12,8},{14,10},{16,20},{18,... | collective-permute-start | bytes 1382408 | tf_op jit(solution)/shard_map/ppermute | solution.py:393
  52.3 16.5 %collective-permute-start.13 = (bf16[360,640]{1,0:T(8,128)(2,1)S(1)}, bf16[360,640]{1,0:T(8,128)(2,1)S(1)}, u32[]{:S(2)}, u32[]{:S(2)}) collective-permute-start(bf16[360,640]{1,0:T(8,128)(2,1)S(1)} %collective-permute-done.11.refs_4_), channel_id=1, source_target_pairs={{0,8},{2,10},{4,28},{6,30},{8,16},{10,18},{12,4},{14,6},{16,24},{1... | collective-permute-start | bytes 1382408 | tf_op jit(solution)/shard_map/ppermute | solution.py:393
  52.6 18.2 %collective-permute-start.17 = (bf16[360,640]{1,0:T(8,128)(2,1)S(1)}, bf16[360,640]{1,0:T(8,128)(2,1)S(1)}, u32[]{:S(2)}, u32[]{:S(2)}) collective-permute-start(bf16[360,640]{1,0:T(8,128)(2,1)S(1)} %collective-permute-done.15.refs_2_), channel_id=1, source_target_pairs={{0,4},{2,6},{4,0},{6,2},{8,12},{10,14},{12,8},{14,10},{16,20},{18,... | collective-permute-start | bytes 1382408 | tf_op jit(solution)/shard_map/ppermute | solution.py:393
  54.6 37.2 %collective-permute-start.7 = (bf16[360,640]{1,0:T(8,128)(2,1)S(1)}, bf16[360,640]{1,0:T(8,128)(2,1)S(1)}, u32[]{:S(2)}, u32[]{:S(2)}) collective-permute-start(bf16[360,640]{1,0:T(8,128)(2,1)S(1)} %get-tuple-element.46), channel_id=1, source_target_pairs={{0,4},{2,6},{4,0},{6,2},{8,12},{10,14},{12,8},{14,10},{16,20},{18,... | collective-permute-start | bytes 1382408 | tf_op jit(solution)/shard_map/ppermute | solution.py:393
  61.0 20.9 %collective-permute-start.18 = (bf16[360,640]{1,0:T(8,128)(2,1)S(1)}, bf16[360,640]{1,0:T(8,128)(2,1)S(1)}, u32[]{:S(2)}, u32[]{:S(2)}) collective-permute-start(bf16[360,640]{1,0:T(8,128)(2,1)S(1)} %collective-permute-done.16.refs_3_), channel_id=1, source_target_pairs={{0,8},{2,10},{4,28},{6,30},{8,16},{10,18},{12,4},{14,6},{16,24},{1... | collective-permute-start | bytes 1382408 | tf_op jit(solution)/shard_map/ppermute | solution.py:393
  64.5 27.3 %collective-permute-start.20 = (bf16[360,640]{1,0:T(8,128)(2,1)S(1)}, bf16[360,640]{1,0:T(8,128)(2,1)S(1)}, u32[]{:S(2)}, u32[]{:S(2)}) collective-permute-start(bf16[360,640]{1,0:T(8,128)(2,1)S(1)} %get-tuple-element.64), channel_id=1, source_target_pairs={{0,2},{2,0},{4,6},{6,4},{8,10},{10,8},{12,14},{14,12},{16,18},{18,... | collective-permute-start | bytes 1382408 | tf_op jit(solution)/shard_map/ppermute | solution.py:393
  70.9 17.7 %collective-permute-start.19 = (bf16[360,640]{1,0:T(8,128)(2,1)S(1)}, bf16[360,640]{1,0:T(8,128)(2,1)S(1)}, u32[]{:S(2)}, u32[]{:S(2)}) collective-permute-start(bf16[360,640]{1,0:T(8,128)(2,1)S(1)} %collective-permute-done.17.refs_4_), channel_id=1, source_target_pairs={{0,8},{2,10},{4,28},{6,30},{8,16},{10,18},{12,4},{14,6},{16,24},{1... | collective-permute-start | bytes 1382408 | tf_op jit(solution)/shard_map/ppermute | solution.py:393
  71.4 20.4 %collective-permute-start.21 = (bf16[360,640]{1,0:T(8,128)(2,1)S(1)}, bf16[360,640]{1,0:T(8,128)(2,1)S(1)}, u32[]{:S(2)}, u32[]{:S(2)}) collective-permute-start(bf16[360,640]{1,0:T(8,128)(2,1)S(1)} %get-tuple-element.66), channel_id=1, source_target_pairs={{0,6},{2,4},{4,2},{6,0},{8,14},{10,12},{12,10},{14,8},{16,22},{18,... | collective-permute-start | bytes 1382408 | tf_op jit(solution)/shard_map/ppermute | solution.py:393
  81.9 9.9 %collective-permute-start.22 = (bf16[360,640]{1,0:T(8,128)(2,1)S(1)}, bf16[360,640]{1,0:T(8,128)(2,1)S(1)}, u32[]{:S(2)}, u32[]{:S(2)}) collective-permute-start(bf16[360,640]{1,0:T(8,128)(2,1)S(1)} %get-tuple-element.67), channel_id=1, source_target_pairs={{0,2},{2,0},{4,6},{6,4},{8,10},{10,8},{12,14},{14,12},{16,18},{18,... | collective-permute-start | bytes 1382408 | tf_op jit(solution)/shard_map/ppermute | solution.py:393
  89.9 3.3 %collective-permute-start.23 = (bf16[360,640]{1,0:T(8,128)(2,1)S(1)}, bf16[360,640]{1,0:T(8,128)(2,1)S(1)}, u32[]{:S(2)}, u32[]{:S(2)}) collective-permute-start(bf16[360,640]{1,0:T(8,128)(2,1)S(1)} %get-tuple-element.68), channel_id=1, source_target_pairs={{0,2},{2,0},{4,6},{6,4},{8,10},{10,8},{12,14},{14,12},{16,18},{18,... | collective-permute-start | bytes 1382408 | tf_op jit(solution)/shard_map/ppermute | solution.py:393
